TPU v7x, 32 devices: a whole 2x2x4 slice. The times are simulated.
32 devices in a mesh: group: 2 (over x), seq: 16 (over z, y, core).
Axes of the slice: x: 2, y: 2, z: 4, core: 2. Of those that a mesh axis runs over, the one named last changes fastest.
Arguments:
- hidden: bfloat16 [8, 256, 1408], P('group', 'seq'), parts along dimension 0, may hold values from -14 to 14
- skip: bfloat16 [8, 256, 1408], P('group', 'seq'), parts along dimension 0, may hold values from -6 to 6
- timestep: int32 [8], P('group'), parts along dimension 0, may hold values from 0 to 999
- w_skip: bfloat16 [2816, 1408], P('seq'), may hold values from -0.109375 to 0.109375
- w_mod: bfloat16 [256, 4224], replicated, may hold values from -5 to 5
- w_qkv: bfloat16 [1408, 4224], P('seq'), may hold values from -0.15625 to 0.15625
- w_out: bfloat16 [1408, 1408], P('seq'), may hold values from -0.15625 to 0.15625
Outputs:
- result: bfloat16 [8, 256, 1408], P('group', 'seq'), parts along dimension 0
There are 2 independent parts, one for each index of `group`. A program takes and returns all parts, laid end to end along the dimension named above; an argument that names none is the same for every part. Nothing has to cross between parts.
All inputs are finite; a program needn't handle non-finite values.
Results may differ from a plain program's by a relative error of at most 0.0095.
Values may be sent and summed in bfloat16 or wider, within the bound.
No kernel may reach another device: no remote copies, remote signals or barrier semaphores. Data moves between devices by JAX's collectives and lax.ppermute only.
A program may use at most 128 MiB of HBM per device.

v0:
```python
import math

import jax
import jax.numpy as jnp
from jax import lax
from jax.sharding import PartitionSpec as P

H = 16
HD = 88
TDIM = 256


def layer_norm(x):
    mean = jnp.mean(x, axis=-1, keepdims=True)
    var = jnp.mean((x - mean) ** 2, axis=-1, keepdims=True)
    return (x - mean) * lax.rsqrt(var + 1e-06)


def attend_pair(trio):
    qpair, kpair, vpair = trio
    length = qpair.shape[0]
    block = min(512, length)
    qblocks = qpair.reshape(length // block, block, qpair.shape[1])

    def one_block(qblk):
        scores = jnp.einsum("qd,kd->qk", qblk, kpair, preferred_element_type=jnp.float32)
        probs = jax.nn.softmax(scores, axis=-1).astype(jnp.bfloat16)
        return jnp.dot(probs, vpair, preferred_element_type=jnp.float32).astype(jnp.bfloat16)

    return lax.map(one_block, qblocks).reshape(length, qpair.shape[1])


def to_heads(x, seqs, local):
    return jnp.transpose(x, (0, 2, 1, 3)).reshape(seqs * H, local, HD)


def per_device(hidden, skip, timestep, w_skip, w_mod, w_qkv, w_out):
    seqs, local, width = hidden.shape
    tok_rows = seqs * local
    combined = jnp.concatenate([hidden, skip], axis=2).reshape(tok_rows, 2 * width)
    full_skip = lax.all_gather(w_skip, "seq", axis=0, tiled=True)
    merged = jnp.dot(combined, full_skip, preferred_element_type=jnp.float32).astype(jnp.bfloat16)
    half = TDIM // 2
    freqs = jnp.exp(-math.log(10000.0) * jnp.arange(half, dtype=jnp.float32) / half)
    angles = timestep.astype(jnp.float32)[:, None] * freqs[None, :]
    embed = jnp.concatenate([jnp.cos(angles), jnp.sin(angles)], axis=1)
    act = jax.nn.silu(embed).astype(jnp.bfloat16)
    mod = jnp.dot(act, w_mod, preferred_element_type=jnp.float32)
    shift, scale, gate = (mod[:, :width], mod[:, width : 2 * width], mod[:, 2 * width :])
    base = merged.astype(jnp.float32).reshape(seqs, local, width)
    normed = (layer_norm(base) * (1.0 + scale[:, None, :]) + shift[:, None, :]).astype(jnp.bfloat16)
    normed = normed.reshape(tok_rows, width)
    full_qkv = lax.all_gather(w_qkv, "seq", axis=0, tiled=True)
    qkv = jnp.dot(normed, full_qkv, preferred_element_type=jnp.float32)
    qkv = qkv.reshape(seqs, local, 3, H, HD)
    query = (layer_norm(qkv[:, :, 0]) * HD ** (-0.5)).astype(jnp.bfloat16)
    key = layer_norm(qkv[:, :, 1]).astype(jnp.bfloat16)
    value = qkv[:, :, 2].astype(jnp.bfloat16)
    query = to_heads(query, seqs, local)
    key = to_heads(key, seqs, local)
    value = to_heads(value, seqs, local)
    query, key, value = (
        lax.all_to_all(query, "seq", split_axis=0, concat_axis=1, tiled=True),
        lax.all_to_all(key, "seq", split_axis=0, concat_axis=1, tiled=True),
        lax.all_to_all(value, "seq", split_axis=0, concat_axis=1, tiled=True),
    )
    attended = lax.map(attend_pair, (query, key, value))
    attended = lax.all_to_all(attended, "seq", split_axis=1, concat_axis=0, tiled=True)
    attended = jnp.transpose(attended.reshape(seqs, H, local, HD), (0, 2, 1, 3)).reshape(
        tok_rows, width
    )
    full_out = lax.all_gather(w_out, "seq", axis=0, tiled=True)
    projected = jnp.dot(attended, full_out, preferred_element_type=jnp.float32)
    projected = projected.reshape(seqs, local, width)
    return (base + gate[:, None, :] * projected).astype(jnp.bfloat16)


def solution(mesh):
    placed = (
        P("group", "seq", None),
        P("group", "seq", None),
        P("group"),
        P("seq", None),
        P(),
        P("seq", None),
        P("seq", None),
    )
    return jax.shard_map(
        per_device, mesh=mesh, in_specs=placed, out_specs=P("group", "seq", None), check_vma=False
    )
```

profile of v0, /device:TPU:1, one launch (start us, length us, event | category | flops | bytes accessed | tf_op | source)
XLA Modules:
  0.0 280.8 jit_solution(14518361080193916510)
XLA Ops:
  6.5 0.0 copy-start
  6.5 0.0 all-gather.4.cloned.1.call-start
  6.5 0.7 all-gather.4.cloned.1.call-update
  7.3 0.0 all-gather.6.cloned.1.call-start
  7.3 0.7 all-gather.6.cloned.1.call-update
  8.0 0.0 all-gather.8.cloned.1.call-start
  8.1 0.7 all-gather.8.cloned.1.call-update
  8.8 0.7 convert_element_type.39
  9.4 1.0 pad_maximum_fusion
  10.5 0.1 multiply_cosine_fusion
  10.6 0.0 copy-done
  10.6 0.4 fusion.28
  11.0 73.1 %all-gather.4.cloned.1.call-done = bf16[2816,1408]{1,0:T(8,128)(2,1)} async-done(((bf16[176,1408]{1,0:T(8,128)(2,1)}), bf16[2816,1408]{1,0:T(8,128)(2,1)}) %all-gather.4.cloned.1.call-update) | async-done | bytes 7929872 | tf_op jit(solution)/shard_map/all_gather | solution.py:41
  84.1 4.8 %fusion.35 = (f32[64]{0:T(128)S(1)}, f32[64,1408]{1,0:T(8,128)S(1)}) fusion(bf16[64,2816]{1,0:T(8,128)(2,1)S(1)} %bitcast.105, bf16[2816,1408]{1,0:T(8,128)(2,1)} %all-gather.4.cloned.1.call-done), kind=kOutput, calls=%fused_computation.57 | convolution fusion | flops 507781056 | bytes 8651008 | tf_op jit(solution)/shard_map/dot_general | solution.py:42
  88.9 0.2 multiply_reduce_fusion.2
  89.1 0.1 fusion.26
  89.3 91.9 %all-gather.6.cloned.1.call-done = bf16[1408,4224]{1,0:T(8,128)(2,1)} async-done(((bf16[88,4224]{1,0:T(8,128)(2,1)}), bf16[1408,4224]{1,0:T(8,128)(2,1)}) %all-gather.6.cloned.1.call-update) | async-done | bytes 11894800 | tf_op jit(solution)/shard_map/all_gather | solution.py:53
  181.1 16.3 %copy.19 = bf16[4224,1408]{1,0:T(8,128)(2,1)} copy(bf16[4224,1408]{0,1:T(8,128)(2,1)} %bitcast.102) | data formatting | bytes 23789568 | tf_op jit(solution)/shard_map/dot_general | solution.py:54
  197.4 7.9 %fusion.36 = f32[4,16,3,16,88]{4,1,3,2,0:T(8,128)S(1)} fusion(bf16[4,16,1408,1,1]{2,1,4,3,0:T(8,128)(2,1)S(1)} %bitcast.114, bf16[3,16,88,1408,1]{3,2,1,0,4:T(8,128)(2,1)} %bitcast.103), kind=kOutput, calls=%fused_computation.58 | convolution fusion | flops 761266176 | bytes 13156352 | tf_op jit(solution)/shard_map/dot_general | solution.py:54
  205.3 0.0 copy-start.1
  205.3 0.3 slice_reduce_fusion
  205.7 0.6 multiply_reduce_fusion
  206.4 0.1 copy-done.1
  206.5 1.3 multiply_convert_fusion
  207.8 16.2 %all_to_all.69 = bf16[64,16,88]{2,1,0:T(8,128)(2,1)S(1)} all-to-all(bf16[64,16,88]{2,1,0:T(8,128)(2,1)S(1)} %bitcast.112), channel_id=1, replica_groups=mesh['group'=2,'seq'=16] {'seq'}, dimensions={0} | all-to-all | bytes 360448 | tf_op jit(solution)/shard_map/all_to_all | solution.py:63
  224.0 6.4 %all-to-all-start.1 = ((bf16[64,16,88]{2,1,0:T(8,128)(2,1)}), bf16[64,16,88]{2,1,0:T(8,128)(2,1)S(1)}, u32[]{:S(2)}, u32[]{:S(2)}) async-start(bf16[64,16,88]{2,1,0:T(8,128)(2,1)} %bitcast.22), calls=%async_computation.1 | async-start | bytes 524288 | tf_op jit(solution)/shard_map/all_to_all | solution.py:64
  230.4 1.8 slice.39
  232.2 7.7 %all-to-all-done.1 = bf16[64,16,88]{2,1,0:T(8,128)(2,1)S(1)} async-done(((bf16[64,16,88]{2,1,0:T(8,128)(2,1)}), bf16[64,16,88]{2,1,0:T(8,128)(2,1)S(1)}, u32[]{:S(2)}, u32[]{:S(2)}) %all-to-all-start.1) | async-done | bytes 180256 | tf_op jit(solution)/shard_map/all_to_all | solution.py:64
  239.9 4.6 %all-to-all-start.2 = ((bf16[64,16,88]{2,1,0:T(8,128)(2,1)}), bf16[64,16,88]{2,1,0:T(8,128)(2,1)}, u32[]{:S(2)}, u32[]{:S(2)}) async-start(bf16[64,16,88]{2,1,0:T(8,128)(2,1)} %bitcast.28), calls=%async_computation.2 | async-start | bytes 524288 | tf_op jit(solution)/shard_map/all_to_all | solution.py:65
  244.5 9.6 %all-to-all-done.2 = bf16[64,16,88]{2,1,0:T(8,128)(2,1)} async-done(((bf16[64,16,88]{2,1,0:T(8,128)(2,1)}), bf16[64,16,88]{2,1,0:T(8,128)(2,1)}, u32[]{:S(2)}, u32[]{:S(2)}) %all-to-all-start.2) | async-done | bytes 180256 | tf_op jit(solution)/shard_map/all_to_all | solution.py:65
  254.1 1.0 copy.22
  255.1 2.1 while.10
  255.1 0.2 fusion.48
  255.3 0.1 fusion.49
  255.4 0.2 fusion.50
  255.7 0.2 fusion.48
  255.9 0.1 fusion.49
  255.9 0.2 fusion.50
  256.2 0.2 fusion.48
  256.4 0.1 fusion.49
  256.5 0.2 fusion.50
  256.7 0.2 fusion.48
  256.9 0.1 fusion.49
  257.0 0.2 fusion.50
  257.2 0.2 copy.23
  257.4 12.9 %all_to_all.70 = bf16[4,256,88]{2,0,1:T(4,128)(2,1)S(1)} all-to-all(bf16[4,256,88]{2,0,1:T(4,128)(2,1)S(1)} %copy.23), channel_id=1, replica_groups=mesh['group'=2,'seq'=16] {'seq'}, dimensions={1} | all-to-all | bytes 360448 | tf_op jit(solution)/shard_map/all_to_all | solution.py:68
  270.3 0.1 copy.26
  270.4 0.3 dot_general.34
  270.7 0.0 all-gather.8.cloned.1.call-done
  270.7 3.5 %fusion.22 = bf16[4,16,1408]{2,1,0:T(8,128)(2,1)} fusion(f32[4,16,1408]{2,1,0:T(8,128)S(1)} %bitcast.104, bf16[4,16,1408]{2,1,0:T(8,128)(2,1)S(1)} %dot_general.34, bf16[1408,1408]{1,0:T(8,128)(2,1)} %all-gather.8.cloned.1.call-done, f32[4,1408]{1,0:T(4,128)S(1)} %get-tuple-element.66), kind=kOutput, calls=%fused_computation.21 | convolution fusion | flops 254025728 | bytes 4708352 | tf_op jit(solution)/shard_map/dot_general | solution.py:73
  (12 shorter events, 0.2 us)
Async XLA Ops:
  6.5 4.0 %copy-start = (bf16[256,4224]{1,0:T(8,128)(2,1)S(1)}, bf16[256,4224]{1,0:T(8,128)(2,1)}, u32[]{:S(2)}) copy-start(bf16[256,4224]{1,0:T(8,128)(2,1)} %param.13) | copy-start | bytes 6488068
  6.5 77.5 %all-gather.4.cloned.1.call-start = ((), (), s32[]{:S(2)}) async-start(), calls=%async_computation.4 | async-start | bytes 8425472 | tf_op jit(solution)/shard_map/all_gather | solution.py:41
  7.3 173.9 %all-gather.6.cloned.1.call-start = ((), (), s32[]{:S(2)}) async-start(), calls=%async_computation.5 | async-start | bytes 12638208 | tf_op jit(solution)/shard_map/all_gather | solution.py:53
  8.0 262.7 %all-gather.8.cloned.1.call-start = ((), (), s32[]{:S(2)}) async-start(), calls=%async_computation.6 | async-start | bytes 4212736 | tf_op jit(solution)/shard_map/all_gather | solution.py:72
  205.3 1.2 copy-start.1
  224.0 15.9 %all-to-all-start.1 = ((bf16[64,16,88]{2,1,0:T(8,128)(2,1)}), bf16[64,16,88]{2,1,0:T(8,128)(2,1)S(1)}, u32[]{:S(2)}, u32[]{:S(2)}) async-start(bf16[64,16,88]{2,1,0:T(8,128)(2,1)} %bitcast.22), calls=%async_computation.1 | async-start | bytes 524288 | tf_op jit(solution)/shard_map/all_to_all | solution.py:64
  239.9 14.2 %all-to-all-start.2 = ((bf16[64,16,88]{2,1,0:T(8,128)(2,1)}), bf16[64,16,88]{2,1,0:T(8,128)(2,1)}, u32[]{:S(2)}, u32[]{:S(2)}) async-start(bf16[64,16,88]{2,1,0:T(8,128)(2,1)} %bitcast.28), calls=%async_computation.2 | async-start | bytes 524288 | tf_op jit(solution)/shard_map/all_to_all | solution.py:65
Sparse Core Ops, SparseCore 0:
  9.5 74.4 all-gather.3
  86.2 94.8 all-gather.5
  183.3 50.6 all-gather.7
where the time goes:
time: 282 us; the launch traced here: 281 us
  waiting for transfers between devices  184 us (65%)
  blocking collectives  29.1 us (10%)
  local copies, waits for them, and re-layouts  19.8 us (7%)
  matrix products  18.3 us (6%)
  between operations  13.3 us (5%)
  starting transfers between devices  11.1 us (4%)
  other arithmetic  4.82 us (2%)
    all_gather x1, waiting for transfers between devices, per_device(): full_qkv = lax.all_gather(w_qkv, 'seq', axis=0, tiled=True)  91.9 us
    all_gather x1, waiting for transfers between devices, per_device(): full_skip = lax.all_gather(w_skip, 'seq', axis=0, tiled=True)  73.1 us
    dot_general x1, local copies, waits for them, and re-layouts, per_device(): qkv = jnp.dot(normed, full_qkv, preferred_element_type=jnp.float32)  16.3 us
    all_to_all x1, blocking collectives, per_device(): lax.all_to_all(query, 'seq', split_axis=0, concat_axis=1, tiled=True)  16.2 us
    all_to_all x1, blocking collectives, per_device(): lax.all_to_all(attended, 'seq', split_axis=1, concat_axis=0, tiled=True)  12.9 us
    all_to_all x1, waiting for transfers between devices, per_device(): lax.all_to_all(value, 'seq', split_axis=0, concat_axis=1, tiled=True)  9.6 us
    dot_general x1, matrix products, per_device(): qkv = jnp.dot(normed, full_qkv, preferred_element_type=jnp.float32)  7.87 us
    all_to_all x1, waiting for transfers between devices, per_device(): lax.all_to_all(key, 'seq', split_axis=0, concat_axis=1, tiled=True)  7.68 us
  transfers between devices with their start and end apart: 5, of which 4 were waited for; matrix products, arithmetic and copies ran while one was open for 14% of the time, Pallas kernels for 0%

commit v1 on v0

v1 whole, which is shorter than its diff:
```python
import math

import jax
import jax.numpy as jnp
from jax import lax
from jax.sharding import PartitionSpec as P

H = 16
HD = 88
TDIM = 256
BF = jnp.bfloat16
F32 = jnp.float32


def layer_norm(x):
    mean = jnp.mean(x, axis=-1, keepdims=True)
    var = jnp.mean((x - mean) ** 2, axis=-1, keepdims=True)
    return (x - mean) * lax.rsqrt(var + 1e-06)


def modulation(timestep, w_mod):
    half = TDIM // 2
    freqs = jnp.exp(-math.log(10000.0) * jnp.arange(half, dtype=F32) / half)
    angles = timestep.astype(F32)[:, None] * freqs[None, :]
    embed = jnp.concatenate([jnp.cos(angles), jnp.sin(angles)], axis=1)
    act = jax.nn.silu(embed).astype(BF)
    return jnp.dot(act, w_mod, preferred_element_type=F32)


def attend_pair(trio):
    qpair, kpair, vpair = trio
    scores = jnp.einsum("qd,kd->qk", qpair, kpair, preferred_element_type=F32)
    probs = jax.nn.softmax(scores, axis=-1).astype(BF)
    return jnp.dot(probs, vpair, preferred_element_type=F32).astype(BF)


def to_heads(x, seqs, local):
    return jnp.transpose(x, (0, 2, 1, 3)).reshape(seqs * H, local, HD)


def gathered(hidden, skip, timestep, w_skip, w_mod, w_qkv, w_out):
    seqs, local, width = hidden.shape
    tok_rows = seqs * local
    combined = jnp.concatenate([hidden, skip], axis=2).reshape(tok_rows, 2 * width)
    full_skip = lax.all_gather(w_skip, "seq", axis=0, tiled=True)
    merged = jnp.dot(combined, full_skip, preferred_element_type=F32).astype(BF)
    mod = modulation(timestep, w_mod)
    shift, scale, gate = (mod[:, :width], mod[:, width : 2 * width], mod[:, 2 * width :])
    base = merged.astype(F32).reshape(seqs, local, width)
    normed = (layer_norm(base) * (1.0 + scale[:, None, :]) + shift[:, None, :]).astype(BF)
    full_qkv = lax.all_gather(w_qkv, "seq", axis=0, tiled=True)
    qkv = jnp.dot(normed.reshape(tok_rows, width), full_qkv, preferred_element_type=F32)
    qkv = qkv.reshape(seqs, local, 3, H, HD)
    query = (layer_norm(qkv[:, :, 0]) * HD ** (-0.5)).astype(BF)
    key = layer_norm(qkv[:, :, 1]).astype(BF)
    value = qkv[:, :, 2].astype(BF)
    trio = [
        lax.all_to_all(to_heads(x, seqs, local), "seq", split_axis=0, concat_axis=1, tiled=True)
        for x in (query, key, value)
    ]
    attended = lax.map(attend_pair, tuple(trio))
    attended = lax.all_to_all(attended, "seq", split_axis=1, concat_axis=0, tiled=True)
    attended = jnp.transpose(attended.reshape(seqs, H, local, HD), (0, 2, 1, 3))
    full_out = lax.all_gather(w_out, "seq", axis=0, tiled=True)
    projected = jnp.dot(
        attended.reshape(tok_rows, width), full_out, preferred_element_type=F32
    ).reshape(seqs, local, width)
    return (base + gate[:, None, :] * projected).astype(BF)


def in_planes(groups, n, hidden, skip, timestep, w_skip, w_mod, w_qkv, w_out):
    seqs, local, width = hidden.shape
    inner = n // seqs
    per = seqs // groups
    cols = width // groups
    g = lax.axis_index("group")
    j = lax.axis_index("seq")
    z = j // inner
    plane = [[p * inner + i for i in range(inner)] for p in range(seqs)]
    column = [[p * inner + i for p in range(seqs)] for i in range(inner)]
    toks = seqs * local

    rows = w_skip.shape[0]
    ws = lax.dynamic_slice(w_skip, (0, g * cols), (rows, cols))
    ws = lax.all_gather(ws, "seq", axis=0, tiled=True, axis_index_groups=column)
    qrows = w_qkv.shape[0]
    wq = w_qkv.reshape(qrows, 3, groups, per, inner, HD)
    wq = lax.dynamic_index_in_dim(wq, g, axis=2, keepdims=False)
    wq = wq.transpose(3, 0, 1, 2, 4).reshape(inner, qrows, 3 * per * HD)
    wq = lax.all_to_all(wq, "seq", 0, 0, tiled=True, axis_index_groups=plane)
    wq = wq.reshape(inner * qrows, 3 * per * HD)
    wq = lax.all_gather(wq, "seq", axis=0, tiled=True, axis_index_groups=column)
    wo = lax.dynamic_slice(w_out, (0, g * cols), (HD, cols))
    wo = lax.all_gather(wo, "seq", axis=0, tiled=True, axis_index_groups=column)

    times = lax.all_gather(timestep, "group", axis=0)
    mod = modulation(lax.dynamic_index_in_dim(times, z, axis=1, keepdims=False), w_mod)
    shift, scale, gate = (mod[:, :width], mod[:, width : 2 * width], mod[:, 2 * width :])
    gate = lax.dynamic_slice(gate, (0, g * cols), (groups, cols))

    x = jnp.concatenate([hidden, skip], axis=2).reshape(seqs, local, seqs, inner, rows)
    x = x.transpose(0, 3, 1, 2, 4).reshape(n, local, seqs * rows)
    x = lax.all_to_all(x, "seq", 0, 0, tiled=True).reshape(n * local, seqs * rows)
    x = lax.all_gather(x, "group", axis=0, tiled=True)
    part = jnp.dot(x, ws, preferred_element_type=F32).astype(BF)
    part = part.reshape(groups, seqs, inner, local, cols).transpose(2, 0, 1, 3, 4)
    part = part.reshape(inner, groups * toks, cols)
    part = lax.all_to_all(part, "seq", 0, 0, tiled=True, axis_index_groups=plane)
    base = jnp.sum(part.astype(F32), axis=0).astype(BF)

    merged = lax.all_gather(base, "group", axis=1, tiled=True).reshape(groups, toks, width)
    merged = jnp.stack(
        [
            lax.all_gather(merged[h], "seq", axis=0, tiled=True, axis_index_groups=plane)
            for h in range(groups)
        ]
    )
    normed = (
        layer_norm(merged.astype(F32)) * (1.0 + scale[:, None, :]) + shift[:, None, :]
    ).astype(BF)
    total = inner * toks
    qkv = jnp.dot(normed.reshape(groups * total, width), wq, preferred_element_type=F32)
    qkv = qkv.reshape(groups, total, 3, per, HD)
    query = (layer_norm(qkv[:, :, 0]) * HD ** (-0.5)).astype(BF)
    key = layer_norm(qkv[:, :, 1]).astype(BF)
    value = qkv[:, :, 2].astype(BF)
    scores = jnp.einsum("gqhd,gkhd->ghqk", query, key, preferred_element_type=F32)
    probs = jax.nn.softmax(scores, axis=-1).astype(BF)
    attended = jnp.einsum("ghqk,gkhd->gqhd", probs, value, preferred_element_type=F32)
    attended = attended.astype(BF).reshape(groups * total, per * HD)

    attended = lax.all_gather(attended, "group", axis=1, tiled=True)
    part = jnp.dot(attended, wo, preferred_element_type=F32).astype(BF)
    part = part.reshape(groups, inner, toks, cols).transpose(1, 0, 2, 3)
    part = lax.all_to_all(part, "seq", 0, 0, tiled=True, axis_index_groups=plane)
    projected = jnp.sum(part.astype(F32), axis=0)
    base = base.reshape(groups, toks, cols).astype(F32)
    out = (base + gate[:, None, :] * projected).astype(BF)
    out = lax.all_to_all(out, "group", 0, 2, tiled=True)
    out = out.reshape(seqs, local, width)
    return lax.all_to_all(out, "seq", 0, 0, tiled=True, axis_index_groups=column)


def solution(mesh):
    groups, n = mesh.shape["group"], mesh.shape["seq"]

    def per_device(*args):
        hidden, w_out = args[0], args[6]
        seqs, _, width = hidden.shape
        fits = n % seqs == 0 and w_out.shape[0] == HD and seqs % groups == 0 and width % groups == 0
        if fits:
            return in_planes(groups, n, *args)
        return gathered(*args)

    placed = (
        P("group", "seq", None),
        P("group", "seq", None),
        P("group"),
        P("seq", None),
        P(),
        P("seq", None),
        P("seq", None),
    )
    return jax.shard_map(
        per_device, mesh=mesh, in_specs=placed, out_specs=P("group", "seq", None), check_vma=False
    )
```

time: 282 us -> 212 us (0.75)
  the two profiles are of different devices: /device:TPU:1 before, /device:TPU:0 now
where the time goes in v1:
time: 212 us; the launch traced here: 211 us
  blocking collectives  104 us (49%)
  local copies, waits for them, and re-layouts  34.6 us (16%)
  waiting for transfers between devices  22.8 us (11%)
  starting transfers between devices  18.2 us (9%)
  between operations  14.3 us (7%)
  matrix products  13.8 us (7%)
  other arithmetic  2.79 us (1%)
    all_gather x1, blocking collectives, in_planes(): ws = lax.all_gather(ws, 'seq', axis=0, tiled=True, axis_index_groups=column)  23.7 us
    all_gather x2, blocking collectives, in_planes(): lax.all_gather(merged[h], 'seq', axis=0, tiled=True, axis_index_groups=pl...  17.3 us
    all_gather x1, blocking collectives, in_planes(): wo = lax.all_gather(wo, 'seq', axis=0, tiled=True, axis_index_groups=column)  16.8 us
    all_gather x1, blocking collectives, in_planes(): x = lax.all_gather(x, 'group', axis=0, tiled=True)  12.4 us
    all_gather x1, waiting for transfers between devices, in_planes(): wq = lax.all_gather(wq, 'seq', axis=0, tiled=True, axis_index_groups=column)  12.2 us
    all_to_all x2, waiting for transfers between devices, in_planes(): lax.all_to_all(part, 'seq', 0, 0, tiled=True, axis_index_groups=plane)  10.6 us
    all_to_all x1, blocking collectives, in_planes(): lax.all_to_all(out, 'seq', 0, 0, tiled=True, axis_index_groups=column)  9.33 us
    all_to_all x1, starting transfers between devices, in_planes(): lax.all_to_all(x, 'seq', 0, 0, tiled=True).reshape(n * local, seqs * rows)  7.56 us
  transfers between devices with their start and end apart: 5, of which 2 were waited for; matrix products, arithmetic and copies ran while one was open for 12% of the time, Pallas kernels for 0%

profile of v1, /device:TPU:0, one launch (start us, length us, event | category | flops | bytes accessed | tf_op | source)
XLA Modules:
  0.0 210.7 jit_solution(8858241112060528976)
XLA Ops:
  6.5 1.2 pad_maximum_fusion.2
  7.7 1.0 reshape.134
  8.7 0.2 copy.70
  8.9 1.1 reshape.135
  10.1 7.6 %all-to-all-start = ((bf16[16,16,704]{2,1,0:T(8,128)(2,1)}), bf16[16,16,704]{2,1,0:T(8,128)(2,1)}, u32[]{:S(2)}, u32[]{:S(2)}) async-start(bf16[16,16,704]{2,1,0:T(8,128)(2,1)} %reshape.135), calls=%async_computation | async-start | bytes 786432 | tf_op jit(solution)/shard_map/all_to_all | solution.py:103
  17.7 5.2 %reshape.139 = bf16[88,3,2,2,4,88]{5,4,3,2,1,0:T(4,128)(2,1)S(1)} reshape(bf16[88,4224]{1,0:T(8,128)(2,1)} %param.12) | data formatting | bytes 1486848 | tf_op jit(solution)/shard_map/reshape | solution.py:87
  22.9 0.6 dynamic-slice
  24.2 0.2 dynamic-update-slice
  24.4 0.1 reshape.146
  24.5 4.3 %all-reduce.1 = s32[2,4]{1,0:T(2,128)S(1)} all-reduce(s32[2,4]{1,0:T(2,128)S(1)} %reshape.146), channel_id=2, replica_groups=mesh['group'=2,'seq'=16] {'group'}, use_global_device_ids=true, to_apply=%add | all-reduce | flops 8 | bytes 64
  28.8 1.1 constant_dynamic-slice_fusion.4
  29.9 1.0 constant_dynamic-slice_fusion.1
  30.9 0.2 fusion.29
  31.1 0.1 multiply_cosine_fusion
  31.2 1.7 constant_dynamic-slice_fusion
  32.9 1.5 copy.69
  34.3 1.1 reshape.140
  35.5 1.0 fusion.26
  36.5 23.7 %all_gather.31 = bf16[704,704]{1,0:T(8,128)(2,1)} all-gather(bf16[176,704]{1,0:T(8,128)(2,1)S(1)} %constant_dynamic-slice_fusion.4), channel_id=1, replica_groups={{0,4,8,12},{1,5,9,13},{2,6,10,14},{3,7,11,15},{16,20,24,28},{17,21,25,2..., dimensions={0}, use_global_device_ids=true | all-gather | bytes 1239040 | tf_op jit(solution)/shard_map/all_gather | solution.py:85
  60.2 3.5 %all-to-all-start.2 = ((bf16[4,88,528]{2,1,0:T(8,128)(2,1)}), bf16[4,88,528]{2,1,0:T(8,128)(2,1)S(1)}, u32[]{:S(2)}, u32[]{:S(2)}) async-start(bf16[4,88,528]{2,1,0:T(8,128)(2,1)} %reshape.140), calls=%async_computation.2 | async-start | bytes 901120 | tf_op jit(solution)/shard_map/all_to_all | solution.py:90
  63.6 12.4 %all_gather.30 = bf16[512,704]{1,0:T(8,128)(2,1)S(1)} all-gather(bf16[256,704]{1,0:T(8,128)(2,1)} %bitcast.1), channel_id=1, replica_groups=mesh['group'=2,'seq'=16] {'group'}, dimensions={0}, use_global_device_ids=true | all-gather | bytes 1081344 | tf_op jit(solution)/shard_map/all_gather | solution.py:104
  76.0 2.9 %convolution_convert_fusion = bf16[512,704]{0,1:T(8,128)(2,1)} fusion(bf16[512,704]{1,0:T(8,128)(2,1)S(1)} %all_gather.30, bf16[704,704]{1,0:T(8,128)(2,1)} %all_gather.31), kind=kOutput, calls=%fused_computation.18 | convolution fusion | flops 507871232 | bytes 2433024 | tf_op jit(solution)/shard_map/dot_general | solution.py:105
  78.9 1.4 copy.48
  80.3 1.0 copy.49
  81.3 2.3 %copy.50 = bf16[4,128,704]{1,2,0:T(8,128)(2,1)} copy(bf16[4,128,704]{2,1,0:T(8,128)(2,1)} %bitcast.82) | data formatting | bytes 1441792 | tf_op jit(solution)/shard_map/reshape | solution.py:107
  83.6 3.6 %all-to-all-start.1 = ((bf16[4,128,704]{1,2,0:T(8,128)(2,1)}), bf16[4,128,704]{1,2,0:T(8,128)(2,1)S(1)}, u32[]{:S(2)}, u32[]{:S(2)}) async-start(bf16[4,128,704]{1,2,0:T(8,128)(2,1)} %copy.50), calls=%async_computation.1 | async-start | bytes 1441792 | tf_op jit(solution)/shard_map/all_to_all | solution.py:108
  87.2 0.0 all-gather.4.cloned.1.call-start
  87.3 16.8 %all_gather.39 = bf16[352,704]{1,0:T(8,128)(2,1)} all-gather(bf16[88,704]{1,0:T(8,128)(2,1)S(1)} %copy-done.6), channel_id=1, replica_groups={{0,4,8,12},{1,5,9,13},{2,6,10,14},{3,7,11,15},{16,20,24,28},{17,21,25,2..., dimensions={0}, use_global_device_ids=true | all-gather | bytes 619520 | tf_op jit(solution)/shard_map/all_gather | solution.py:94
  104.0 0.9 copy.55
  105.0 0.2 reduce_sum.84
  105.2 6.2 %all_gather.34 = bf16[128,1408]{0,1:T(8,128)(2,1)S(1)} all-gather(bf16[128,704]{0,1:T(8,128)(2,1)S(1)} %reduce_sum.84), channel_id=1, replica_groups=mesh['group'=2,'seq'=16] {'group'}, dimensions={1}, use_global_device_ids=true | all-gather | bytes 540672 | tf_op jit(solution)/shard_map/all_gather | solution.py:111
  111.4 0.2 fusion.38
  111.5 0.2 copy.53
  111.7 0.2 copy.52
  111.9 8.7 %all_gather.36 = bf16[256,1408]{1,0:T(8,128)(2,1)S(1)} all-gather(bf16[64,1408]{1,0:T(8,128)(2,1)S(1)} %copy.53), channel_id=1, replica_groups={{0,1,2,3},{4,5,6,7},{8,9,10,11},{12,13,14,15},{16,17,18,19},{20,21,22,2..., dimensions={0}, use_global_device_ids=true | all-gather | bytes 901120 | tf_op jit(solution)/shard_map/all_gather | solution.py:114
  120.6 8.5 %all_gather.35 = bf16[256,1408]{1,0:T(8,128)(2,1)S(1)} all-gather(bf16[64,1408]{1,0:T(8,128)(2,1)S(1)} %copy.52), channel_id=1, replica_groups={{0,1,2,3},{4,5,6,7},{8,9,10,11},{12,13,14,15},{16,17,18,19},{20,21,22,2..., dimensions={0}, use_global_device_ids=true | all-gather | bytes 901120 | tf_op jit(solution)/shard_map/all_gather | solution.py:114
  129.1 0.3 convert_reduce_fusion
  129.4 0.5 fusion.3
  129.9 0.1 copy-done.1
  130.0 12.2 %all-gather.4.cloned.1.call-done = bf16[4,352,528]{1,2,0:T(8,128)(2,1)} async-done(((bf16[1,352,528]{1,2,0:T(8,128)(2,1)}), bf16[4,352,528]{1,2,0:T(8,128)(2,1)}) %all-gather.4.cloned.1.call-update) | async-done | bytes 1486864 | tf_op jit(solution)/shard_map/all_gather | solution.py:92
  142.2 3.2 %copy.56 = bf16[4,352,528]{1,0,2:T(4,128)(2,1)} copy(bf16[4,352,528]{1,2,0:T(8,128)(2,1)} %all-gather.4.cloned.1.call-done) | data formatting | bytes 2973696 | tf_op jit(solution)/shard_map/all_gather | solution.py:92
  145.4 4.0 %reshape.151 = bf16[1408,528]{0,1:T(8,128)(2,1)} reshape(bf16[4,352,528]{1,0,2:T(4,128)(2,1)} %copy.56) | data formatting | bytes 2973696
  149.4 2.8 %fusion.9 = f32[2,256,3,2,88]{1,4,3,2,0:T(8,128)S(1)} fusion(bf16[3,2,88,1408,1]{3,2,1,0,4:T(8,128)(2,1)} %bitcast.88, f32[2,1408]{1,0:T(2,128)S(1)} %get-tuple-element.12, f32[2,1408]{1,0:T(2,128)S(1)} %get-tuple-element.13, f32[2,256]{1,0:T(2,128)S(1)} %add_rsqrt_fusion.2, f32[2,256]{1,0:T(2,128)S(1)} %broadcast_multiply_fusion.2, ...), kind=kOutput, calls=%fused_computation.12 | convolution fusion | flops 767754240 | bytes 4036608 | tf_op jit(solution)/shard_map/dot_general | solution.py:122
  152.2 0.1 slice_reduce_fusion.1
  152.3 0.9 copy-done.2
  153.2 0.1 multiply_reduce_fusion.1
  153.3 1.7 fusion.40
  155.0 1.3 fusion.17
  156.3 2.6 %fusion.16 = bf16[2,256,2,88]{1,3,2,0:T(8,128)(2,1)} fusion(f32[2,2,256]{2,1,0:T(2,128)S(1)} %fusion.40, f32[2,256,3,2,88]{1,4,3,2,0:T(8,128)S(1)} %copy-done.3, f32[2,2,256,256]{2,3,1,0:T(8,128)} %fusion.17), kind=kOutput, calls=%fused_computation.22 | convolution fusion | flops 47015168 | bytes 2461696 | tf_op jit(solution)/shard_map/ghqk,gkhd->gqhd/dot_general | solution.py:129
  158.9 1.1 copy.58
  160.1 6.9 %all_gather.38 = bf16[512,352]{0,1:T(8,128)(2,1)S(1)} all-gather(bf16[512,176]{0,1:T(8,128)(2,1)S(1)} %bitcast.91), channel_id=1, replica_groups=mesh['group'=2,'seq'=16] {'group'}, dimensions={1}, use_global_device_ids=true | all-gather | bytes 540672 | tf_op jit(solution)/shard_map/all_gather | solution.py:132
  167.0 1.4 convolution_convert_fusion.1
  168.4 1.4 copy.59
  169.8 0.9 copy.60
  170.8 3.5 %all-to-all-start.3 = ((bf16[4,2,64,704]{3,2,1,0:T(8,128)(2,1)}), bf16[4,2,64,704]{3,2,1,0:T(8,128)(2,1)S(1)}, u32[]{:S(2)}, u32[]{:S(2)}) async-start(bf16[4,2,64,704]{3,2,1,0:T(8,128)(2,1)} %copy.60), calls=%async_computation.3 | async-start | bytes 1572864 | tf_op jit(solution)/shard_map/all_to_all | solution.py:135
  174.3 0.1 constant_dynamic-slice_fusion.2
  174.3 0.9 copy.51
  175.2 10.6 %all-to-all-done.3 = bf16[4,2,64,704]{3,2,1,0:T(8,128)(2,1)S(1)} async-done(((bf16[4,2,64,704]{3,2,1,0:T(8,128)(2,1)}), bf16[4,2,64,704]{3,2,1,0:T(8,128)(2,1)S(1)}, u32[]{:S(2)}, u32[]{:S(2)}) %all-to-all-start.3) | async-done | bytes 720928 | tf_op jit(solution)/shard_map/all_to_all | solution.py:135
  185.9 0.1 convert_reduce_fusion.1
  186.1 7.4 %all_to_all.40 = bf16[2,64,704]{2,1,0:T(8,128)(2,1)S(1)} all-to-all(bf16[2,64,704]{2,1,0:T(8,128)(2,1)S(1)} %add_convert_fusion), channel_id=1, replica_groups=mesh['group'=2,'seq'=16] {'group'}, dimensions={0} | all-to-all | bytes 360448 | tf_op jit(solution)/shard_map/all_to_all | solution.py:139
  193.4 0.2 copy.62
  193.6 0.2 reshape.144
  193.8 9.3 %all_to_all.41 = bf16[4,16,1408]{2,1,0:T(8,128)(2,1)S(1)} all-to-all(bf16[4,16,1408]{2,1,0:T(8,128)(2,1)S(1)} %reshape.144), channel_id=1, replica_groups={{0,4,8,12},{1,5,9,13},{2,6,10,14},{3,7,11,15},{16,20,24,28},{17,21,25,2..., dimensions={0} | all-to-all | bytes 360448 | tf_op jit(solution)/shard_map/all_to_all | solution.py:141
  203.1 0.7 copy.73
  (32 shorter events, 0.2 us)
Async XLA Ops:
  6.5 28.9 %copy-start = (bf16[256,4224]{1,0:T(8,128)(2,1)S(1)}, bf16[256,4224]{1,0:T(8,128)(2,1)}, u32[]{:S(2)}) copy-start(bf16[256,4224]{1,0:T(8,128)(2,1)} %param.11) | copy-start | bytes 6488068
  10.1 12.9 %copy-start.9 = (u32[32]{0:T(128)S(1)}, u32[32]{0:T(128)}, u32[]{:S(2)}) copy-start(u32[32]{0:T(128)} %constant.74) | copy-start | bytes 388
  10.1 14.1 %copy-start.8 = (s32[4]{0:T(128)S(1)}, s32[4]{0:T(128)}, u32[]{:S(2)}) copy-start(s32[4]{0:T(128)} %param.9) | copy-start | bytes 52
  10.1 50.1 %all-to-all-start = ((bf16[16,16,704]{2,1,0:T(8,128)(2,1)}), bf16[16,16,704]{2,1,0:T(8,128)(2,1)}, u32[]{:S(2)}, u32[]{:S(2)}) async-start(bf16[16,16,704]{2,1,0:T(8,128)(2,1)} %reshape.135), calls=%async_computation | async-start | bytes 786432 | tf_op jit(solution)/shard_map/all_to_all | solution.py:103
  60.2 23.4 %all-to-all-start.2 = ((bf16[4,88,528]{2,1,0:T(8,128)(2,1)}), bf16[4,88,528]{2,1,0:T(8,128)(2,1)S(1)}, u32[]{:S(2)}, u32[]{:S(2)}) async-start(bf16[4,88,528]{2,1,0:T(8,128)(2,1)} %reshape.140), calls=%async_computation.2 | async-start | bytes 901120 | tf_op jit(solution)/shard_map/all_to_all | solution.py:90
  81.3 6.0 %copy-start.6 = (bf16[88,704]{1,0:T(8,128)(2,1)S(1)}, bf16[88,704]{1,0:T(8,128)(2,1)}, u32[]{:S(2)}) copy-start(bf16[88,704]{1,0:T(8,128)(2,1)} %constant_dynamic-slice_fusion) | copy-start | bytes 371716
  83.6 21.4 %copy-start.7 = (f32[2,4224]{1,0:T(2,128)S(1)}, f32[2,4224]{1,0:T(2,128)}, u32[]{:S(2)}) copy-start(f32[2,4224]{1,0:T(2,128)} %fusion.26) | copy-start | bytes 101380
  83.6 21.4 %all-to-all-start.1 = ((bf16[4,128,704]{1,2,0:T(8,128)(2,1)}), bf16[4,128,704]{1,2,0:T(8,128)(2,1)S(1)}, u32[]{:S(2)}, u32[]{:S(2)}) async-start(bf16[4,128,704]{1,2,0:T(8,128)(2,1)} %copy.50), calls=%async_computation.1 | async-start | bytes 1441792 | tf_op jit(solution)/shard_map/all_to_all | solution.py:108
  87.2 54.9 %all-gather.4.cloned.1.call-start = ((), (), s32[]{:S(2)}) async-start(), calls=%async_computation.6 | async-start | bytes 2027520 | tf_op jit(solution)/shard_map/all_gather | solution.py:92
  129.1 0.8 copy-start.1
  152.2 1.0 copy-start.2
  153.3 1.7 copy-start.3
  158.9 8.0 %copy-start.4 = (bf16[352,704]{1,0:T(8,128)(2,1)S(1)}, bf16[352,704]{1,0:T(8,128)(2,1)}, u32[]{:S(2)}) copy-start(bf16[352,704]{1,0:T(8,128)(2,1)} %all_gather.39) | copy-start | bytes 1486852
  170.8 15.1 %all-to-all-start.3 = ((bf16[4,2,64,704]{3,2,1,0:T(8,128)(2,1)}), bf16[4,2,64,704]{3,2,1,0:T(8,128)(2,1)S(1)}, u32[]{:S(2)}, u32[]{:S(2)}) async-start(bf16[4,2,64,704]{3,2,1,0:T(8,128)(2,1)} %copy.60), calls=%async_computation.3 | async-start | bytes 1572864 | tf_op jit(solution)/shard_map/all_to_all | solution.py:135
  175.2 10.8 %copy-start.5 = (f32[128,704]{1,0:T(8,128)S(1)}, f32[128,704]{1,0:T(8,128)}, u32[]{:S(2)}) copy-start(f32[128,704]{1,0:T(8,128)} %copy.51) | copy-start | bytes 1081348
Sparse Core Ops, SparseCore 0:
  105.1 36.9 all-gather.3

commit v2 on v1

v2 whole, which is shorter than its diff:
```python
import math
from functools import partial

import jax
import jax.numpy as jnp
from jax import lax
from jax.experimental import pallas as pl
from jax.experimental.pallas import tpu as pltpu
from jax.sharding import PartitionSpec as P

H = 16
HD = 88
TDIM = 256
BF = jnp.bfloat16
F32 = jnp.float32


def layer_norm(x):
    mean = jnp.mean(x, axis=-1, keepdims=True)
    var = jnp.mean((x - mean) ** 2, axis=-1, keepdims=True)
    return (x - mean) * lax.rsqrt(var + 1e-06)


def modulation(timestep, w_mod):
    half = TDIM // 2
    freqs = jnp.exp(-math.log(10000.0) * jnp.arange(half, dtype=F32) / half)
    angles = timestep.astype(F32)[:, None] * freqs[None, :]
    embed = jnp.concatenate([jnp.cos(angles), jnp.sin(angles)], axis=1)
    act = jax.nn.silu(embed).astype(BF)
    return jnp.dot(act, w_mod, preferred_element_type=F32)


def attend_pair(trio):
    qpair, kpair, vpair = trio
    scores = jnp.einsum("qd,kd->qk", qpair, kpair, preferred_element_type=F32)
    probs = jax.nn.softmax(scores, axis=-1).astype(BF)
    return jnp.dot(probs, vpair, preferred_element_type=F32).astype(BF)


def to_heads(x, seqs, local):
    return jnp.transpose(x, (0, 2, 1, 3)).reshape(seqs * H, local, HD)


def gathered(hidden, skip, timestep, w_skip, w_mod, w_qkv, w_out):
    seqs, local, width = hidden.shape
    tok_rows = seqs * local
    combined = jnp.concatenate([hidden, skip], axis=2).reshape(tok_rows, 2 * width)
    full_skip = lax.all_gather(w_skip, "seq", axis=0, tiled=True)
    merged = jnp.dot(combined, full_skip, preferred_element_type=F32).astype(BF)
    mod = modulation(timestep, w_mod)
    shift, scale, gate = (mod[:, :width], mod[:, width : 2 * width], mod[:, 2 * width :])
    base = merged.astype(F32).reshape(seqs, local, width)
    normed = (layer_norm(base) * (1.0 + scale[:, None, :]) + shift[:, None, :]).astype(BF)
    full_qkv = lax.all_gather(w_qkv, "seq", axis=0, tiled=True)
    qkv = jnp.dot(normed.reshape(tok_rows, width), full_qkv, preferred_element_type=F32)
    qkv = qkv.reshape(seqs, local, 3, H, HD)
    query = (layer_norm(qkv[:, :, 0]) * HD ** (-0.5)).astype(BF)
    key = layer_norm(qkv[:, :, 1]).astype(BF)
    value = qkv[:, :, 2].astype(BF)
    trio = [
        lax.all_to_all(to_heads(x, seqs, local), "seq", split_axis=0, concat_axis=1, tiled=True)
        for x in (query, key, value)
    ]
    attended = lax.map(attend_pair, tuple(trio))
    attended = lax.all_to_all(attended, "seq", split_axis=1, concat_axis=0, tiled=True)
    attended = jnp.transpose(attended.reshape(seqs, H, local, HD), (0, 2, 1, 3))
    full_out = lax.all_gather(w_out, "seq", axis=0, tiled=True)
    projected = jnp.dot(
        attended.reshape(tok_rows, width), full_out, preferred_element_type=F32
    ).reshape(seqs, local, width)
    return (base + gate[:, None, :] * projected).astype(BF)


class Place:
    def __init__(self, groups, n, seqs):
        self.G, self.S = groups, seqs
        self.Y = n // seqs // groups
        self.n = n
        g, j = lax.axis_index("group"), lax.axis_index("seq")
        self.x, self.z = g, j // (n // seqs)
        self.y, self.c = (j // groups) % self.Y, j % groups
        self.where = jnp.stack([self.x, self.z, self.y, self.c]).astype(jnp.int32)

    def send(self, value, to):
        pairs = []
        for x in range(self.G):
            for z in range(self.S):
                for y in range(self.Y):
                    for c in range(self.G):
                        tx, tz, ty, tc = to(x, z, y, c)
                        there = (tx % self.G, tz % self.S, ty % self.Y, tc % self.G)
                        pairs.append((self.flat(x, z, y, c), self.flat(*there)))
        return lax.ppermute(value, ("group", "seq"), pairs)

    def flat(self, x, z, y, c):
        return x * self.n + (z * self.Y + y) * self.G + c


def call(kernel, outs, where, *arrays, scratch=(), flops=0):
    moved = sum(a.size * a.dtype.itemsize for a in arrays)
    return pl.pallas_call(
        kernel,
        out_shape=[jax.ShapeDtypeStruct(s, d) for s, d in outs],
        in_specs=[pl.BlockSpec(memory_space=pltpu.SMEM)]
        + [pl.BlockSpec(memory_space=pltpu.VMEM)] * len(arrays),
        out_specs=[pl.BlockSpec(memory_space=pltpu.VMEM)] * len(outs),
        scratch_shapes=list(scratch),
        compiler_params=pltpu.CompilerParams(vmem_limit_bytes=40 * 2**20),
        cost_estimate=pl.CostEstimate(flops=flops, bytes_accessed=2 * moved, transcendentals=0),
    )(where, *arrays)


def pieces_kernel(S, where, hidden, skip, *outs):
    z = where[1]
    for s in range(S):
        outs[s][...] = hidden[(z + s) % S]
        outs[S + s][...] = skip[(z + s) % S]


def slices_kernel(G, S, Y, where, w_skip, w_qkv, w_out, *outs):
    x, y, c = where[0], where[2], where[3]
    width = w_skip.shape[1]
    block, part, half = width // (G * Y), S // G * HD, width // G
    skips, qkvs, rest = outs[:Y], outs[Y : Y + Y * G], outs[Y + Y * G :]
    for gx in range(G):
        for gy in range(Y):
            for e in range(Y):

                @pl.when((x == gx) & ((y + e) % Y == gy))
                def _():
                    b = gx * Y + gy
                    skips[e][...] = w_skip[:, b * block : (b + 1) * block]
                    for gc in range(G):
                        for f in range(G):

                            @pl.when((c + f) % G == gc)
                            def _():
                                for p in range(3):
                                    for t in range(S // G):
                                        head = ((gc * (S // G) + t) * Y + gy) * G + gx
                                        at = p * width + head * HD
                                        to = p * part + t * HD
                                        qkvs[e * G + f][:, to : to + HD] = w_qkv[:, at : at + HD]

    for gc in range(G):
        for f in range(G):

            @pl.when((c + f) % G == gc)
            def _():
                rest[f][...] = w_out[:, gc * half : (gc + 1) * half]


def merged_kernel(G, S, Y, where, *refs):
    z, y, c = where[1], where[2], where[3]
    blocks = Y * G
    hid, skp = refs[:blocks], refs[blocks : 2 * blocks]
    weights = refs[2 * blocks : 2 * blocks + G * S]
    out, xs, ws = refs[2 * blocks + G * S :]
    toks, width = hid[0].shape
    for k in range(blocks):
        xs[k * toks : (k + 1) * toks, :width] = hid[k][...]
        xs[k * toks : (k + 1) * toks, width:] = skp[k][...]
    rows = weights[0].shape[0] // Y
    for f in range(G):
        for s in range(S):
            for e in range(Y):
                j = (((z + S - s) % S) * Y + (y + Y - e) % Y) * G + (c + G - f) % G
                at = pl.multiple_of(j * rows, 16)
                ws[pl.ds(at, rows), :] = weights[f * S + s][e * rows : (e + 1) * rows, :]
    out[...] = jnp.dot(xs[...], ws[...], preferred_element_type=F32).astype(BF)


def norm88(v):
    mean = jnp.sum(v, axis=-1, keepdims=True) * (1.0 / HD)
    d = v - mean
    var = jnp.sum(d * d, axis=-1, keepdims=True) * (1.0 / HD)
    return d * lax.rsqrt(var + 1e-06)


def attend_kernel(G, S, Y, where, *refs):
    x, z, y, c = where[0], where[1], where[2], where[3]
    blocks = Y * G
    merged, (shift, scale) = refs[:blocks], refs[blocks : blocks + 2]
    refs = refs[blocks + 2 :]
    wq, wo, refs = refs[: G * S], refs[G * S : 2 * G * S], refs[2 * G * S :]
    outs, base, (norm, wqs, att) = refs[:blocks], refs[blocks], refs[blocks + 1 :]
    rows, cols = merged[0].shape
    toks = rows // blocks
    width = cols * blocks

    for f in range(G):
        for s in range(S):
            wqs[f, (z + S - s) % S] = wq[f * S + s][...]
    total = jnp.zeros((rows, 1), F32)
    wide = []
    for e in range(Y):
        for d in range(G):
            m = merged[e * G + d]
            own = [
                m[pl.ds((((em - e) % Y) * G + (dm - d) % G) * toks, toks), :]
                for em in range(Y)
                for dm in range(G)
            ]
            base[(x + d) % G * Y + (y + e) % Y] = own[0]
            wide.append(jnp.concatenate(own, axis=0).astype(F32))
            total = total + jnp.sum(wide[-1], axis=-1, keepdims=True)
    mean = total * (1.0 / width)
    square = jnp.zeros((rows, 1), F32)
    for m in wide:
        square = square + jnp.sum((m - mean) ** 2, axis=-1, keepdims=True)
    inv = lax.rsqrt(square * (1.0 / width) + 1e-06)
    for e in range(Y):
        for d in range(G):
            b = (x + d) % G * Y + (y + e) % Y
            m = wide[e * G + d]
            norm[b] = ((m - mean) * inv * (1.0 + scale[b]) + shift[b]).astype(BF)
    per = S // G
    for f in range(G):
        qkv = jnp.dot(norm[0], wqs[f, 0], preferred_element_type=F32)
        for b in range(1, blocks):
            qkv = qkv + jnp.dot(norm[b], wqs[f, b], preferred_element_type=F32)
        first = (c + G - f) % G * per
        for t in range(per):
            q, k, v = (qkv[:, (p * per + t) * HD : (p * per + t + 1) * HD] for p in range(3))
            q = (norm88(q) * HD ** (-0.5)).astype(BF)
            k = norm88(k).astype(BF)
            v = v.astype(BF)
            scores = lax.dot_general(q, k, (((1,), (1,)), ((), ())), preferred_element_type=F32)
            top = jnp.max(scores, axis=-1, keepdims=True)
            probs = jnp.exp(scores - top)
            probs = (probs / jnp.sum(probs, axis=-1, keepdims=True)).astype(BF)
            att[first + t] = jnp.dot(probs, v, preferred_element_type=F32).astype(BF)
    for f in range(G):
        acc = jnp.dot(att[z], wo[f * S][...], preferred_element_type=F32)
        for s in range(1, S):
            acc = acc + jnp.dot(
                att[(z + S - s) % S], wo[f * S + s][...], preferred_element_type=F32
            )
        acc = acc.astype(BF)
        for k in range(blocks):
            outs[k][(c + G - f) % G] = acc[k * toks : (k + 1) * toks, :]


def result_kernel(G, S, Y, where, gate, base, *refs):
    blocks = Y * G
    parts, outs = refs[:blocks], refs[blocks:]
    toks = base.shape[1]
    local = toks // S
    halves = []
    for h in range(G):
        acc = parts[0][h].astype(F32)
        for k in range(1, blocks):
            acc = acc + parts[k][h].astype(F32)
        halves.append(acc)
    projected = jnp.concatenate(halves, axis=1)
    merged = jnp.concatenate([base[b] for b in range(blocks)], axis=1).astype(F32)
    result = (merged + gate[...] * projected).astype(BF)
    for s in range(S):
        outs[s][...] = result[s * local : (s + 1) * local, :]


def home_kernel(S, where, *refs):
    z = where[1]
    for s in range(S):
        refs[S][(z + s) % S] = refs[s][...]


def in_planes(groups, n, hidden, skip, timestep, w_skip, w_mod, w_qkv, w_out):
    S, local, width = hidden.shape
    p = Place(groups, n, S)
    G, Y = p.G, p.Y
    blocks = Y * G
    cols, half = width // blocks, width // G
    toks, rows = S * local, w_skip.shape[0]
    per = S // G

    piece = ((local, width), BF)
    cut = call(partial(pieces_kernel, S), [piece] * (2 * S), p.where, hidden, skip)
    outs = [((rows, cols), BF)] * Y + [((HD, 3 * per * HD), BF)] * (Y * G) + [((HD, half), BF)] * G
    slices = call(partial(slices_kernel, G, S, Y), outs, p.where, w_skip, w_qkv, w_out)
    skips, qkvs, rest = slices[:Y], slices[Y : Y + Y * G], slices[Y + Y * G :]

    def to_plane(part):
        moved = [part[0]] + [
            p.send(part[s], lambda x, z, y, c, s=s: (x, z + s, y, c)) for s in range(1, S)
        ]
        return jnp.concatenate(moved, axis=0)

    def over_plane(value):
        return [
            p.send(value, lambda x, z, y, c, e=e, d=d: (c - d, z, y - e, x))
            for e in range(Y)
            for d in range(G)
        ]

    hid = over_plane(to_plane(cut[:S]))
    skp = over_plane(to_plane(cut[S:]))

    def ring(value):
        held = [value]
        for _ in range(1, S):
            held.append(p.send(held[-1], lambda x, z, y, c: (x, z + 1, y, c)))
        return held

    def over_cores(held):
        return held + [
            p.send(v, lambda x, z, y, c, f=f: (x, z, y, c + f)) for f in range(1, G) for v in held
        ]

    ws = [skips[0]] + [
        p.send(skips[e], lambda x, z, y, c, e=e: (x, z, y + e, c)) for e in range(1, Y)
    ]
    ws = over_cores(ring(jnp.concatenate(ws, axis=0)))

    got = {}
    for e in range(Y):
        for f in range(G):
            v = qkvs[e * G + f]
            if e or f:
                v = p.send(v, lambda x, z, y, c, e=e, f=f: (x, z, y + e, c + f))
            got[e, f] = v
    ordered = []
    for gy in range(Y):
        for gc in range(G):
            v = got[0, 0]
            for e in range(Y):
                for f in range(G):
                    if e or f:
                        here = ((p.y - e) % Y == gy) & ((p.c - f) % G == gc)
                        v = jnp.where(here, got[e, f], v)
            ordered.append(v)
    wq = over_cores(ring(jnp.concatenate(ordered, axis=0)))

    wo = rest[0]
    for f in range(1, G):
        other = lax.ppermute(
            rest[f],
            ("group", "seq"),
            [
                (p.flat(x, z, y, x), p.flat(x, z, y, (x + f) % G))
                for x in range(G)
                for z in range(S)
                for y in range(Y)
            ],
        )
        wo = jnp.where((p.c - p.x) % G == f, other, wo)
    wo = over_cores(ring(wo))

    times = lax.all_gather(timestep, "group", axis=0)
    mine = lax.dynamic_slice(times, (p.c, p.z), (1, 1)).reshape(1)
    mod = modulation(mine, w_mod)
    shift = mod[:, :width].reshape(blocks, 1, cols)
    scale = mod[:, width : 2 * width].reshape(blocks, 1, cols)
    gate = mod[:, 2 * width :]

    every = blocks * toks
    (merged,) = call(
        partial(merged_kernel, G, S, Y),
        [((every, cols), BF)],
        p.where,
        *hid,
        *skp,
        *ws,
        scratch=[pltpu.VMEM((every, 2 * width), BF), pltpu.VMEM((2 * width, cols), BF)],
        flops=4 * every * width * cols,
    )
    merged = [
        p.send(merged, lambda x, z, y, c, e=e, d=d: (x - d, z, y - e, c)) if e or d else merged
        for e in range(Y)
        for d in range(G)
    ]
    *parts, base = call(
        partial(attend_kernel, G, S, Y),
        [((G, toks, half), BF)] * blocks + [((blocks, toks, cols), BF)],
        p.where,
        *merged,
        shift,
        scale,
        *wq,
        *wo,
        scratch=[
            pltpu.VMEM((blocks, every, cols), BF),
            pltpu.VMEM((G, S, cols, 3 * per * HD), BF),
            pltpu.VMEM((S, every, HD), BF),
        ],
        flops=10 * every * width * cols,
    )
    parts = [
        p.send(parts[e * G + d], lambda x, z, y, c, e=e, d=d: (x + d, z, y + e, c))
        if e or d
        else parts[0]
        for e in range(Y)
        for d in range(G)
    ]
    result = call(partial(result_kernel, G, S, Y), [piece] * S, p.where, gate, base, *parts)
    result = [
        p.send(result[s], lambda x, z, y, c, s=s: (c, z - s, y, x)) for s in range(S)
    ]
    (out,) = call(partial(home_kernel, S), [((S, local, width), BF)], p.where, *result)
    return out


def solution(mesh):
    groups, n = mesh.shape["group"], mesh.shape["seq"]

    def per_device(*args):
        hidden, w_out = args[0], args[6]
        seqs, _, width = hidden.shape
        blocks = n // seqs
        fits = (
            n % seqs == 0
            and blocks % groups == 0
            and blocks == seqs
            and seqs % groups == 0
            and w_out.shape[0] == HD
            and width % blocks == 0
            and (width // blocks) % 16 == 0
        )
        return in_planes(groups, n, *args) if fits else gathered(*args)

    placed = (
        P("group", "seq", None),
        P("group", "seq", None),
        P("group"),
        P("seq", None),
        P(),
        P("seq", None),
        P("seq", None),
    )
    return jax.shard_map(
        per_device, mesh=mesh, in_specs=placed, out_specs=P("group", "seq", None), check_vma=False
    )
```

time: 212 us -> 169 us (0.80)
  the two profiles are of different devices: /device:TPU:0 before, /device:TPU:1 now
where the time goes in v2:
time: 169 us; the launch traced here: 168 us
  starting transfers between devices  60.1 us (36%)
  waiting for transfers between devices  52.1 us (31%)
  local copies, waits for them, and re-layouts  31.3 us (19%)
  Pallas kernels  17.6 us (10%)
  blocking collectives  3.5 us (2%)
  between operations  1.71 us (1%)
    ppermute x49, starting transfers between devices, send(): return lax.ppermute(value, ('group', 'seq'), pairs)  58.8 us
    ppermute x49, waiting for transfers between devices, send(): return lax.ppermute(value, ('group', 'seq'), pairs)  52.1 us
    unnamed x80, local copies, waits for them, and re-layouts  28.4 us
    pallas_call x6, Pallas kernels, call(): pl.pallas_call(kernel, out_shape=[jax.ShapeDtypeStruct(s, d) for s, d in...  17.6 us
    unnamed x1, blocking collectives  3.5 us
  transfers between devices with their start and end apart: 50, of which 13 were waited for; matrix products, arithmetic and copies ran while one was open for 7% of the time, Pallas kernels for 2%

profile of v2, /device:TPU:1, one launch (start us, length us, event | category | flops | bytes accessed | tf_op | source)
XLA Modules:
  0.0 167.9 jit_solution(11965782289889675908)
XLA Ops:
  0.1 1.1 copy-done.20
  1.1 0.9 copy-done.21
  2.6 2.2 %collective-permute-start = (bf16[16,1408]{1,0:T(8,128)(2,1)S(1)}, bf16[16,1408]{1,0:T(8,128)(2,1)}, u32[]{:S(2)}, u32[]{:S(2)}) collective-permute-start(bf16[16,1408]{1,0:T(8,128)(2,1)S(1)} %get-tuple-element.31), channel_id=1, source_target_pairs={{0,4},{1,5},{2,6},{3,7},{4,8},{5,9},{6,10},{7,11},{8,12},{9,13},{1... | collective-permute-start | bytes 135176 | tf_op jit(solution)/shard_map/ppermute | solution.py:93
  4.8 2.3 %collective-permute-start.1 = (bf16[16,1408]{1,0:T(8,128)(2,1)S(1)}, bf16[16,1408]{1,0:T(8,128)(2,1)}, u32[]{:S(2)}, u32[]{:S(2)}) collective-permute-start(bf16[16,1408]{1,0:T(8,128)(2,1)S(1)} %get-tuple-element.32), channel_id=1, source_target_pairs={{0,8},{1,9},{2,10},{3,11},{4,12},{5,13},{6,14},{7,15},{8,0},{9,1},... | collective-permute-start | bytes 135176 | tf_op jit(solution)/shard_map/ppermute | solution.py:93
  7.1 1.1 collective-permute-start.2
  9.9 1.1 copy-done.1
  11.0 1.0 copy-done.2
  12.1 0.9 copy-done.9
  13.0 1.4 shard_map.74
  15.2 2.9 %collective-permute-start.9 = (bf16[16,1408]{1,0:T(8,128)(2,1)S(1)}, bf16[16,1408]{1,0:T(8,128)(2,1)S(1)}, u32[]{:S(2)}, u32[]{:S(2)}) collective-permute-start(bf16[16,1408]{1,0:T(8,128)(2,1)S(1)} %get-tuple-element.37), channel_id=1, source_target_pairs={{0,12},{1,13},{2,14},{3,15},{4,0},{5,1},{6,2},{7,3},{8,4},{9,5},{1... | collective-permute-start | bytes 135176 | tf_op jit(solution)/shard_map/ppermute | solution.py:93
  18.0 1.4 constant_dynamic-update-slice_fusion.2
  19.4 3.2 %collective-permute-start.25 = (bf16[88,528]{1,0:T(8,128)(2,1)S(1)}, bf16[88,528]{1,0:T(8,128)(2,1)S(1)}, u32[]{:S(2)}, u32[]{:S(2)}) collective-permute-start(bf16[88,528]{1,0:T(8,128)(2,1)S(1)} %get-tuple-element.40), channel_id=1, source_target_pairs={{0,3},{1,2},{2,1},{3,0},{4,7},{5,6},{6,5},{7,4},{8,11},{9,10},{10,... | collective-permute-start | bytes 278792 | tf_op jit(solution)/shard_map/ppermute | solution.py:93
  22.6 1.4 constant_dynamic-update-slice_fusion.1
  24.3 1.4 constant_dynamic-update-slice_fusion.6
  26.5 1.1 collective-permute-start.14
  28.2 1.3 collective-permute-start.35
  29.5 2.0 %collective-permute-start.13 = (bf16[64,1408]{1,0:T(8,128)(2,1)}, bf16[64,1408]{1,0:T(8,128)(2,1)S(1)}, u32[]{:S(2)}, u32[]{:S(2)}) collective-permute-start(bf16[64,1408]{1,0:T(8,128)(2,1)} %constant_dynamic-update-slice_fusion.4), channel_id=1, source_target_pairs={{0,18},{1,2},{2,16},{3,0},{4,22},{5,6},{6,20},{7,4},{8,26},{9,10},... | collective-permute-start | bytes 540680 | tf_op jit(solution)/shard_map/ppermute | solution.py:93
  31.5 2.8 %collective-permute-start.12 = (bf16[64,1408]{1,0:T(8,128)(2,1)}, bf16[64,1408]{1,0:T(8,128)(2,1)S(1)}, u32[]{:S(2)}, u32[]{:S(2)}) collective-permute-start(bf16[64,1408]{1,0:T(8,128)(2,1)} %constant_dynamic-update-slice_fusion.4), channel_id=1, source_target_pairs={{0,2},{1,18},{2,0},{3,16},{4,6},{5,22},{6,4},{7,20},{8,10},{9,26},... | collective-permute-start | bytes 540680 | tf_op jit(solution)/shard_map/ppermute | solution.py:93
  34.8 1.8 %collective-permute-start.15 = (bf16[352,352]{1,0:T(8,128)(2,1)S(1)}, bf16[352,352]{1,0:T(8,128)(2,1)S(1)}, u32[]{:S(2)}, u32[]{:S(2)}) collective-permute-start(bf16[352,352]{1,0:T(8,128)(2,1)S(1)} %constant_dynamic-update-slice_fusion.8.refs_8_), channel_id=1, source_target_pairs={{0,4},{1,5},{2,6},{3,7},{4,8},{5,9},{6,10},{7,11},{8,12},{9,13},{1... | collective-permute-start | bytes 743432 | tf_op jit(solution)/shard_map/ppermute | solution.py:93
  36.6 1.4 constant_dynamic-update-slice_fusion
  38.0 0.9 collective-permute-done.13.refs_7_
  38.9 5.0 %collective-permute-start.10 = (bf16[64,1408]{1,0:T(8,128)(2,1)}, bf16[64,1408]{1,0:T(8,128)(2,1)}, u32[]{:S(2)}, u32[]{:S(2)}) collective-permute-start(bf16[64,1408]{1,0:T(8,128)(2,1)} %constant_dynamic-update-slice_fusion.4), channel_id=1, source_target_pairs={{0,0},{1,16},{2,2},{3,18},{4,4},{5,20},{6,6},{7,22},{8,8},{9,24},{... | collective-permute-start | bytes 540680 | tf_op jit(solution)/shard_map/ppermute | solution.py:93
  44.9 3.9 %collective-permute-start.5 = (bf16[64,1408]{1,0:T(8,128)(2,1)}, bf16[64,1408]{1,0:T(8,128)(2,1)S(1)}, u32[]{:S(2)}, u32[]{:S(2)}) collective-permute-start(bf16[64,1408]{1,0:T(8,128)(2,1)} %constant_dynamic-update-slice_fusion), channel_id=1, source_target_pairs={{0,2},{1,18},{2,0},{3,16},{4,6},{5,22},{6,4},{7,20},{8,10},{9,26},... | collective-permute-start | bytes 540680 | tf_op jit(solution)/shard_map/ppermute | solution.py:93
  48.7 2.0 %collective-permute-done.6.refs_3_ = bf16[64,1408]{1,0:T(8,128)(2,1)} collective-permute-done((bf16[64,1408]{1,0:T(8,128)(2,1)}, bf16[64,1408]{1,0:T(8,128)(2,1)}, u32[]{:S(2)}, u32[]{:S(2)}) %collective-permute-start.6) | collective-permute-done | bytes 180256 | tf_op jit(solution)/shard_map/ppermute | solution.py:93
  50.7 7.3 %collective-permute-start.3 = (bf16[64,1408]{1,0:T(8,128)(2,1)}, bf16[64,1408]{1,0:T(8,128)(2,1)S(1)}, u32[]{:S(2)}, u32[]{:S(2)}) collective-permute-start(bf16[64,1408]{1,0:T(8,128)(2,1)} %constant_dynamic-update-slice_fusion), channel_id=1, source_target_pairs={{0,0},{1,16},{2,2},{3,18},{4,4},{5,20},{6,6},{7,22},{8,8},{9,24},{... | collective-permute-start | bytes 540680 | tf_op jit(solution)/shard_map/ppermute | solution.py:93
  58.4 1.7 %collective-permute-start.29 = (bf16[352,528]{1,0:T(8,128)(2,1)}, bf16[352,528]{1,0:T(8,128)(2,1)}, u32[]{:S(2)}, u32[]{:S(2)}) collective-permute-start(bf16[352,528]{1,0:T(8,128)(2,1)} %collective-permute-done.28.refs_7_), channel_id=1, source_target_pairs={{0,4},{1,5},{2,6},{3,7},{4,8},{5,9},{6,10},{7,11},{8,12},{9,13},{1... | collective-permute-start | bytes 1115144 | tf_op jit(solution)/shard_map/ppermute | solution.py:93
  60.1 0.9 broadcast_select_fusion.refs_14_
  62.6 0.7 copy-done.18
  63.6 17.2 %collective-permute-done.36.refs_15_ = bf16[88,704]{1,0:T(8,128)(2,1)S(1)} collective-permute-done((bf16[88,704]{1,0:T(8,128)(2,1)S(1)}, bf16[88,704]{1,0:T(8,128)(2,1)S(1)}, u32[]{:S(2)}, u32[]{:S(2)}) %collective-permute-start.36) | collective-permute-done | bytes 123936 | tf_op jit(solution)/shard_map/ppermute | solution.py:93
  83.8 10.7 %collective-permute-done.37.refs_16_ = bf16[88,704]{1,0:T(8,128)(2,1)} collective-permute-done((bf16[88,704]{1,0:T(8,128)(2,1)S(1)}, bf16[88,704]{1,0:T(8,128)(2,1)}, u32[]{:S(2)}, u32[]{:S(2)}) %collective-permute-start.37) | collective-permute-done | bytes 123936 | tf_op jit(solution)/shard_map/ppermute | solution.py:93
  94.6 2.2 %collective-permute-start.19 = (bf16[352,352]{1,0:T(8,128)(2,1)S(1)}, bf16[352,352]{1,0:T(8,128)(2,1)}, u32[]{:S(2)}, u32[]{:S(2)}) collective-permute-start(bf16[352,352]{1,0:T(8,128)(2,1)S(1)} %collective-permute-done.15.refs_9_), channel_id=1, source_target_pairs={{0,1},{1,0},{2,3},{3,2},{4,5},{5,4},{6,7},{7,6},{8,9},{9,8},{10,11... | collective-permute-start | bytes 743432 | tf_op jit(solution)/shard_map/ppermute | solution.py:93
  96.8 0.7 copy-done.7
  98.1 0.8 copy-done.3
  100.5 3.5 %all-reduce.1 = s32[2,4]{1,0:T(2,128)S(1)} all-reduce(s32[2,4]{1,0:T(2,128)S(1)} %reshape.43), channel_id=2, replica_groups=mesh['group'=2,'seq'=16] {'group'}, use_global_device_ids=true, to_apply=%add | all-reduce | flops 8 | bytes 64
  105.2 1.9 %collective-permute-done.38.refs_17_ = bf16[88,704]{1,0:T(8,128)(2,1)} collective-permute-done((bf16[88,704]{1,0:T(8,128)(2,1)}, bf16[88,704]{1,0:T(8,128)(2,1)}, u32[]{:S(2)}, u32[]{:S(2)}) %collective-permute-start.38) | collective-permute-done | bytes 123936 | tf_op jit(solution)/shard_map/ppermute | solution.py:93
  107.1 1.3 collective-permute-start.32
  110.0 0.9 copy-done.11
  111.0 2.6 %shard_map.75.refs_0_ = bf16[256,352]{1,0:T(8,128)(2,1)S(1)} custom-call(s32[4]{0:T(128)S(1)} %pad_add_fusion.where, bf16[64,1408]{1,0:T(8,128)(2,1)S(1)} %copy-done.19, bf16[64,1408]{1,0:T(8,128)(2,1)S(1)} %copy-done.17, bf16[64,1408]{1,0:T(8,128)(2,1)S(1)} %copy-done.15, bf16[64,1408]{1,0:T(8,128)(2,1)} %collective-permute-done.6.refs_3_, ...), custom_call_target="tpu_custom_call" | custom-call | flops 507510784 | bytes 6848512 | tf_op jit(solution)/shard_map/pallas_call | solution.py:101
  114.2 0.9 collective-permute-start.24
  115.8 0.9 collective-permute-start.23
  116.7 0.8 copy-done.5
  117.5 0.9 collective-permute-start.22
  118.5 3.1 %collective-permute-done.24.refs_3_ = bf16[256,352]{1,0:T(8,128)(2,1)S(1)} collective-permute-done((bf16[256,352]{1,0:T(8,128)(2,1)S(1)}, bf16[256,352]{1,0:T(8,128)(2,1)S(1)}, u32[]{:S(2)}, u32[]{:S(2)}) %collective-permute-start.24) | collective-permute-done | bytes 180256 | tf_op jit(solution)/shard_map/ppermute | solution.py:93
  121.7 4.6 %collective-permute-done.23.refs_2_ = bf16[256,352]{1,0:T(8,128)(2,1)S(1)} collective-permute-done((bf16[256,352]{1,0:T(8,128)(2,1)S(1)}, bf16[256,352]{1,0:T(8,128)(2,1)S(1)}, u32[]{:S(2)}, u32[]{:S(2)}) %collective-permute-start.23) | collective-permute-done | bytes 180256 | tf_op jit(solution)/shard_map/ppermute | solution.py:93
  126.2 1.0 copy-done.4
  127.2 1.0 copy-done.6
  128.3 0.9 copy-done.23
  129.2 0.9 copy-done.25
  130.1 0.9 copy-done.27
  131.0 0.9 copy-done.29
  131.9 0.9 copy-done.31
  132.8 11.1 %shard_map.76 = (bf16[2,64,704]{2,1,0:T(8,128)(2,1)S(1)}, bf16[2,64,704]{2,1,0:T(8,128)(2,1)S(1)}, bf16[2,64,704]{2,1,0:T(8,128)(2,1)S(1)}, bf16[2,64,704]{2,1,0:T(8,128)(2,1)S(1)}, bf16[4,64,352]{2,1,0:T(8,128)(2,1)S(1)}) custom-call(s32[4]{0:T(128)S(1)} %pad_add_fusion.where, bf16[256,352]{1,0:T(8,128)(2,1)S(1)} %shard_map.75.refs_0_, ...), custom_call_target="tpu_custom_call" | custom-call | flops 1268776960 | bytes 9394176 | tf_op jit(solution)/shard_map/pallas_call | solution.py:101
  143.9 0.7 collective-permute-start.43
  145.2 1.4 collective-permute-start.45
  146.6 3.4 %collective-permute-done.43.refs_1_ = bf16[2,64,704]{2,1,0:T(8,128)(2,1)S(1)} collective-permute-done((bf16[2,64,704]{2,1,0:T(8,128)(2,1)S(1)}, bf16[2,64,704]{2,1,0:T(8,128)(2,1)S(1)}, u32[]{:S(2)}, u32[]{:S(2)}) %collective-permute-start.43) | collective-permute-done | bytes 180256 | tf_op jit(solution)/shard_map/ppermute | solution.py:93
  150.0 1.4 collective-permute-done.44.refs_2_
  151.4 2.2 %collective-permute-done.45.refs_3_ = bf16[2,64,704]{2,1,0:T(8,128)(2,1)S(1)} collective-permute-done((bf16[2,64,704]{2,1,0:T(8,128)(2,1)S(1)}, bf16[2,64,704]{2,1,0:T(8,128)(2,1)S(1)}, u32[]{:S(2)}, u32[]{:S(2)}) %collective-permute-start.45) | collective-permute-done | bytes 180256 | tf_op jit(solution)/shard_map/ppermute | solution.py:93
  153.5 0.7 shard_map.77
  154.2 5.2 %collective-permute-start.46 = (bf16[16,1408]{1,0:T(8,128)(2,1)S(1)}, bf16[16,1408]{1,0:T(8,128)(2,1)S(1)}, u32[]{:S(2)}, u32[]{:S(2)}) collective-permute-start(bf16[16,1408]{1,0:T(8,128)(2,1)S(1)} %get-tuple-element.51), channel_id=1, source_target_pairs={{0,0},{1,16},{2,2},{3,18},{4,4},{5,20},{6,6},{7,22},{8,8},{9,24},{... | collective-permute-start | bytes 135176 | tf_op jit(solution)/shard_map/ppermute | solution.py:93
  159.5 0.9 collective-permute-start.47
  160.4 1.8 %collective-permute-start.49 = (bf16[16,1408]{1,0:T(8,128)(2,1)S(1)}, bf16[16,1408]{1,0:T(8,128)(2,1)S(1)}, u32[]{:S(2)}, u32[]{:S(2)}) collective-permute-start(bf16[16,1408]{1,0:T(8,128)(2,1)S(1)} %get-tuple-element.54), channel_id=1, source_target_pairs={{0,4},{1,20},{2,6},{3,22},{4,8},{5,24},{6,10},{7,26},{8,12},{9,28}... | collective-permute-start | bytes 135176 | tf_op jit(solution)/shard_map/ppermute | solution.py:93
  162.2 2.0 %collective-permute-done.47.refs_1_ = bf16[16,1408]{1,0:T(8,128)(2,1)S(1)} collective-permute-done((bf16[16,1408]{1,0:T(8,128)(2,1)S(1)}, bf16[16,1408]{1,0:T(8,128)(2,1)S(1)}, u32[]{:S(2)}, u32[]{:S(2)}) %collective-permute-start.47) | collective-permute-done | bytes 45088 | tf_op jit(solution)/shard_map/ppermute | solution.py:93
  164.2 2.4 %collective-permute-done.48.refs_2_ = bf16[16,1408]{1,0:T(8,128)(2,1)S(1)} collective-permute-done((bf16[16,1408]{1,0:T(8,128)(2,1)S(1)}, bf16[16,1408]{1,0:T(8,128)(2,1)S(1)}, u32[]{:S(2)}, u32[]{:S(2)}) %collective-permute-start.48) | collective-permute-done | bytes 45088 | tf_op jit(solution)/shard_map/ppermute | solution.py:93
  166.6 1.2 shard_map.78
  (139 shorter events, 17.2 us)
Async XLA Ops:
  0.0 109.6 %copy-start = (bf16[256,4224]{1,0:T(8,128)(2,1)S(1)}, bf16[256,4224]{1,0:T(8,128)(2,1)}, u32[]{:S(2)}) copy-start(bf16[256,4224]{1,0:T(8,128)(2,1)} %param.11) | copy-start | bytes 6488068
  0.1 1.1 copy-start.20
  2.6 12.5 %collective-permute-start = (bf16[16,1408]{1,0:T(8,128)(2,1)S(1)}, bf16[16,1408]{1,0:T(8,128)(2,1)}, u32[]{:S(2)}, u32[]{:S(2)}) collective-permute-start(bf16[16,1408]{1,0:T(8,128)(2,1)S(1)} %get-tuple-element.31), channel_id=1, source_target_pairs={{0,4},{1,5},{2,6},{3,7},{4,8},{5,9},{6,10},{7,11},{8,12},{9,13},{1... | collective-permute-start | bytes 135176 | tf_op jit(solution)/shard_map/ppermute | solution.py:93
  4.8 14.6 %collective-permute-start.1 = (bf16[16,1408]{1,0:T(8,128)(2,1)S(1)}, bf16[16,1408]{1,0:T(8,128)(2,1)}, u32[]{:S(2)}, u32[]{:S(2)}) collective-permute-start(bf16[16,1408]{1,0:T(8,128)(2,1)S(1)} %get-tuple-element.32), channel_id=1, source_target_pairs={{0,8},{1,9},{2,10},{3,11},{4,12},{5,13},{6,14},{7,15},{8,0},{9,1},... | collective-permute-start | bytes 135176 | tf_op jit(solution)/shard_map/ppermute | solution.py:93
  7.1 27.7 %collective-permute-start.2 = (bf16[16,1408]{1,0:T(8,128)(2,1)S(1)}, bf16[16,1408]{1,0:T(8,128)(2,1)}, u32[]{:S(2)}, u32[]{:S(2)}) collective-permute-start(bf16[16,1408]{1,0:T(8,128)(2,1)S(1)} %get-tuple-element.33), channel_id=1, source_target_pairs={{0,12},{1,13},{2,14},{3,15},{4,0},{5,1},{6,2},{7,3},{8,4},{9,5},{1... | collective-permute-start | bytes 135176 | tf_op jit(solution)/shard_map/ppermute | solution.py:93
  8.2 15.8 %collective-permute-start.7 = (bf16[16,1408]{1,0:T(8,128)(2,1)S(1)}, bf16[16,1408]{1,0:T(8,128)(2,1)}, u32[]{:S(2)}, u32[]{:S(2)}) collective-permute-start(bf16[16,1408]{1,0:T(8,128)(2,1)S(1)} %get-tuple-element.35), channel_id=1, source_target_pairs={{0,4},{1,5},{2,6},{3,7},{4,8},{5,9},{6,10},{7,11},{8,12},{9,13},{1... | collective-permute-start | bytes 135176 | tf_op jit(solution)/shard_map/ppermute | solution.py:93
  8.6 17.1 %collective-permute-start.8 = (bf16[16,1408]{1,0:T(8,128)(2,1)S(1)}, bf16[16,1408]{1,0:T(8,128)(2,1)S(1)}, u32[]{:S(2)}, u32[]{:S(2)}) collective-permute-start(bf16[16,1408]{1,0:T(8,128)(2,1)S(1)} %get-tuple-element.36), channel_id=1, source_target_pairs={{0,8},{1,9},{2,10},{3,11},{4,12},{5,13},{6,14},{7,15},{8,0},{9,1},... | collective-permute-start | bytes 135176 | tf_op jit(solution)/shard_map/ppermute | solution.py:93
  9.9 1.1 copy-start.1
  11.0 1.0 copy-start.2
  13.0 85.9 %copy-start.34 = (u32[32]{0:T(128)S(1)}, u32[32]{0:T(128)}, u32[]{:S(2)}) copy-start(u32[32]{0:T(128)} %constant.127) | copy-start | bytes 388
  13.0 87.2 %copy-start.33 = (s32[4]{0:T(128)S(1)}, s32[4]{0:T(128)}, u32[]{:S(2)}) copy-start(s32[4]{0:T(128)} %param.9) | copy-start | bytes 52
  15.2 11.3 %collective-permute-start.9 = (bf16[16,1408]{1,0:T(8,128)(2,1)S(1)}, bf16[16,1408]{1,0:T(8,128)(2,1)S(1)}, u32[]{:S(2)}, u32[]{:S(2)}) collective-permute-start(bf16[16,1408]{1,0:T(8,128)(2,1)S(1)} %get-tuple-element.37), channel_id=1, source_target_pairs={{0,12},{1,13},{2,14},{3,15},{4,0},{5,1},{6,2},{7,3},{8,4},{9,5},{1... | collective-permute-start | bytes 135176 | tf_op jit(solution)/shard_map/ppermute | solution.py:93
  19.4 8.7 %collective-permute-start.25 = (bf16[88,528]{1,0:T(8,128)(2,1)S(1)}, bf16[88,528]{1,0:T(8,128)(2,1)S(1)}, u32[]{:S(2)}, u32[]{:S(2)}) collective-permute-start(bf16[88,528]{1,0:T(8,128)(2,1)S(1)} %get-tuple-element.40), channel_id=1, source_target_pairs={{0,3},{1,2},{2,1},{3,0},{4,7},{5,6},{6,5},{7,4},{8,11},{9,10},{10,... | collective-permute-start | bytes 278792 | tf_op jit(solution)/shard_map/ppermute | solution.py:93
  24.0 5.4 %collective-permute-start.26 = (bf16[88,528]{1,0:T(8,128)(2,1)S(1)}, bf16[88,528]{1,0:T(8,128)(2,1)S(1)}, u32[]{:S(2)}, u32[]{:S(2)}) collective-permute-start(bf16[88,528]{1,0:T(8,128)(2,1)S(1)} %get-tuple-element.41), channel_id=1, source_target_pairs={{0,2},{1,3},{2,0},{3,1},{4,6},{5,7},{6,4},{7,5},{8,10},{9,11},{10,... | collective-permute-start | bytes 278792 | tf_op jit(solution)/shard_map/ppermute | solution.py:93
  25.7 5.8 %collective-permute-start.27 = (bf16[88,528]{1,0:T(8,128)(2,1)S(1)}, bf16[88,528]{1,0:T(8,128)(2,1)S(1)}, u32[]{:S(2)}, u32[]{:S(2)}) collective-permute-start(bf16[88,528]{1,0:T(8,128)(2,1)S(1)} %get-tuple-element.42), channel_id=1, source_target_pairs={{0,1},{1,0},{2,3},{3,2},{4,5},{5,4},{6,7},{7,6},{8,9},{9,8},{10,11... | collective-permute-start | bytes 278792 | tf_op jit(solution)/shard_map/ppermute | solution.py:93
  26.5 7.9 %collective-permute-start.14 = (bf16[176,352]{1,0:T(8,128)(2,1)S(1)}, bf16[176,352]{1,0:T(8,128)(2,1)S(1)}, u32[]{:S(2)}, u32[]{:S(2)}) collective-permute-start(bf16[176,352]{1,0:T(8,128)(2,1)S(1)} %get-tuple-element.39), channel_id=1, source_target_pairs={{0,2},{1,3},{2,0},{3,1},{4,6},{5,7},{6,4},{7,5},{8,10},{9,11},{10,... | collective-permute-start | bytes 371720 | tf_op jit(solution)/shard_map/ppermute | solution.py:93
  28.2 9.8 %collective-permute-start.35 = (bf16[88,704]{1,0:T(8,128)(2,1)S(1)}, bf16[88,704]{1,0:T(8,128)(2,1)}, u32[]{:S(2)}, u32[]{:S(2)}) collective-permute-start(bf16[88,704]{1,0:T(8,128)(2,1)S(1)} %get-tuple-element.44), channel_id=1, source_target_pairs={{0,1},{2,3},{4,5},{6,7},{8,9},{10,11},{12,13},{14,15},{17,16},{19,... | collective-permute-start | bytes 371720 | tf_op jit(solution)/shard_map/ppermute | solution.py:336
  29.5 9.4 %collective-permute-start.13 = (bf16[64,1408]{1,0:T(8,128)(2,1)}, bf16[64,1408]{1,0:T(8,128)(2,1)S(1)}, u32[]{:S(2)}, u32[]{:S(2)}) collective-permute-start(bf16[64,1408]{1,0:T(8,128)(2,1)} %constant_dynamic-update-slice_fusion.4), channel_id=1, source_target_pairs={{0,18},{1,2},{2,16},{3,0},{4,22},{5,6},{6,20},{7,4},{8,26},{9,10},... | collective-permute-start | bytes 540680 | tf_op jit(solution)/shard_map/ppermute | solution.py:93
  31.5 12.3 %collective-permute-start.12 = (bf16[64,1408]{1,0:T(8,128)(2,1)}, bf16[64,1408]{1,0:T(8,128)(2,1)S(1)}, u32[]{:S(2)}, u32[]{:S(2)}) collective-permute-start(bf16[64,1408]{1,0:T(8,128)(2,1)} %constant_dynamic-update-slice_fusion.4), channel_id=1, source_target_pairs={{0,2},{1,18},{2,0},{3,16},{4,6},{5,22},{6,4},{7,20},{8,10},{9,26},... | collective-permute-start | bytes 540680 | tf_op jit(solution)/shard_map/ppermute | solution.py:93
  34.4 23.9 %collective-permute-start.28 = (bf16[352,528]{1,0:T(8,128)(2,1)S(1)}, bf16[352,528]{1,0:T(8,128)(2,1)}, u32[]{:S(2)}, u32[]{:S(2)}) collective-permute-start(bf16[352,528]{1,0:T(8,128)(2,1)S(1)} %pad_maximum_fusion.refs_6_), channel_id=1, source_target_pairs={{0,4},{1,5},{2,6},{3,7},{4,8},{5,9},{6,10},{7,11},{8,12},{9,13},{1... | collective-permute-start | bytes 1115144 | tf_op jit(solution)/shard_map/ppermute | solution.py:93
  34.8 23.2 %collective-permute-start.15 = (bf16[352,352]{1,0:T(8,128)(2,1)S(1)}, bf16[352,352]{1,0:T(8,128)(2,1)S(1)}, u32[]{:S(2)}, u32[]{:S(2)}) collective-permute-start(bf16[352,352]{1,0:T(8,128)(2,1)S(1)} %constant_dynamic-update-slice_fusion.8.refs_8_), channel_id=1, source_target_pairs={{0,4},{1,5},{2,6},{3,7},{4,8},{5,9},{6,10},{7,11},{8,12},{9,13},{1... | collective-permute-start | bytes 743432 | tf_op jit(solution)/shard_map/ppermute | solution.py:93
  38.0 6.9 %collective-permute-start.11 = (bf16[64,1408]{1,0:T(8,128)(2,1)}, bf16[64,1408]{1,0:T(8,128)(2,1)}, u32[]{:S(2)}, u32[]{:S(2)}) collective-permute-start(bf16[64,1408]{1,0:T(8,128)(2,1)} %constant_dynamic-update-slice_fusion.4), channel_id=1, source_target_pairs={{0,16},{1,0},{2,18},{3,2},{4,20},{5,4},{6,22},{7,6},{8,24},{9,8},{... | collective-permute-start | bytes 540680 | tf_op jit(solution)/shard_map/ppermute | solution.py:93
  38.9 70.7 %copy-start.10 = (bf16[64,1408]{1,0:T(8,128)(2,1)}, bf16[64,1408]{1,0:T(8,128)(2,1)S(1)}, u32[]{:S(2)}) copy-start(bf16[64,1408]{1,0:T(8,128)(2,1)S(1)} %collective-permute-done.13.refs_7_) | copy-start | bytes 540676
  38.9 9.9 %collective-permute-start.10 = (bf16[64,1408]{1,0:T(8,128)(2,1)}, bf16[64,1408]{1,0:T(8,128)(2,1)}, u32[]{:S(2)}, u32[]{:S(2)}) collective-permute-start(bf16[64,1408]{1,0:T(8,128)(2,1)} %constant_dynamic-update-slice_fusion.4), channel_id=1, source_target_pairs={{0,0},{1,16},{2,2},{3,18},{4,4},{5,20},{6,6},{7,22},{8,8},{9,24},{... | collective-permute-start | bytes 540680 | tf_op jit(solution)/shard_map/ppermute | solution.py:93
  44.5 6.2 %collective-permute-start.6 = (bf16[64,1408]{1,0:T(8,128)(2,1)}, bf16[64,1408]{1,0:T(8,128)(2,1)}, u32[]{:S(2)}, u32[]{:S(2)}) collective-permute-start(bf16[64,1408]{1,0:T(8,128)(2,1)} %constant_dynamic-update-slice_fusion), channel_id=1, source_target_pairs={{0,18},{1,2},{2,16},{3,0},{4,22},{5,6},{6,20},{7,4},{8,26},{9,10},... | collective-permute-start | bytes 540680 | tf_op jit(solution)/shard_map/ppermute | solution.py:93
  44.9 16.1 %collective-permute-start.5 = (bf16[64,1408]{1,0:T(8,128)(2,1)}, bf16[64,1408]{1,0:T(8,128)(2,1)S(1)}, u32[]{:S(2)}, u32[]{:S(2)}) collective-permute-start(bf16[64,1408]{1,0:T(8,128)(2,1)} %constant_dynamic-update-slice_fusion), channel_id=1, source_target_pairs={{0,2},{1,18},{2,0},{3,16},{4,6},{5,22},{6,4},{7,20},{8,10},{9,26},... | collective-permute-start | bytes 540680 | tf_op jit(solution)/shard_map/ppermute | solution.py:93
  48.7 13.0 %collective-permute-start.4 = (bf16[64,1408]{1,0:T(8,128)(2,1)}, bf16[64,1408]{1,0:T(8,128)(2,1)S(1)}, u32[]{:S(2)}, u32[]{:S(2)}) collective-permute-start(bf16[64,1408]{1,0:T(8,128)(2,1)} %constant_dynamic-update-slice_fusion), channel_id=1, source_target_pairs={{0,16},{1,0},{2,18},{3,2},{4,20},{5,4},{6,22},{7,6},{8,24},{9,8},{... | collective-permute-start | bytes 540680 | tf_op jit(solution)/shard_map/ppermute | solution.py:93
  50.7 11.9 %collective-permute-start.3 = (bf16[64,1408]{1,0:T(8,128)(2,1)}, bf16[64,1408]{1,0:T(8,128)(2,1)S(1)}, u32[]{:S(2)}, u32[]{:S(2)}) collective-permute-start(bf16[64,1408]{1,0:T(8,128)(2,1)} %constant_dynamic-update-slice_fusion), channel_id=1, source_target_pairs={{0,0},{1,16},{2,2},{3,18},{4,4},{5,20},{6,6},{7,22},{8,8},{9,24},{... | collective-permute-start | bytes 540680 | tf_op jit(solution)/shard_map/ppermute | solution.py:93
  58.0 24.0 %collective-permute-start.16 = (bf16[352,352]{1,0:T(8,128)(2,1)S(1)}, bf16[352,352]{1,0:T(8,128)(2,1)}, u32[]{:S(2)}, u32[]{:S(2)}) collective-permute-start(bf16[352,352]{1,0:T(8,128)(2,1)S(1)} %collective-permute-done.15.refs_9_), channel_id=1, source_target_pairs={{0,4},{1,5},{2,6},{3,7},{4,8},{5,9},{6,10},{7,11},{8,12},{9,13},{1... | collective-permute-start | bytes 743432 | tf_op jit(solution)/shard_map/ppermute | solution.py:93
  58.4 25.3 %collective-permute-start.29 = (bf16[352,528]{1,0:T(8,128)(2,1)}, bf16[352,528]{1,0:T(8,128)(2,1)}, u32[]{:S(2)}, u32[]{:S(2)}) collective-permute-start(bf16[352,528]{1,0:T(8,128)(2,1)} %collective-permute-done.28.refs_7_), channel_id=1, source_target_pairs={{0,4},{1,5},{2,6},{3,7},{4,8},{5,9},{6,10},{7,11},{8,12},{9,13},{1... | collective-permute-start | bytes 1115144 | tf_op jit(solution)/shard_map/ppermute | solution.py:93
  61.7 19.1 %collective-permute-start.36 = (bf16[88,704]{1,0:T(8,128)(2,1)S(1)}, bf16[88,704]{1,0:T(8,128)(2,1)S(1)}, u32[]{:S(2)}, u32[]{:S(2)}) collective-permute-start(bf16[88,704]{1,0:T(8,128)(2,1)S(1)} %broadcast_select_fusion.refs_14_), channel_id=1, source_target_pairs={{0,4},{1,5},{2,6},{3,7},{4,8},{5,9},{6,10},{7,11},{8,12},{9,13},{1... | collective-permute-start | bytes 371720 | tf_op jit(solution)/shard_map/ppermute | solution.py:93
  62.4 18.9 %collective-permute-start.39 = (bf16[88,704]{1,0:T(8,128)(2,1)S(1)}, bf16[88,704]{1,0:T(8,128)(2,1)S(1)}, u32[]{:S(2)}, u32[]{:S(2)}) collective-permute-start(bf16[88,704]{1,0:T(8,128)(2,1)S(1)} %broadcast_select_fusion.refs_14_), channel_id=1, source_target_pairs={{0,1},{1,0},{2,3},{3,2},{4,5},{5,4},{6,7},{7,6},{8,9},{9,8},{10,11... | collective-permute-start | bytes 371720 | tf_op jit(solution)/shard_map/ppermute | solution.py:93
  63.3 34.8 %collective-permute-start.31 = (bf16[352,528]{1,0:T(8,128)(2,1)S(1)}, bf16[352,528]{1,0:T(8,128)(2,1)S(1)}, u32[]{:S(2)}, u32[]{:S(2)}) collective-permute-start(bf16[352,528]{1,0:T(8,128)(2,1)S(1)} %pad_maximum_fusion.refs_6_), channel_id=1, source_target_pairs={{0,1},{1,0},{2,3},{3,2},{4,5},{5,4},{6,7},{7,6},{8,9},{9,8},{10,11... | collective-permute-start | bytes 1115144 | tf_op jit(solution)/shard_map/ppermute | solution.py:93
  80.8 1.5 collective-permute-start.40
  82.0 14.9 %collective-permute-start.18 = (bf16[352,352]{1,0:T(8,128)(2,1)S(1)}, bf16[352,352]{1,0:T(8,128)(2,1)S(1)}, u32[]{:S(2)}, u32[]{:S(2)}) collective-permute-start(bf16[352,352]{1,0:T(8,128)(2,1)S(1)} %constant_dynamic-update-slice_fusion.8.refs_8_), channel_id=1, source_target_pairs={{0,1},{1,0},{2,3},{3,2},{4,5},{5,4},{6,7},{7,6},{8,9},{9,8},{10,11... | collective-permute-start | bytes 743432 | tf_op jit(solution)/shard_map/ppermute | solution.py:93
  82.0 15.6 %collective-permute-start.17 = (bf16[352,352]{1,0:T(8,128)(2,1)}, bf16[352,352]{1,0:T(8,128)(2,1)}, u32[]{:S(2)}, u32[]{:S(2)}) collective-permute-start(bf16[352,352]{1,0:T(8,128)(2,1)} %collective-permute-done.16.refs_10_), channel_id=1, source_target_pairs={{0,4},{1,5},{2,6},{3,7},{4,8},{5,9},{6,10},{7,11},{8,12},{9,13},{1... | collective-permute-start | bytes 743432 | tf_op jit(solution)/shard_map/ppermute | solution.py:93
  83.0 11.6 %collective-permute-start.37 = (bf16[88,704]{1,0:T(8,128)(2,1)S(1)}, bf16[88,704]{1,0:T(8,128)(2,1)}, u32[]{:S(2)}, u32[]{:S(2)}) collective-permute-start(bf16[88,704]{1,0:T(8,128)(2,1)S(1)} %collective-permute-done.36.refs_15_), channel_id=1, source_target_pairs={{0,4},{1,5},{2,6},{3,7},{4,8},{5,9},{6,10},{7,11},{8,12},{9,13},{1... | collective-permute-start | bytes 371720 | tf_op jit(solution)/shard_map/ppermute | solution.py:93
  83.6 25.6 %collective-permute-start.30 = (bf16[352,528]{1,0:T(8,128)(2,1)}, bf16[352,528]{1,0:T(8,128)(2,1)}, u32[]{:S(2)}, u32[]{:S(2)}) collective-permute-start(bf16[352,528]{1,0:T(8,128)(2,1)} %collective-permute-done.29.refs_8_), channel_id=1, source_target_pairs={{0,4},{1,5},{2,6},{3,7},{4,8},{5,9},{6,10},{7,11},{8,12},{9,13},{1... | collective-permute-start | bytes 1115144 | tf_op jit(solution)/shard_map/ppermute | solution.py:93
  94.6 13.9 %collective-permute-start.19 = (bf16[352,352]{1,0:T(8,128)(2,1)S(1)}, bf16[352,352]{1,0:T(8,128)(2,1)}, u32[]{:S(2)}, u32[]{:S(2)}) collective-permute-start(bf16[352,352]{1,0:T(8,128)(2,1)S(1)} %collective-permute-done.15.refs_9_), channel_id=1, source_target_pairs={{0,1},{1,0},{2,3},{3,2},{4,5},{5,4},{6,7},{7,6},{8,9},{9,8},{10,11... | collective-permute-start | bytes 743432 | tf_op jit(solution)/shard_map/ppermute | solution.py:93
  97.6 11.0 %collective-permute-start.20 = (bf16[352,352]{1,0:T(8,128)(2,1)}, bf16[352,352]{1,0:T(8,128)(2,1)}, u32[]{:S(2)}, u32[]{:S(2)}) collective-permute-start(bf16[352,352]{1,0:T(8,128)(2,1)} %collective-permute-done.16.refs_10_), channel_id=1, source_target_pairs={{0,1},{1,0},{2,3},{3,2},{4,5},{5,4},{6,7},{7,6},{8,9},{9,8},{10,11... | collective-permute-start | bytes 743432 | tf_op jit(solution)/shard_map/ppermute | solution.py:93
  97.6 11.5 %collective-permute-start.21 = (bf16[352,352]{1,0:T(8,128)(2,1)}, bf16[352,352]{1,0:T(8,128)(2,1)}, u32[]{:S(2)}, u32[]{:S(2)}) collective-permute-start(bf16[352,352]{1,0:T(8,128)(2,1)} %collective-permute-done.17.refs_11_), channel_id=1, source_target_pairs={{0,1},{1,0},{2,3},{3,2},{4,5},{5,4},{6,7},{7,6},{8,9},{9,8},{10,11... | collective-permute-start | bytes 743432 | tf_op jit(solution)/shard_map/ppermute | solution.py:93
  98.8 8.3 %collective-permute-start.38 = (bf16[88,704]{1,0:T(8,128)(2,1)}, bf16[88,704]{1,0:T(8,128)(2,1)}, u32[]{:S(2)}, u32[]{:S(2)}) collective-permute-start(bf16[88,704]{1,0:T(8,128)(2,1)} %collective-permute-done.37.refs_16_), channel_id=1, source_target_pairs={{0,4},{1,5},{2,6},{3,7},{4,8},{5,9},{6,10},{7,11},{8,12},{9,13},{1... | collective-permute-start | bytes 371720 | tf_op jit(solution)/shard_map/ppermute | solution.py:93
  104.0 6.0 %copy-start.8 = (bf16[352,352]{1,0:T(8,128)(2,1)S(1)}, bf16[352,352]{1,0:T(8,128)(2,1)}, u32[]{:S(2)}) copy-start(bf16[352,352]{1,0:T(8,128)(2,1)} %copy-done.7) | copy-start | bytes 743428
  104.0 6.0 %copy-start.13 = (bf16[64,1408]{1,0:T(8,128)(2,1)S(1)}, bf16[64,1408]{1,0:T(8,128)(2,1)}, u32[]{:S(2)}) copy-start(bf16[64,1408]{1,0:T(8,128)(2,1)} %copy-done.12) | copy-start | bytes 540676
  104.0 6.0 %copy-start.15 = (bf16[64,1408]{1,0:T(8,128)(2,1)S(1)}, bf16[64,1408]{1,0:T(8,128)(2,1)}, u32[]{:S(2)}) copy-start(bf16[64,1408]{1,0:T(8,128)(2,1)} %copy-done.14) | copy-start | bytes 540676
  104.0 6.0 %copy-start.17 = (bf16[64,1408]{1,0:T(8,128)(2,1)S(1)}, bf16[64,1408]{1,0:T(8,128)(2,1)}, u32[]{:S(2)}) copy-start(bf16[64,1408]{1,0:T(8,128)(2,1)} %copy-done.16) | copy-start | bytes 540676
  104.0 6.0 %copy-start.19 = (bf16[64,1408]{1,0:T(8,128)(2,1)S(1)}, bf16[64,1408]{1,0:T(8,128)(2,1)}, u32[]{:S(2)}) copy-start(bf16[64,1408]{1,0:T(8,128)(2,1)} %copy-done.18) | copy-start | bytes 540676
  107.1 9.6 %collective-permute-start.32 = (bf16[352,528]{1,0:T(8,128)(2,1)}, bf16[352,528]{1,0:T(8,128)(2,1)S(1)}, u32[]{:S(2)}, u32[]{:S(2)}) collective-permute-start(bf16[352,528]{1,0:T(8,128)(2,1)} %collective-permute-done.28.refs_7_), channel_id=1, source_target_pairs={{0,1},{1,0},{2,3},{3,2},{4,5},{5,4},{6,7},{7,6},{8,9},{9,8},{10,11... | collective-permute-start | bytes 1115144 | tf_op jit(solution)/shard_map/ppermute | solution.py:93
  108.5 5.1 %collective-permute-start.41 = (bf16[88,704]{1,0:T(8,128)(2,1)}, bf16[88,704]{1,0:T(8,128)(2,1)S(1)}, u32[]{:S(2)}, u32[]{:S(2)}) collective-permute-start(bf16[88,704]{1,0:T(8,128)(2,1)} %collective-permute-done.37.refs_16_), channel_id=1, source_target_pairs={{0,1},{1,0},{2,3},{3,2},{4,5},{5,4},{6,7},{7,6},{8,9},{9,8},{10,11... | collective-permute-start | bytes 371720 | tf_op jit(solution)/shard_map/ppermute | solution.py:93
  108.6 6.6 %collective-permute-start.42 = (bf16[88,704]{1,0:T(8,128)(2,1)}, bf16[88,704]{1,0:T(8,128)(2,1)S(1)}, u32[]{:S(2)}, u32[]{:S(2)}) collective-permute-start(bf16[88,704]{1,0:T(8,128)(2,1)} %collective-permute-done.38.refs_17_), channel_id=1, source_target_pairs={{0,1},{1,0},{2,3},{3,2},{4,5},{5,4},{6,7},{7,6},{8,9},{9,8},{10,11... | collective-permute-start | bytes 371720 | tf_op jit(solution)/shard_map/ppermute | solution.py:93
  109.1 9.5 %collective-permute-start.33 = (bf16[352,528]{1,0:T(8,128)(2,1)}, bf16[352,528]{1,0:T(8,128)(2,1)}, u32[]{:S(2)}, u32[]{:S(2)}) collective-permute-start(bf16[352,528]{1,0:T(8,128)(2,1)} %collective-permute-done.29.refs_8_), channel_id=1, source_target_pairs={{0,1},{1,0},{2,3},{3,2},{4,5},{5,4},{6,7},{7,6},{8,9},{9,8},{10,11... | collective-permute-start | bytes 1115144 | tf_op jit(solution)/shard_map/ppermute | solution.py:93
  109.2 17.1 %collective-permute-start.34 = (bf16[352,528]{1,0:T(8,128)(2,1)}, bf16[352,528]{1,0:T(8,128)(2,1)}, u32[]{:S(2)}, u32[]{:S(2)}) collective-permute-start(bf16[352,528]{1,0:T(8,128)(2,1)} %collective-permute-done.30.refs_9_), channel_id=1, source_target_pairs={{0,1},{1,0},{2,3},{3,2},{4,5},{5,4},{6,7},{7,6},{8,9},{9,8},{10,11... | collective-permute-start | bytes 1115144 | tf_op jit(solution)/shard_map/ppermute | solution.py:93
  114.2 7.4 %collective-permute-start.24 = (bf16[256,352]{1,0:T(8,128)(2,1)S(1)}, bf16[256,352]{1,0:T(8,128)(2,1)S(1)}, u32[]{:S(2)}, u32[]{:S(2)}) collective-permute-start(bf16[256,352]{1,0:T(8,128)(2,1)S(1)} %shard_map.75.refs_0_), channel_id=1, source_target_pairs={{0,18},{1,19},{2,16},{3,17},{4,22},{5,23},{6,20},{7,21},{8,26},{9,... | collective-permute-start | bytes 540680 | tf_op jit(solution)/shard_map/ppermute | solution.py:93
  115.8 10.4 %collective-permute-start.23 = (bf16[256,352]{1,0:T(8,128)(2,1)S(1)}, bf16[256,352]{1,0:T(8,128)(2,1)S(1)}, u32[]{:S(2)}, u32[]{:S(2)}) collective-permute-start(bf16[256,352]{1,0:T(8,128)(2,1)S(1)} %shard_map.75.refs_0_), channel_id=1, source_target_pairs={{0,2},{1,3},{2,0},{3,1},{4,6},{5,7},{6,4},{7,5},{8,10},{9,11},{10,... | collective-permute-start | bytes 540680 | tf_op jit(solution)/shard_map/ppermute | solution.py:93
  117.5 8.7 %collective-permute-start.22 = (bf16[256,352]{1,0:T(8,128)(2,1)S(1)}, bf16[256,352]{1,0:T(8,128)(2,1)}, u32[]{:S(2)}, u32[]{:S(2)}) collective-permute-start(bf16[256,352]{1,0:T(8,128)(2,1)S(1)} %shard_map.75.refs_0_), channel_id=1, source_target_pairs={{0,16},{1,17},{2,18},{3,19},{4,20},{5,21},{6,22},{7,23},{8,24},{9,... | collective-permute-start | bytes 540680 | tf_op jit(solution)/shard_map/ppermute | solution.py:93
  126.2 1.0 copy-start.4
  127.2 1.0 copy-start.6
  143.9 6.1 %collective-permute-start.43 = (bf16[2,64,704]{2,1,0:T(8,128)(2,1)S(1)}, bf16[2,64,704]{2,1,0:T(8,128)(2,1)S(1)}, u32[]{:S(2)}, u32[]{:S(2)}) collective-permute-start(bf16[2,64,704]{2,1,0:T(8,128)(2,1)S(1)} %get-tuple-element.48), channel_id=1, source_target_pairs={{0,16},{1,17},{2,18},{3,19},{4,20},{5,21},{6,22},{7,23},{8,24},{9,... | collective-permute-start | bytes 540680 | tf_op jit(solution)/shard_map/ppermute | solution.py:93
  144.6 6.8 %collective-permute-start.44 = (bf16[2,64,704]{2,1,0:T(8,128)(2,1)S(1)}, bf16[2,64,704]{2,1,0:T(8,128)(2,1)S(1)}, u32[]{:S(2)}, u32[]{:S(2)}) collective-permute-start(bf16[2,64,704]{2,1,0:T(8,128)(2,1)S(1)} %get-tuple-element.49), channel_id=1, source_target_pairs={{0,2},{1,3},{2,0},{3,1},{4,6},{5,7},{6,4},{7,5},{8,10},{9,11},{10,... | collective-permute-start | bytes 540680 | tf_op jit(solution)/shard_map/ppermute | solution.py:93
  145.2 8.4 %collective-permute-start.45 = (bf16[2,64,704]{2,1,0:T(8,128)(2,1)S(1)}, bf16[2,64,704]{2,1,0:T(8,128)(2,1)S(1)}, u32[]{:S(2)}, u32[]{:S(2)}) collective-permute-start(bf16[2,64,704]{2,1,0:T(8,128)(2,1)S(1)} %get-tuple-element.50), channel_id=1, source_target_pairs={{0,18},{1,19},{2,16},{3,17},{4,22},{5,23},{6,20},{7,21},{8,26},{9,... | collective-permute-start | bytes 540680 | tf_op jit(solution)/shard_map/ppermute | solution.py:93
  154.2 8.0 %collective-permute-start.46 = (bf16[16,1408]{1,0:T(8,128)(2,1)S(1)}, bf16[16,1408]{1,0:T(8,128)(2,1)S(1)}, u32[]{:S(2)}, u32[]{:S(2)}) collective-permute-start(bf16[16,1408]{1,0:T(8,128)(2,1)S(1)} %get-tuple-element.51), channel_id=1, source_target_pairs={{0,0},{1,16},{2,2},{3,18},{4,4},{5,20},{6,6},{7,22},{8,8},{9,24},{... | collective-permute-start | bytes 135176 | tf_op jit(solution)/shard_map/ppermute | solution.py:93
  159.5 4.7 %collective-permute-start.47 = (bf16[16,1408]{1,0:T(8,128)(2,1)S(1)}, bf16[16,1408]{1,0:T(8,128)(2,1)S(1)}, u32[]{:S(2)}, u32[]{:S(2)}) collective-permute-start(bf16[16,1408]{1,0:T(8,128)(2,1)S(1)} %get-tuple-element.52), channel_id=1, source_target_pairs={{0,12},{1,28},{2,14},{3,30},{4,0},{5,16},{6,2},{7,18},{8,4},{9,20}... | collective-permute-start | bytes 135176 | tf_op jit(solution)/shard_map/ppermute | solution.py:93
  160.4 6.2 %collective-permute-start.48 = (bf16[16,1408]{1,0:T(8,128)(2,1)S(1)}, bf16[16,1408]{1,0:T(8,128)(2,1)S(1)}, u32[]{:S(2)}, u32[]{:S(2)}) collective-permute-start(bf16[16,1408]{1,0:T(8,128)(2,1)S(1)} %get-tuple-element.53), channel_id=1, source_target_pairs={{0,8},{1,24},{2,10},{3,26},{4,12},{5,28},{6,14},{7,30},{8,0},{9,16... | collective-permute-start | bytes 135176 | tf_op jit(solution)/shard_map/ppermute | solution.py:93
  160.4 6.2 %collective-permute-start.49 = (bf16[16,1408]{1,0:T(8,128)(2,1)S(1)}, bf16[16,1408]{1,0:T(8,128)(2,1)S(1)}, u32[]{:S(2)}, u32[]{:S(2)}) collective-permute-start(bf16[16,1408]{1,0:T(8,128)(2,1)S(1)} %get-tuple-element.54), channel_id=1, source_target_pairs={{0,4},{1,20},{2,6},{3,22},{4,8},{5,24},{6,10},{7,26},{8,12},{9,28}... | collective-permute-start | bytes 135176 | tf_op jit(solution)/shard_map/ppermute | solution.py:93
  (21 other events, 16.2 us)

commit v3 on v2

--- a/solution.py
+++ b/solution.py
@@ -80,6 +80,8 @@
         self.x, self.z = g, j // (n // seqs)
         self.y, self.c = (j // groups) % self.Y, j % groups
         self.where = jnp.stack([self.x, self.z, self.y, self.c]).astype(jnp.int32)
+        self.cores = [[k * groups + f for f in range(groups)] for k in range(n // groups)]
+        self.column = [[k * n // seqs + i for k in range(seqs)] for i in range(n // seqs)]
 
     def send(self, value, to):
         pairs = []
@@ -96,32 +98,50 @@
         return x * self.n + (z * self.Y + y) * self.G + c
 
 
-def call(kernel, outs, where, *arrays, scratch=(), flops=0):
+def call(kernel, outs, where, *arrays, scratch=(), copies=0, flops=0, vmem_out=True, vmem_in=False):
     moved = sum(a.size * a.dtype.itemsize for a in arrays)
+    space = pltpu.VMEM if vmem_in else pl.ANY
+    where_out = pltpu.VMEM if vmem_out else pl.ANY
+    sems = [pltpu.SemaphoreType.DMA((copies,))] if copies else []
     return pl.pallas_call(
         kernel,
         out_shape=[jax.ShapeDtypeStruct(s, d) for s, d in outs],
         in_specs=[pl.BlockSpec(memory_space=pltpu.SMEM)]
-        + [pl.BlockSpec(memory_space=pltpu.VMEM)] * len(arrays),
-        out_specs=[pl.BlockSpec(memory_space=pltpu.VMEM)] * len(outs),
-        scratch_shapes=list(scratch),
+        + [pl.BlockSpec(memory_space=space)] * len(arrays),
+        out_specs=[pl.BlockSpec(memory_space=where_out)] * len(outs),
+        scratch_shapes=list(scratch) + sems,
         compiler_params=pltpu.CompilerParams(vmem_limit_bytes=40 * 2**20),
         cost_estimate=pl.CostEstimate(flops=flops, bytes_accessed=2 * moved, transcendentals=0),
     )(where, *arrays)
 
 
-def pieces_kernel(S, where, hidden, skip, *outs):
+def copy_all(pairs, sems):
+    copies = [pltpu.make_async_copy(a, b, sems.at[k]) for k, (a, b) in enumerate(pairs)]
+    for copy in copies:
+        copy.start()
+    for copy in copies:
+        copy.wait()
+
+
+def pieces_kernel(S, where, hidden, skip, *refs):
+    outs, sems = refs[:S], refs[S]
     z = where[1]
+    local = hidden.shape[1]
+    pairs = []
     for s in range(S):
-        outs[s][...] = hidden[(z + s) % S]
-        outs[S + s][...] = skip[(z + s) % S]
-
-
-def slices_kernel(G, S, Y, where, w_skip, w_qkv, w_out, *outs):
+        at = (z + s) % S
+        pairs.append((hidden.at[at], outs[s].at[pl.ds(0, local)]))
+        pairs.append((skip.at[at], outs[s].at[pl.ds(local, local)]))
+    copy_all(pairs, sems)
+
+
+def slices_kernel(G, S, Y, where, w_skip_any, w_qkv_any, w_out_any, *refs):
+    outs, (w_skip, w_qkv, w_out, sems) = refs[:-4], refs[-4:]
+    copy_all([(w_skip_any, w_skip), (w_qkv_any, w_qkv), (w_out_any, w_out)], sems)
     x, y, c = where[0], where[2], where[3]
     width = w_skip.shape[1]
     block, part, half = width // (G * Y), S // G * HD, width // G
-    skips, qkvs, rest = outs[:Y], outs[Y : Y + Y * G], outs[Y + Y * G :]
+    skips, qkvs, rest = outs[:Y], outs[Y : Y + Y * G], outs[Y + Y * G]
     for gx in range(G):
         for gy in range(Y):
             for e in range(Y):
@@ -147,26 +167,66 @@
 
             @pl.when((c + f) % G == gc)
             def _():
-                rest[f][...] = w_out[:, gc * half : (gc + 1) * half]
+                to = rest if f == 0 else qkvs[f]
+                at = 0 if f == 0 else 3 * part
+                to[:, at : at + half] = w_out[:, gc * half : (gc + 1) * half]
+
+
+def join_kernel(S, where, *refs):
+    rows = refs[0].shape[0]
+    copy_all([(refs[s], refs[S].at[pl.ds(s * rows, rows)]) for s in range(S)], refs[S + 1])
+
+
+def shards_kernel(G, S, Y, where, *refs):
+    skips, qkvs, rest = refs[:Y], refs[Y : Y + Y * G], refs[Y + Y * G]
+    ring, qkv, out = refs[Y + Y * G + 1 :]
+    x, y, c = where[0], where[2], where[3]
+    rows, part = skips[0].shape[0], S // G * HD
+    for e in range(Y):
+        ring[e * rows : (e + 1) * rows, :] = skips[e][...]
+    for gy in range(Y):
+        for gc in range(G):
+            for e in range(Y):
+                for f in range(G):
+
+                    @pl.when(((y + Y - e) % Y == gy) & ((c + G - f) % G == gc))
+                    def _():
+                        at = (gy * G + gc) * HD
+                        qkv[at : at + HD, :] = qkvs[e * G + f][:, : 3 * part]
+
+    out[...] = rest[...]
+    for f in range(1, G):
+
+        @pl.when((c + G - f) % G == x)
+        def _():
+            out[...] = qkvs[f][:, 3 * part :]
 
 
 def merged_kernel(G, S, Y, where, *refs):
-    z, y, c = where[1], where[2], where[3]
+    z, y = where[1], where[2]
     blocks = Y * G
-    hid, skp = refs[:blocks], refs[blocks : 2 * blocks]
-    weights = refs[2 * blocks : 2 * blocks + G * S]
-    out, xs, ws = refs[2 * blocks + G * S :]
-    toks, width = hid[0].shape
+    parts, weights, held = refs[:blocks], refs[blocks : blocks + S], refs[blocks + S]
+    out, on, xs, ws, sems = refs[blocks + S + 1 :]
+    width = parts[0].shape[1]
+    local = parts[0].shape[0] // (2 * S)
+    rows = weights[0].shape[1] // Y
+    pairs = [(held, on)]
     for k in range(blocks):
-        xs[k * toks : (k + 1) * toks, :width] = hid[k][...]
-        xs[k * toks : (k + 1) * toks, width:] = skp[k][...]
-    rows = weights[0].shape[0] // Y
-    for f in range(G):
         for s in range(S):
+            for h in range(2):
+                pairs.append(
+                    (
+                        parts[k].at[pl.ds((2 * s + h) * local, local)],
+                        xs.at[pl.ds((k * S + s) * local, local), pl.ds(h * width, width)],
+                    )
+                )
+    for s in range(S):
+        for f in range(G):
             for e in range(Y):
-                j = (((z + S - s) % S) * Y + (y + Y - e) % Y) * G + (c + G - f) % G
+                j = (((z + S - s) % S) * Y + (y + Y - e) % Y) * G + f
                 at = pl.multiple_of(j * rows, 16)
-                ws[pl.ds(at, rows), :] = weights[f * S + s][e * rows : (e + 1) * rows, :]
+                pairs.append((weights[s].at[f, pl.ds(e * rows, rows)], ws.at[pl.ds(at, rows)]))
+    copy_all(pairs, sems)
     out[...] = jnp.dot(xs[...], ws[...], preferred_element_type=F32).astype(BF)
 
 
@@ -178,48 +238,53 @@
 
 
 def attend_kernel(G, S, Y, where, *refs):
-    x, z, y, c = where[0], where[1], where[2], where[3]
+    x, z, y = where[0], where[1], where[2]
     blocks = Y * G
-    merged, (shift, scale) = refs[:blocks], refs[blocks : blocks + 2]
-    refs = refs[blocks + 2 :]
-    wq, wo, refs = refs[: G * S], refs[G * S : 2 * G * S], refs[2 * G * S :]
-    outs, base, (norm, wqs, att) = refs[:blocks], refs[blocks], refs[blocks + 1 :]
-    rows, cols = merged[0].shape
+    merged_any, (shift, scale) = refs[:blocks], refs[blocks : blocks + 2]
+    wq_any, wo_any, refs = refs[blocks + 2], refs[blocks + 3 : blocks + 3 + S], refs[blocks + 3 + S :]
+    outs, base, (merged, norm, shifts, scales, wq, wo, att, sems) = (
+        refs[:blocks],
+        refs[blocks],
+        refs[blocks + 1 :],
+    )
+    rows, cols = merged_any[0].shape
     toks = rows // blocks
     width = cols * blocks
 
-    for f in range(G):
-        for s in range(S):
-            wqs[f, (z + S - s) % S] = wq[f * S + s][...]
+    pairs = [(shift, shifts), (scale, scales), (wq_any, wq)]
+    for s in range(S):
+        pairs.append((wo_any[s], wo.at[(z + S - s) % S]))
+    for e in range(Y):
+        for d in range(G):
+            b = (x + d) % G * Y + (y + e) % Y
+            for em in range(Y):
+                for dm in range(G):
+                    at = (((em - e) % Y) * G + (dm - d) % G) * toks
+                    to = (em * G + dm) * toks
+                    pairs.append(
+                        (merged_any[e * G + d].at[pl.ds(at, toks)], merged.at[b, pl.ds(to, toks)])
+                    )
+    copy_all(pairs, sems)
     total = jnp.zeros((rows, 1), F32)
     wide = []
-    for e in range(Y):
-        for d in range(G):
-            m = merged[e * G + d]
-            own = [
-                m[pl.ds((((em - e) % Y) * G + (dm - d) % G) * toks, toks), :]
-                for em in range(Y)
-                for dm in range(G)
-            ]
-            base[(x + d) % G * Y + (y + e) % Y] = own[0]
-            wide.append(jnp.concatenate(own, axis=0).astype(F32))
-            total = total + jnp.sum(wide[-1], axis=-1, keepdims=True)
+    for b in range(blocks):
+        base[b] = merged[b, :toks, :]
+        wide.append(merged[b].astype(F32))
+        total = total + jnp.sum(wide[-1], axis=-1, keepdims=True)
     mean = total * (1.0 / width)
     square = jnp.zeros((rows, 1), F32)
     for m in wide:
         square = square + jnp.sum((m - mean) ** 2, axis=-1, keepdims=True)
     inv = lax.rsqrt(square * (1.0 / width) + 1e-06)
-    for e in range(Y):
-        for d in range(G):
-            b = (x + d) % G * Y + (y + e) % Y
-            m = wide[e * G + d]
-            norm[b] = ((m - mean) * inv * (1.0 + scale[b]) + shift[b]).astype(BF)
+    for b in range(blocks):
+        norm[b] = ((wide[b] - mean) * inv * (1.0 + scales[b]) + shifts[b]).astype(BF)
     per = S // G
     for f in range(G):
-        qkv = jnp.dot(norm[0], wqs[f, 0], preferred_element_type=F32)
+        qkv = jnp.dot(norm[0], wq[f, :cols], preferred_element_type=F32)
         for b in range(1, blocks):
-            qkv = qkv + jnp.dot(norm[b], wqs[f, b], preferred_element_type=F32)
-        first = (c + G - f) % G * per
+            qkv = qkv + jnp.dot(
+                norm[b], wq[f, b * cols : (b + 1) * cols], preferred_element_type=F32
+            )
         for t in range(per):
             q, k, v = (qkv[:, (p * per + t) * HD : (p * per + t + 1) * HD] for p in range(3))
             q = (norm88(q) * HD ** (-0.5)).astype(BF)
@@ -229,16 +294,14 @@
             top = jnp.max(scores, axis=-1, keepdims=True)
             probs = jnp.exp(scores - top)
             probs = (probs / jnp.sum(probs, axis=-1, keepdims=True)).astype(BF)
-            att[first + t] = jnp.dot(probs, v, preferred_element_type=F32).astype(BF)
+            att[f * per + t] = jnp.dot(probs, v, preferred_element_type=F32).astype(BF)
     for f in range(G):
-        acc = jnp.dot(att[z], wo[f * S][...], preferred_element_type=F32)
+        acc = jnp.dot(att[0], wo[0, f], preferred_element_type=F32)
         for s in range(1, S):
-            acc = acc + jnp.dot(
-                att[(z + S - s) % S], wo[f * S + s][...], preferred_element_type=F32
-            )
+            acc = acc + jnp.dot(att[s], wo[s, f], preferred_element_type=F32)
         acc = acc.astype(BF)
         for k in range(blocks):
-            outs[k][(c + G - f) % G] = acc[k * toks : (k + 1) * toks, :]
+            outs[k][f] = acc[k * toks : (k + 1) * toks, :]
 
 
 def result_kernel(G, S, Y, where, gate, base, *refs):
@@ -261,8 +324,7 @@
 
 def home_kernel(S, where, *refs):
     z = where[1]
-    for s in range(S):
-        refs[S][(z + s) % S] = refs[s][...]
+    copy_all([(refs[s], refs[S].at[(z + s) % S]) for s in range(S)], refs[S + 1])
 
 
 def in_planes(groups, n, hidden, skip, timestep, w_skip, w_mod, w_qkv, w_out):
@@ -272,98 +334,96 @@
     blocks = Y * G
     cols, half = width // blocks, width // G
     toks, rows = S * local, w_skip.shape[0]
-    per = S // G
-
-    piece = ((local, width), BF)
-    cut = call(partial(pieces_kernel, S), [piece] * (2 * S), p.where, hidden, skip)
-    outs = [((rows, cols), BF)] * Y + [((HD, 3 * per * HD), BF)] * (Y * G) + [((HD, half), BF)] * G
-    slices = call(partial(slices_kernel, G, S, Y), outs, p.where, w_skip, w_qkv, w_out)
-    skips, qkvs, rest = slices[:Y], slices[Y : Y + Y * G], slices[Y + Y * G :]
-
-    def to_plane(part):
-        moved = [part[0]] + [
-            p.send(part[s], lambda x, z, y, c, s=s: (x, z + s, y, c)) for s in range(1, S)
-        ]
-        return jnp.concatenate(moved, axis=0)
-
-    def over_plane(value):
-        return [
-            p.send(value, lambda x, z, y, c, e=e, d=d: (c - d, z, y - e, x))
-            for e in range(Y)
-            for d in range(G)
-        ]
-
-    hid = over_plane(to_plane(cut[:S]))
-    skp = over_plane(to_plane(cut[S:]))
-
-    def ring(value):
+    part = 3 * (S // G) * HD
+    every = blocks * toks
+
+    cut = call(
+        partial(pieces_kernel, S),
+        [((2 * local, width), BF)] * S,
+        p.where,
+        hidden,
+        skip,
+        copies=2 * S,
+        vmem_out=False,
+    )
+    outs = [((rows, cols), BF)] * Y
+    for e in range(Y):
+        for f in range(G):
+            outs.append(((HD, part + (half if f and not e else 0)), BF))
+    outs.append(((HD, half), BF))
+    slices = call(
+        partial(slices_kernel, G, S, Y),
+        outs,
+        p.where,
+        w_skip,
+        w_qkv,
+        w_out,
+        scratch=[pltpu.VMEM(w.shape, BF) for w in (w_skip, w_qkv, w_out)],
+        copies=3,
+    )
+    skips, qkvs, rest = list(slices[:Y]), list(slices[Y : Y + Y * G]), slices[Y + Y * G]
+
+    cut = [cut[0]] + [
+        p.send(cut[s], lambda x, z, y, c, s=s: (x, z + s, y, c)) for s in range(1, S)
+    ]
+    (joined,) = call(
+        partial(join_kernel, S), [((2 * toks, width), BF)], p.where, *cut, copies=S, vmem_out=False
+    )
+    parts = [
+        p.send(joined, lambda x, z, y, c, e=e, d=d: (c - d, z, y - e, x))
+        for e in range(Y)
+        for d in range(G)
+    ]
+
+    for e in range(1, Y):
+        skips[e] = p.send(skips[e], lambda x, z, y, c, e=e: (x, z, y + e, c))
+    for e in range(Y):
+        for f in range(G):
+            if e or f:
+                qkvs[e * G + f] = p.send(
+                    qkvs[e * G + f], lambda x, z, y, c, e=e, f=f: (x, z, y + e, c + f)
+                )
+    ring, wq, wo = call(
+        partial(shards_kernel, G, S, Y),
+        [((Y * rows, cols), BF), ((blocks * HD, part), BF), ((HD, half), BF)],
+        p.where,
+        *skips,
+        *qkvs,
+        rest,
+        vmem_in=True,
+    )
+
+    def round_planes(value):
         held = [value]
         for _ in range(1, S):
             held.append(p.send(held[-1], lambda x, z, y, c: (x, z + 1, y, c)))
         return held
 
-    def over_cores(held):
-        return held + [
-            p.send(v, lambda x, z, y, c, f=f: (x, z, y, c + f)) for f in range(1, G) for v in held
-        ]
-
-    ws = [skips[0]] + [
-        p.send(skips[e], lambda x, z, y, c, e=e: (x, z, y + e, c)) for e in range(1, Y)
-    ]
-    ws = over_cores(ring(jnp.concatenate(ws, axis=0)))
-
-    got = {}
-    for e in range(Y):
-        for f in range(G):
-            v = qkvs[e * G + f]
-            if e or f:
-                v = p.send(v, lambda x, z, y, c, e=e, f=f: (x, z, y + e, c + f))
-            got[e, f] = v
-    ordered = []
-    for gy in range(Y):
-        for gc in range(G):
-            v = got[0, 0]
-            for e in range(Y):
-                for f in range(G):
-                    if e or f:
-                        here = ((p.y - e) % Y == gy) & ((p.c - f) % G == gc)
-                        v = jnp.where(here, got[e, f], v)
-            ordered.append(v)
-    wq = over_cores(ring(jnp.concatenate(ordered, axis=0)))
-
-    wo = rest[0]
-    for f in range(1, G):
-        other = lax.ppermute(
-            rest[f],
-            ("group", "seq"),
-            [
-                (p.flat(x, z, y, x), p.flat(x, z, y, (x + f) % G))
-                for x in range(G)
-                for z in range(S)
-                for y in range(Y)
-            ],
-        )
-        wo = jnp.where((p.c - p.x) % G == f, other, wo)
-    wo = over_cores(ring(wo))
-
-    times = lax.all_gather(timestep, "group", axis=0)
-    mine = lax.dynamic_slice(times, (p.c, p.z), (1, 1)).reshape(1)
-    mod = modulation(mine, w_mod)
+    def both_cores(value):
+        return lax.all_gather(value, "seq", axis=0, axis_index_groups=p.cores)
+
+    ws = [both_cores(v) for v in round_planes(ring)]
+    wq = lax.all_gather(wq, "seq", axis=0, tiled=True, axis_index_groups=p.column)
+    wq = both_cores(wq)
+
+    times = p.send(timestep, lambda x, z, y, c: (c, z, y, x))
+    mod = modulation(lax.dynamic_slice(times, (p.z,), (1,)), w_mod)
     shift = mod[:, :width].reshape(blocks, 1, cols)
     scale = mod[:, width : 2 * width].reshape(blocks, 1, cols)
     gate = mod[:, 2 * width :]
 
-    every = blocks * toks
-    (merged,) = call(
+    merged, wo = call(
         partial(merged_kernel, G, S, Y),
-        [((every, cols), BF)],
-        p.where,
-        *hid,
-        *skp,
+        [((every, cols), BF), ((HD, half), BF)],
+        p.where,
+        *parts,
         *ws,
+        wo,
         scratch=[pltpu.VMEM((every, 2 * width), BF), pltpu.VMEM((2 * width, cols), BF)],
+        copies=1 + 2 * blocks * S + S * G * Y,
         flops=4 * every * width * cols,
     )
+    wo = [both_cores(v) for v in round_planes(wo)]
     merged = [
         p.send(merged, lambda x, z, y, c, e=e, d=d: (x - d, z, y - e, c)) if e or d else merged
         for e in range(Y)
@@ -376,13 +436,18 @@
         *merged,
         shift,
         scale,
-        *wq,
+        wq,
         *wo,
         scratch=[
             pltpu.VMEM((blocks, every, cols), BF),
-            pltpu.VMEM((G, S, cols, 3 * per * HD), BF),
+            pltpu.VMEM((blocks, every, cols), BF),
+            pltpu.VMEM((blocks, 1, cols), F32),
+            pltpu.VMEM((blocks, 1, cols), F32),
+            pltpu.VMEM((G, width, part), BF),
+            pltpu.VMEM((S, G, HD, half), BF),
             pltpu.VMEM((S, every, HD), BF),
         ],
+        copies=3 + S + blocks * blocks,
         flops=10 * every * width * cols,
     )
     parts = [
@@ -392,11 +457,24 @@
         for e in range(Y)
         for d in range(G)
     ]
-    result = call(partial(result_kernel, G, S, Y), [piece] * S, p.where, gate, base, *parts)
-    result = [
-        p.send(result[s], lambda x, z, y, c, s=s: (c, z - s, y, x)) for s in range(S)
-    ]
-    (out,) = call(partial(home_kernel, S), [((S, local, width), BF)], p.where, *result)
+    result = call(
+        partial(result_kernel, G, S, Y),
+        [((local, width), BF)] * S,
+        p.where,
+        gate,
+        base,
+        *parts,
+        vmem_in=True,
+    )
+    result = [p.send(result[s], lambda x, z, y, c, s=s: (c, z - s, y, x)) for s in range(S)]
+    (out,) = call(
+        partial(home_kernel, S),
+        [((S, local, width), BF)],
+        p.where,
+        *result,
+        copies=S,
+        vmem_out=False,
+    )
     return out
 
 

time: 169 us -> 197 us (1.17)
  blocking collectives: 3.5 us -> 23.2 us
  waiting for transfers between devices: 52.1 us -> 71.7 us
  starting transfers between devices: 60.1 us -> 42.2 us
  between operations: 1.71 us -> 14.3 us
  local copies, waits for them, and re-layouts: 31.3 us -> 19.7 us
  Pallas kernels: 17.6 us -> 25 us
    all_gather x0 -> x2, waiting for transfers between devices: none -> 39.1 us  [the longest x1 39.1 us: in_planes(): lax.all_gather(wq, 'seq', axis=0, tiled=True, axis_index_groups=p.column)]
    all_gather x0 -> x8, blocking collectives: none -> 23.2 us  [both_cores(): return lax.all_gather(value, 'seq', axis=0, axis_index_groups=p.cores)]
    ppermute x49 -> x28, waiting for transfers between devices: 52.1 us -> 32.6 us  [send(): return lax.ppermute(value, ('group', 'seq'), pairs)]
    unnamed x80 -> x18, local copies, waits for them, and re-layouts: 28.4 us -> 10.2 us
    ppermute x49 -> x28, starting transfers between devices: 58.8 us -> 42.2 us  [send(): return lax.ppermute(value, ('group', 'seq'), pairs)]
    all_gather x1 -> x2, local copies, waits for them, and re-layouts: 0.08 us -> 8.71 us  [the longest x1 5.5 us: both_cores(): return lax.all_gather(value, 'seq', axis=0, axis_index_groups=p.cores)]
    pallas_call x6 -> x8, Pallas kernels: 17.6 us -> 25 us  [call(): pl.pallas_call(kernel, out_shape=[jax.ShapeDtypeStruct(s, d) for s, d in...]
    unnamed x1 -> x0, blocking collectives: 3.5 us -> none
  transfers between devices with their start and end apart: 50 -> 30, of which waited for: 13 -> 15; matrix products, arithmetic and copies ran while one was open for 7% -> 3% of each run, Pallas kernels for 2% -> 4%
where the time goes in v3:
time: 197 us
  waiting for transfers between devices  71.7 us (36%)
  starting transfers between devices  42.2 us (21%)
  Pallas kernels  25 us (13%)
  blocking collectives  23.2 us (12%)
  local copies, waits for them, and re-layouts  19.7 us (10%)
  between operations  14.3 us (7%)
    ppermute x28, starting transfers between devices, send(): return lax.ppermute(value, ('group', 'seq'), pairs)  42.2 us
    all_gather x1, waiting for transfers between devices, in_planes(): lax.all_gather(wq, 'seq', axis=0, tiled=True, axis_index_groups=p.column)  39.1 us
    ppermute x28, waiting for transfers between devices, send(): return lax.ppermute(value, ('group', 'seq'), pairs)  32.6 us
    pallas_call x8, Pallas kernels, call(): pl.pallas_call(kernel, out_shape=[jax.ShapeDtypeStruct(s, d) for s, d in...  25 us
    all_gather x8, blocking collectives, both_cores(): return lax.all_gather(value, 'seq', axis=0, axis_index_groups=p.cores)  23.2 us
    unnamed x18, local copies, waits for them, and re-layouts  10.2 us
    all_gather x1, local copies, waits for them, and re-layouts, both_cores(): return lax.all_gather(value, 'seq', axis=0, axis_index_groups=p.cores)  5.5 us
  transfers between devices with their start and end apart: 30, of which 15 were waited for; matrix products, arithmetic and copies ran while one was open for 3% of the time, Pallas kernels for 4%

profile of v3, /device:TPU:1, one launch (start us, length us, event | category | flops | bytes accessed | tf_op | source)
XLA Modules:
  0.0 196.7 jit_solution(152716514832741769)
XLA Ops:
  6.5 0.1 pad_add_fusion.where
  6.6 1.3 copy-done.2
  7.9 1.0 copy-done.3
  8.9 0.9 copy-done.4
  9.9 2.5 %shard_map.75 = (bf16[176,352]{1,0:T(8,128)(2,1)S(1)}, bf16[176,352]{1,0:T(8,128)(2,1)S(1)}, bf16[88,528]{1,0:T(8,128)(2,1)S(1)}, bf16[88,1232]{1,0:T(8,128)(2,1...) custom-call(s32[4]{0:T(128)S(1)} %pad_add_fusion.where, ...), custom_call_target="tpu_custom_call" | custom-call | bytes 2973696 | tf_op jit(solution)/shard_map/pallas_call | solution.py:106
  12.4 2.6 %collective-permute-start.8 = (bf16[176,352]{1,0:T(8,128)(2,1)S(1)}, bf16[176,352]{1,0:T(8,128)(2,1)S(1)}, u32[]{:S(2)}, u32[]{:S(2)}) collective-permute-start(bf16[176,352]{1,0:T(8,128)(2,1)S(1)} %get-tuple-element.35), channel_id=1, source_target_pairs={{0,2},{1,3},{2,0},{3,1},{4,6},{5,7},{6,4},{7,5},{8,10},{9,11},{10,... | collective-permute-start | bytes 371720 | tf_op jit(solution)/shard_map/ppermute | solution.py:95
  15.1 2.0 collective-permute-start.11
  17.0 4.3 %collective-permute-done.10.refs_4_ = bf16[88,528]{1,0:T(8,128)(2,1)S(1)} collective-permute-done((bf16[88,528]{1,0:T(8,128)(2,1)S(1)}, bf16[88,528]{1,0:T(8,128)(2,1)S(1)}, u32[]{:S(2)}, u32[]{:S(2)}) %collective-permute-start.10) | collective-permute-done | bytes 92960 | tf_op jit(solution)/shard_map/ppermute | solution.py:95
  21.3 2.4 %collective-permute-done.11.refs_5_ = bf16[88,528]{1,0:T(8,128)(2,1)S(1)} collective-permute-done((bf16[88,528]{1,0:T(8,128)(2,1)S(1)}, bf16[88,528]{1,0:T(8,128)(2,1)S(1)}, u32[]{:S(2)}, u32[]{:S(2)}) %collective-permute-start.11) | collective-permute-done | bytes 92960 | tf_op jit(solution)/shard_map/ppermute | solution.py:95
  23.7 0.8 shard_map.76
  24.5 0.9 copy.13
  25.5 39.1 %all-gather.15.cloned.1.call-done = bf16[4,352,528]{1,2,0:T(8,128)(2,1)} async-done(((bf16[1,352,528]{1,2,0:T(8,128)(2,1)}), bf16[4,352,528]{1,2,0:T(8,128)(2,1)}) %all-gather.15.cloned.1.call-update) | async-done | bytes 1486864 | tf_op jit(solution)/shard_map/all_gather | solution.py:406
  64.6 3.2 %copy.14 = bf16[4,352,528]{1,0,2:T(4,128)(2,1)} copy(bf16[4,352,528]{1,2,0:T(8,128)(2,1)} %all-gather.15.cloned.1.call-done) | data formatting | bytes 2973696 | tf_op jit(solution)/shard_map/all_gather | solution.py:406
  67.8 4.0 %reshape.50 = bf16[1408,528]{0,1:T(8,128)(2,1)} reshape(bf16[4,352,528]{1,0,2:T(4,128)(2,1)} %copy.14) | data formatting | bytes 2973696
  71.9 4.1 %collective-permute-start = (s32[4]{0:T(128)S(1)}, s32[4]{0:T(128)S(1)}, u32[]{:S(2)}, u32[]{:S(2)}) collective-permute-start(s32[4]{0:T(128)S(1)} %copy-done.7), channel_id=1, source_target_pairs={{0,0},{1,16},{2,2},{3,18},{4,4},{5,20},{6,6},{7,22},{8,8},{9,24},{... | collective-permute-start | bytes 56 | tf_op jit(solution)/shard_map/ppermute | solution.py:95
  76.1 1.1 shard_map.73
  77.2 1.2 collective-permute-start.1
  78.4 2.3 %collective-permute-start.2 = (bf16[32,1408]{1,0:T(8,128)(2,1)S(1)}, bf16[32,1408]{1,0:T(8,128)(2,1)S(1)}, u32[]{:S(2)}, u32[]{:S(2)}) collective-permute-start(bf16[32,1408]{1,0:T(8,128)(2,1)S(1)} %get-tuple-element.32), channel_id=1, source_target_pairs={{0,8},{1,9},{2,10},{3,11},{4,12},{5,13},{6,14},{7,15},{8,0},{9,1},... | collective-permute-start | bytes 270344 | tf_op jit(solution)/shard_map/ppermute | solution.py:95
  80.7 0.6 dynamic_slice.3
  82.0 1.4 collective-permute-start.13
  83.5 0.3 collective-permute-done.1.refs_1_
  83.8 4.7 %collective-permute-done.2.refs_2_ = bf16[32,1408]{1,0:T(8,128)(2,1)S(1)} collective-permute-done((bf16[32,1408]{1,0:T(8,128)(2,1)S(1)}, bf16[32,1408]{1,0:T(8,128)(2,1)S(1)}, u32[]{:S(2)}, u32[]{:S(2)}) %collective-permute-start.2) | collective-permute-done | bytes 90144 | tf_op jit(solution)/shard_map/ppermute | solution.py:95
  88.5 1.0 shard_map.74
  89.6 8.8 %collective-permute-start.4 = (bf16[128,1408]{1,0:T(8,128)(2,1)S(1)}, bf16[128,1408]{1,0:T(8,128)(2,1)S(1)}, u32[]{:S(2)}, u32[]{:S(2)}) collective-permute-start(bf16[128,1408]{1,0:T(8,128)(2,1)S(1)} %shard_map.74), channel_id=1, source_target_pairs={{0,0},{1,16},{2,2},{3,18},{4,4},{5,20},{6,6},{7,22},{8,8},{9,24},{... | collective-permute-start | bytes 1081352 | tf_op jit(solution)/shard_map/ppermute | solution.py:95
  98.4 1.0 collective-permute-start.6
  99.4 1.0 collective-permute-start.7
  100.4 2.9 %all-gather = bf16[704,352]{1,0:T(8,128)(2,1)S(1)} all-gather(bf16[352,352]{1,0:T(8,128)(2,1)S(1)} %get-tuple-element.41), channel_id=2, replica_groups={{0,1},{2,3},{4,5},{6,7},{8,9},{10,11},{12,13},{14,15},{16,17},{18,19},{..., dimensions={0}, use_global_device_ids=true | all-gather | bytes 743424 | tf_op jit(solution)/shard_map/all_gather | solution.py:403
  103.3 2.1 %collective-permute-start.14 = (bf16[352,352]{1,0:T(8,128)(2,1)S(1)}, bf16[352,352]{1,0:T(8,128)(2,1)S(1)}, u32[]{:S(2)}, u32[]{:S(2)}) collective-permute-start(bf16[352,352]{1,0:T(8,128)(2,1)S(1)} %collective-permute-done.13), channel_id=1, source_target_pairs={{0,4},{1,5},{2,6},{3,7},{4,8},{5,9},{6,10},{7,11},{8,12},{9,13},{1... | collective-permute-start | bytes 743432 | tf_op jit(solution)/shard_map/ppermute | solution.py:95
  105.4 2.7 %all-gather.1 = bf16[704,352]{1,0:T(8,128)(2,1)S(1)} all-gather(bf16[352,352]{1,0:T(8,128)(2,1)} %collective-permute-done.12), channel_id=3, replica_groups={{0,1},{2,3},{4,5},{6,7},{8,9},{10,11},{12,13},{14,15},{16,17},{18,19},{..., dimensions={0}, use_global_device_ids=true | all-gather | bytes 743424 | tf_op jit(solution)/shard_map/all_gather | solution.py:403
  108.1 2.2 %all-gather.2 = bf16[704,352]{1,0:T(8,128)(2,1)S(1)} all-gather(bf16[352,352]{1,0:T(8,128)(2,1)S(1)} %collective-permute-done.13), channel_id=4, replica_groups={{0,1},{2,3},{4,5},{6,7},{8,9},{10,11},{12,13},{14,15},{16,17},{18,19},{..., dimensions={0}, use_global_device_ids=true | all-gather | bytes 743424 | tf_op jit(solution)/shard_map/all_gather | solution.py:403
  110.3 2.5 %collective-permute-done.14 = bf16[352,352]{1,0:T(8,128)(2,1)S(1)} collective-permute-done((bf16[352,352]{1,0:T(8,128)(2,1)S(1)}, bf16[352,352]{1,0:T(8,128)(2,1)S(1)}, u32[]{:S(2)}, u32[]{:S(2)}) %collective-permute-start.14) | collective-permute-done | bytes 247840 | tf_op jit(solution)/shard_map/ppermute | solution.py:95
  112.8 3.0 %all-gather.3 = bf16[704,352]{1,0:T(8,128)(2,1)S(1)} all-gather(bf16[352,352]{1,0:T(8,128)(2,1)S(1)} %collective-permute-done.14), channel_id=5, replica_groups={{0,1},{2,3},{4,5},{6,7},{8,9},{10,11},{12,13},{14,15},{16,17},{18,19},{..., dimensions={0}, use_global_device_ids=true | all-gather | bytes 743424 | tf_op jit(solution)/shard_map/all_gather | solution.py:403
  115.8 0.5 collective-permute-done.7.refs_3_
  116.4 6.3 %shard_map.77 = (bf16[256,352]{1,0:T(8,128)(2,1)S(1)}, bf16[88,704]{1,0:T(8,128)(2,1)S(1)}) custom-call(s32[4]{0:T(128)S(1)} %pad_add_fusion.where, bf16[128,1408]{1,0:T(8,128)(2,1)S(1)} %collective-permute-done.4.refs_0_, bf16[128,1408]{1,0:T(8,128)(2,1)S(1)} %collective-permute-done.5.refs_1_, bf16[128,1408]{1,0:T(8,128)(2,1)S(1)} %collective-permute-done.6.refs_2_, ...), custom_call_target="tpu_custom_call" | custom-call | flops 507510784 | bytes 7096320 | tf_op jit(solution)/shard_map/pallas_call | solution.py:106
  122.6 2.3 %collective-permute-start.18 = (bf16[88,704]{1,0:T(8,128)(2,1)S(1)}, bf16[88,704]{1,0:T(8,128)(2,1)S(1)}, u32[]{:S(2)}, u32[]{:S(2)}) collective-permute-start(bf16[88,704]{1,0:T(8,128)(2,1)S(1)} %get-tuple-element.45), channel_id=1, source_target_pairs={{0,4},{1,5},{2,6},{3,7},{4,8},{5,9},{6,10},{7,11},{8,12},{9,13},{1... | collective-permute-start | bytes 371720 | tf_op jit(solution)/shard_map/ppermute | solution.py:95
  125.0 0.4 fusion.3
  125.4 3.0 %collective-permute-done.18 = bf16[88,704]{1,0:T(8,128)(2,1)S(1)} collective-permute-done((bf16[88,704]{1,0:T(8,128)(2,1)S(1)}, bf16[88,704]{1,0:T(8,128)(2,1)S(1)}, u32[]{:S(2)}, u32[]{:S(2)}) %collective-permute-start.18) | collective-permute-done | bytes 123936 | tf_op jit(solution)/shard_map/ppermute | solution.py:95
  128.4 0.5 collective-permute-start.19
  128.9 0.1 reshape.54.refs_4_
  129.0 0.1 reshape.55.refs_5_
  129.0 2.4 %collective-permute-start.15 = (bf16[256,352]{1,0:T(8,128)(2,1)S(1)}, bf16[256,352]{1,0:T(8,128)(2,1)}, u32[]{:S(2)}, u32[]{:S(2)}) collective-permute-start(bf16[256,352]{1,0:T(8,128)(2,1)S(1)} %get-tuple-element.43.refs_0_), channel_id=1, source_target_pairs={{0,16},{1,17},{2,18},{3,19},{4,20},{5,21},{6,22},{7,23},{8,24},{9,... | collective-permute-start | bytes 540680 | tf_op jit(solution)/shard_map/ppermute | solution.py:95
  131.4 1.3 collective-permute-start.16
  132.7 4.4 %all-gather.5 = bf16[176,704]{1,0:T(8,128)(2,1)S(1)} all-gather(bf16[88,704]{1,0:T(8,128)(2,1)S(1)} %get-tuple-element.45), channel_id=7, replica_groups={{0,1},{2,3},{4,5},{6,7},{8,9},{10,11},{12,13},{14,15},{16,17},{18,19},{..., dimensions={0}, use_global_device_ids=true | all-gather | bytes 371712 | tf_op jit(solution)/shard_map/all_gather | solution.py:403
  137.1 2.4 %all-gather.6 = bf16[176,704]{1,0:T(8,128)(2,1)S(1)} all-gather(bf16[88,704]{1,0:T(8,128)(2,1)S(1)} %collective-permute-done.18), channel_id=8, replica_groups={{0,1},{2,3},{4,5},{6,7},{8,9},{10,11},{12,13},{14,15},{16,17},{18,19},{..., dimensions={0}, use_global_device_ids=true | all-gather | bytes 371712 | tf_op jit(solution)/shard_map/all_gather | solution.py:403
  139.5 2.2 %all-gather.7 = bf16[176,704]{1,0:T(8,128)(2,1)S(1)} all-gather(bf16[88,704]{1,0:T(8,128)(2,1)} %collective-permute-done.19), channel_id=9, replica_groups={{0,1},{2,3},{4,5},{6,7},{8,9},{10,11},{12,13},{14,15},{16,17},{18,19},{..., dimensions={0}, use_global_device_ids=true | all-gather | bytes 371712 | tf_op jit(solution)/shard_map/all_gather | solution.py:403
  141.7 1.7 collective-permute-done.20
  143.4 3.5 %all-gather.8 = bf16[176,704]{1,0:T(8,128)(2,1)S(1)} all-gather(bf16[88,704]{1,0:T(8,128)(2,1)S(1)} %collective-permute-done.20), channel_id=10, replica_groups={{0,1},{2,3},{4,5},{6,7},{8,9},{10,11},{12,13},{14,15},{16,17},{18,19},{..., dimensions={0}, use_global_device_ids=true | all-gather | bytes 371712 | tf_op jit(solution)/shard_map/all_gather | solution.py:403
  146.9 5.5 %copy.15 = bf16[2816,528]{1,0:T(8,128)(2,1)} copy(bf16[2816,528]{0,1:T(8,128)(2,1)} %all-gather.13.cloned.1.call-done) | data formatting | bytes 5947392 | tf_op jit(solution)/shard_map/all_gather | solution.py:403
  152.4 2.0 %copy-done.1 = bf16[2816,528]{1,0:T(8,128)(2,1)S(1)} copy-done((bf16[2816,528]{1,0:T(8,128)(2,1)S(1)}, bf16[2816,528]{1,0:T(8,128)(2,1)}, u32[]{:S(2)}) %copy-start.1) | copy-done | bytes 2973720
  154.4 11.4 %shard_map.78 = (bf16[2,64,704]{2,1,0:T(8,128)(2,1)S(1)}, bf16[2,64,704]{2,1,0:T(8,128)(2,1)S(1)}, bf16[2,64,704]{2,1,0:T(8,128)(2,1)S(1)}, bf16[2,64,704]{2,1,0:T(8,128)(2,1)S(1)}, bf16[4,64,352]{2,1,0:T(8,128)(2,1)S(1)}) custom-call(s32[4]{0:T(128)S(1)} %pad_add_fusion.where, bf16[256,352]{1,0:T(8,128)(2,1)S(1)} %get-tuple-element.43.refs_0_, ...), custom_call_target="tpu_custom_call" | custom-call | flops 1268776960 | bytes 9394176 | tf_op jit(solution)/shard_map/pallas_call | solution.py:106
  165.9 0.8 collective-permute-start.21
  166.7 1.2 collective-permute-start.22
  167.9 0.7 collective-permute-start.23
  168.6 3.4 %collective-permute-done.21.refs_1_ = bf16[2,64,704]{2,1,0:T(8,128)(2,1)S(1)} collective-permute-done((bf16[2,64,704]{2,1,0:T(8,128)(2,1)S(1)}, bf16[2,64,704]{2,1,0:T(8,128)(2,1)S(1)}, u32[]{:S(2)}, u32[]{:S(2)}) %collective-permute-start.21) | collective-permute-done | bytes 180256 | tf_op jit(solution)/shard_map/ppermute | solution.py:95
  172.1 0.4 collective-permute-done.22.refs_2_
  172.5 5.0 %collective-permute-done.23.refs_3_ = bf16[2,64,704]{2,1,0:T(8,128)(2,1)S(1)} collective-permute-done((bf16[2,64,704]{2,1,0:T(8,128)(2,1)S(1)}, bf16[2,64,704]{2,1,0:T(8,128)(2,1)S(1)}, u32[]{:S(2)}, u32[]{:S(2)}) %collective-permute-start.23) | collective-permute-done | bytes 180256 | tf_op jit(solution)/shard_map/ppermute | solution.py:95
  177.5 0.7 shard_map.79
  178.2 3.4 %collective-permute-start.24 = (bf16[16,1408]{1,0:T(8,128)(2,1)S(1)}, bf16[16,1408]{1,0:T(8,128)(2,1)S(1)}, u32[]{:S(2)}, u32[]{:S(2)}) collective-permute-start(bf16[16,1408]{1,0:T(8,128)(2,1)S(1)} %get-tuple-element.51), channel_id=1, source_target_pairs={{0,0},{1,16},{2,2},{3,18},{4,4},{5,20},{6,6},{7,22},{8,8},{9,24},{... | collective-permute-start | bytes 135176 | tf_op jit(solution)/shard_map/ppermute | solution.py:95
  181.7 0.7 collective-permute-start.25
  182.3 2.0 %collective-permute-start.27 = (bf16[16,1408]{1,0:T(8,128)(2,1)S(1)}, bf16[16,1408]{1,0:T(8,128)(2,1)S(1)}, u32[]{:S(2)}, u32[]{:S(2)}) collective-permute-start(bf16[16,1408]{1,0:T(8,128)(2,1)S(1)} %get-tuple-element.54), channel_id=1, source_target_pairs={{0,4},{1,20},{2,6},{3,22},{4,8},{5,24},{6,10},{7,26},{8,12},{9,28}... | collective-permute-start | bytes 135176 | tf_op jit(solution)/shard_map/ppermute | solution.py:95
  184.4 2.0 %collective-permute-done.25.refs_1_ = bf16[16,1408]{1,0:T(8,128)(2,1)S(1)} collective-permute-done((bf16[16,1408]{1,0:T(8,128)(2,1)S(1)}, bf16[16,1408]{1,0:T(8,128)(2,1)S(1)}, u32[]{:S(2)}, u32[]{:S(2)}) %collective-permute-start.25) | collective-permute-done | bytes 45088 | tf_op jit(solution)/shard_map/ppermute | solution.py:95
  186.4 1.2 collective-permute-done.26.refs_2_
  187.6 1.0 collective-permute-done.27.refs_3_
  188.6 1.2 shard_map.80
  (43 shorter events, 0.5 us)
Async XLA Ops:
  6.5 118.4 %copy-start = (bf16[256,4224]{1,0:T(8,128)(2,1)S(1)}, bf16[256,4224]{1,0:T(8,128)(2,1)}, u32[]{:S(2)}) copy-start(bf16[256,4224]{1,0:T(8,128)(2,1)} %param.11) | copy-start | bytes 6488068
  6.5 58.1 %all-gather.15.cloned.1.call-start = ((), (), s32[]{:S(2)}) async-start(), calls=%async_computation.1 | async-start | bytes 2027520 | tf_op jit(solution)/shard_map/all_gather | solution.py:406
  6.6 1.3 copy-start.2
  7.9 1.0 copy-start.3
  8.9 0.9 copy-start.4
  12.3 11.4 %collective-permute-start.9 = (bf16[88,1232]{1,0:T(8,128)(2,1)S(1)}, bf16[88,1232]{1,0:T(8,128)(2,1)S(1)}, u32[]{:S(2)}, u32[]{:S(2)}) collective-permute-start(bf16[88,1232]{1,0:T(8,128)(2,1)S(1)} %get-tuple-element.37), channel_id=1, source_target_pairs={{0,1},{1,0},{2,3},{3,2},{4,5},{5,4},{6,7},{7,6},{8,9},{9,8},{10,11... | collective-permute-start | bytes 650504 | tf_op jit(solution)/shard_map/ppermute | solution.py:95
  12.4 11.3 %collective-permute-start.8 = (bf16[176,352]{1,0:T(8,128)(2,1)S(1)}, bf16[176,352]{1,0:T(8,128)(2,1)S(1)}, u32[]{:S(2)}, u32[]{:S(2)}) collective-permute-start(bf16[176,352]{1,0:T(8,128)(2,1)S(1)} %get-tuple-element.35), channel_id=1, source_target_pairs={{0,2},{1,3},{2,0},{3,1},{4,6},{5,7},{6,4},{7,5},{8,10},{9,11},{10,... | collective-permute-start | bytes 371720 | tf_op jit(solution)/shard_map/ppermute | solution.py:95
  15.0 6.3 %collective-permute-start.10 = (bf16[88,528]{1,0:T(8,128)(2,1)S(1)}, bf16[88,528]{1,0:T(8,128)(2,1)S(1)}, u32[]{:S(2)}, u32[]{:S(2)}) collective-permute-start(bf16[88,528]{1,0:T(8,128)(2,1)S(1)} %get-tuple-element.38), channel_id=1, source_target_pairs={{0,2},{1,3},{2,0},{3,1},{4,6},{5,7},{6,4},{7,5},{8,10},{9,11},{10,... | collective-permute-start | bytes 278792 | tf_op jit(solution)/shard_map/ppermute | solution.py:95
  15.1 8.7 %collective-permute-start.11 = (bf16[88,528]{1,0:T(8,128)(2,1)S(1)}, bf16[88,528]{1,0:T(8,128)(2,1)S(1)}, u32[]{:S(2)}, u32[]{:S(2)}) collective-permute-start(bf16[88,528]{1,0:T(8,128)(2,1)S(1)} %get-tuple-element.39), channel_id=1, source_target_pairs={{0,3},{1,2},{2,1},{3,0},{4,7},{5,6},{6,5},{7,4},{8,11},{9,10},{10,... | collective-permute-start | bytes 278792 | tf_op jit(solution)/shard_map/ppermute | solution.py:95
  25.5 121.4 %all-gather.13.cloned.1.call-start = ((), (), s32[]{:S(2)}) async-start(), calls=%async_computation | async-start | bytes 4460544 | tf_op jit(solution)/shard_map/all_gather | solution.py:403
  67.8 4.1 %copy-start.7 = (s32[4]{0:T(128)S(1)}, s32[4]{0:T(128)}, u32[]{:S(2)}) copy-start(s32[4]{0:T(128)} %param.9) | copy-start | bytes 52
  67.8 8.3 %copy-start.5 = (bf16[4,16,1408]{2,1,0:T(8,128)(2,1)S(1)}, bf16[4,16,1408]{2,1,0:T(8,128)(2,1)}, u32[]{:S(2)}) copy-start(bf16[4,16,1408]{2,1,0:T(8,128)(2,1)} %hidden.1) | copy-start | bytes 540676
  67.8 8.3 %copy-start.6 = (bf16[4,16,1408]{2,1,0:T(8,128)(2,1)S(1)}, bf16[4,16,1408]{2,1,0:T(8,128)(2,1)}, u32[]{:S(2)}) copy-start(bf16[4,16,1408]{2,1,0:T(8,128)(2,1)} %skip.1) | copy-start | bytes 540676
  71.9 10.1 %collective-permute-start.12 = (bf16[352,352]{1,0:T(8,128)(2,1)S(1)}, bf16[352,352]{1,0:T(8,128)(2,1)}, u32[]{:S(2)}, u32[]{:S(2)}) collective-permute-start(bf16[352,352]{1,0:T(8,128)(2,1)S(1)} %get-tuple-element.41), channel_id=1, source_target_pairs={{0,4},{1,5},{2,6},{3,7},{4,8},{5,9},{6,10},{7,11},{8,12},{9,13},{1... | collective-permute-start | bytes 743432 | tf_op jit(solution)/shard_map/ppermute | solution.py:95
  71.9 8.8 %collective-permute-start = (s32[4]{0:T(128)S(1)}, s32[4]{0:T(128)S(1)}, u32[]{:S(2)}, u32[]{:S(2)}) collective-permute-start(s32[4]{0:T(128)S(1)} %copy-done.7), channel_id=1, source_target_pairs={{0,0},{1,16},{2,2},{3,18},{4,4},{5,20},{6,6},{7,22},{8,8},{9,24},{... | collective-permute-start | bytes 56 | tf_op jit(solution)/shard_map/ppermute | solution.py:95
  77.2 6.6 %collective-permute-start.1 = (bf16[32,1408]{1,0:T(8,128)(2,1)S(1)}, bf16[32,1408]{1,0:T(8,128)(2,1)S(1)}, u32[]{:S(2)}, u32[]{:S(2)}) collective-permute-start(bf16[32,1408]{1,0:T(8,128)(2,1)S(1)} %get-tuple-element.31), channel_id=1, source_target_pairs={{0,4},{1,5},{2,6},{3,7},{4,8},{5,9},{6,10},{7,11},{8,12},{9,13},{1... | collective-permute-start | bytes 270344 | tf_op jit(solution)/shard_map/ppermute | solution.py:95
  78.4 10.1 %collective-permute-start.2 = (bf16[32,1408]{1,0:T(8,128)(2,1)S(1)}, bf16[32,1408]{1,0:T(8,128)(2,1)S(1)}, u32[]{:S(2)}, u32[]{:S(2)}) collective-permute-start(bf16[32,1408]{1,0:T(8,128)(2,1)S(1)} %get-tuple-element.32), channel_id=1, source_target_pairs={{0,8},{1,9},{2,10},{3,11},{4,12},{5,13},{6,14},{7,15},{8,0},{9,1},... | collective-permute-start | bytes 270344 | tf_op jit(solution)/shard_map/ppermute | solution.py:95
  80.7 7.9 %collective-permute-start.3 = (bf16[32,1408]{1,0:T(8,128)(2,1)S(1)}, bf16[32,1408]{1,0:T(8,128)(2,1)S(1)}, u32[]{:S(2)}, u32[]{:S(2)}) collective-permute-start(bf16[32,1408]{1,0:T(8,128)(2,1)S(1)} %get-tuple-element.33), channel_id=1, source_target_pairs={{0,12},{1,13},{2,14},{3,15},{4,0},{5,1},{6,2},{7,3},{8,4},{9,5},{1... | collective-permute-start | bytes 270344 | tf_op jit(solution)/shard_map/ppermute | solution.py:95
  82.0 21.3 %collective-permute-start.13 = (bf16[352,352]{1,0:T(8,128)(2,1)}, bf16[352,352]{1,0:T(8,128)(2,1)S(1)}, u32[]{:S(2)}, u32[]{:S(2)}) collective-permute-start(bf16[352,352]{1,0:T(8,128)(2,1)} %collective-permute-done.12), channel_id=1, source_target_pairs={{0,4},{1,5},{2,6},{3,7},{4,8},{5,9},{6,10},{7,11},{8,12},{9,13},{1... | collective-permute-start | bytes 743432 | tf_op jit(solution)/shard_map/ppermute | solution.py:95
  89.6 26.3 %collective-permute-start.4 = (bf16[128,1408]{1,0:T(8,128)(2,1)S(1)}, bf16[128,1408]{1,0:T(8,128)(2,1)S(1)}, u32[]{:S(2)}, u32[]{:S(2)}) collective-permute-start(bf16[128,1408]{1,0:T(8,128)(2,1)S(1)} %shard_map.74), channel_id=1, source_target_pairs={{0,0},{1,16},{2,2},{3,18},{4,4},{5,20},{6,6},{7,22},{8,8},{9,24},{... | collective-permute-start | bytes 1081352 | tf_op jit(solution)/shard_map/ppermute | solution.py:95
  98.4 17.5 %collective-permute-start.5 = (bf16[128,1408]{1,0:T(8,128)(2,1)S(1)}, bf16[128,1408]{1,0:T(8,128)(2,1)S(1)}, u32[]{:S(2)}, u32[]{:S(2)}) collective-permute-start(bf16[128,1408]{1,0:T(8,128)(2,1)S(1)} %shard_map.74), channel_id=1, source_target_pairs={{0,16},{1,0},{2,18},{3,2},{4,20},{5,4},{6,22},{7,6},{8,24},{9,8},{... | collective-permute-start | bytes 1081352 | tf_op jit(solution)/shard_map/ppermute | solution.py:95
  98.4 17.4 %collective-permute-start.6 = (bf16[128,1408]{1,0:T(8,128)(2,1)S(1)}, bf16[128,1408]{1,0:T(8,128)(2,1)S(1)}, u32[]{:S(2)}, u32[]{:S(2)}) collective-permute-start(bf16[128,1408]{1,0:T(8,128)(2,1)S(1)} %shard_map.74), channel_id=1, source_target_pairs={{0,2},{1,18},{2,0},{3,16},{4,6},{5,22},{6,4},{7,20},{8,10},{9,26},... | collective-permute-start | bytes 1081352 | tf_op jit(solution)/shard_map/ppermute | solution.py:95
  99.4 17.0 %collective-permute-start.7 = (bf16[128,1408]{1,0:T(8,128)(2,1)S(1)}, bf16[128,1408]{1,0:T(8,128)(2,1)S(1)}, u32[]{:S(2)}, u32[]{:S(2)}) collective-permute-start(bf16[128,1408]{1,0:T(8,128)(2,1)S(1)} %shard_map.74), channel_id=1, source_target_pairs={{0,18},{1,2},{2,16},{3,0},{4,22},{5,6},{6,20},{7,4},{8,26},{9,10},... | collective-permute-start | bytes 1081352 | tf_op jit(solution)/shard_map/ppermute | solution.py:95
  103.3 9.5 %collective-permute-start.14 = (bf16[352,352]{1,0:T(8,128)(2,1)S(1)}, bf16[352,352]{1,0:T(8,128)(2,1)S(1)}, u32[]{:S(2)}, u32[]{:S(2)}) collective-permute-start(bf16[352,352]{1,0:T(8,128)(2,1)S(1)} %collective-permute-done.13), channel_id=1, source_target_pairs={{0,4},{1,5},{2,6},{3,7},{4,8},{5,9},{6,10},{7,11},{8,12},{9,13},{1... | collective-permute-start | bytes 743432 | tf_op jit(solution)/shard_map/ppermute | solution.py:95
  122.6 5.7 %collective-permute-start.18 = (bf16[88,704]{1,0:T(8,128)(2,1)S(1)}, bf16[88,704]{1,0:T(8,128)(2,1)S(1)}, u32[]{:S(2)}, u32[]{:S(2)}) collective-permute-start(bf16[88,704]{1,0:T(8,128)(2,1)S(1)} %get-tuple-element.45), channel_id=1, source_target_pairs={{0,4},{1,5},{2,6},{3,7},{4,8},{5,9},{6,10},{7,11},{8,12},{9,13},{1... | collective-permute-start | bytes 371720 | tf_op jit(solution)/shard_map/ppermute | solution.py:95
  128.4 8.7 %collective-permute-start.19 = (bf16[88,704]{1,0:T(8,128)(2,1)S(1)}, bf16[88,704]{1,0:T(8,128)(2,1)}, u32[]{:S(2)}, u32[]{:S(2)}) collective-permute-start(bf16[88,704]{1,0:T(8,128)(2,1)S(1)} %collective-permute-done.18), channel_id=1, source_target_pairs={{0,4},{1,5},{2,6},{3,7},{4,8},{5,9},{6,10},{7,11},{8,12},{9,13},{1... | collective-permute-start | bytes 371720 | tf_op jit(solution)/shard_map/ppermute | solution.py:95
  129.0 23.4 %collective-permute-start.15 = (bf16[256,352]{1,0:T(8,128)(2,1)S(1)}, bf16[256,352]{1,0:T(8,128)(2,1)}, u32[]{:S(2)}, u32[]{:S(2)}) collective-permute-start(bf16[256,352]{1,0:T(8,128)(2,1)S(1)} %get-tuple-element.43.refs_0_), channel_id=1, source_target_pairs={{0,16},{1,17},{2,18},{3,19},{4,20},{5,21},{6,22},{7,23},{8,24},{9,... | collective-permute-start | bytes 540680 | tf_op jit(solution)/shard_map/ppermute | solution.py:95
  131.4 21.0 %collective-permute-start.16 = (bf16[256,352]{1,0:T(8,128)(2,1)S(1)}, bf16[256,352]{1,0:T(8,128)(2,1)}, u32[]{:S(2)}, u32[]{:S(2)}) collective-permute-start(bf16[256,352]{1,0:T(8,128)(2,1)S(1)} %get-tuple-element.43.refs_0_), channel_id=1, source_target_pairs={{0,2},{1,3},{2,0},{3,1},{4,6},{5,7},{6,4},{7,5},{8,10},{9,11},{10,... | collective-permute-start | bytes 540680 | tf_op jit(solution)/shard_map/ppermute | solution.py:95
  132.7 19.7 %collective-permute-start.17 = (bf16[256,352]{1,0:T(8,128)(2,1)S(1)}, bf16[256,352]{1,0:T(8,128)(2,1)}, u32[]{:S(2)}, u32[]{:S(2)}) collective-permute-start(bf16[256,352]{1,0:T(8,128)(2,1)S(1)} %get-tuple-element.43.refs_0_), channel_id=1, source_target_pairs={{0,18},{1,19},{2,16},{3,17},{4,22},{5,23},{6,20},{7,21},{8,26},{9,... | collective-permute-start | bytes 540680 | tf_op jit(solution)/shard_map/ppermute | solution.py:95
  137.1 6.3 %collective-permute-start.20 = (bf16[88,704]{1,0:T(8,128)(2,1)}, bf16[88,704]{1,0:T(8,128)(2,1)S(1)}, u32[]{:S(2)}, u32[]{:S(2)}) collective-permute-start(bf16[88,704]{1,0:T(8,128)(2,1)} %collective-permute-done.19), channel_id=1, source_target_pairs={{0,4},{1,5},{2,6},{3,7},{4,8},{5,9},{6,10},{7,11},{8,12},{9,13},{1... | collective-permute-start | bytes 371720 | tf_op jit(solution)/shard_map/ppermute | solution.py:95
  152.4 2.0 %copy-start.1 = (bf16[2816,528]{1,0:T(8,128)(2,1)S(1)}, bf16[2816,528]{1,0:T(8,128)(2,1)}, u32[]{:S(2)}) copy-start(bf16[2816,528]{1,0:T(8,128)(2,1)} %copy.15) | copy-start | bytes 8921092
  165.9 6.2 %collective-permute-start.21 = (bf16[2,64,704]{2,1,0:T(8,128)(2,1)S(1)}, bf16[2,64,704]{2,1,0:T(8,128)(2,1)S(1)}, u32[]{:S(2)}, u32[]{:S(2)}) collective-permute-start(bf16[2,64,704]{2,1,0:T(8,128)(2,1)S(1)} %get-tuple-element.48), channel_id=1, source_target_pairs={{0,16},{1,17},{2,18},{3,19},{4,20},{5,21},{6,22},{7,23},{8,24},{9,... | collective-permute-start | bytes 540680 | tf_op jit(solution)/shard_map/ppermute | solution.py:95
  166.7 5.8 %collective-permute-start.22 = (bf16[2,64,704]{2,1,0:T(8,128)(2,1)S(1)}, bf16[2,64,704]{2,1,0:T(8,128)(2,1)S(1)}, u32[]{:S(2)}, u32[]{:S(2)}) collective-permute-start(bf16[2,64,704]{2,1,0:T(8,128)(2,1)S(1)} %get-tuple-element.49), channel_id=1, source_target_pairs={{0,2},{1,3},{2,0},{3,1},{4,6},{5,7},{6,4},{7,5},{8,10},{9,11},{10,... | collective-permute-start | bytes 540680 | tf_op jit(solution)/shard_map/ppermute | solution.py:95
  167.9 9.6 %collective-permute-start.23 = (bf16[2,64,704]{2,1,0:T(8,128)(2,1)S(1)}, bf16[2,64,704]{2,1,0:T(8,128)(2,1)S(1)}, u32[]{:S(2)}, u32[]{:S(2)}) collective-permute-start(bf16[2,64,704]{2,1,0:T(8,128)(2,1)S(1)} %get-tuple-element.50), channel_id=1, source_target_pairs={{0,18},{1,19},{2,16},{3,17},{4,22},{5,23},{6,20},{7,21},{8,26},{9,... | collective-permute-start | bytes 540680 | tf_op jit(solution)/shard_map/ppermute | solution.py:95
  178.2 6.1 %collective-permute-start.24 = (bf16[16,1408]{1,0:T(8,128)(2,1)S(1)}, bf16[16,1408]{1,0:T(8,128)(2,1)S(1)}, u32[]{:S(2)}, u32[]{:S(2)}) collective-permute-start(bf16[16,1408]{1,0:T(8,128)(2,1)S(1)} %get-tuple-element.51), channel_id=1, source_target_pairs={{0,0},{1,16},{2,2},{3,18},{4,4},{5,20},{6,6},{7,22},{8,8},{9,24},{... | collective-permute-start | bytes 135176 | tf_op jit(solution)/shard_map/ppermute | solution.py:95
  181.7 4.7 %collective-permute-start.25 = (bf16[16,1408]{1,0:T(8,128)(2,1)S(1)}, bf16[16,1408]{1,0:T(8,128)(2,1)S(1)}, u32[]{:S(2)}, u32[]{:S(2)}) collective-permute-start(bf16[16,1408]{1,0:T(8,128)(2,1)S(1)} %get-tuple-element.52), channel_id=1, source_target_pairs={{0,12},{1,28},{2,14},{3,30},{4,0},{5,16},{6,2},{7,18},{8,4},{9,20}... | collective-permute-start | bytes 135176 | tf_op jit(solution)/shard_map/ppermute | solution.py:95
  182.3 5.3 %collective-permute-start.26 = (bf16[16,1408]{1,0:T(8,128)(2,1)S(1)}, bf16[16,1408]{1,0:T(8,128)(2,1)S(1)}, u32[]{:S(2)}, u32[]{:S(2)}) collective-permute-start(bf16[16,1408]{1,0:T(8,128)(2,1)S(1)} %get-tuple-element.53), channel_id=1, source_target_pairs={{0,8},{1,24},{2,10},{3,26},{4,12},{5,28},{6,14},{7,30},{8,0},{9,16... | collective-permute-start | bytes 135176 | tf_op jit(solution)/shard_map/ppermute | solution.py:95
  182.3 6.3 %collective-permute-start.27 = (bf16[16,1408]{1,0:T(8,128)(2,1)S(1)}, bf16[16,1408]{1,0:T(8,128)(2,1)S(1)}, u32[]{:S(2)}, u32[]{:S(2)}) collective-permute-start(bf16[16,1408]{1,0:T(8,128)(2,1)S(1)} %get-tuple-element.54), channel_id=1, source_target_pairs={{0,4},{1,20},{2,6},{3,22},{4,8},{5,24},{6,10},{7,26},{8,12},{9,28}... | collective-permute-start | bytes 135176 | tf_op jit(solution)/shard_map/ppermute | solution.py:95
Sparse Core Ops, SparseCore 0:
  25.6 38.9 all-gather.14
  72.0 11.1 all-gather.12

commit v4 on v3

--- a/solution.py
+++ b/solution.py
@@ -98,21 +98,27 @@
         return x * self.n + (z * self.Y + y) * self.G + c
 
 
-def call(kernel, outs, where, *arrays, scratch=(), copies=0, flops=0, vmem_out=True, vmem_in=False):
+def call(kernel, outs, where, *arrays, scratch=(), copies=0, flops=0, fast=(), fast_in=False):
     moved = sum(a.size * a.dtype.itemsize for a in arrays)
-    space = pltpu.VMEM if vmem_in else pl.ANY
-    where_out = pltpu.VMEM if vmem_out else pl.ANY
+    space = pltpu.VMEM if fast_in else pltpu.HBM
     sems = [pltpu.SemaphoreType.DMA((copies,))] if copies else []
     return pl.pallas_call(
         kernel,
-        out_shape=[jax.ShapeDtypeStruct(s, d) for s, d in outs],
+        out_shape=[jax.ShapeDtypeStruct(s, BF) for s in outs],
         in_specs=[pl.BlockSpec(memory_space=pltpu.SMEM)]
         + [pl.BlockSpec(memory_space=space)] * len(arrays),
-        out_specs=[pl.BlockSpec(memory_space=where_out)] * len(outs),
+        out_specs=[
+            pl.BlockSpec(memory_space=pltpu.VMEM if k in fast else pl.ANY)
+            for k in range(len(outs))
+        ],
         scratch_shapes=list(scratch) + sems,
         compiler_params=pltpu.CompilerParams(vmem_limit_bytes=40 * 2**20),
         cost_estimate=pl.CostEstimate(flops=flops, bytes_accessed=2 * moved, transcendentals=0),
     )(where, *arrays)
+
+
+def after(value, *others):
+    return lax.optimization_barrier((value, *others))[0]
 
 
 def copy_all(pairs, sems):
@@ -123,25 +129,18 @@
         copy.wait()
 
 
-def pieces_kernel(S, where, hidden, skip, *refs):
-    outs, sems = refs[:S], refs[S]
-    z = where[1]
-    local = hidden.shape[1]
-    pairs = []
-    for s in range(S):
-        at = (z + s) % S
-        pairs.append((hidden.at[at], outs[s].at[pl.ds(0, local)]))
-        pairs.append((skip.at[at], outs[s].at[pl.ds(local, local)]))
-    copy_all(pairs, sems)
-
-
-def slices_kernel(G, S, Y, where, w_skip_any, w_qkv_any, w_out_any, *refs):
+def join_kernel(where, hidden, skip, out, sems):
+    copy_all([(hidden, out.at[0]), (skip, out.at[1])], sems)
+
+
+def cut_kernel(G, S, Y, where, w_skip_any, w_qkv_any, w_out_any, *refs):
     outs, (w_skip, w_qkv, w_out, sems) = refs[:-4], refs[-4:]
+    skips, qkvs, rest = outs[0], outs[1 : 1 + Y * G], outs[1 + Y * G]
     copy_all([(w_skip_any, w_skip), (w_qkv_any, w_qkv), (w_out_any, w_out)], sems)
     x, y, c = where[0], where[2], where[3]
     width = w_skip.shape[1]
-    block, part, half = width // (G * Y), S // G * HD, width // G
-    skips, qkvs, rest = outs[:Y], outs[Y : Y + Y * G], outs[Y + Y * G]
+    block, part, half = width // (G * Y), 3 * (S // G) * HD, width // G
+    rows = w_skip.shape[0]
     for gx in range(G):
         for gy in range(Y):
             for e in range(Y):
@@ -149,7 +148,13 @@
                 @pl.when((x == gx) & ((y + e) % Y == gy))
                 def _():
                     b = gx * Y + gy
-                    skips[e][...] = w_skip[:, b * block : (b + 1) * block]
+                    if e == 0:
+                        skips[...] = w_skip[:, b * block : (b + 1) * block]
+                    else:
+                        for r in range(rows // HD):
+                            qkvs[e * G][:, part + r * block : part + (r + 1) * block] = w_skip[
+                                r * HD : (r + 1) * HD, b * block : (b + 1) * block
+                            ]
                     for gc in range(G):
                         for f in range(G):
 
@@ -159,7 +164,7 @@
                                     for t in range(S // G):
                                         head = ((gc * (S // G) + t) * Y + gy) * G + gx
                                         at = p * width + head * HD
-                                        to = p * part + t * HD
+                                        to = (p * (S // G) + t) * HD
                                         qkvs[e * G + f][:, to : to + HD] = w_qkv[:, at : at + HD]
 
     for gc in range(G):
@@ -168,22 +173,34 @@
             @pl.when((c + f) % G == gc)
             def _():
                 to = rest if f == 0 else qkvs[f]
-                at = 0 if f == 0 else 3 * part
+                at = 0 if f == 0 else part
                 to[:, at : at + half] = w_out[:, gc * half : (gc + 1) * half]
 
-
-def join_kernel(S, where, *refs):
-    rows = refs[0].shape[0]
-    copy_all([(refs[s], refs[S].at[pl.ds(s * rows, rows)]) for s in range(S)], refs[S + 1])
+def stack_kernel(where, *refs):
+    *pieces, out, sems = refs
+    copy_all([(v, out.at[s]) for s, v in enumerate(pieces)], sems)
+
+
+def ring_kernel(Y, part, where, own, *refs):
+    others, out = refs[:-1], refs[-1]
+    y = where[2]
+    rows, cols = own.shape
+
+    def place(e):
+        return pl.multiple_of((y + Y - e) % Y * rows, 16)
+
+    out[pl.ds(place(0), rows), :] = own[...]
+    for e in range(1, Y):
+        v = others[e - 1]
+        both = [v[:, part + r * cols : part + (r + 1) * cols] for r in range(rows // HD)]
+        out[pl.ds(place(e), rows), :] = jnp.concatenate(both, axis=0)
 
 
 def shards_kernel(G, S, Y, where, *refs):
-    skips, qkvs, rest = refs[:Y], refs[Y : Y + Y * G], refs[Y + Y * G]
-    ring, qkv, out = refs[Y + Y * G + 1 :]
+    qkvs, rest = refs[: Y * G], refs[Y * G]
+    qkv, out = refs[Y * G + 1 :]
     x, y, c = where[0], where[2], where[3]
-    rows, part = skips[0].shape[0], S // G * HD
-    for e in range(Y):
-        ring[e * rows : (e + 1) * rows, :] = skips[e][...]
+    part = 3 * (S // G) * HD
     for gy in range(Y):
         for gc in range(G):
             for e in range(Y):
@@ -192,42 +209,39 @@
                     @pl.when(((y + Y - e) % Y == gy) & ((c + G - f) % G == gc))
                     def _():
                         at = (gy * G + gc) * HD
-                        qkv[at : at + HD, :] = qkvs[e * G + f][:, : 3 * part]
+                        qkv[at : at + HD, :] = qkvs[e * G + f][:, :part]
 
     out[...] = rest[...]
     for f in range(1, G):
 
         @pl.when((c + G - f) % G == x)
         def _():
-            out[...] = qkvs[f][:, 3 * part :]
+            out[...] = qkvs[f][:, part:]
 
 
 def merged_kernel(G, S, Y, where, *refs):
-    z, y = where[1], where[2]
+    z, c = where[1], where[3]
     blocks = Y * G
-    parts, weights, held = refs[:blocks], refs[blocks : blocks + S], refs[blocks + S]
-    out, on, xs, ws, sems = refs[blocks + S + 1 :]
-    width = parts[0].shape[1]
-    local = parts[0].shape[0] // (2 * S)
-    rows = weights[0].shape[1] // Y
-    pairs = [(held, on)]
+    parts, weights = refs[:blocks], refs[blocks : blocks + G * S]
+    outs, (xs, ws, ms, sems) = refs[blocks + G * S : -4], refs[-4:]
+    width = parts[0].shape[3]
+    rows = weights[0].shape[0] // Y
+    pairs = []
     for k in range(blocks):
+        for h in range(2):
+            pairs.append((parts[k].at[h], xs.at[k, :, :, pl.ds(h * width, width)]))
+    for f in range(G):
         for s in range(S):
-            for h in range(2):
-                pairs.append(
-                    (
-                        parts[k].at[pl.ds((2 * s + h) * local, local)],
-                        xs.at[pl.ds((k * S + s) * local, local), pl.ds(h * width, width)],
-                    )
-                )
+            for y in range(Y):
+                to = ws.at[(z + S - s) % S, y, (c + G - f) % G]
+                pairs.append((weights[f * S + s].at[pl.ds(y * rows, rows)], to))
+    copy_all(pairs, sems)
+    weight = ws[...].reshape(2 * width, ws.shape[-1])
+    tokens = xs[...].reshape(-1, 2 * width)
+    merged = jnp.dot(tokens, weight, preferred_element_type=F32).astype(BF)
+    ms[...] = merged.reshape(ms.shape)
     for s in range(S):
-        for f in range(G):
-            for e in range(Y):
-                j = (((z + S - s) % S) * Y + (y + Y - e) % Y) * G + f
-                at = pl.multiple_of(j * rows, 16)
-                pairs.append((weights[s].at[f, pl.ds(e * rows, rows)], ws.at[pl.ds(at, rows)]))
-    copy_all(pairs, sems)
-    out[...] = jnp.dot(xs[...], ws[...], preferred_element_type=F32).astype(BF)
+        outs[s][...] = ms[:, (z + s) % S]
 
 
 def norm88(v):
@@ -238,38 +252,42 @@
 
 
 def attend_kernel(G, S, Y, where, *refs):
-    x, z, y = where[0], where[1], where[2]
+    x, z, y, c = where[0], where[1], where[2], where[3]
     blocks = Y * G
     merged_any, (shift, scale) = refs[:blocks], refs[blocks : blocks + 2]
-    wq_any, wo_any, refs = refs[blocks + 2], refs[blocks + 3 : blocks + 3 + S], refs[blocks + 3 + S :]
+    refs = refs[blocks + 2 :]
+    wq_any, wo_any, refs = refs[: G * S], refs[G * S : 2 * G * S], refs[2 * G * S :]
     outs, base, (merged, norm, shifts, scales, wq, wo, att, sems) = (
         refs[:blocks],
         refs[blocks],
         refs[blocks + 1 :],
     )
-    rows, cols = merged_any[0].shape
-    toks = rows // blocks
+    cols = merged_any[0].shape[3]
+    toks = S * merged_any[0].shape[2]
+    rows = blocks * toks
     width = cols * blocks
 
-    pairs = [(shift, shifts), (scale, scales), (wq_any, wq)]
-    for s in range(S):
-        pairs.append((wo_any[s], wo.at[(z + S - s) % S]))
+    pairs = [(shift, shifts), (scale, scales)]
+    for f in range(G):
+        for s in range(S):
+            pairs.append((wq_any[f * S + s], wq.at[(c + G - f) % G, (z + S - s) % S]))
+        for s in range(S):
+            pairs.append((wo_any[f * S + s], wo.at[(z + S - s) % S, (c + G - f) % G]))
     for e in range(Y):
         for d in range(G):
             b = (x + d) % G * Y + (y + e) % Y
             for em in range(Y):
                 for dm in range(G):
-                    at = (((em - e) % Y) * G + (dm - d) % G) * toks
-                    to = (em * G + dm) * toks
+                    at = (em - e) % Y * G + (dm - d) % G
                     pairs.append(
-                        (merged_any[e * G + d].at[pl.ds(at, toks)], merged.at[b, pl.ds(to, toks)])
+                        (merged_any[e * G + d].at[:, at], merged.at[b, em * G + dm])
                     )
     copy_all(pairs, sems)
     total = jnp.zeros((rows, 1), F32)
     wide = []
     for b in range(blocks):
-        base[b] = merged[b, :toks, :]
-        wide.append(merged[b].astype(F32))
+        base[b] = merged[b, 0].reshape(toks, cols)
+        wide.append(merged[b].reshape(rows, cols).astype(F32))
         total = total + jnp.sum(wide[-1], axis=-1, keepdims=True)
     mean = total * (1.0 / width)
     square = jnp.zeros((rows, 1), F32)
@@ -280,11 +298,9 @@
         norm[b] = ((wide[b] - mean) * inv * (1.0 + scales[b]) + shifts[b]).astype(BF)
     per = S // G
     for f in range(G):
-        qkv = jnp.dot(norm[0], wq[f, :cols], preferred_element_type=F32)
+        qkv = jnp.dot(norm[0], wq[f, 0], preferred_element_type=F32)
         for b in range(1, blocks):
-            qkv = qkv + jnp.dot(
-                norm[b], wq[f, b * cols : (b + 1) * cols], preferred_element_type=F32
-            )
+            qkv = qkv + jnp.dot(norm[b], wq[f, b], preferred_element_type=F32)
         for t in range(per):
             q, k, v = (qkv[:, (p * per + t) * HD : (p * per + t + 1) * HD] for p in range(3))
             q = (norm88(q) * HD ** (-0.5)).astype(BF)
@@ -337,22 +353,20 @@
     part = 3 * (S // G) * HD
     every = blocks * toks
 
-    cut = call(
-        partial(pieces_kernel, S),
-        [((2 * local, width), BF)] * S,
-        p.where,
-        hidden,
-        skip,
-        copies=2 * S,
-        vmem_out=False,
-    )
-    outs = [((rows, cols), BF)] * Y
+    def swap(value, e, f):
+        return p.send(value, lambda x, z, y, c: (x, z, y + e, c + f))
+
+    (joined,) = call(
+        join_kernel, [(2, S, local, width)], p.where, hidden, skip, copies=2
+    )
+    outs = [(rows, cols)]
     for e in range(Y):
         for f in range(G):
-            outs.append(((HD, part + (half if f and not e else 0)), BF))
-    outs.append(((HD, half), BF))
-    slices = call(
-        partial(slices_kernel, G, S, Y),
+            more = (half if f and not e else 0) + (2 * cols if e and not f else 0)
+            outs.append((HD, part + more))
+    outs.append((HD, half))
+    skips, *qkvs, rest = call(
+        partial(cut_kernel, G, S, Y),
         outs,
         p.where,
         w_skip,
@@ -360,70 +374,77 @@
         w_out,
         scratch=[pltpu.VMEM(w.shape, BF) for w in (w_skip, w_qkv, w_out)],
         copies=3,
-    )
-    skips, qkvs, rest = list(slices[:Y]), list(slices[Y : Y + Y * G]), slices[Y + Y * G]
-
-    cut = [cut[0]] + [
-        p.send(cut[s], lambda x, z, y, c, s=s: (x, z + s, y, c)) for s in range(1, S)
-    ]
-    (joined,) = call(
-        partial(join_kernel, S), [((2 * toks, width), BF)], p.where, *cut, copies=S, vmem_out=False
-    )
-    parts = [
-        p.send(joined, lambda x, z, y, c, e=e, d=d: (c - d, z, y - e, x))
-        for e in range(Y)
-        for d in range(G)
-    ]
-
-    for e in range(1, Y):
-        skips[e] = p.send(skips[e], lambda x, z, y, c, e=e: (x, z, y + e, c))
+        fast=range(len(outs)),
+    )
+    own = qkvs[0]
+    qkvs = [swap(qkvs[e * G + f], e, f) if e or f else own for e in range(Y) for f in range(G)]
+    parts = []
     for e in range(Y):
-        for f in range(G):
-            if e or f:
-                qkvs[e * G + f] = p.send(
-                    qkvs[e * G + f], lambda x, z, y, c, e=e, f=f: (x, z, y + e, c + f)
-                )
-    ring, wq, wo = call(
+        for d in range(G):
+            value = joined if len(parts) < 2 else after(joined, qkvs[G], qkvs[len(parts)])
+            parts.append(p.send(value, lambda x, z, y, c, e=e, d=d: (c - d, z, y - e, x)))
+
+    def step(value):
+        return p.send(value, lambda x, z, y, c: (x, z + 1, y, c))
+
+    def over_cores(held):
+        return held + [swap(v, 0, f) for f in range(1, G) for v in held]
+
+    (ring,) = call(
+        partial(ring_kernel, Y, part),
+        [(Y * rows, cols)],
+        p.where,
+        skips,
+        *[qkvs[e * G] for e in range(1, Y)],
+        fast=[0],
+        fast_in=True,
+    )
+    wq, wo = call(
         partial(shards_kernel, G, S, Y),
-        [((Y * rows, cols), BF), ((blocks * HD, part), BF), ((HD, half), BF)],
+        [(blocks * HD, part), (HD, half)],
         p.where,
-        *skips,
         *qkvs,
         rest,
-        vmem_in=True,
-    )
-
-    def round_planes(value):
-        held = [value]
-        for _ in range(1, S):
-            held.append(p.send(held[-1], lambda x, z, y, c: (x, z + 1, y, c)))
-        return held
-
-    def both_cores(value):
-        return lax.all_gather(value, "seq", axis=0, axis_index_groups=p.cores)
-
-    ws = [both_cores(v) for v in round_planes(ring)]
-    wq = lax.all_gather(wq, "seq", axis=0, tiled=True, axis_index_groups=p.column)
-    wq = both_cores(wq)
+        fast=[0, 1],
+        fast_in=True,
+    )
+    ws = [ring]
+    for _ in range(1, S):
+        ws.append(step(ws[-1]))
+    wq = [after(wq, ws[2])]
+    for _ in range(1, S):
+        wq.append(step(wq[-1]))
+    wo = [after(wo, wq[2])]
+    for _ in range(1, S):
+        wo.append(step(wo[-1]))
+    ws, wq, wo = over_cores(ws), over_cores(wq), over_cores(wo)
 
     times = p.send(timestep, lambda x, z, y, c: (c, z, y, x))
     mod = modulation(lax.dynamic_slice(times, (p.z,), (1,)), w_mod)
     shift = mod[:, :width].reshape(blocks, 1, cols)
     scale = mod[:, width : 2 * width].reshape(blocks, 1, cols)
     gate = mod[:, 2 * width :]
-
-    merged, wo = call(
+    parts[0] = after(parts[0], mod)
+
+    pieces = call(
         partial(merged_kernel, G, S, Y),
-        [((every, cols), BF), ((HD, half), BF)],
+        [(blocks, local, cols)] * S,
         p.where,
         *parts,
         *ws,
-        wo,
-        scratch=[pltpu.VMEM((every, 2 * width), BF), pltpu.VMEM((2 * width, cols), BF)],
-        copies=1 + 2 * blocks * S + S * G * Y,
+        scratch=[
+            pltpu.VMEM((blocks, S, local, 2 * width), BF),
+            pltpu.VMEM((S, Y, G, rows, cols), BF),
+            pltpu.VMEM((blocks, S, local, cols), BF),
+        ],
+        copies=2 * blocks + S * G * Y,
         flops=4 * every * width * cols,
-    )
-    wo = [both_cores(v) for v in round_planes(wo)]
+        fast=range(S),
+    )
+    pieces = [pieces[0]] + [
+        p.send(pieces[s], lambda x, z, y, c, s=s: (x, z + s, y, c)) for s in range(1, S)
+    ]
+    (merged,) = call(stack_kernel, [(S, blocks, local, cols)], p.where, *pieces, copies=S)
     merged = [
         p.send(merged, lambda x, z, y, c, e=e, d=d: (x - d, z, y - e, c)) if e or d else merged
         for e in range(Y)
@@ -431,24 +452,25 @@
     ]
     *parts, base = call(
         partial(attend_kernel, G, S, Y),
-        [((G, toks, half), BF)] * blocks + [((blocks, toks, cols), BF)],
+        [(G, toks, half)] * blocks + [(blocks, toks, cols)],
         p.where,
         *merged,
         shift,
         scale,
-        wq,
+        *wq,
         *wo,
         scratch=[
-            pltpu.VMEM((blocks, every, cols), BF),
+            pltpu.VMEM((blocks, blocks, S, local, cols), BF),
             pltpu.VMEM((blocks, every, cols), BF),
             pltpu.VMEM((blocks, 1, cols), F32),
             pltpu.VMEM((blocks, 1, cols), F32),
-            pltpu.VMEM((G, width, part), BF),
+            pltpu.VMEM((G, S, cols, part), BF),
             pltpu.VMEM((S, G, HD, half), BF),
             pltpu.VMEM((S, every, HD), BF),
         ],
-        copies=3 + S + blocks * blocks,
+        copies=2 + 2 * G * S + blocks * blocks,
         flops=10 * every * width * cols,
+        fast=range(blocks + 1),
     )
     parts = [
         p.send(parts[e * G + d], lambda x, z, y, c, e=e, d=d: (x + d, z, y + e, c))
@@ -459,21 +481,17 @@
     ]
     result = call(
         partial(result_kernel, G, S, Y),
-        [((local, width), BF)] * S,
+        [(local, width)] * S,
         p.where,
         gate,
         base,
         *parts,
-        vmem_in=True,
+        fast=range(S),
+        fast_in=True,
     )
     result = [p.send(result[s], lambda x, z, y, c, s=s: (c, z - s, y, x)) for s in range(S)]
     (out,) = call(
-        partial(home_kernel, S),
-        [((S, local, width), BF)],
-        p.where,
-        *result,
-        copies=S,
-        vmem_out=False,
+        partial(home_kernel, S), [(S, local, width)], p.where, *result, copies=S
     )
     return out
 

time: 197 us -> 143 us (0.73)
  waiting for transfers between devices: 71.7 us -> 47.2 us
  blocking collectives: 23.2 us -> 0 us
  between operations: 14.3 us -> 1.01 us
  starting transfers between devices: 42.2 us -> 54.4 us
  local copies, waits for them, and re-layouts: 19.7 us -> 15.5 us
    all_gather x2 -> x0, waiting for transfers between devices: 39.1 us -> none  [the longest x1 39.1 us: in_planes(): lax.all_gather(wq, 'seq', axis=0, tiled=True, axis_index_groups=p.column)]
    all_gather x8 -> x0, blocking collectives: 23.2 us -> none  [both_cores(): return lax.all_gather(value, 'seq', axis=0, axis_index_groups=p.cores)]
    ppermute x28 -> x42, waiting for transfers between devices: 32.6 us -> 47.2 us  [send(): return lax.ppermute(value, ('group', 'seq'), pairs)]
    ppermute x28 -> x42, starting transfers between devices: 42.2 us -> 54.4 us  [send(): return lax.ppermute(value, ('group', 'seq'), pairs)]
    all_gather x2 -> x0, local copies, waits for them, and re-layouts: 8.71 us -> none  [the longest x1 5.5 us: both_cores(): return lax.all_gather(value, 'seq', axis=0, axis_index_groups=p.cores)]
    unnamed x18 -> x52, local copies, waits for them, and re-layouts: 10.2 us -> 14.7 us
    pallas_call x8 -> x9, Pallas kernels: 25 us -> 24.2 us  [call(): pl.pallas_call(kernel, out_shape=[jax.ShapeDtypeStruct(s, BF) for s in ou...]
  transfers between devices with their start and end apart: 30 -> 42, of which waited for: 15 -> 20; matrix products, arithmetic and copies ran while one was open for 3% -> 1% of each run, Pallas kernels for 4% -> 5%
where the time goes in v4:
time: 143 us
  starting transfers between devices  54.4 us (38%)
  waiting for transfers between devices  47.2 us (33%)
  Pallas kernels  24.2 us (17%)
  local copies, waits for them, and re-layouts  15.5 us (11%)
    ppermute x42, starting transfers between devices, send(): return lax.ppermute(value, ('group', 'seq'), pairs)  54.4 us
    ppermute x42, waiting for transfers between devices, send(): return lax.ppermute(value, ('group', 'seq'), pairs)  47.2 us
    pallas_call x9, Pallas kernels, call(): pl.pallas_call(kernel, out_shape=[jax.ShapeDtypeStruct(s, BF) for s in ou...  24.2 us
    unnamed x52, local copies, waits for them, and re-layouts  14.7 us
  transfers between devices with their start and end apart: 42, of which 20 were waited for; matrix products, arithmetic and copies ran while one was open for 1% of the time, Pallas kernels for 5%

profile of v4, /device:TPU:1, one launch (start us, length us, event | category | flops | bytes accessed | tf_op | source)
XLA Modules:
  0.0 142.9 jit_solution(4389012329912957692)
XLA Ops:
  0.1 1.3 copy-done.1
  1.3 1.0 copy-done.2
  2.4 0.9 copy-done.13
  3.3 2.5 %shard_map.74 = (bf16[176,352]{1,0:T(8,128)(2,1)S(1)}, bf16[88,528]{1,0:T(8,128)(2,1)S(1)}, bf16[88,1232]{1,0:T(8,128)(2,1)S(1)}, bf16[88,1232]{1,0:T(8,128)(2,1...) custom-call(s32[4]{0:T(128)S(1)} %pad_add_fusion.where, bf16[176,1408]{1,0:T(8,128)(2,1)S(1)} %copy-done.2, ...), custom_call_target="tpu_custom_call" | custom-call | bytes 2973696 | tf_op jit(solution)/shard_map/pallas_call | solution.py:105
  5.8 2.2 %collective-permute-start.3 = (bf16[88,1232]{1,0:T(8,128)(2,1)S(1)}, bf16[88,1232]{1,0:T(8,128)(2,1)S(1)}, u32[]{:S(2)}, u32[]{:S(2)}) collective-permute-start(bf16[88,1232]{1,0:T(8,128)(2,1)S(1)} %get-tuple-element.32), channel_id=1, source_target_pairs={{0,2},{1,3},{2,0},{3,1},{4,6},{5,7},{6,4},{7,5},{8,10},{9,11},{10,... | collective-permute-start | bytes 650504 | tf_op jit(solution)/shard_map/ppermute | solution.py:95
  8.0 5.4 %collective-permute-done.3.refs_0_.refs_2_ = bf16[88,1232]{1,0:T(8,128)(2,1)S(1)} collective-permute-done((bf16[88,1232]{1,0:T(8,128)(2,1)S(1)}, bf16[88,1232]{1,0:T(8,128)(2,1)S(1)}, u32[]{:S(2)}, u32[]{:S(2)}) %collective-permute-start.3) | collective-permute-done | bytes 216864 | tf_op jit(solution)/shard_map/ppermute | solution.py:95
  14.1 1.2 collective-permute-start.7
  15.2 7.5 %collective-permute-done.7.refs_5_ = bf16[352,352]{1,0:T(8,128)(2,1)S(1)} collective-permute-done((bf16[352,352]{1,0:T(8,128)(2,1)S(1)}, bf16[352,352]{1,0:T(8,128)(2,1)S(1)}, u32[]{:S(2)}, u32[]{:S(2)}) %collective-permute-start.7) | collective-permute-done | bytes 247840 | tf_op jit(solution)/shard_map/ppermute | solution.py:95
  22.8 2.0 %collective-permute-start.20 = (bf16[88,1232]{1,0:T(8,128)(2,1)S(1)}, bf16[88,1232]{1,0:T(8,128)(2,1)S(1)}, u32[]{:S(2)}, u32[]{:S(2)}) collective-permute-start(bf16[88,1232]{1,0:T(8,128)(2,1)S(1)} %get-tuple-element.42), channel_id=1, source_target_pairs={{0,1},{1,0},{2,3},{3,2},{4,5},{5,4},{6,7},{7,6},{8,9},{9,8},{10,11... | collective-permute-start | bytes 650504 | tf_op jit(solution)/shard_map/ppermute | solution.py:95
  24.8 1.3 shard_map.73
  26.2 3.5 %collective-permute-start.1 = (bf16[2,4,16,1408]{3,2,1,0:T(8,128)(2,1)}, bf16[2,4,16,1408]{3,2,1,0:T(8,128)(2,1)S(1)}, u32[]{:S(2)}, u32[]{:S(2)}) collective-permute-start(bf16[2,4,16,1408]{3,2,1,0:T(8,128)(2,1)} %shard_map.73), channel_id=1, source_target_pairs={{0,0},{1,16},{2,2},{3,18},{4,4},{5,20},{6,6},{7,22},{8,8},{9,24},{... | collective-permute-start | bytes 1081352 | tf_op jit(solution)/shard_map/ppermute | solution.py:95
  29.7 0.7 collective-permute-start.5
  30.4 3.9 %collective-permute-done.5.refs_3_ = bf16[88,528]{1,0:T(8,128)(2,1)S(1)} collective-permute-done((bf16[88,528]{1,0:T(8,128)(2,1)S(1)}, bf16[88,528]{1,0:T(8,128)(2,1)S(1)}, u32[]{:S(2)}, u32[]{:S(2)}) %collective-permute-start.5) | collective-permute-done | bytes 92960 | tf_op jit(solution)/shard_map/ppermute | solution.py:95
  34.3 0.8 shard_map.78
  35.8 1.0 collective-permute-start.21
  36.8 2.9 %collective-permute-start = (s32[4]{0:T(128)S(1)}, s32[4]{0:T(128)S(1)}, u32[]{:S(2)}, u32[]{:S(2)}) collective-permute-start(s32[4]{0:T(128)S(1)} %copy-done.25), channel_id=1, source_target_pairs={{0,0},{1,16},{2,2},{3,18},{4,4},{5,20},{6,6},{7,22},{8,8},{9,24},{... | collective-permute-start | bytes 56 | tf_op jit(solution)/shard_map/ppermute | solution.py:95
  39.7 1.4 %collective-permute-start.4 = (bf16[2,4,16,1408]{3,2,1,0:T(8,128)(2,1)}, bf16[2,4,16,1408]{3,2,1,0:T(8,128)(2,1)}, u32[]{:S(2)}, u32[]{:S(2)}) collective-permute-start(bf16[2,4,16,1408]{3,2,1,0:T(8,128)(2,1)} %shard_map.73), channel_id=1, source_target_pairs={{0,2},{1,18},{2,0},{3,16},{4,6},{5,22},{6,4},{7,20},{8,10},{9,26},... | collective-permute-start | bytes 1081352 | tf_op jit(solution)/shard_map/ppermute | solution.py:95
  41.1 0.9 collective-permute-done
  42.8 2.1 %collective-permute-start.10 = (bf16[352,352]{1,0:T(8,128)(2,1)S(1)}, bf16[352,352]{1,0:T(8,128)(2,1)}, u32[]{:S(2)}, u32[]{:S(2)}) collective-permute-start(bf16[352,352]{1,0:T(8,128)(2,1)S(1)} %shard_map.75.refs_4_), channel_id=1, source_target_pairs={{0,1},{1,0},{2,3},{3,2},{4,5},{5,4},{6,7},{7,6},{8,9},{9,8},{10,11... | collective-permute-start | bytes 743432 | tf_op jit(solution)/shard_map/ppermute | solution.py:95
  44.9 0.8 copy-done.9
  45.6 1.3 collective-permute-start.9
  48.3 1.9 %collective-permute-done.21.refs_7_ = bf16[352,528]{1,0:T(8,128)(2,1)S(1)} collective-permute-done((bf16[352,528]{1,0:T(8,128)(2,1)S(1)}, bf16[352,528]{1,0:T(8,128)(2,1)S(1)}, u32[]{:S(2)}, u32[]{:S(2)}) %collective-permute-start.21) | collective-permute-done | bytes 371744 | tf_op jit(solution)/shard_map/ppermute | solution.py:95
  50.8 2.8 %collective-permute-start.24 = (bf16[352,528]{1,0:T(8,128)(2,1)S(1)}, bf16[352,528]{1,0:T(8,128)(2,1)S(1)}, u32[]{:S(2)}, u32[]{:S(2)}) collective-permute-start(bf16[352,528]{1,0:T(8,128)(2,1)S(1)} %get-tuple-element.45.refs_6_), channel_id=1, source_target_pairs={{0,1},{1,0},{2,3},{3,2},{4,5},{5,4},{6,7},{7,6},{8,9},{9,8},{10,11... | collective-permute-start | bytes 1115144 | tf_op jit(solution)/shard_map/ppermute | solution.py:95
  53.6 1.2 collective-permute-done.6.refs_3_
  54.8 2.1 %collective-permute-start.12 = (bf16[352,352]{1,0:T(8,128)(2,1)}, bf16[352,352]{1,0:T(8,128)(2,1)S(1)}, u32[]{:S(2)}, u32[]{:S(2)}) collective-permute-start(bf16[352,352]{1,0:T(8,128)(2,1)} %collective-permute-done.8.refs_6_), channel_id=1, source_target_pairs={{0,1},{1,0},{2,3},{3,2},{4,5},{5,4},{6,7},{7,6},{8,9},{9,8},{10,11... | collective-permute-start | bytes 743432 | tf_op jit(solution)/shard_map/ppermute | solution.py:95
  57.4 0.9 collective-permute-done.12.refs_10_
  58.7 3.8 %shard_map.76 = (bf16[4,16,352]{2,1,0:T(8,128)(2,1)S(1)}, bf16[4,16,352]{2,1,0:T(8,128)(2,1)S(1)}, bf16[4,16,352]{2,1,0:T(8,128)(2,1)S(1)}, bf16[4,16,352]{2,1,0:T(8,128)(2,1)S(1)}) custom-call(s32[4]{0:T(128)S(1)} %pad_add_fusion.where, bf16[2,4,16,1408]{3,2,1,0:T(8,128)(2,1)S(1)} %copy-done.10, bf16[2,4,16,1408]{3,2,1,0:T(8,128)(2,1)S(1)} %copy-done.8, ...), custom_call_target="tpu_custom_call" | custom-call | flops 507510784 | bytes 6848512 | tf_op jit(solution)/shard_map/pallas_call | solution.py:105
  62.5 1.3 collective-permute-start.14
  63.9 1.6 %collective-permute-start.15 = (bf16[4,16,352]{2,1,0:T(8,128)(2,1)S(1)}, bf16[4,16,352]{2,1,0:T(8,128)(2,1)S(1)}, u32[]{:S(2)}, u32[]{:S(2)}) collective-permute-start(bf16[4,16,352]{2,1,0:T(8,128)(2,1)S(1)} %get-tuple-element.39), channel_id=1, source_target_pairs={{0,8},{1,9},{2,10},{3,11},{4,12},{5,13},{6,14},{7,15},{8,0},{9,1},... | collective-permute-start | bytes 135176 | tf_op jit(solution)/shard_map/ppermute | solution.py:95
  65.5 2.3 %collective-permute-start.16 = (bf16[4,16,352]{2,1,0:T(8,128)(2,1)S(1)}, bf16[4,16,352]{2,1,0:T(8,128)(2,1)S(1)}, u32[]{:S(2)}, u32[]{:S(2)}) collective-permute-start(bf16[4,16,352]{2,1,0:T(8,128)(2,1)S(1)} %get-tuple-element.40), channel_id=1, source_target_pairs={{0,12},{1,13},{2,14},{3,15},{4,0},{5,1},{6,2},{7,3},{8,4},{9,5},{1... | collective-permute-start | bytes 135176 | tf_op jit(solution)/shard_map/ppermute | solution.py:95
  67.8 0.9 collective-permute-done.15.refs_2_
  68.7 0.8 collective-permute-done.16.refs_3_
  69.6 0.8 shard_map.77.refs_0_
  70.4 1.5 %collective-permute-start.19 = (bf16[4,4,16,352]{3,2,1,0:T(8,128)(2,1)S(1)}, bf16[4,4,16,352]{3,2,1,0:T(8,128)(2,1)S(1)}, u32[]{:S(2)}, u32[]{:S(2)}) collective-permute-start(bf16[4,4,16,352]{3,2,1,0:T(8,128)(2,1)S(1)} %shard_map.77.refs_0_), channel_id=1, source_target_pairs={{0,18},{1,19},{2,16},{3,17},{4,22},{5,23},{6,20},{7,21},{8,26},{9,... | collective-permute-start | bytes 540680 | tf_op jit(solution)/shard_map/ppermute | solution.py:95
  71.9 1.5 %collective-permute-start.25 = (bf16[352,528]{1,0:T(8,128)(2,1)S(1)}, bf16[352,528]{1,0:T(8,128)(2,1)S(1)}, u32[]{:S(2)}, u32[]{:S(2)}) collective-permute-start(bf16[352,528]{1,0:T(8,128)(2,1)S(1)} %collective-permute-done.21.refs_7_), channel_id=1, source_target_pairs={{0,1},{1,0},{2,3},{3,2},{4,5},{5,4},{6,7},{7,6},{8,9},{9,8},{10,11... | collective-permute-start | bytes 1115144 | tf_op jit(solution)/shard_map/ppermute | solution.py:95
  73.4 1.0 collective-permute-start.28
  74.4 0.8 copy-done.3
  75.4 0.8 collective-permute-done.19.refs_3_
  76.3 0.9 collective-permute-start.17
  77.2 6.2 %collective-permute-done.28.refs_15_ = bf16[88,704]{1,0:T(8,128)(2,1)} collective-permute-done((bf16[88,704]{1,0:T(8,128)(2,1)S(1)}, bf16[88,704]{1,0:T(8,128)(2,1)}, u32[]{:S(2)}, u32[]{:S(2)}) %collective-permute-start.28) | collective-permute-done | bytes 123936 | tf_op jit(solution)/shard_map/ppermute | solution.py:95
  84.1 2.1 %collective-permute-start.26 = (bf16[352,528]{1,0:T(8,128)(2,1)}, bf16[352,528]{1,0:T(8,128)(2,1)}, u32[]{:S(2)}, u32[]{:S(2)}) collective-permute-start(bf16[352,528]{1,0:T(8,128)(2,1)} %collective-permute-done.22.refs_8_), channel_id=1, source_target_pairs={{0,1},{1,0},{2,3},{3,2},{4,5},{5,4},{6,7},{7,6},{8,9},{9,8},{10,11... | collective-permute-start | bytes 1115144 | tf_op jit(solution)/shard_map/ppermute | solution.py:95
  87.4 1.9 %collective-permute-done.29.refs_16_ = bf16[88,704]{1,0:T(8,128)(2,1)} collective-permute-done((bf16[88,704]{1,0:T(8,128)(2,1)}, bf16[88,704]{1,0:T(8,128)(2,1)}, u32[]{:S(2)}, u32[]{:S(2)}) %collective-permute-start.29) | collective-permute-done | bytes 123936 | tf_op jit(solution)/shard_map/ppermute | solution.py:95
  89.4 0.8 copy-done.5
  90.2 3.3 %collective-permute-start.32 = (bf16[88,704]{1,0:T(8,128)(2,1)}, bf16[88,704]{1,0:T(8,128)(2,1)}, u32[]{:S(2)}, u32[]{:S(2)}) collective-permute-start(bf16[88,704]{1,0:T(8,128)(2,1)} %collective-permute-done.28.refs_15_), channel_id=1, source_target_pairs={{0,1},{1,0},{2,3},{3,2},{4,5},{5,4},{6,7},{7,6},{8,9},{9,8},{10,11... | collective-permute-start | bytes 371720 | tf_op jit(solution)/shard_map/ppermute | solution.py:95
  94.2 1.2 collective-permute-done.30.refs_17_
  95.4 4.4 %collective-permute-start.34 = (bf16[88,704]{1,0:T(8,128)(2,1)}, bf16[88,704]{1,0:T(8,128)(2,1)}, u32[]{:S(2)}, u32[]{:S(2)}) collective-permute-start(bf16[88,704]{1,0:T(8,128)(2,1)} %collective-permute-done.30.refs_17_), channel_id=1, source_target_pairs={{0,1},{1,0},{2,3},{3,2},{4,5},{5,4},{6,7},{7,6},{8,9},{9,8},{10,11... | collective-permute-start | bytes 371720 | tf_op jit(solution)/shard_map/ppermute | solution.py:95
  100.0 1.1 collective-permute-done.34.refs_21_
  101.1 1.0 copy-done.4
  102.2 1.0 copy-done.6
  103.2 0.9 copy-done.15
  104.1 0.9 copy-done.17
  105.0 0.9 copy-done.22
  105.9 0.9 copy-done.24
  106.8 12.4 %shard_map.79 = (bf16[2,64,704]{2,1,0:T(8,128)(2,1)S(1)}, bf16[2,64,704]{2,1,0:T(8,128)(2,1)S(1)}, bf16[2,64,704]{2,1,0:T(8,128)(2,1)S(1)}, bf16[2,64,704]{2,1,0:T(8,128)(2,1)S(1)}, bf16[4,64,352]{2,1,0:T(8,128)(2,1)S(1)}) custom-call(s32[4]{0:T(128)S(1)} %pad_add_fusion.where, bf16[4,4,16,352]{3,2,1,0:T(8,128)(2,1)S(1)} %shard_map.77.refs_0_, ...), custom_call_target="tpu_custom_call" | custom-call | flops 1268776960 | bytes 9394176 | tf_op jit(solution)/shard_map/pallas_call | solution.py:105
  119.3 1.1 collective-permute-start.36
  120.4 1.6 %collective-permute-start.37 = (bf16[2,64,704]{2,1,0:T(8,128)(2,1)S(1)}, bf16[2,64,704]{2,1,0:T(8,128)(2,1)S(1)}, u32[]{:S(2)}, u32[]{:S(2)}) collective-permute-start(bf16[2,64,704]{2,1,0:T(8,128)(2,1)S(1)} %get-tuple-element.52), channel_id=1, source_target_pairs={{0,18},{1,19},{2,16},{3,17},{4,22},{5,23},{6,20},{7,21},{8,26},{9,... | collective-permute-start | bytes 540680 | tf_op jit(solution)/shard_map/ppermute | solution.py:95
  121.9 3.5 %collective-permute-done.35.refs_1_ = bf16[2,64,704]{2,1,0:T(8,128)(2,1)S(1)} collective-permute-done((bf16[2,64,704]{2,1,0:T(8,128)(2,1)S(1)}, bf16[2,64,704]{2,1,0:T(8,128)(2,1)S(1)}, u32[]{:S(2)}, u32[]{:S(2)}) %collective-permute-start.35) | collective-permute-done | bytes 180256 | tf_op jit(solution)/shard_map/ppermute | solution.py:95
  125.4 4.5 %collective-permute-done.37.refs_3_ = bf16[2,64,704]{2,1,0:T(8,128)(2,1)S(1)} collective-permute-done((bf16[2,64,704]{2,1,0:T(8,128)(2,1)S(1)}, bf16[2,64,704]{2,1,0:T(8,128)(2,1)S(1)}, u32[]{:S(2)}, u32[]{:S(2)}) %collective-permute-start.37) | collective-permute-done | bytes 180256 | tf_op jit(solution)/shard_map/ppermute | solution.py:95
  130.6 4.2 %collective-permute-start.38 = (bf16[16,1408]{1,0:T(8,128)(2,1)S(1)}, bf16[16,1408]{1,0:T(8,128)(2,1)S(1)}, u32[]{:S(2)}, u32[]{:S(2)}) collective-permute-start(bf16[16,1408]{1,0:T(8,128)(2,1)S(1)} %get-tuple-element.53), channel_id=1, source_target_pairs={{0,0},{1,16},{2,2},{3,18},{4,4},{5,20},{6,6},{7,22},{8,8},{9,24},{... | collective-permute-start | bytes 135176 | tf_op jit(solution)/shard_map/ppermute | solution.py:95
  135.2 2.4 %collective-permute-start.41 = (bf16[16,1408]{1,0:T(8,128)(2,1)S(1)}, bf16[16,1408]{1,0:T(8,128)(2,1)S(1)}, u32[]{:S(2)}, u32[]{:S(2)}) collective-permute-start(bf16[16,1408]{1,0:T(8,128)(2,1)S(1)} %get-tuple-element.56), channel_id=1, source_target_pairs={{0,4},{1,20},{2,6},{3,22},{4,8},{5,24},{6,10},{7,26},{8,12},{9,28}... | collective-permute-start | bytes 135176 | tf_op jit(solution)/shard_map/ppermute | solution.py:95
  137.5 1.7 %collective-permute-done.39.refs_1_ = bf16[16,1408]{1,0:T(8,128)(2,1)S(1)} collective-permute-done((bf16[16,1408]{1,0:T(8,128)(2,1)S(1)}, bf16[16,1408]{1,0:T(8,128)(2,1)S(1)}, u32[]{:S(2)}, u32[]{:S(2)}) %collective-permute-start.39) | collective-permute-done | bytes 45088 | tf_op jit(solution)/shard_map/ppermute | solution.py:95
  139.2 1.0 collective-permute-done.40.refs_2_
  140.2 1.3 collective-permute-done.41.refs_3_
  141.5 1.2 shard_map.81
  (90 shorter events, 8.6 us)
Async XLA Ops:
  0.0 57.0 %copy-start = (bf16[256,4224]{1,0:T(8,128)(2,1)S(1)}, bf16[256,4224]{1,0:T(8,128)(2,1)}, u32[]{:S(2)}) copy-start(bf16[256,4224]{1,0:T(8,128)(2,1)} %param.11) | copy-start | bytes 6488068
  0.0 36.8 %copy-start.25 = (s32[4]{0:T(128)S(1)}, s32[4]{0:T(128)}, u32[]{:S(2)}) copy-start(s32[4]{0:T(128)} %param.9) | copy-start | bytes 52
  0.1 1.3 copy-start.1
  1.3 1.0 copy-start.2
  2.4 0.9 copy-start.13
  3.3 21.5 %copy-start.18 = (bf16[4,16,1408]{2,1,0:T(8,128)(2,1)S(1)}, bf16[4,16,1408]{2,1,0:T(8,128)(2,1)}, u32[]{:S(2)}) copy-start(bf16[4,16,1408]{2,1,0:T(8,128)(2,1)} %hidden.1) | copy-start | bytes 540676
  3.3 21.5 %copy-start.19 = (bf16[4,16,1408]{2,1,0:T(8,128)(2,1)S(1)}, bf16[4,16,1408]{2,1,0:T(8,128)(2,1)}, u32[]{:S(2)}) copy-start(bf16[4,16,1408]{2,1,0:T(8,128)(2,1)} %skip.1) | copy-start | bytes 540676
  5.8 7.6 %collective-permute-start.3 = (bf16[88,1232]{1,0:T(8,128)(2,1)S(1)}, bf16[88,1232]{1,0:T(8,128)(2,1)S(1)}, u32[]{:S(2)}, u32[]{:S(2)}) collective-permute-start(bf16[88,1232]{1,0:T(8,128)(2,1)S(1)} %get-tuple-element.32), channel_id=1, source_target_pairs={{0,2},{1,3},{2,0},{3,1},{4,6},{5,7},{6,4},{7,5},{8,10},{9,11},{10,... | collective-permute-start | bytes 650504 | tf_op jit(solution)/shard_map/ppermute | solution.py:95
  14.1 8.7 %collective-permute-start.7 = (bf16[352,352]{1,0:T(8,128)(2,1)S(1)}, bf16[352,352]{1,0:T(8,128)(2,1)S(1)}, u32[]{:S(2)}, u32[]{:S(2)}) collective-permute-start(bf16[352,352]{1,0:T(8,128)(2,1)S(1)} %shard_map.75.refs_4_), channel_id=1, source_target_pairs={{0,4},{1,5},{2,6},{3,7},{4,8},{5,9},{6,10},{7,11},{8,12},{9,13},{1... | collective-permute-start | bytes 743432 | tf_op jit(solution)/shard_map/ppermute | solution.py:95
  22.8 22.1 %copy-start.11 = (bf16[352,352]{1,0:T(8,128)(2,1)}, bf16[352,352]{1,0:T(8,128)(2,1)S(1)}, u32[]{:S(2)}) copy-start(bf16[352,352]{1,0:T(8,128)(2,1)S(1)} %collective-permute-done.7.refs_5_) | copy-start | bytes 743428
  22.8 13.0 %collective-permute-start.8 = (bf16[352,352]{1,0:T(8,128)(2,1)S(1)}, bf16[352,352]{1,0:T(8,128)(2,1)}, u32[]{:S(2)}, u32[]{:S(2)}) collective-permute-start(bf16[352,352]{1,0:T(8,128)(2,1)S(1)} %collective-permute-done.7.refs_5_), channel_id=1, source_target_pairs={{0,4},{1,5},{2,6},{3,7},{4,8},{5,9},{6,10},{7,11},{8,12},{9,13},{1... | collective-permute-start | bytes 743432 | tf_op jit(solution)/shard_map/ppermute | solution.py:95
  22.8 11.5 %collective-permute-start.20 = (bf16[88,1232]{1,0:T(8,128)(2,1)S(1)}, bf16[88,1232]{1,0:T(8,128)(2,1)S(1)}, u32[]{:S(2)}, u32[]{:S(2)}) collective-permute-start(bf16[88,1232]{1,0:T(8,128)(2,1)S(1)} %get-tuple-element.42), channel_id=1, source_target_pairs={{0,1},{1,0},{2,3},{3,2},{4,5},{5,4},{6,7},{7,6},{8,9},{9,8},{10,11... | collective-permute-start | bytes 650504 | tf_op jit(solution)/shard_map/ppermute | solution.py:95
  26.1 15.9 %collective-permute-start.2 = (bf16[2,4,16,1408]{3,2,1,0:T(8,128)(2,1)}, bf16[2,4,16,1408]{3,2,1,0:T(8,128)(2,1)S(1)}, u32[]{:S(2)}, u32[]{:S(2)}) collective-permute-start(bf16[2,4,16,1408]{3,2,1,0:T(8,128)(2,1)} %shard_map.73), channel_id=1, source_target_pairs={{0,16},{1,0},{2,18},{3,2},{4,20},{5,4},{6,22},{7,6},{8,24},{9,8},{... | collective-permute-start | bytes 1081352 | tf_op jit(solution)/shard_map/ppermute | solution.py:95
  26.2 18.7 %collective-permute-start.1 = (bf16[2,4,16,1408]{3,2,1,0:T(8,128)(2,1)}, bf16[2,4,16,1408]{3,2,1,0:T(8,128)(2,1)S(1)}, u32[]{:S(2)}, u32[]{:S(2)}) collective-permute-start(bf16[2,4,16,1408]{3,2,1,0:T(8,128)(2,1)} %shard_map.73), channel_id=1, source_target_pairs={{0,0},{1,16},{2,2},{3,18},{4,4},{5,20},{6,6},{7,22},{8,8},{9,24},{... | collective-permute-start | bytes 1081352 | tf_op jit(solution)/shard_map/ppermute | solution.py:95
  29.7 4.7 %collective-permute-start.5 = (bf16[88,528]{1,0:T(8,128)(2,1)S(1)}, bf16[88,528]{1,0:T(8,128)(2,1)S(1)}, u32[]{:S(2)}, u32[]{:S(2)}) collective-permute-start(bf16[88,528]{1,0:T(8,128)(2,1)S(1)} %get-tuple-element.34), channel_id=1, source_target_pairs={{0,3},{1,2},{2,1},{3,0},{4,7},{5,6},{6,5},{7,4},{8,11},{9,10},{10,... | collective-permute-start | bytes 278792 | tf_op jit(solution)/shard_map/ppermute | solution.py:95
  35.8 14.4 %collective-permute-start.21 = (bf16[352,528]{1,0:T(8,128)(2,1)S(1)}, bf16[352,528]{1,0:T(8,128)(2,1)S(1)}, u32[]{:S(2)}, u32[]{:S(2)}) collective-permute-start(bf16[352,528]{1,0:T(8,128)(2,1)S(1)} %get-tuple-element.45.refs_6_), channel_id=1, source_target_pairs={{0,4},{1,5},{2,6},{3,7},{4,8},{5,9},{6,10},{7,11},{8,12},{9,13},{1... | collective-permute-start | bytes 1115144 | tf_op jit(solution)/shard_map/ppermute | solution.py:95
  36.8 5.2 %collective-permute-start = (s32[4]{0:T(128)S(1)}, s32[4]{0:T(128)S(1)}, u32[]{:S(2)}, u32[]{:S(2)}) collective-permute-start(s32[4]{0:T(128)S(1)} %copy-done.25), channel_id=1, source_target_pairs={{0,0},{1,16},{2,2},{3,18},{4,4},{5,20},{6,6},{7,22},{8,8},{9,24},{... | collective-permute-start | bytes 56 | tf_op jit(solution)/shard_map/ppermute | solution.py:95
  39.7 11.1 %collective-permute-start.4 = (bf16[2,4,16,1408]{3,2,1,0:T(8,128)(2,1)}, bf16[2,4,16,1408]{3,2,1,0:T(8,128)(2,1)}, u32[]{:S(2)}, u32[]{:S(2)}) collective-permute-start(bf16[2,4,16,1408]{3,2,1,0:T(8,128)(2,1)} %shard_map.73), channel_id=1, source_target_pairs={{0,2},{1,18},{2,0},{3,16},{4,6},{5,22},{6,4},{7,20},{8,10},{9,26},... | collective-permute-start | bytes 1081352 | tf_op jit(solution)/shard_map/ppermute | solution.py:95
  42.0 12.8 %collective-permute-start.6 = (bf16[2,4,16,1408]{3,2,1,0:T(8,128)(2,1)}, bf16[2,4,16,1408]{3,2,1,0:T(8,128)(2,1)}, u32[]{:S(2)}, u32[]{:S(2)}) collective-permute-start(bf16[2,4,16,1408]{3,2,1,0:T(8,128)(2,1)} %shard_map.73), channel_id=1, source_target_pairs={{0,18},{1,2},{2,16},{3,0},{4,22},{5,6},{6,20},{7,4},{8,26},{9,10},... | collective-permute-start | bytes 1081352 | tf_op jit(solution)/shard_map/ppermute | solution.py:95
  42.0 0.7 copy-start.7
  42.8 7.4 %collective-permute-start.10 = (bf16[352,352]{1,0:T(8,128)(2,1)S(1)}, bf16[352,352]{1,0:T(8,128)(2,1)}, u32[]{:S(2)}, u32[]{:S(2)}) collective-permute-start(bf16[352,352]{1,0:T(8,128)(2,1)S(1)} %shard_map.75.refs_4_), channel_id=1, source_target_pairs={{0,1},{1,0},{2,3},{3,2},{4,5},{5,4},{6,7},{7,6},{8,9},{9,8},{10,11... | collective-permute-start | bytes 743432 | tf_op jit(solution)/shard_map/ppermute | solution.py:95
  44.9 0.8 copy-start.9
  45.6 11.3 %collective-permute-start.9 = (bf16[352,352]{1,0:T(8,128)(2,1)}, bf16[352,352]{1,0:T(8,128)(2,1)}, u32[]{:S(2)}, u32[]{:S(2)}) collective-permute-start(bf16[352,352]{1,0:T(8,128)(2,1)} %collective-permute-done.8.refs_6_), channel_id=1, source_target_pairs={{0,4},{1,5},{2,6},{3,7},{4,8},{5,9},{6,10},{7,11},{8,12},{9,13},{1... | collective-permute-start | bytes 743432 | tf_op jit(solution)/shard_map/ppermute | solution.py:95
  46.9 11.8 %copy-start.8 = (bf16[2,4,16,1408]{3,2,1,0:T(8,128)(2,1)S(1)}, bf16[2,4,16,1408]{3,2,1,0:T(8,128)(2,1)}, u32[]{:S(2)}) copy-start(bf16[2,4,16,1408]{3,2,1,0:T(8,128)(2,1)} %copy-done.7) | copy-start | bytes 1081348
  46.9 11.8 %copy-start.10 = (bf16[2,4,16,1408]{3,2,1,0:T(8,128)(2,1)S(1)}, bf16[2,4,16,1408]{3,2,1,0:T(8,128)(2,1)}, u32[]{:S(2)}) copy-start(bf16[2,4,16,1408]{3,2,1,0:T(8,128)(2,1)} %copy-done.9) | copy-start | bytes 1081348
  46.9 11.8 %copy-start.12 = (bf16[352,352]{1,0:T(8,128)(2,1)S(1)}, bf16[352,352]{1,0:T(8,128)(2,1)}, u32[]{:S(2)}) copy-start(bf16[352,352]{1,0:T(8,128)(2,1)} %copy-done.11) | copy-start | bytes 743428
  50.2 17.6 %collective-permute-start.22 = (bf16[352,528]{1,0:T(8,128)(2,1)S(1)}, bf16[352,528]{1,0:T(8,128)(2,1)}, u32[]{:S(2)}, u32[]{:S(2)}) collective-permute-start(bf16[352,528]{1,0:T(8,128)(2,1)S(1)} %collective-permute-done.21.refs_7_), channel_id=1, source_target_pairs={{0,4},{1,5},{2,6},{3,7},{4,8},{5,9},{6,10},{7,11},{8,12},{9,13},{1... | collective-permute-start | bytes 1115144 | tf_op jit(solution)/shard_map/ppermute | solution.py:95
  50.2 7.2 %collective-permute-start.11 = (bf16[352,352]{1,0:T(8,128)(2,1)}, bf16[352,352]{1,0:T(8,128)(2,1)S(1)}, u32[]{:S(2)}, u32[]{:S(2)}) collective-permute-start(bf16[352,352]{1,0:T(8,128)(2,1)} %copy-done.11), channel_id=1, source_target_pairs={{0,1},{1,0},{2,3},{3,2},{4,5},{5,4},{6,7},{7,6},{8,9},{9,8},{10,11... | collective-permute-start | bytes 743432 | tf_op jit(solution)/shard_map/ppermute | solution.py:95
  50.8 23.6 %collective-permute-start.24 = (bf16[352,528]{1,0:T(8,128)(2,1)S(1)}, bf16[352,528]{1,0:T(8,128)(2,1)S(1)}, u32[]{:S(2)}, u32[]{:S(2)}) collective-permute-start(bf16[352,528]{1,0:T(8,128)(2,1)S(1)} %get-tuple-element.45.refs_6_), channel_id=1, source_target_pairs={{0,1},{1,0},{2,3},{3,2},{4,5},{5,4},{6,7},{7,6},{8,9},{9,8},{10,11... | collective-permute-start | bytes 1115144 | tf_op jit(solution)/shard_map/ppermute | solution.py:95
  54.8 3.5 %collective-permute-start.12 = (bf16[352,352]{1,0:T(8,128)(2,1)}, bf16[352,352]{1,0:T(8,128)(2,1)S(1)}, u32[]{:S(2)}, u32[]{:S(2)}) collective-permute-start(bf16[352,352]{1,0:T(8,128)(2,1)} %collective-permute-done.8.refs_6_), channel_id=1, source_target_pairs={{0,1},{1,0},{2,3},{3,2},{4,5},{5,4},{6,7},{7,6},{8,9},{9,8},{10,11... | collective-permute-start | bytes 743432 | tf_op jit(solution)/shard_map/ppermute | solution.py:95
  56.9 1.8 %collective-permute-start.13 = (bf16[352,352]{1,0:T(8,128)(2,1)}, bf16[352,352]{1,0:T(8,128)(2,1)S(1)}, u32[]{:S(2)}, u32[]{:S(2)}) collective-permute-start(bf16[352,352]{1,0:T(8,128)(2,1)} %collective-permute-done.9.refs_7_), channel_id=1, source_target_pairs={{0,1},{1,0},{2,3},{3,2},{4,5},{5,4},{6,7},{7,6},{8,9},{9,8},{10,11... | collective-permute-start | bytes 743432 | tf_op jit(solution)/shard_map/ppermute | solution.py:95
  57.4 16.0 %copy-start.21 = (bf16[88,704]{1,0:T(8,128)(2,1)S(1)}, bf16[88,704]{1,0:T(8,128)(2,1)}, u32[]{:S(2)}) copy-start(bf16[88,704]{1,0:T(8,128)(2,1)} %copy-done.20) | copy-start | bytes 371716
  62.5 5.2 %collective-permute-start.14 = (bf16[4,16,352]{2,1,0:T(8,128)(2,1)S(1)}, bf16[4,16,352]{2,1,0:T(8,128)(2,1)S(1)}, u32[]{:S(2)}, u32[]{:S(2)}) collective-permute-start(bf16[4,16,352]{2,1,0:T(8,128)(2,1)S(1)} %get-tuple-element.38), channel_id=1, source_target_pairs={{0,4},{1,5},{2,6},{3,7},{4,8},{5,9},{6,10},{7,11},{8,12},{9,13},{1... | collective-permute-start | bytes 135176 | tf_op jit(solution)/shard_map/ppermute | solution.py:95
  63.9 4.8 %collective-permute-start.15 = (bf16[4,16,352]{2,1,0:T(8,128)(2,1)S(1)}, bf16[4,16,352]{2,1,0:T(8,128)(2,1)S(1)}, u32[]{:S(2)}, u32[]{:S(2)}) collective-permute-start(bf16[4,16,352]{2,1,0:T(8,128)(2,1)S(1)} %get-tuple-element.39), channel_id=1, source_target_pairs={{0,8},{1,9},{2,10},{3,11},{4,12},{5,13},{6,14},{7,15},{8,0},{9,1},... | collective-permute-start | bytes 135176 | tf_op jit(solution)/shard_map/ppermute | solution.py:95
  65.5 4.1 %collective-permute-start.16 = (bf16[4,16,352]{2,1,0:T(8,128)(2,1)S(1)}, bf16[4,16,352]{2,1,0:T(8,128)(2,1)S(1)}, u32[]{:S(2)}, u32[]{:S(2)}) collective-permute-start(bf16[4,16,352]{2,1,0:T(8,128)(2,1)S(1)} %get-tuple-element.40), channel_id=1, source_target_pairs={{0,12},{1,13},{2,14},{3,15},{4,0},{5,1},{6,2},{7,3},{8,4},{9,5},{1... | collective-permute-start | bytes 135176 | tf_op jit(solution)/shard_map/ppermute | solution.py:95
  67.8 18.5 %collective-permute-start.23 = (bf16[352,528]{1,0:T(8,128)(2,1)}, bf16[352,528]{1,0:T(8,128)(2,1)}, u32[]{:S(2)}, u32[]{:S(2)}) collective-permute-start(bf16[352,528]{1,0:T(8,128)(2,1)} %collective-permute-done.22.refs_8_), channel_id=1, source_target_pairs={{0,4},{1,5},{2,6},{3,7},{4,8},{5,9},{6,10},{7,11},{8,12},{9,13},{1... | collective-permute-start | bytes 1115144 | tf_op jit(solution)/shard_map/ppermute | solution.py:95
  70.4 5.9 %collective-permute-start.19 = (bf16[4,4,16,352]{3,2,1,0:T(8,128)(2,1)S(1)}, bf16[4,4,16,352]{3,2,1,0:T(8,128)(2,1)S(1)}, u32[]{:S(2)}, u32[]{:S(2)}) collective-permute-start(bf16[4,4,16,352]{3,2,1,0:T(8,128)(2,1)S(1)} %shard_map.77.refs_0_), channel_id=1, source_target_pairs={{0,18},{1,19},{2,16},{3,17},{4,22},{5,23},{6,20},{7,21},{8,26},{9,... | collective-permute-start | bytes 540680 | tf_op jit(solution)/shard_map/ppermute | solution.py:95
  71.9 17.5 %collective-permute-start.25 = (bf16[352,528]{1,0:T(8,128)(2,1)S(1)}, bf16[352,528]{1,0:T(8,128)(2,1)S(1)}, u32[]{:S(2)}, u32[]{:S(2)}) collective-permute-start(bf16[352,528]{1,0:T(8,128)(2,1)S(1)} %collective-permute-done.21.refs_7_), channel_id=1, source_target_pairs={{0,1},{1,0},{2,3},{3,2},{4,5},{5,4},{6,7},{7,6},{8,9},{9,8},{10,11... | collective-permute-start | bytes 1115144 | tf_op jit(solution)/shard_map/ppermute | solution.py:95
  73.4 10.0 %collective-permute-start.28 = (bf16[88,704]{1,0:T(8,128)(2,1)S(1)}, bf16[88,704]{1,0:T(8,128)(2,1)}, u32[]{:S(2)}, u32[]{:S(2)}) collective-permute-start(bf16[88,704]{1,0:T(8,128)(2,1)S(1)} %copy-done.21), channel_id=1, source_target_pairs={{0,4},{1,5},{2,6},{3,7},{4,8},{5,9},{6,10},{7,11},{8,12},{9,13},{1... | collective-permute-start | bytes 371720 | tf_op jit(solution)/shard_map/ppermute | solution.py:95
  74.4 0.8 copy-start.3
  75.2 8.2 %collective-permute-start.18 = (bf16[4,4,16,352]{3,2,1,0:T(8,128)(2,1)S(1)}, bf16[4,4,16,352]{3,2,1,0:T(8,128)(2,1)S(1)}, u32[]{:S(2)}, u32[]{:S(2)}) collective-permute-start(bf16[4,4,16,352]{3,2,1,0:T(8,128)(2,1)S(1)} %shard_map.77.refs_0_), channel_id=1, source_target_pairs={{0,2},{1,3},{2,0},{3,1},{4,6},{5,7},{6,4},{7,5},{8,10},{9,11},{10,... | collective-permute-start | bytes 540680 | tf_op jit(solution)/shard_map/ppermute | solution.py:95
  76.3 10.0 %collective-permute-start.17 = (bf16[4,4,16,352]{3,2,1,0:T(8,128)(2,1)S(1)}, bf16[4,4,16,352]{3,2,1,0:T(8,128)(2,1)S(1)}, u32[]{:S(2)}, u32[]{:S(2)}) collective-permute-start(bf16[4,4,16,352]{3,2,1,0:T(8,128)(2,1)S(1)} %shard_map.77.refs_0_), channel_id=1, source_target_pairs={{0,16},{1,17},{2,18},{3,19},{4,20},{5,21},{6,22},{7,23},{8,24},{9,... | collective-permute-start | bytes 540680 | tf_op jit(solution)/shard_map/ppermute | solution.py:95
  83.4 6.0 %collective-permute-start.29 = (bf16[88,704]{1,0:T(8,128)(2,1)}, bf16[88,704]{1,0:T(8,128)(2,1)}, u32[]{:S(2)}, u32[]{:S(2)}) collective-permute-start(bf16[88,704]{1,0:T(8,128)(2,1)} %collective-permute-done.28.refs_15_), channel_id=1, source_target_pairs={{0,4},{1,5},{2,6},{3,7},{4,8},{5,9},{6,10},{7,11},{8,12},{9,13},{1... | collective-permute-start | bytes 371720 | tf_op jit(solution)/shard_map/ppermute | solution.py:95
  84.1 15.9 %collective-permute-start.26 = (bf16[352,528]{1,0:T(8,128)(2,1)}, bf16[352,528]{1,0:T(8,128)(2,1)}, u32[]{:S(2)}, u32[]{:S(2)}) collective-permute-start(bf16[352,528]{1,0:T(8,128)(2,1)} %collective-permute-done.22.refs_8_), channel_id=1, source_target_pairs={{0,1},{1,0},{2,3},{3,2},{4,5},{5,4},{6,7},{7,6},{8,9},{9,8},{10,11... | collective-permute-start | bytes 1115144 | tf_op jit(solution)/shard_map/ppermute | solution.py:95
  86.2 14.9 %collective-permute-start.27 = (bf16[352,528]{1,0:T(8,128)(2,1)}, bf16[352,528]{1,0:T(8,128)(2,1)}, u32[]{:S(2)}, u32[]{:S(2)}) collective-permute-start(bf16[352,528]{1,0:T(8,128)(2,1)} %collective-permute-done.23.refs_9_), channel_id=1, source_target_pairs={{0,1},{1,0},{2,3},{3,2},{4,5},{5,4},{6,7},{7,6},{8,9},{9,8},{10,11... | collective-permute-start | bytes 1115144 | tf_op jit(solution)/shard_map/ppermute | solution.py:95
  86.9 6.6 %collective-permute-start.31 = (bf16[88,704]{1,0:T(8,128)(2,1)S(1)}, bf16[88,704]{1,0:T(8,128)(2,1)S(1)}, u32[]{:S(2)}, u32[]{:S(2)}) collective-permute-start(bf16[88,704]{1,0:T(8,128)(2,1)S(1)} %copy-done.21), channel_id=1, source_target_pairs={{0,1},{1,0},{2,3},{3,2},{4,5},{5,4},{6,7},{7,6},{8,9},{9,8},{10,11... | collective-permute-start | bytes 371720 | tf_op jit(solution)/shard_map/ppermute | solution.py:95
  89.4 6.0 %collective-permute-start.30 = (bf16[88,704]{1,0:T(8,128)(2,1)}, bf16[88,704]{1,0:T(8,128)(2,1)}, u32[]{:S(2)}, u32[]{:S(2)}) collective-permute-start(bf16[88,704]{1,0:T(8,128)(2,1)} %collective-permute-done.29.refs_16_), channel_id=1, source_target_pairs={{0,4},{1,5},{2,6},{3,7},{4,8},{5,9},{6,10},{7,11},{8,12},{9,13},{1... | collective-permute-start | bytes 371720 | tf_op jit(solution)/shard_map/ppermute | solution.py:95
  89.4 0.8 copy-start.5
  90.2 9.8 %collective-permute-start.32 = (bf16[88,704]{1,0:T(8,128)(2,1)}, bf16[88,704]{1,0:T(8,128)(2,1)}, u32[]{:S(2)}, u32[]{:S(2)}) collective-permute-start(bf16[88,704]{1,0:T(8,128)(2,1)} %collective-permute-done.28.refs_15_), channel_id=1, source_target_pairs={{0,1},{1,0},{2,3},{3,2},{4,5},{5,4},{6,7},{7,6},{8,9},{9,8},{10,11... | collective-permute-start | bytes 371720 | tf_op jit(solution)/shard_map/ppermute | solution.py:95
  94.2 5.9 %collective-permute-start.33 = (bf16[88,704]{1,0:T(8,128)(2,1)}, bf16[88,704]{1,0:T(8,128)(2,1)}, u32[]{:S(2)}, u32[]{:S(2)}) collective-permute-start(bf16[88,704]{1,0:T(8,128)(2,1)} %collective-permute-done.29.refs_16_), channel_id=1, source_target_pairs={{0,1},{1,0},{2,3},{3,2},{4,5},{5,4},{6,7},{7,6},{8,9},{9,8},{10,11... | collective-permute-start | bytes 371720 | tf_op jit(solution)/shard_map/ppermute | solution.py:95
  95.4 5.8 %collective-permute-start.34 = (bf16[88,704]{1,0:T(8,128)(2,1)}, bf16[88,704]{1,0:T(8,128)(2,1)}, u32[]{:S(2)}, u32[]{:S(2)}) collective-permute-start(bf16[88,704]{1,0:T(8,128)(2,1)} %collective-permute-done.30.refs_17_), channel_id=1, source_target_pairs={{0,1},{1,0},{2,3},{3,2},{4,5},{5,4},{6,7},{7,6},{8,9},{9,8},{10,11... | collective-permute-start | bytes 371720 | tf_op jit(solution)/shard_map/ppermute | solution.py:95
  101.1 1.0 copy-start.4
  102.2 1.0 copy-start.6
  103.2 0.9 copy-start.15
  104.1 0.9 copy-start.17
  105.0 0.9 copy-start.22
  105.9 0.9 copy-start.24
  119.2 6.2 %collective-permute-start.35 = (bf16[2,64,704]{2,1,0:T(8,128)(2,1)S(1)}, bf16[2,64,704]{2,1,0:T(8,128)(2,1)S(1)}, u32[]{:S(2)}, u32[]{:S(2)}) collective-permute-start(bf16[2,64,704]{2,1,0:T(8,128)(2,1)S(1)} %get-tuple-element.50), channel_id=1, source_target_pairs={{0,16},{1,17},{2,18},{3,19},{4,20},{5,21},{6,22},{7,23},{8,24},{9,... | collective-permute-start | bytes 540680 | tf_op jit(solution)/shard_map/ppermute | solution.py:95
  119.3 6.1 %collective-permute-start.36 = (bf16[2,64,704]{2,1,0:T(8,128)(2,1)S(1)}, bf16[2,64,704]{2,1,0:T(8,128)(2,1)S(1)}, u32[]{:S(2)}, u32[]{:S(2)}) collective-permute-start(bf16[2,64,704]{2,1,0:T(8,128)(2,1)S(1)} %get-tuple-element.51), channel_id=1, source_target_pairs={{0,2},{1,3},{2,0},{3,1},{4,6},{5,7},{6,4},{7,5},{8,10},{9,11},{10,... | collective-permute-start | bytes 540680 | tf_op jit(solution)/shard_map/ppermute | solution.py:95
  120.4 9.5 %collective-permute-start.37 = (bf16[2,64,704]{2,1,0:T(8,128)(2,1)S(1)}, bf16[2,64,704]{2,1,0:T(8,128)(2,1)S(1)}, u32[]{:S(2)}, u32[]{:S(2)}) collective-permute-start(bf16[2,64,704]{2,1,0:T(8,128)(2,1)S(1)} %get-tuple-element.52), channel_id=1, source_target_pairs={{0,18},{1,19},{2,16},{3,17},{4,22},{5,23},{6,20},{7,21},{8,26},{9,... | collective-permute-start | bytes 540680 | tf_op jit(solution)/shard_map/ppermute | solution.py:95
  130.6 6.9 %collective-permute-start.38 = (bf16[16,1408]{1,0:T(8,128)(2,1)S(1)}, bf16[16,1408]{1,0:T(8,128)(2,1)S(1)}, u32[]{:S(2)}, u32[]{:S(2)}) collective-permute-start(bf16[16,1408]{1,0:T(8,128)(2,1)S(1)} %get-tuple-element.53), channel_id=1, source_target_pairs={{0,0},{1,16},{2,2},{3,18},{4,4},{5,20},{6,6},{7,22},{8,8},{9,24},{... | collective-permute-start | bytes 135176 | tf_op jit(solution)/shard_map/ppermute | solution.py:95
  134.8 4.4 %collective-permute-start.39 = (bf16[16,1408]{1,0:T(8,128)(2,1)S(1)}, bf16[16,1408]{1,0:T(8,128)(2,1)S(1)}, u32[]{:S(2)}, u32[]{:S(2)}) collective-permute-start(bf16[16,1408]{1,0:T(8,128)(2,1)S(1)} %get-tuple-element.54), channel_id=1, source_target_pairs={{0,12},{1,28},{2,14},{3,30},{4,0},{5,16},{6,2},{7,18},{8,4},{9,20}... | collective-permute-start | bytes 135176 | tf_op jit(solution)/shard_map/ppermute | solution.py:95
  134.9 5.3 %collective-permute-start.40 = (bf16[16,1408]{1,0:T(8,128)(2,1)S(1)}, bf16[16,1408]{1,0:T(8,128)(2,1)S(1)}, u32[]{:S(2)}, u32[]{:S(2)}) collective-permute-start(bf16[16,1408]{1,0:T(8,128)(2,1)S(1)} %get-tuple-element.55), channel_id=1, source_target_pairs={{0,8},{1,24},{2,10},{3,26},{4,12},{5,28},{6,14},{7,30},{8,0},{9,16... | collective-permute-start | bytes 135176 | tf_op jit(solution)/shard_map/ppermute | solution.py:95
  135.2 6.4 %collective-permute-start.41 = (bf16[16,1408]{1,0:T(8,128)(2,1)S(1)}, bf16[16,1408]{1,0:T(8,128)(2,1)S(1)}, u32[]{:S(2)}, u32[]{:S(2)}) collective-permute-start(bf16[16,1408]{1,0:T(8,128)(2,1)S(1)} %get-tuple-element.56), channel_id=1, source_target_pairs={{0,4},{1,20},{2,6},{3,22},{4,8},{5,24},{6,10},{7,26},{8,12},{9,28}... | collective-permute-start | bytes 135176 | tf_op jit(solution)/shard_map/ppermute | solution.py:95
  (4 other events, 2.7 us)

commit v5 on v4

--- a/solution.py
+++ b/solution.py
@@ -98,7 +98,7 @@
         return x * self.n + (z * self.Y + y) * self.G + c
 
 
-def call(kernel, outs, where, *arrays, scratch=(), copies=0, flops=0, fast=(), fast_in=False):
+def call(kernel, outs, where, *arrays, scratch=(), copies=0, flops=0, fast=(), fast_in=False, still=False):
     moved = sum(a.size * a.dtype.itemsize for a in arrays)
     space = pltpu.VMEM if fast_in else pltpu.HBM
     sems = [pltpu.SemaphoreType.DMA((copies,))] if copies else []
@@ -114,7 +114,7 @@
         scratch_shapes=list(scratch) + sems,
         compiler_params=pltpu.CompilerParams(vmem_limit_bytes=40 * 2**20),
         cost_estimate=pl.CostEstimate(flops=flops, bytes_accessed=2 * moved, transcendentals=0),
-    )(where, *arrays)
+    )(where, *(pltpu.with_memory_space_constraint(a, pltpu.HBM) if still else a for a in arrays))
 
 
 def after(value, *others):
@@ -356,9 +356,6 @@
     def swap(value, e, f):
         return p.send(value, lambda x, z, y, c: (x, z, y + e, c + f))
 
-    (joined,) = call(
-        join_kernel, [(2, S, local, width)], p.where, hidden, skip, copies=2
-    )
     outs = [(rows, cols)]
     for e in range(Y):
         for f in range(G):
@@ -375,14 +372,23 @@
         scratch=[pltpu.VMEM(w.shape, BF) for w in (w_skip, w_qkv, w_out)],
         copies=3,
         fast=range(len(outs)),
+        still=True,
+    )
+    (joined,) = call(
+        join_kernel, [(2, S, local, width)], p.where, hidden, skip, copies=2, fast=[0], still=True
     )
     own = qkvs[0]
-    qkvs = [swap(qkvs[e * G + f], e, f) if e or f else own for e in range(Y) for f in range(G)]
-    parts = []
+    parts = [
+        p.send(joined, lambda x, z, y, c, e=e, d=d: (c - d, z, y - e, x))
+        for e in range(Y)
+        for d in range(G)
+    ]
     for e in range(Y):
-        for d in range(G):
-            value = joined if len(parts) < 2 else after(joined, qkvs[G], qkvs[len(parts)])
-            parts.append(p.send(value, lambda x, z, y, c, e=e, d=d: (c - d, z, y - e, x)))
+        for f in range(G):
+            if f:
+                qkvs[e * G + f] = swap(after(qkvs[e * G + f], *parts[:1]), e, f)
+            elif e:
+                qkvs[e * G] = swap(qkvs[e * G], e, 0)
 
     def step(value):
         return p.send(value, lambda x, z, y, c: (x, z + 1, y, c))
@@ -409,12 +415,13 @@
         fast_in=True,
     )
     ws = [ring]
-    for _ in range(1, S):
-        ws.append(step(ws[-1]))
+    ws.append(step(ring))
+    ws.append(step(after(ws[1], *parts[:G])))
+    ws.append(step(after(ws[2], *parts[G:])))
     wq = [after(wq, ws[2])]
     for _ in range(1, S):
         wq.append(step(wq[-1]))
-    wo = [after(wo, wq[2])]
+    wo = [after(wo, ws[2])]
     for _ in range(1, S):
         wo.append(step(wo[-1]))
     ws, wq, wo = over_cores(ws), over_cores(wq), over_cores(wo)
@@ -439,6 +446,7 @@
         ],
         copies=2 * blocks + S * G * Y,
         flops=4 * every * width * cols,
+        still=True,
         fast=range(S),
     )
     pieces = [pieces[0]] + [
@@ -470,6 +478,7 @@
         ],
         copies=2 + 2 * G * S + blocks * blocks,
         flops=10 * every * width * cols,
+        still=True,
         fast=range(blocks + 1),
     )
     parts = [

time: 143 us -> 138 us (0.965)
  local copies, waits for them, and re-layouts: 15.5 us -> 4.1 us
  waiting for transfers between devices: 47.2 us -> 56 us
  starting transfers between devices: 54.4 us -> 51.8 us
    unnamed x52 -> x46, local copies, waits for them, and re-layouts: 14.7 us -> 2.13 us
    ppermute x42, waiting for transfers between devices: 47.2 us -> 56 us  [send(): return lax.ppermute(value, ('group', 'seq'), pairs)]
    ppermute x42, starting transfers between devices: 54.4 us -> 51.8 us  [send(): return lax.ppermute(value, ('group', 'seq'), pairs)]
  transfers between devices with their start and end apart: 42 -> 42, of which waited for: 20 -> 21; matrix products, arithmetic and copies ran while one was open for 1% -> 2% of each run, Pallas kernels for 5% -> 6%
where the time goes in v5:
time: 138 us
  waiting for transfers between devices  56 us (41%)
  starting transfers between devices  51.8 us (38%)
  Pallas kernels  24.5 us (18%)
  local copies, waits for them, and re-layouts  4.1 us (3%)
    ppermute x42, waiting for transfers between devices, send(): return lax.ppermute(value, ('group', 'seq'), pairs)  56 us
    ppermute x42, starting transfers between devices, send(): return lax.ppermute(value, ('group', 'seq'), pairs)  51.8 us
    pallas_call x9, Pallas kernels, call(): pl.pallas_call(kernel, out_shape=[jax.ShapeDtypeStruct(s, BF) for s in ou...  24.5 us
  transfers between devices with their start and end apart: 42, of which 21 were waited for; matrix products, arithmetic and copies ran while one was open for 2% of the time, Pallas kernels for 6%

profile of v5, /device:TPU:1, one launch (start us, length us, event | category | flops | bytes accessed | tf_op | source)
XLA Modules:
  0.0 138.0 jit_solution(13797721002214413620)
XLA Ops:
  0.1 2.9 %shard_map.74 = (bf16[176,352]{1,0:T(8,128)(2,1)S(1)}, bf16[88,528]{1,0:T(8,128)(2,1)S(1)}, bf16[88,1232]{1,0:T(8,128)(2,1)S(1)}, bf16[88,1232]{1,0:T(8,128)(2,1...) custom-call(s32[4]{0:T(128)S(1)} %pad_add_fusion.where, bf16[176,1408]{1,0:T(8,128)(2,1)} %w_skip_any.1, ...), custom_call_target="tpu_custom_call" | custom-call | bytes 2973696 | tf_op jit(solution)/shard_map/pallas_call | solution.py:105
  2.9 2.2 %collective-permute-start.5 = (bf16[88,1232]{1,0:T(8,128)(2,1)S(1)}, bf16[88,1232]{1,0:T(8,128)(2,1)S(1)}, u32[]{:S(2)}, u32[]{:S(2)}) collective-permute-start(bf16[88,1232]{1,0:T(8,128)(2,1)S(1)} %get-tuple-element.35), channel_id=1, source_target_pairs={{0,2},{1,3},{2,0},{3,1},{4,6},{5,7},{6,4},{7,5},{8,10},{9,11},{10,... | collective-permute-start | bytes 650504 | tf_op jit(solution)/shard_map/ppermute | solution.py:95
  5.2 1.6 %shard_map.73 = bf16[2,4,16,1408]{3,2,1,0:T(8,128)(2,1)S(1)} custom-call(s32[4]{0:T(128)S(1)} %pad_add_fusion.where, bf16[4,16,1408]{2,1,0:T(8,128)(2,1)} %hidden.1, bf16[4,16,1408]{2,1,0:T(8,128)(2,1)} %skip.1), custom_call_target="tpu_custom_call" | custom-call | bytes 720896 | tf_op jit(solution)/shard_map/pallas_call | solution.py:105
  6.7 0.9 collective-permute-start.2
  7.6 3.0 %collective-permute-start.1 = (bf16[2,4,16,1408]{3,2,1,0:T(8,128)(2,1)S(1)}, bf16[2,4,16,1408]{3,2,1,0:T(8,128)(2,1)S(1)}, u32[]{:S(2)}, u32[]{:S(2)}) collective-permute-start(bf16[2,4,16,1408]{3,2,1,0:T(8,128)(2,1)S(1)} %shard_map.73), channel_id=1, source_target_pairs={{0,0},{1,16},{2,2},{3,18},{4,4},{5,20},{6,6},{7,22},{8,8},{9,24},{... | collective-permute-start | bytes 1081352 | tf_op jit(solution)/shard_map/ppermute | solution.py:95
  10.6 0.7 shard_map.75.refs_4_
  11.3 1.3 collective-permute-start.6
  12.7 0.8 collective-permute-done.2.refs_1_
  13.5 4.0 %collective-permute-done.1.refs_0_ = bf16[2,4,16,1408]{3,2,1,0:T(8,128)(2,1)S(1)} collective-permute-done((bf16[2,4,16,1408]{3,2,1,0:T(8,128)(2,1)S(1)}, bf16[2,4,16,1408]{3,2,1,0:T(8,128)(2,1)S(1)}, u32[]{:S(2)}, u32[]{:S(2)}) %collective-permute-start.1) | collective-permute-done | bytes 360480 | tf_op jit(solution)/shard_map/ppermute | solution.py:95
  17.5 2.9 %collective-permute-done.6.refs_5_ = bf16[352,352]{1,0:T(8,128)(2,1)} collective-permute-done((bf16[352,352]{1,0:T(8,128)(2,1)S(1)}, bf16[352,352]{1,0:T(8,128)(2,1)}, u32[]{:S(2)}, u32[]{:S(2)}) %collective-permute-start.6) | collective-permute-done | bytes 247840 | tf_op jit(solution)/shard_map/ppermute | solution.py:95
  20.4 1.9 %collective-permute-start.19 = (bf16[88,1232]{1,0:T(8,128)(2,1)S(1)}, bf16[88,1232]{1,0:T(8,128)(2,1)S(1)}, u32[]{:S(2)}, u32[]{:S(2)}) collective-permute-start(bf16[88,1232]{1,0:T(8,128)(2,1)S(1)} %get-tuple-element.44), channel_id=1, source_target_pairs={{0,1},{1,0},{2,3},{3,2},{4,5},{5,4},{6,7},{7,6},{8,9},{9,8},{10,11... | collective-permute-start | bytes 650504 | tf_op jit(solution)/shard_map/ppermute | solution.py:95
  22.3 0.9 collective-permute-start.20
  23.2 3.8 %collective-permute-done.20.refs_3_ = bf16[88,528]{1,0:T(8,128)(2,1)S(1)} collective-permute-done((bf16[88,528]{1,0:T(8,128)(2,1)S(1)}, bf16[88,528]{1,0:T(8,128)(2,1)S(1)}, u32[]{:S(2)}, u32[]{:S(2)}) %collective-permute-start.20) | collective-permute-done | bytes 92960 | tf_op jit(solution)/shard_map/ppermute | solution.py:95
  27.0 0.8 shard_map.78
  27.8 0.9 collective-permute-done.7.refs_6_
  29.3 2.6 %collective-permute-start.4 = (bf16[2,4,16,1408]{3,2,1,0:T(8,128)(2,1)S(1)}, bf16[2,4,16,1408]{3,2,1,0:T(8,128)(2,1)S(1)}, u32[]{:S(2)}, u32[]{:S(2)}) collective-permute-start(bf16[2,4,16,1408]{3,2,1,0:T(8,128)(2,1)S(1)} %shard_map.73), channel_id=1, source_target_pairs={{0,18},{1,2},{2,16},{3,0},{4,22},{5,6},{6,20},{7,4},{8,26},{9,10},... | collective-permute-start | bytes 1081352 | tf_op jit(solution)/shard_map/ppermute | solution.py:95
  31.9 1.0 collective-permute-start.3
  32.9 0.9 collective-permute-start.9
  33.8 5.7 %collective-permute-done.21.refs_7_ = bf16[352,528]{1,0:T(8,128)(2,1)S(1)} collective-permute-done((bf16[352,528]{1,0:T(8,128)(2,1)S(1)}, bf16[352,528]{1,0:T(8,128)(2,1)S(1)}, u32[]{:S(2)}, u32[]{:S(2)}) %collective-permute-start.21) | collective-permute-done | bytes 371744 | tf_op jit(solution)/shard_map/ppermute | solution.py:95
  39.5 1.2 collective-permute-start.22
  40.7 4.7 %collective-permute-start = (s32[4]{0:T(128)S(1)}, s32[4]{0:T(128)S(1)}, u32[]{:S(2)}, u32[]{:S(2)}) collective-permute-start(s32[4]{0:T(128)S(1)} %copy-done.22), channel_id=1, source_target_pairs={{0,0},{1,16},{2,2},{3,18},{4,4},{5,20},{6,6},{7,22},{8,8},{9,24},{... | collective-permute-start | bytes 56 | tf_op jit(solution)/shard_map/ppermute | solution.py:95
  45.4 1.6 %collective-permute-done.4.refs_3_ = bf16[2,4,16,1408]{3,2,1,0:T(8,128)(2,1)S(1)} collective-permute-done((bf16[2,4,16,1408]{3,2,1,0:T(8,128)(2,1)S(1)}, bf16[2,4,16,1408]{3,2,1,0:T(8,128)(2,1)S(1)}, u32[]{:S(2)}, u32[]{:S(2)}) %collective-permute-start.4) | collective-permute-done | bytes 360480 | tf_op jit(solution)/shard_map/ppermute | solution.py:95
  47.0 1.6 %collective-permute-start.10 = (bf16[352,352]{1,0:T(8,128)(2,1)}, bf16[352,352]{1,0:T(8,128)(2,1)}, u32[]{:S(2)}, u32[]{:S(2)}) collective-permute-start(bf16[352,352]{1,0:T(8,128)(2,1)} %collective-permute-done.6.refs_5_), channel_id=1, source_target_pairs={{0,1},{1,0},{2,3},{3,2},{4,5},{5,4},{6,7},{7,6},{8,9},{9,8},{10,11... | collective-permute-start | bytes 743432 | tf_op jit(solution)/shard_map/ppermute | solution.py:95
  48.7 0.7 copy-done.10
  50.7 1.6 %collective-permute-start.28 = (bf16[88,704]{1,0:T(8,128)(2,1)S(1)}, bf16[88,704]{1,0:T(8,128)(2,1)S(1)}, u32[]{:S(2)}, u32[]{:S(2)}) collective-permute-start(bf16[88,704]{1,0:T(8,128)(2,1)S(1)} %get-tuple-element.51.refs_14_), channel_id=1, source_target_pairs={{0,4},{1,5},{2,6},{3,7},{4,8},{5,9},{6,10},{7,11},{8,12},{9,13},{1... | collective-permute-start | bytes 371720 | tf_op jit(solution)/shard_map/ppermute | solution.py:95
  52.7 9.4 %collective-permute-done.28.refs_15_ = bf16[88,704]{1,0:T(8,128)(2,1)S(1)} collective-permute-done((bf16[88,704]{1,0:T(8,128)(2,1)S(1)}, bf16[88,704]{1,0:T(8,128)(2,1)S(1)}, u32[]{:S(2)}, u32[]{:S(2)}) %collective-permute-start.28) | collective-permute-done | bytes 123936 | tf_op jit(solution)/shard_map/ppermute | solution.py:95
  62.1 1.3 collective-permute-start.24
  63.6 1.1 collective-permute-start.23
  65.5 0.7 copy-done.11
  66.2 3.7 %shard_map.76 = (bf16[4,16,352]{2,1,0:T(8,128)(2,1)S(1)}, bf16[4,16,352]{2,1,0:T(8,128)(2,1)S(1)}, bf16[4,16,352]{2,1,0:T(8,128)(2,1)S(1)}, bf16[4,16,352]{2,1,0:T(8,128)(2,1)S(1)}) custom-call(s32[4]{0:T(128)S(1)} %pad_add_fusion.where, bf16[2,4,16,1408]{3,2,1,0:T(8,128)(2,1)} %copy-done.8, bf16[2,4,16,1408]{3,2,1,0:T(8,128)(2,1)} %copy-done.7, ...), custom_call_target="tpu_custom_call" | custom-call | flops 507510784 | bytes 6848512 | tf_op jit(solution)/shard_map/pallas_call | solution.py:105
  70.0 0.8 collective-permute-start.13
  70.8 2.5 %collective-permute-start.14 = (bf16[4,16,352]{2,1,0:T(8,128)(2,1)S(1)}, bf16[4,16,352]{2,1,0:T(8,128)(2,1)S(1)}, u32[]{:S(2)}, u32[]{:S(2)}) collective-permute-start(bf16[4,16,352]{2,1,0:T(8,128)(2,1)S(1)} %get-tuple-element.40), channel_id=1, source_target_pairs={{0,8},{1,9},{2,10},{3,11},{4,12},{5,13},{6,14},{7,15},{8,0},{9,1},... | collective-permute-start | bytes 135176 | tf_op jit(solution)/shard_map/ppermute | solution.py:95
  73.3 1.4 collective-permute-start.15
  74.7 6.5 %collective-permute-done.13.refs_1_ = bf16[4,16,352]{2,1,0:T(8,128)(2,1)S(1)} collective-permute-done((bf16[4,16,352]{2,1,0:T(8,128)(2,1)S(1)}, bf16[4,16,352]{2,1,0:T(8,128)(2,1)S(1)}, u32[]{:S(2)}, u32[]{:S(2)}) %collective-permute-start.13) | collective-permute-done | bytes 45088 | tf_op jit(solution)/shard_map/ppermute | solution.py:95
  81.2 1.3 collective-permute-start.32
  82.5 1.1 collective-permute-done.14.refs_2_
  84.2 0.7 collective-permute-start.30
  84.9 0.8 shard_map.77.refs_0_
  85.8 1.7 %collective-permute-start.18 = (bf16[4,4,16,352]{3,2,1,0:T(8,128)(2,1)S(1)}, bf16[4,4,16,352]{3,2,1,0:T(8,128)(2,1)S(1)}, u32[]{:S(2)}, u32[]{:S(2)}) collective-permute-start(bf16[4,4,16,352]{3,2,1,0:T(8,128)(2,1)S(1)} %shard_map.77.refs_0_), channel_id=1, source_target_pairs={{0,18},{1,19},{2,16},{3,17},{4,22},{5,23},{6,20},{7,21},{8,26},{9,... | collective-permute-start | bytes 540680 | tf_op jit(solution)/shard_map/ppermute | solution.py:95
  87.5 1.1 collective-permute-start.25
  88.6 2.6 %collective-permute-done.30.refs_17_ = bf16[88,704]{1,0:T(8,128)(2,1)S(1)} collective-permute-done((bf16[88,704]{1,0:T(8,128)(2,1)S(1)}, bf16[88,704]{1,0:T(8,128)(2,1)S(1)}, u32[]{:S(2)}, u32[]{:S(2)}) %collective-permute-start.30) | collective-permute-done | bytes 123936 | tf_op jit(solution)/shard_map/ppermute | solution.py:95
  91.2 0.8 collective-permute-start.26
  92.5 1.3 collective-permute-done.34.refs_21_
  93.8 1.0 collective-permute-start.17
  94.8 0.9 collective-permute-start.16
  95.9 0.7 reshape.44.refs_5_
  96.5 0.7 reshape.43.refs_4_
  97.2 2.7 %collective-permute-done.17.refs_2_ = bf16[4,4,16,352]{3,2,1,0:T(8,128)(2,1)S(1)} collective-permute-done((bf16[4,4,16,352]{3,2,1,0:T(8,128)(2,1)S(1)}, bf16[4,4,16,352]{3,2,1,0:T(8,128)(2,1)S(1)}, u32[]{:S(2)}, u32[]{:S(2)}) %collective-permute-start.17) | collective-permute-done | bytes 180256 | tf_op jit(solution)/shard_map/ppermute | solution.py:95
  99.9 0.8 collective-permute-done.16.refs_1_
  100.7 0.7 copy-done.14
  101.4 12.1 %shard_map.79 = (bf16[2,64,704]{2,1,0:T(8,128)(2,1)S(1)}, bf16[2,64,704]{2,1,0:T(8,128)(2,1)S(1)}, bf16[2,64,704]{2,1,0:T(8,128)(2,1)S(1)}, bf16[2,64,704]{2,1,0:T(8,128)(2,1)S(1)}, bf16[4,64,352]{2,1,0:T(8,128)(2,1)S(1)}) custom-call(s32[4]{0:T(128)S(1)} %pad_add_fusion.where, bf16[4,4,16,352]{3,2,1,0:T(8,128)(2,1)} %copy-done.2, ...), custom_call_target="tpu_custom_call" | custom-call | flops 1268776960 | bytes 9394176 | tf_op jit(solution)/shard_map/pallas_call | solution.py:105
  113.5 0.9 collective-permute-start.35
  114.7 1.5 %collective-permute-start.37 = (bf16[2,64,704]{2,1,0:T(8,128)(2,1)S(1)}, bf16[2,64,704]{2,1,0:T(8,128)(2,1)S(1)}, u32[]{:S(2)}, u32[]{:S(2)}) collective-permute-start(bf16[2,64,704]{2,1,0:T(8,128)(2,1)S(1)} %get-tuple-element.56), channel_id=1, source_target_pairs={{0,18},{1,19},{2,16},{3,17},{4,22},{5,23},{6,20},{7,21},{8,26},{9,... | collective-permute-start | bytes 540680 | tf_op jit(solution)/shard_map/ppermute | solution.py:95
  116.2 2.2 %collective-permute-done.35.refs_1_ = bf16[2,64,704]{2,1,0:T(8,128)(2,1)S(1)} collective-permute-done((bf16[2,64,704]{2,1,0:T(8,128)(2,1)S(1)}, bf16[2,64,704]{2,1,0:T(8,128)(2,1)S(1)}, u32[]{:S(2)}, u32[]{:S(2)}) %collective-permute-start.35) | collective-permute-done | bytes 180256 | tf_op jit(solution)/shard_map/ppermute | solution.py:95
  118.4 1.8 %collective-permute-done.36.refs_2_ = bf16[2,64,704]{2,1,0:T(8,128)(2,1)S(1)} collective-permute-done((bf16[2,64,704]{2,1,0:T(8,128)(2,1)S(1)}, bf16[2,64,704]{2,1,0:T(8,128)(2,1)S(1)}, u32[]{:S(2)}, u32[]{:S(2)}) %collective-permute-start.36) | collective-permute-done | bytes 180256 | tf_op jit(solution)/shard_map/ppermute | solution.py:95
  120.2 2.6 %collective-permute-done.37.refs_3_ = bf16[2,64,704]{2,1,0:T(8,128)(2,1)S(1)} collective-permute-done((bf16[2,64,704]{2,1,0:T(8,128)(2,1)S(1)}, bf16[2,64,704]{2,1,0:T(8,128)(2,1)S(1)}, u32[]{:S(2)}, u32[]{:S(2)}) %collective-permute-start.37) | collective-permute-done | bytes 180256 | tf_op jit(solution)/shard_map/ppermute | solution.py:95
  122.8 0.7 shard_map.80
  123.5 5.5 %collective-permute-start.38 = (bf16[16,1408]{1,0:T(8,128)(2,1)S(1)}, bf16[16,1408]{1,0:T(8,128)(2,1)S(1)}, u32[]{:S(2)}, u32[]{:S(2)}) collective-permute-start(bf16[16,1408]{1,0:T(8,128)(2,1)S(1)} %get-tuple-element.57), channel_id=1, source_target_pairs={{0,0},{1,16},{2,2},{3,18},{4,4},{5,20},{6,6},{7,22},{8,8},{9,24},{... | collective-permute-start | bytes 135176 | tf_op jit(solution)/shard_map/ppermute | solution.py:95
  129.1 1.3 collective-permute-start.40
  130.4 1.3 collective-permute-start.41
  131.7 2.0 %collective-permute-done.39.refs_1_ = bf16[16,1408]{1,0:T(8,128)(2,1)S(1)} collective-permute-done((bf16[16,1408]{1,0:T(8,128)(2,1)S(1)}, bf16[16,1408]{1,0:T(8,128)(2,1)S(1)}, u32[]{:S(2)}, u32[]{:S(2)}) %collective-permute-start.39) | collective-permute-done | bytes 45088 | tf_op jit(solution)/shard_map/ppermute | solution.py:95
  133.8 0.7 collective-permute-done.40.refs_2_
  134.4 2.1 %collective-permute-done.41.refs_3_ = bf16[16,1408]{1,0:T(8,128)(2,1)S(1)} collective-permute-done((bf16[16,1408]{1,0:T(8,128)(2,1)S(1)}, bf16[16,1408]{1,0:T(8,128)(2,1)S(1)}, u32[]{:S(2)}, u32[]{:S(2)}) %collective-permute-start.41) | collective-permute-done | bytes 45088 | tf_op jit(solution)/shard_map/ppermute | solution.py:95
  136.6 1.2 shard_map.81
  (84 shorter events, 4.4 us)
Async XLA Ops:
  0.0 64.7 %copy-start = (bf16[256,4224]{1,0:T(8,128)(2,1)S(1)}, bf16[256,4224]{1,0:T(8,128)(2,1)}, u32[]{:S(2)}) copy-start(bf16[256,4224]{1,0:T(8,128)(2,1)} %param.11) | copy-start | bytes 6488068
  0.0 40.7 %copy-start.22 = (s32[4]{0:T(128)S(1)}, s32[4]{0:T(128)}, u32[]{:S(2)}) copy-start(s32[4]{0:T(128)} %param.9) | copy-start | bytes 52
  2.9 7.7 %collective-permute-start.5 = (bf16[88,1232]{1,0:T(8,128)(2,1)S(1)}, bf16[88,1232]{1,0:T(8,128)(2,1)S(1)}, u32[]{:S(2)}, u32[]{:S(2)}) collective-permute-start(bf16[88,1232]{1,0:T(8,128)(2,1)S(1)} %get-tuple-element.35), channel_id=1, source_target_pairs={{0,2},{1,3},{2,0},{3,1},{4,6},{5,7},{6,4},{7,5},{8,10},{9,11},{10,... | collective-permute-start | bytes 650504 | tf_op jit(solution)/shard_map/ppermute | solution.py:95
  6.7 6.8 %collective-permute-start.2 = (bf16[2,4,16,1408]{3,2,1,0:T(8,128)(2,1)S(1)}, bf16[2,4,16,1408]{3,2,1,0:T(8,128)(2,1)S(1)}, u32[]{:S(2)}, u32[]{:S(2)}) collective-permute-start(bf16[2,4,16,1408]{3,2,1,0:T(8,128)(2,1)S(1)} %shard_map.73), channel_id=1, source_target_pairs={{0,16},{1,0},{2,18},{3,2},{4,20},{5,4},{6,22},{7,6},{8,24},{9,8},{... | collective-permute-start | bytes 1081352 | tf_op jit(solution)/shard_map/ppermute | solution.py:95
  7.6 9.9 %collective-permute-start.1 = (bf16[2,4,16,1408]{3,2,1,0:T(8,128)(2,1)S(1)}, bf16[2,4,16,1408]{3,2,1,0:T(8,128)(2,1)S(1)}, u32[]{:S(2)}, u32[]{:S(2)}) collective-permute-start(bf16[2,4,16,1408]{3,2,1,0:T(8,128)(2,1)S(1)} %shard_map.73), channel_id=1, source_target_pairs={{0,0},{1,16},{2,2},{3,18},{4,4},{5,20},{6,6},{7,22},{8,8},{9,24},{... | collective-permute-start | bytes 1081352 | tf_op jit(solution)/shard_map/ppermute | solution.py:95
  11.3 54.1 %copy-start.1 = (bf16[352,352]{1,0:T(8,128)(2,1)}, bf16[352,352]{1,0:T(8,128)(2,1)S(1)}, u32[]{:S(2)}) copy-start(bf16[352,352]{1,0:T(8,128)(2,1)S(1)} %shard_map.75.refs_4_) | copy-start | bytes 743428
  11.3 9.1 %collective-permute-start.6 = (bf16[352,352]{1,0:T(8,128)(2,1)S(1)}, bf16[352,352]{1,0:T(8,128)(2,1)}, u32[]{:S(2)}, u32[]{:S(2)}) collective-permute-start(bf16[352,352]{1,0:T(8,128)(2,1)S(1)} %shard_map.75.refs_4_), channel_id=1, source_target_pairs={{0,4},{1,5},{2,6},{3,7},{4,8},{5,9},{6,10},{7,11},{8,12},{9,13},{1... | collective-permute-start | bytes 743432 | tf_op jit(solution)/shard_map/ppermute | solution.py:95
  13.5 13.5 %copy-start.7 = (bf16[2,4,16,1408]{3,2,1,0:T(8,128)(2,1)}, bf16[2,4,16,1408]{3,2,1,0:T(8,128)(2,1)S(1)}, u32[]{:S(2)}) copy-start(bf16[2,4,16,1408]{3,2,1,0:T(8,128)(2,1)S(1)} %collective-permute-done.2.refs_1_) | copy-start | bytes 1081348
  17.5 31.1 %copy-start.8 = (bf16[2,4,16,1408]{3,2,1,0:T(8,128)(2,1)}, bf16[2,4,16,1408]{3,2,1,0:T(8,128)(2,1)S(1)}, u32[]{:S(2)}) copy-start(bf16[2,4,16,1408]{3,2,1,0:T(8,128)(2,1)S(1)} %collective-permute-done.1.refs_0_) | copy-start | bytes 1081348
  20.4 8.2 %collective-permute-start.7 = (bf16[352,352]{1,0:T(8,128)(2,1)}, bf16[352,352]{1,0:T(8,128)(2,1)}, u32[]{:S(2)}, u32[]{:S(2)}) collective-permute-start(bf16[352,352]{1,0:T(8,128)(2,1)} %collective-permute-done.6.refs_5_), channel_id=1, source_target_pairs={{0,4},{1,5},{2,6},{3,7},{4,8},{5,9},{6,10},{7,11},{8,12},{9,13},{1... | collective-permute-start | bytes 743432 | tf_op jit(solution)/shard_map/ppermute | solution.py:95
  20.4 6.6 %collective-permute-start.19 = (bf16[88,1232]{1,0:T(8,128)(2,1)S(1)}, bf16[88,1232]{1,0:T(8,128)(2,1)S(1)}, u32[]{:S(2)}, u32[]{:S(2)}) collective-permute-start(bf16[88,1232]{1,0:T(8,128)(2,1)S(1)} %get-tuple-element.44), channel_id=1, source_target_pairs={{0,1},{1,0},{2,3},{3,2},{4,5},{5,4},{6,7},{7,6},{8,9},{9,8},{10,11... | collective-permute-start | bytes 650504 | tf_op jit(solution)/shard_map/ppermute | solution.py:95
  22.3 4.7 %collective-permute-start.20 = (bf16[88,528]{1,0:T(8,128)(2,1)S(1)}, bf16[88,528]{1,0:T(8,128)(2,1)S(1)}, u32[]{:S(2)}, u32[]{:S(2)}) collective-permute-start(bf16[88,528]{1,0:T(8,128)(2,1)S(1)} %get-tuple-element.46), channel_id=1, source_target_pairs={{0,3},{1,2},{2,1},{3,0},{4,7},{5,6},{6,5},{7,4},{8,11},{9,10},{10,... | collective-permute-start | bytes 278792 | tf_op jit(solution)/shard_map/ppermute | solution.py:95
  27.8 42.2 %copy-start.3 = (bf16[352,528]{1,0:T(8,128)(2,1)}, bf16[352,528]{1,0:T(8,128)(2,1)S(1)}, u32[]{:S(2)}) copy-start(bf16[352,528]{1,0:T(8,128)(2,1)S(1)} %get-tuple-element.49.refs_6_) | copy-start | bytes 1115140
  27.8 42.2 %copy-start.4 = (bf16[88,704]{1,0:T(8,128)(2,1)}, bf16[88,704]{1,0:T(8,128)(2,1)S(1)}, u32[]{:S(2)}) copy-start(bf16[88,704]{1,0:T(8,128)(2,1)S(1)} %get-tuple-element.51.refs_14_) | copy-start | bytes 371716
  28.6 10.9 %collective-permute-start.21 = (bf16[352,528]{1,0:T(8,128)(2,1)S(1)}, bf16[352,528]{1,0:T(8,128)(2,1)S(1)}, u32[]{:S(2)}, u32[]{:S(2)}) collective-permute-start(bf16[352,528]{1,0:T(8,128)(2,1)S(1)} %get-tuple-element.49.refs_6_), channel_id=1, source_target_pairs={{0,4},{1,5},{2,6},{3,7},{4,8},{5,9},{6,10},{7,11},{8,12},{9,13},{1... | collective-permute-start | bytes 1115144 | tf_op jit(solution)/shard_map/ppermute | solution.py:95
  29.3 17.8 %collective-permute-start.4 = (bf16[2,4,16,1408]{3,2,1,0:T(8,128)(2,1)S(1)}, bf16[2,4,16,1408]{3,2,1,0:T(8,128)(2,1)S(1)}, u32[]{:S(2)}, u32[]{:S(2)}) collective-permute-start(bf16[2,4,16,1408]{3,2,1,0:T(8,128)(2,1)S(1)} %shard_map.73), channel_id=1, source_target_pairs={{0,18},{1,2},{2,16},{3,0},{4,22},{5,6},{6,20},{7,4},{8,26},{9,10},... | collective-permute-start | bytes 1081352 | tf_op jit(solution)/shard_map/ppermute | solution.py:95
  31.9 16.7 %collective-permute-start.3 = (bf16[2,4,16,1408]{3,2,1,0:T(8,128)(2,1)S(1)}, bf16[2,4,16,1408]{3,2,1,0:T(8,128)(2,1)S(1)}, u32[]{:S(2)}, u32[]{:S(2)}) collective-permute-start(bf16[2,4,16,1408]{3,2,1,0:T(8,128)(2,1)S(1)} %shard_map.73), channel_id=1, source_target_pairs={{0,2},{1,18},{2,0},{3,16},{4,6},{5,22},{6,4},{7,20},{8,10},{9,26},... | collective-permute-start | bytes 1081352 | tf_op jit(solution)/shard_map/ppermute | solution.py:95
  32.9 17.8 %collective-permute-start.9 = (bf16[352,352]{1,0:T(8,128)(2,1)S(1)}, bf16[352,352]{1,0:T(8,128)(2,1)}, u32[]{:S(2)}, u32[]{:S(2)}) collective-permute-start(bf16[352,352]{1,0:T(8,128)(2,1)S(1)} %shard_map.75.refs_4_), channel_id=1, source_target_pairs={{0,1},{1,0},{2,3},{3,2},{4,5},{5,4},{6,7},{7,6},{8,9},{9,8},{10,11... | collective-permute-start | bytes 743432 | tf_op jit(solution)/shard_map/ppermute | solution.py:95
  39.5 48.0 %copy-start.5 = (bf16[352,528]{1,0:T(8,128)(2,1)}, bf16[352,528]{1,0:T(8,128)(2,1)S(1)}, u32[]{:S(2)}) copy-start(bf16[352,528]{1,0:T(8,128)(2,1)S(1)} %collective-permute-done.21.refs_7_) | copy-start | bytes 1115140
  39.5 24.1 %collective-permute-start.22 = (bf16[352,528]{1,0:T(8,128)(2,1)S(1)}, bf16[352,528]{1,0:T(8,128)(2,1)}, u32[]{:S(2)}, u32[]{:S(2)}) collective-permute-start(bf16[352,528]{1,0:T(8,128)(2,1)S(1)} %collective-permute-done.21.refs_7_), channel_id=1, source_target_pairs={{0,4},{1,5},{2,6},{3,7},{4,8},{5,9},{6,10},{7,11},{8,12},{9,13},{1... | collective-permute-start | bytes 1115144 | tf_op jit(solution)/shard_map/ppermute | solution.py:95
  40.7 8.0 %collective-permute-start = (s32[4]{0:T(128)S(1)}, s32[4]{0:T(128)S(1)}, u32[]{:S(2)}, u32[]{:S(2)}) collective-permute-start(s32[4]{0:T(128)S(1)} %copy-done.22), channel_id=1, source_target_pairs={{0,0},{1,16},{2,2},{3,18},{4,4},{5,20},{6,6},{7,22},{8,8},{9,24},{... | collective-permute-start | bytes 56 | tf_op jit(solution)/shard_map/ppermute | solution.py:95
  47.0 1.6 %copy-start.9 = (bf16[2,4,16,1408]{3,2,1,0:T(8,128)(2,1)}, bf16[2,4,16,1408]{3,2,1,0:T(8,128)(2,1)S(1)}, u32[]{:S(2)}) copy-start(bf16[2,4,16,1408]{3,2,1,0:T(8,128)(2,1)S(1)} %collective-permute-done.4.refs_3_) | copy-start | bytes 1081348
  47.0 5.3 %collective-permute-start.10 = (bf16[352,352]{1,0:T(8,128)(2,1)}, bf16[352,352]{1,0:T(8,128)(2,1)}, u32[]{:S(2)}, u32[]{:S(2)}) collective-permute-start(bf16[352,352]{1,0:T(8,128)(2,1)} %collective-permute-done.6.refs_5_), channel_id=1, source_target_pairs={{0,1},{1,0},{2,3},{3,2},{4,5},{5,4},{6,7},{7,6},{8,9},{9,8},{10,11... | collective-permute-start | bytes 743432 | tf_op jit(solution)/shard_map/ppermute | solution.py:95
  48.6 0.7 copy-start.10
  48.6 14.8 %collective-permute-start.8 = (bf16[352,352]{1,0:T(8,128)(2,1)}, bf16[352,352]{1,0:T(8,128)(2,1)}, u32[]{:S(2)}, u32[]{:S(2)}) collective-permute-start(bf16[352,352]{1,0:T(8,128)(2,1)} %collective-permute-done.7.refs_6_), channel_id=1, source_target_pairs={{0,4},{1,5},{2,6},{3,7},{4,8},{5,9},{6,10},{7,11},{8,12},{9,13},{1... | collective-permute-start | bytes 743432 | tf_op jit(solution)/shard_map/ppermute | solution.py:95
  49.4 14.1 %collective-permute-start.11 = (bf16[352,352]{1,0:T(8,128)(2,1)}, bf16[352,352]{1,0:T(8,128)(2,1)}, u32[]{:S(2)}, u32[]{:S(2)}) collective-permute-start(bf16[352,352]{1,0:T(8,128)(2,1)} %collective-permute-done.7.refs_6_), channel_id=1, source_target_pairs={{0,1},{1,0},{2,3},{3,2},{4,5},{5,4},{6,7},{7,6},{8,9},{9,8},{10,11... | collective-permute-start | bytes 743432 | tf_op jit(solution)/shard_map/ppermute | solution.py:95
  50.7 11.4 %collective-permute-start.28 = (bf16[88,704]{1,0:T(8,128)(2,1)S(1)}, bf16[88,704]{1,0:T(8,128)(2,1)S(1)}, u32[]{:S(2)}, u32[]{:S(2)}) collective-permute-start(bf16[88,704]{1,0:T(8,128)(2,1)S(1)} %get-tuple-element.51.refs_14_), channel_id=1, source_target_pairs={{0,4},{1,5},{2,6},{3,7},{4,8},{5,9},{6,10},{7,11},{8,12},{9,13},{1... | collective-permute-start | bytes 371720 | tf_op jit(solution)/shard_map/ppermute | solution.py:95
  52.4 18.4 %collective-permute-start.31 = (bf16[88,704]{1,0:T(8,128)(2,1)S(1)}, bf16[88,704]{1,0:T(8,128)(2,1)S(1)}, u32[]{:S(2)}, u32[]{:S(2)}) collective-permute-start(bf16[88,704]{1,0:T(8,128)(2,1)S(1)} %get-tuple-element.51.refs_14_), channel_id=1, source_target_pairs={{0,1},{1,0},{2,3},{3,2},{4,5},{5,4},{6,7},{7,6},{8,9},{9,8},{10,11... | collective-permute-start | bytes 371720 | tf_op jit(solution)/shard_map/ppermute | solution.py:95
  62.1 19.0 %copy-start.15 = (bf16[88,704]{1,0:T(8,128)(2,1)}, bf16[88,704]{1,0:T(8,128)(2,1)S(1)}, u32[]{:S(2)}) copy-start(bf16[88,704]{1,0:T(8,128)(2,1)S(1)} %collective-permute-done.28.refs_15_) | copy-start | bytes 371716
  62.1 29.9 %collective-permute-start.24 = (bf16[352,528]{1,0:T(8,128)(2,1)S(1)}, bf16[352,528]{1,0:T(8,128)(2,1)S(1)}, u32[]{:S(2)}, u32[]{:S(2)}) collective-permute-start(bf16[352,528]{1,0:T(8,128)(2,1)S(1)} %get-tuple-element.49.refs_6_), channel_id=1, source_target_pairs={{0,1},{1,0},{2,3},{3,2},{4,5},{5,4},{6,7},{7,6},{8,9},{9,8},{10,11... | collective-permute-start | bytes 1115144 | tf_op jit(solution)/shard_map/ppermute | solution.py:95
  63.4 9.9 %collective-permute-start.29 = (bf16[88,704]{1,0:T(8,128)(2,1)S(1)}, bf16[88,704]{1,0:T(8,128)(2,1)S(1)}, u32[]{:S(2)}, u32[]{:S(2)}) collective-permute-start(bf16[88,704]{1,0:T(8,128)(2,1)S(1)} %collective-permute-done.28.refs_15_), channel_id=1, source_target_pairs={{0,4},{1,5},{2,6},{3,7},{4,8},{5,9},{6,10},{7,11},{8,12},{9,13},{1... | collective-permute-start | bytes 371720 | tf_op jit(solution)/shard_map/ppermute | solution.py:95
  63.4 2.0 %collective-permute-start.12 = (bf16[352,352]{1,0:T(8,128)(2,1)}, bf16[352,352]{1,0:T(8,128)(2,1)S(1)}, u32[]{:S(2)}, u32[]{:S(2)}) collective-permute-start(bf16[352,352]{1,0:T(8,128)(2,1)} %collective-permute-done.8.refs_7_), channel_id=1, source_target_pairs={{0,1},{1,0},{2,3},{3,2},{4,5},{5,4},{6,7},{7,6},{8,9},{9,8},{10,11... | collective-permute-start | bytes 743432 | tf_op jit(solution)/shard_map/ppermute | solution.py:95
  63.6 28.4 %collective-permute-start.23 = (bf16[352,528]{1,0:T(8,128)(2,1)}, bf16[352,528]{1,0:T(8,128)(2,1)}, u32[]{:S(2)}, u32[]{:S(2)}) collective-permute-start(bf16[352,528]{1,0:T(8,128)(2,1)} %collective-permute-done.22.refs_8_), channel_id=1, source_target_pairs={{0,4},{1,5},{2,6},{3,7},{4,8},{5,9},{6,10},{7,11},{8,12},{9,13},{1... | collective-permute-start | bytes 1115144 | tf_op jit(solution)/shard_map/ppermute | solution.py:95
  65.5 0.7 copy-start.11
  70.0 11.2 %collective-permute-start.13 = (bf16[4,16,352]{2,1,0:T(8,128)(2,1)S(1)}, bf16[4,16,352]{2,1,0:T(8,128)(2,1)S(1)}, u32[]{:S(2)}, u32[]{:S(2)}) collective-permute-start(bf16[4,16,352]{2,1,0:T(8,128)(2,1)S(1)} %get-tuple-element.39), channel_id=1, source_target_pairs={{0,4},{1,5},{2,6},{3,7},{4,8},{5,9},{6,10},{7,11},{8,12},{9,13},{1... | collective-permute-start | bytes 135176 | tf_op jit(solution)/shard_map/ppermute | solution.py:95
  70.8 25.1 %copy-start.16 = (bf16[88,704]{1,0:T(8,128)(2,1)}, bf16[88,704]{1,0:T(8,128)(2,1)S(1)}, u32[]{:S(2)}) copy-start(bf16[88,704]{1,0:T(8,128)(2,1)S(1)} %collective-permute-done.31.refs_18_) | copy-start | bytes 371716
  70.8 12.8 %collective-permute-start.14 = (bf16[4,16,352]{2,1,0:T(8,128)(2,1)S(1)}, bf16[4,16,352]{2,1,0:T(8,128)(2,1)S(1)}, u32[]{:S(2)}, u32[]{:S(2)}) collective-permute-start(bf16[4,16,352]{2,1,0:T(8,128)(2,1)S(1)} %get-tuple-element.40), channel_id=1, source_target_pairs={{0,8},{1,9},{2,10},{3,11},{4,12},{5,13},{6,14},{7,15},{8,0},{9,1},... | collective-permute-start | bytes 135176 | tf_op jit(solution)/shard_map/ppermute | solution.py:95
  73.3 22.5 %copy-start.17 = (bf16[88,704]{1,0:T(8,128)(2,1)}, bf16[88,704]{1,0:T(8,128)(2,1)S(1)}, u32[]{:S(2)}) copy-start(bf16[88,704]{1,0:T(8,128)(2,1)S(1)} %collective-permute-done.29.refs_16_) | copy-start | bytes 371716
  73.3 10.9 %collective-permute-start.15 = (bf16[4,16,352]{2,1,0:T(8,128)(2,1)S(1)}, bf16[4,16,352]{2,1,0:T(8,128)(2,1)S(1)}, u32[]{:S(2)}, u32[]{:S(2)}) collective-permute-start(bf16[4,16,352]{2,1,0:T(8,128)(2,1)S(1)} %get-tuple-element.41), channel_id=1, source_target_pairs={{0,12},{1,13},{2,14},{3,15},{4,0},{5,1},{6,2},{7,3},{8,4},{9,5},{1... | collective-permute-start | bytes 135176 | tf_op jit(solution)/shard_map/ppermute | solution.py:95
  81.2 4.6 %collective-permute-start.32 = (bf16[88,704]{1,0:T(8,128)(2,1)S(1)}, bf16[88,704]{1,0:T(8,128)(2,1)S(1)}, u32[]{:S(2)}, u32[]{:S(2)}) collective-permute-start(bf16[88,704]{1,0:T(8,128)(2,1)S(1)} %collective-permute-done.28.refs_15_), channel_id=1, source_target_pairs={{0,1},{1,0},{2,3},{3,2},{4,5},{5,4},{6,7},{7,6},{8,9},{9,8},{10,11... | collective-permute-start | bytes 371720 | tf_op jit(solution)/shard_map/ppermute | solution.py:95
  83.6 3.9 %collective-permute-start.33 = (bf16[88,704]{1,0:T(8,128)(2,1)S(1)}, bf16[88,704]{1,0:T(8,128)(2,1)S(1)}, u32[]{:S(2)}, u32[]{:S(2)}) collective-permute-start(bf16[88,704]{1,0:T(8,128)(2,1)S(1)} %collective-permute-done.29.refs_16_), channel_id=1, source_target_pairs={{0,1},{1,0},{2,3},{3,2},{4,5},{5,4},{6,7},{7,6},{8,9},{9,8},{10,11... | collective-permute-start | bytes 371720 | tf_op jit(solution)/shard_map/ppermute | solution.py:95
  84.2 7.0 %collective-permute-start.30 = (bf16[88,704]{1,0:T(8,128)(2,1)S(1)}, bf16[88,704]{1,0:T(8,128)(2,1)S(1)}, u32[]{:S(2)}, u32[]{:S(2)}) collective-permute-start(bf16[88,704]{1,0:T(8,128)(2,1)S(1)} %collective-permute-done.29.refs_16_), channel_id=1, source_target_pairs={{0,4},{1,5},{2,6},{3,7},{4,8},{5,9},{6,10},{7,11},{8,12},{9,13},{1... | collective-permute-start | bytes 371720 | tf_op jit(solution)/shard_map/ppermute | solution.py:95
  85.8 15.6 %copy-start.2 = (bf16[4,4,16,352]{3,2,1,0:T(8,128)(2,1)}, bf16[4,4,16,352]{3,2,1,0:T(8,128)(2,1)S(1)}, u32[]{:S(2)}) copy-start(bf16[4,4,16,352]{3,2,1,0:T(8,128)(2,1)S(1)} %shard_map.77.refs_0_) | copy-start | bytes 540676
  85.8 6.7 %copy-start.18 = (bf16[88,704]{1,0:T(8,128)(2,1)}, bf16[88,704]{1,0:T(8,128)(2,1)S(1)}, u32[]{:S(2)}) copy-start(bf16[88,704]{1,0:T(8,128)(2,1)S(1)} %collective-permute-done.32.refs_19_) | copy-start | bytes 371716
  85.8 9.0 %collective-permute-start.18 = (bf16[4,4,16,352]{3,2,1,0:T(8,128)(2,1)S(1)}, bf16[4,4,16,352]{3,2,1,0:T(8,128)(2,1)S(1)}, u32[]{:S(2)}, u32[]{:S(2)}) collective-permute-start(bf16[4,4,16,352]{3,2,1,0:T(8,128)(2,1)S(1)} %shard_map.77.refs_0_), channel_id=1, source_target_pairs={{0,18},{1,19},{2,16},{3,17},{4,22},{5,23},{6,20},{7,21},{8,26},{9,... | collective-permute-start | bytes 540680 | tf_op jit(solution)/shard_map/ppermute | solution.py:95
  87.5 8.3 %copy-start.19 = (bf16[88,704]{1,0:T(8,128)(2,1)}, bf16[88,704]{1,0:T(8,128)(2,1)S(1)}, u32[]{:S(2)}) copy-start(bf16[88,704]{1,0:T(8,128)(2,1)S(1)} %collective-permute-done.33.refs_20_) | copy-start | bytes 371716
  87.5 13.2 %collective-permute-start.25 = (bf16[352,528]{1,0:T(8,128)(2,1)S(1)}, bf16[352,528]{1,0:T(8,128)(2,1)}, u32[]{:S(2)}, u32[]{:S(2)}) collective-permute-start(bf16[352,528]{1,0:T(8,128)(2,1)S(1)} %collective-permute-done.21.refs_7_), channel_id=1, source_target_pairs={{0,1},{1,0},{2,3},{3,2},{4,5},{5,4},{6,7},{7,6},{8,9},{9,8},{10,11... | collective-permute-start | bytes 1115144 | tf_op jit(solution)/shard_map/ppermute | solution.py:95
  91.2 4.6 %copy-start.20 = (bf16[88,704]{1,0:T(8,128)(2,1)}, bf16[88,704]{1,0:T(8,128)(2,1)S(1)}, u32[]{:S(2)}) copy-start(bf16[88,704]{1,0:T(8,128)(2,1)S(1)} %collective-permute-done.30.refs_17_) | copy-start | bytes 371716
  91.2 9.5 %collective-permute-start.26 = (bf16[352,528]{1,0:T(8,128)(2,1)}, bf16[352,528]{1,0:T(8,128)(2,1)}, u32[]{:S(2)}, u32[]{:S(2)}) collective-permute-start(bf16[352,528]{1,0:T(8,128)(2,1)} %collective-permute-done.22.refs_8_), channel_id=1, source_target_pairs={{0,1},{1,0},{2,3},{3,2},{4,5},{5,4},{6,7},{7,6},{8,9},{9,8},{10,11... | collective-permute-start | bytes 1115144 | tf_op jit(solution)/shard_map/ppermute | solution.py:95
  92.0 9.4 %collective-permute-start.27 = (bf16[352,528]{1,0:T(8,128)(2,1)}, bf16[352,528]{1,0:T(8,128)(2,1)}, u32[]{:S(2)}, u32[]{:S(2)}) collective-permute-start(bf16[352,528]{1,0:T(8,128)(2,1)} %collective-permute-done.23.refs_9_), channel_id=1, source_target_pairs={{0,1},{1,0},{2,3},{3,2},{4,5},{5,4},{6,7},{7,6},{8,9},{9,8},{10,11... | collective-permute-start | bytes 1115144 | tf_op jit(solution)/shard_map/ppermute | solution.py:95
  92.1 2.8 %copy-start.6 = (bf16[352,528]{1,0:T(8,128)(2,1)}, bf16[352,528]{1,0:T(8,128)(2,1)S(1)}, u32[]{:S(2)}) copy-start(bf16[352,528]{1,0:T(8,128)(2,1)S(1)} %collective-permute-done.24.refs_10_) | copy-start | bytes 1115140
  92.1 1.7 %collective-permute-start.34 = (bf16[88,704]{1,0:T(8,128)(2,1)S(1)}, bf16[88,704]{1,0:T(8,128)(2,1)S(1)}, u32[]{:S(2)}, u32[]{:S(2)}) collective-permute-start(bf16[88,704]{1,0:T(8,128)(2,1)S(1)} %collective-permute-done.30.refs_17_), channel_id=1, source_target_pairs={{0,1},{1,0},{2,3},{3,2},{4,5},{5,4},{6,7},{7,6},{8,9},{9,8},{10,11... | collective-permute-start | bytes 371720 | tf_op jit(solution)/shard_map/ppermute | solution.py:95
  93.8 2.1 %copy-start.21 = (bf16[88,704]{1,0:T(8,128)(2,1)}, bf16[88,704]{1,0:T(8,128)(2,1)S(1)}, u32[]{:S(2)}) copy-start(bf16[88,704]{1,0:T(8,128)(2,1)S(1)} %collective-permute-done.34.refs_21_) | copy-start | bytes 371716
  93.8 6.1 %collective-permute-start.17 = (bf16[4,4,16,352]{3,2,1,0:T(8,128)(2,1)S(1)}, bf16[4,4,16,352]{3,2,1,0:T(8,128)(2,1)S(1)}, u32[]{:S(2)}, u32[]{:S(2)}) collective-permute-start(bf16[4,4,16,352]{3,2,1,0:T(8,128)(2,1)S(1)} %shard_map.77.refs_0_), channel_id=1, source_target_pairs={{0,2},{1,3},{2,0},{3,1},{4,6},{5,7},{6,4},{7,5},{8,10},{9,11},{10,... | collective-permute-start | bytes 540680 | tf_op jit(solution)/shard_map/ppermute | solution.py:95
  94.8 0.9 copy-start.12
  94.8 5.9 %collective-permute-start.16 = (bf16[4,4,16,352]{3,2,1,0:T(8,128)(2,1)S(1)}, bf16[4,4,16,352]{3,2,1,0:T(8,128)(2,1)S(1)}, u32[]{:S(2)}, u32[]{:S(2)}) collective-permute-start(bf16[4,4,16,352]{3,2,1,0:T(8,128)(2,1)S(1)} %shard_map.77.refs_0_), channel_id=1, source_target_pairs={{0,16},{1,17},{2,18},{3,19},{4,20},{5,21},{6,22},{7,23},{8,24},{9,... | collective-permute-start | bytes 540680 | tf_op jit(solution)/shard_map/ppermute | solution.py:95
  99.9 1.5 %copy-start.13 = (bf16[4,4,16,352]{3,2,1,0:T(8,128)(2,1)}, bf16[4,4,16,352]{3,2,1,0:T(8,128)(2,1)S(1)}, u32[]{:S(2)}) copy-start(bf16[4,4,16,352]{3,2,1,0:T(8,128)(2,1)S(1)} %collective-permute-done.17.refs_2_) | copy-start | bytes 540676
  113.5 4.9 %collective-permute-start.35 = (bf16[2,64,704]{2,1,0:T(8,128)(2,1)S(1)}, bf16[2,64,704]{2,1,0:T(8,128)(2,1)S(1)}, u32[]{:S(2)}, u32[]{:S(2)}) collective-permute-start(bf16[2,64,704]{2,1,0:T(8,128)(2,1)S(1)} %get-tuple-element.54), channel_id=1, source_target_pairs={{0,16},{1,17},{2,18},{3,19},{4,20},{5,21},{6,22},{7,23},{8,24},{9,... | collective-permute-start | bytes 540680 | tf_op jit(solution)/shard_map/ppermute | solution.py:95
  114.4 5.8 %collective-permute-start.36 = (bf16[2,64,704]{2,1,0:T(8,128)(2,1)S(1)}, bf16[2,64,704]{2,1,0:T(8,128)(2,1)S(1)}, u32[]{:S(2)}, u32[]{:S(2)}) collective-permute-start(bf16[2,64,704]{2,1,0:T(8,128)(2,1)S(1)} %get-tuple-element.55), channel_id=1, source_target_pairs={{0,2},{1,3},{2,0},{3,1},{4,6},{5,7},{6,4},{7,5},{8,10},{9,11},{10,... | collective-permute-start | bytes 540680 | tf_op jit(solution)/shard_map/ppermute | solution.py:95
  114.7 8.1 %collective-permute-start.37 = (bf16[2,64,704]{2,1,0:T(8,128)(2,1)S(1)}, bf16[2,64,704]{2,1,0:T(8,128)(2,1)S(1)}, u32[]{:S(2)}, u32[]{:S(2)}) collective-permute-start(bf16[2,64,704]{2,1,0:T(8,128)(2,1)S(1)} %get-tuple-element.56), channel_id=1, source_target_pairs={{0,18},{1,19},{2,16},{3,17},{4,22},{5,23},{6,20},{7,21},{8,26},{9,... | collective-permute-start | bytes 540680 | tf_op jit(solution)/shard_map/ppermute | solution.py:95
  123.5 8.2 %collective-permute-start.38 = (bf16[16,1408]{1,0:T(8,128)(2,1)S(1)}, bf16[16,1408]{1,0:T(8,128)(2,1)S(1)}, u32[]{:S(2)}, u32[]{:S(2)}) collective-permute-start(bf16[16,1408]{1,0:T(8,128)(2,1)S(1)} %get-tuple-element.57), channel_id=1, source_target_pairs={{0,0},{1,16},{2,2},{3,18},{4,4},{5,20},{6,6},{7,22},{8,8},{9,24},{... | collective-permute-start | bytes 135176 | tf_op jit(solution)/shard_map/ppermute | solution.py:95
  129.0 4.7 %collective-permute-start.39 = (bf16[16,1408]{1,0:T(8,128)(2,1)S(1)}, bf16[16,1408]{1,0:T(8,128)(2,1)S(1)}, u32[]{:S(2)}, u32[]{:S(2)}) collective-permute-start(bf16[16,1408]{1,0:T(8,128)(2,1)S(1)} %get-tuple-element.58), channel_id=1, source_target_pairs={{0,12},{1,28},{2,14},{3,30},{4,0},{5,16},{6,2},{7,18},{8,4},{9,20}... | collective-permute-start | bytes 135176 | tf_op jit(solution)/shard_map/ppermute | solution.py:95
  129.1 5.3 %collective-permute-start.40 = (bf16[16,1408]{1,0:T(8,128)(2,1)S(1)}, bf16[16,1408]{1,0:T(8,128)(2,1)S(1)}, u32[]{:S(2)}, u32[]{:S(2)}) collective-permute-start(bf16[16,1408]{1,0:T(8,128)(2,1)S(1)} %get-tuple-element.59), channel_id=1, source_target_pairs={{0,8},{1,24},{2,10},{3,26},{4,12},{5,28},{6,14},{7,30},{8,0},{9,16... | collective-permute-start | bytes 135176 | tf_op jit(solution)/shard_map/ppermute | solution.py:95
  130.4 6.2 %collective-permute-start.41 = (bf16[16,1408]{1,0:T(8,128)(2,1)S(1)}, bf16[16,1408]{1,0:T(8,128)(2,1)S(1)}, u32[]{:S(2)}, u32[]{:S(2)}) collective-permute-start(bf16[16,1408]{1,0:T(8,128)(2,1)S(1)} %get-tuple-element.60), channel_id=1, source_target_pairs={{0,4},{1,20},{2,6},{3,22},{4,8},{5,24},{6,10},{7,26},{8,12},{9,28}... | collective-permute-start | bytes 135176 | tf_op jit(solution)/shard_map/ppermute | solution.py:95
  (1 other events, 0.7 us)

commit v6 on v5

--- a/solution.py
+++ b/solution.py
@@ -197,26 +197,27 @@
 
 
 def shards_kernel(G, S, Y, where, *refs):
-    qkvs, rest = refs[: Y * G], refs[Y * G]
-    qkv, out = refs[Y * G + 1 :]
+    qkvs, rest, out = refs[: Y * G], refs[Y * G], refs[Y * G + 1]
     x, y, c = where[0], where[2], where[3]
     part = 3 * (S // G) * HD
+    wide = out.shape[1] - part
     for gy in range(Y):
         for gc in range(G):
+            at = (gy * G + gc) * HD
             for e in range(Y):
                 for f in range(G):
 
                     @pl.when(((y + Y - e) % Y == gy) & ((c + G - f) % G == gc))
                     def _():
-                        at = (gy * G + gc) * HD
-                        qkv[at : at + HD, :] = qkvs[e * G + f][:, :part]
-
-    out[...] = rest[...]
-    for f in range(1, G):
-
-        @pl.when((c + G - f) % G == x)
-        def _():
-            out[...] = qkvs[f][:, part:]
+                        out[at : at + HD, :part] = qkvs[e * G + f][:, :part]
+
+            for f in range(G):
+
+                @pl.when((c + G - f) % G == x)
+                def _():
+                    v, off = (qkvs[f], part) if f else (rest, 0)
+                    k = gy * G + gc
+                    out[at : at + HD, part:] = v[:, off + k * wide : off + (k + 1) * wide]
 
 
 def merged_kernel(G, S, Y, where, *refs):
@@ -256,8 +257,8 @@
     blocks = Y * G
     merged_any, (shift, scale) = refs[:blocks], refs[blocks : blocks + 2]
     refs = refs[blocks + 2 :]
-    wq_any, wo_any, refs = refs[: G * S], refs[G * S : 2 * G * S], refs[2 * G * S :]
-    outs, base, (merged, norm, shifts, scales, wq, wo, att, sems) = (
+    w_any, refs = refs[: G * S], refs[G * S :]
+    outs, base, (merged, norm, shifts, scales, ws, att, sems) = (
         refs[:blocks],
         refs[blocks],
         refs[blocks + 1 :],
@@ -270,9 +271,8 @@
     pairs = [(shift, shifts), (scale, scales)]
     for f in range(G):
         for s in range(S):
-            pairs.append((wq_any[f * S + s], wq.at[(c + G - f) % G, (z + S - s) % S]))
-        for s in range(S):
-            pairs.append((wo_any[f * S + s], wo.at[(z + S - s) % S, (c + G - f) % G]))
+            at = pl.multiple_of((z ^ s) * cols, 16)
+            pairs.append((w_any[f * S + s], ws.at[(c + G - f) % G, pl.ds(at, cols)]))
     for e in range(Y):
         for d in range(G):
             b = (x + d) % G * Y + (y + e) % Y
@@ -297,10 +297,12 @@
     for b in range(blocks):
         norm[b] = ((wide[b] - mean) * inv * (1.0 + scales[b]) + shifts[b]).astype(BF)
     per = S // G
+    part = 3 * per * HD
     for f in range(G):
-        qkv = jnp.dot(norm[0], wq[f, 0], preferred_element_type=F32)
+        qkv = jnp.dot(norm[0], ws[f, :cols, :part], preferred_element_type=F32)
         for b in range(1, blocks):
-            qkv = qkv + jnp.dot(norm[b], wq[f, b], preferred_element_type=F32)
+            rows_b = slice(b * cols, (b + 1) * cols)
+            qkv = qkv + jnp.dot(norm[b], ws[f, rows_b, :part], preferred_element_type=F32)
         for t in range(per):
             q, k, v = (qkv[:, (p * per + t) * HD : (p * per + t + 1) * HD] for p in range(3))
             q = (norm88(q) * HD ** (-0.5)).astype(BF)
@@ -311,10 +313,17 @@
             probs = jnp.exp(scores - top)
             probs = (probs / jnp.sum(probs, axis=-1, keepdims=True)).astype(BF)
             att[f * per + t] = jnp.dot(probs, v, preferred_element_type=F32).astype(BF)
+    wide = ws.shape[2] - part
     for f in range(G):
-        acc = jnp.dot(att[0], wo[0, f], preferred_element_type=F32)
+        whole = []
+        for s in range(S):
+            pieces = [
+                ws[f, s * cols + k * HD : s * cols + (k + 1) * HD, part:] for k in range(blocks)
+            ]
+            whole.append(jnp.concatenate(pieces, axis=1))
+        acc = jnp.dot(att[0], whole[0], preferred_element_type=F32)
         for s in range(1, S):
-            acc = acc + jnp.dot(att[s], wo[s, f], preferred_element_type=F32)
+            acc = acc + jnp.dot(att[s], whole[s], preferred_element_type=F32)
         acc = acc.astype(BF)
         for k in range(blocks):
             outs[k][f] = acc[k * toks : (k + 1) * toks, :]
@@ -378,17 +387,15 @@
         join_kernel, [(2, S, local, width)], p.where, hidden, skip, copies=2, fast=[0], still=True
     )
     own = qkvs[0]
+    qkvs[1 * G] = swap(qkvs[1 * G], 1, 0)
     parts = [
         p.send(joined, lambda x, z, y, c, e=e, d=d: (c - d, z, y - e, x))
         for e in range(Y)
         for d in range(G)
     ]
     for e in range(Y):
-        for f in range(G):
-            if f:
-                qkvs[e * G + f] = swap(after(qkvs[e * G + f], *parts[:1]), e, f)
-            elif e:
-                qkvs[e * G] = swap(qkvs[e * G], e, 0)
+        for f in range(1, G):
+            qkvs[e * G + f] = swap(after(qkvs[e * G + f], *parts[G:]), e, f)
 
     def step(value):
         return p.send(value, lambda x, z, y, c: (x, z + 1, y, c))
@@ -405,26 +412,22 @@
         fast=[0],
         fast_in=True,
     )
-    wq, wo = call(
+    (held,) = call(
         partial(shards_kernel, G, S, Y),
-        [(blocks * HD, part), (HD, half)],
+        [(blocks * HD, part + half // blocks)],
         p.where,
         *qkvs,
         rest,
-        fast=[0, 1],
+        fast=[0],
         fast_in=True,
     )
     ws = [ring]
     ws.append(step(ring))
     ws.append(step(after(ws[1], *parts[:G])))
     ws.append(step(after(ws[2], *parts[G:])))
-    wq = [after(wq, ws[2])]
-    for _ in range(1, S):
-        wq.append(step(wq[-1]))
-    wo = [after(wo, ws[2])]
-    for _ in range(1, S):
-        wo.append(step(wo[-1]))
-    ws, wq, wo = over_cores(ws), over_cores(wq), over_cores(wo)
+    ws = over_cores(ws)
+    held = [after(held, ws[2])]
+    held += [p.send(held[0], lambda x, z, y, c, k=k: (x, z ^ k, y, c)) for k in (1, 2)]
 
     times = p.send(timestep, lambda x, z, y, c: (c, z, y, x))
     mod = modulation(lax.dynamic_slice(times, (p.z,), (1,)), w_mod)
@@ -450,14 +453,17 @@
         fast=range(S),
     )
     pieces = [pieces[0]] + [
-        p.send(pieces[s], lambda x, z, y, c, s=s: (x, z + s, y, c)) for s in range(1, S)
+        p.send(after(pieces[s], held[1]), lambda x, z, y, c, s=s: (x, z + s, y, c)) for s in range(1, S)
     ]
     (merged,) = call(stack_kernel, [(S, blocks, local, cols)], p.where, *pieces, copies=S)
+    held.append(p.send(after(held[2], merged), lambda x, z, y, c: (x, z ^ 1, y, c)))
     merged = [
         p.send(merged, lambda x, z, y, c, e=e, d=d: (x - d, z, y - e, c)) if e or d else merged
         for e in range(Y)
         for d in range(G)
     ]
+    early = [after(v, *merged[1:]) for v in held[:3]]
+    held += [swap(v, 0, f) for f in range(1, G) for v in (*early, held[3])]
     *parts, base = call(
         partial(attend_kernel, G, S, Y),
         [(G, toks, half)] * blocks + [(blocks, toks, cols)],
@@ -465,18 +471,16 @@
         *merged,
         shift,
         scale,
-        *wq,
-        *wo,
+        *held,
         scratch=[
             pltpu.VMEM((blocks, blocks, S, local, cols), BF),
             pltpu.VMEM((blocks, every, cols), BF),
             pltpu.VMEM((blocks, 1, cols), F32),
             pltpu.VMEM((blocks, 1, cols), F32),
-            pltpu.VMEM((G, S, cols, part), BF),
-            pltpu.VMEM((S, G, HD, half), BF),
+            pltpu.VMEM((G, width, part + half // blocks), BF),
             pltpu.VMEM((S, every, HD), BF),
         ],
-        copies=2 + 2 * G * S + blocks * blocks,
+        copies=2 + G * S + blocks * blocks,
         flops=10 * every * width * cols,
         still=True,
         fast=range(blocks + 1),

time: 138 us -> 130 us (0.942)
  waiting for transfers between devices: 56 us -> 49.2 us
  starting transfers between devices: 51.8 us -> 48 us
  local copies, waits for them, and re-layouts: 4.1 us -> 5.54 us
    ppermute x42 -> x35, waiting for transfers between devices: 56 us -> 49.2 us  [send(): return lax.ppermute(value, ('group', 'seq'), pairs)]
    ppermute x42 -> x35, starting transfers between devices: 51.8 us -> 48 us  [send(): return lax.ppermute(value, ('group', 'seq'), pairs)]
    unnamed x46 -> x42, local copies, waits for them, and re-layouts: 2.13 us -> 3.55 us
  transfers between devices with their start and end apart: 42 -> 35, of which waited for: 21 -> 21; matrix products, arithmetic and copies ran while one was open for 2% -> 2% of each run, Pallas kernels for 6% -> 6%
where the time goes in v6:
time: 130 us; the launch traced here: 129 us
  waiting for transfers between devices  49.2 us (38%)
  starting transfers between devices  48 us (37%)
  Pallas kernels  25.1 us (19%)
  local copies, waits for them, and re-layouts  5.54 us (4%)
    ppermute x35, waiting for transfers between devices, send(): return lax.ppermute(value, ('group', 'seq'), pairs)  49.2 us
    ppermute x35, starting transfers between devices, send(): return lax.ppermute(value, ('group', 'seq'), pairs)  48 us
    pallas_call x9, Pallas kernels, call(): pl.pallas_call(kernel, out_shape=[jax.ShapeDtypeStruct(s, BF) for s in ou...  25.1 us
    unnamed x42, local copies, waits for them, and re-layouts  3.55 us
  transfers between devices with their start and end apart: 35, of which 21 were waited for; matrix products, arithmetic and copies ran while one was open for 2% of the time, Pallas kernels for 6%

profile of v6, /device:TPU:1, one launch (start us, length us, event | category | flops | bytes accessed | tf_op | source)
XLA Modules:
  0.0 129.4 jit_solution(11831570615035534691)
XLA Ops:
  0.1 3.5 %shard_map.74 = (bf16[176,352]{1,0:T(8,128)(2,1)S(1)}, bf16[88,528]{1,0:T(8,128)(2,1)S(1)}, bf16[88,1232]{1,0:T(8,128)(2,1)}, bf16[88,1232]{1,0:T(8,128)(2,1)S(1...) custom-call(s32[4]{0:T(128)S(1)} %pad_add_fusion.where, bf16[176,1408]{1,0:T(8,128)(2,1)} %w_skip_any.1, ...), custom_call_target="tpu_custom_call" | custom-call | bytes 2973696 | tf_op jit(solution)/shard_map/pallas_call | solution.py:105
  3.6 2.2 %collective-permute-start.5 = (bf16[88,1232]{1,0:T(8,128)(2,1)S(1)}, bf16[88,1232]{1,0:T(8,128)(2,1)S(1)}, u32[]{:S(2)}, u32[]{:S(2)}) collective-permute-start(bf16[88,1232]{1,0:T(8,128)(2,1)S(1)} %get-tuple-element.39), channel_id=1, source_target_pairs={{0,2},{1,3},{2,0},{3,1},{4,6},{5,7},{6,4},{7,5},{8,10},{9,11},{10,... | collective-permute-start | bytes 650504 | tf_op jit(solution)/shard_map/ppermute | solution.py:95
  5.9 1.6 %shard_map.73 = bf16[2,4,16,1408]{3,2,1,0:T(8,128)(2,1)S(1)} custom-call(s32[4]{0:T(128)S(1)} %pad_add_fusion.where, bf16[4,16,1408]{2,1,0:T(8,128)(2,1)} %hidden.1, bf16[4,16,1408]{2,1,0:T(8,128)(2,1)} %skip.1), custom_call_target="tpu_custom_call" | custom-call | bytes 720896 | tf_op jit(solution)/shard_map/pallas_call | solution.py:105
  7.4 0.9 collective-permute-start.2
  8.3 3.0 %collective-permute-start.1 = (bf16[2,4,16,1408]{3,2,1,0:T(8,128)(2,1)S(1)}, bf16[2,4,16,1408]{3,2,1,0:T(8,128)(2,1)S(1)}, u32[]{:S(2)}, u32[]{:S(2)}) collective-permute-start(bf16[2,4,16,1408]{3,2,1,0:T(8,128)(2,1)S(1)} %shard_map.73), channel_id=1, source_target_pairs={{0,0},{1,16},{2,2},{3,18},{4,4},{5,20},{6,6},{7,22},{8,8},{9,24},{... | collective-permute-start | bytes 1081352 | tf_op jit(solution)/shard_map/ppermute | solution.py:95
  11.6 0.7 shard_map.75.refs_4_
  12.3 1.8 %collective-permute-start.6 = (bf16[352,352]{1,0:T(8,128)(2,1)S(1)}, bf16[352,352]{1,0:T(8,128)(2,1)S(1)}, u32[]{:S(2)}, u32[]{:S(2)}) collective-permute-start(bf16[352,352]{1,0:T(8,128)(2,1)S(1)} %shard_map.75.refs_4_), channel_id=1, source_target_pairs={{0,4},{1,5},{2,6},{3,7},{4,8},{5,9},{6,10},{7,11},{8,12},{9,13},{1... | collective-permute-start | bytes 743432 | tf_op jit(solution)/shard_map/ppermute | solution.py:95
  14.0 0.5 collective-permute-done.2.refs_1_
  14.5 6.8 %collective-permute-done.1.refs_0_ = bf16[2,4,16,1408]{3,2,1,0:T(8,128)(2,1)S(1)} collective-permute-done((bf16[2,4,16,1408]{3,2,1,0:T(8,128)(2,1)S(1)}, bf16[2,4,16,1408]{3,2,1,0:T(8,128)(2,1)S(1)}, u32[]{:S(2)}, u32[]{:S(2)}) %collective-permute-start.1) | collective-permute-done | bytes 360480 | tf_op jit(solution)/shard_map/ppermute | solution.py:95
  21.3 1.3 %collective-permute-start.7 = (bf16[352,352]{1,0:T(8,128)(2,1)S(1)}, bf16[352,352]{1,0:T(8,128)(2,1)}, u32[]{:S(2)}, u32[]{:S(2)}) collective-permute-start(bf16[352,352]{1,0:T(8,128)(2,1)S(1)} %collective-permute-done.6.refs_5_), channel_id=1, source_target_pairs={{0,4},{1,5},{2,6},{3,7},{4,8},{5,9},{6,10},{7,11},{8,12},{9,13},{1... | collective-permute-start | bytes 743432 | tf_op jit(solution)/shard_map/ppermute | solution.py:95
  22.6 2.4 %collective-permute-done.4.refs_3_ = bf16[2,4,16,1408]{3,2,1,0:T(8,128)(2,1)S(1)} collective-permute-done((bf16[2,4,16,1408]{3,2,1,0:T(8,128)(2,1)S(1)}, bf16[2,4,16,1408]{3,2,1,0:T(8,128)(2,1)S(1)}, u32[]{:S(2)}, u32[]{:S(2)}) %collective-permute-start.4) | collective-permute-done | bytes 360480 | tf_op jit(solution)/shard_map/ppermute | solution.py:95
  25.0 1.0 collective-permute-done.3.refs_2_
  26.0 3.0 %collective-permute-start.13 = (bf16[88,1232]{1,0:T(8,128)(2,1)}, bf16[88,1232]{1,0:T(8,128)(2,1)S(1)}, u32[]{:S(2)}, u32[]{:S(2)}) collective-permute-start(bf16[88,1232]{1,0:T(8,128)(2,1)} %get-tuple-element.46), channel_id=1, source_target_pairs={{0,1},{1,0},{2,3},{3,2},{4,5},{5,4},{6,7},{7,6},{8,9},{9,8},{10,11... | collective-permute-start | bytes 650504 | tf_op jit(solution)/shard_map/ppermute | solution.py:95
  29.0 0.9 collective-permute-start.14
  29.9 0.4 collective-permute-start.9
  30.4 1.3 %collective-permute-start.8 = (bf16[352,352]{1,0:T(8,128)(2,1)}, bf16[352,352]{1,0:T(8,128)(2,1)}, u32[]{:S(2)}, u32[]{:S(2)}) collective-permute-start(bf16[352,352]{1,0:T(8,128)(2,1)} %collective-permute-done.7.refs_6_), channel_id=1, source_target_pairs={{0,4},{1,5},{2,6},{3,7},{4,8},{5,9},{6,10},{7,11},{8,12},{9,13},{1... | collective-permute-start | bytes 743432 | tf_op jit(solution)/shard_map/ppermute | solution.py:95
  31.7 6.0 %collective-permute-start = (s32[4]{0:T(128)S(1)}, s32[4]{0:T(128)S(1)}, u32[]{:S(2)}, u32[]{:S(2)}) collective-permute-start(s32[4]{0:T(128)S(1)} %copy-done.20), channel_id=1, source_target_pairs={{0,0},{1,16},{2,2},{3,18},{4,4},{5,20},{6,6},{7,22},{8,8},{9,24},{... | collective-permute-start | bytes 56 | tf_op jit(solution)/shard_map/ppermute | solution.py:95
  37.7 1.6 %collective-permute-done = s32[4]{0:T(128)S(1)} collective-permute-done((s32[4]{0:T(128)S(1)}, s32[4]{0:T(128)S(1)}, u32[]{:S(2)}, u32[]{:S(2)}) %collective-permute-start) | collective-permute-done | bytes 48 | tf_op jit(solution)/shard_map/ppermute | solution.py:95
  39.3 0.6 dynamic_slice.3
  40.6 0.6 copy-done.6
  41.2 0.9 copy-done.5
  42.1 0.9 copy-done.7
  43.0 0.9 shard_map.77.refs_6_
  44.1 3.4 %collective-permute-start.15 = (bf16[352,704]{1,0:T(8,128)(2,1)S(1)}, bf16[352,704]{1,0:T(8,128)(2,1)}, u32[]{:S(2)}, u32[]{:S(2)}) collective-permute-start(bf16[352,704]{1,0:T(8,128)(2,1)S(1)} %shard_map.77.refs_6_), channel_id=1, source_target_pairs={{0,4},{1,5},{2,6},{3,7},{4,0},{5,1},{6,2},{7,3},{8,12},{9,13},{10,... | collective-permute-start | bytes 1486856 | tf_op jit(solution)/shard_map/ppermute | solution.py:95
  47.7 0.5 collective-permute-start.11
  48.3 0.4 fusion.3
  48.7 0.8 collective-permute-done.10.refs_9_
  49.4 0.4 collective-permute-done.11.refs_10_
  49.8 0.4 collective-permute-done.12.refs_11_
  50.2 0.3 copy-done.15
  50.5 0.7 copy-done.16
  51.3 3.7 %shard_map.76 = (bf16[4,16,352]{2,1,0:T(8,128)(2,1)S(1)}, bf16[4,16,352]{2,1,0:T(8,128)(2,1)S(1)}, bf16[4,16,352]{2,1,0:T(8,128)(2,1)S(1)}, bf16[4,16,352]{2,1,0:T(8,128)(2,1)S(1)}) custom-call(s32[4]{0:T(128)S(1)} %pad_add_fusion.where, bf16[2,4,16,1408]{3,2,1,0:T(8,128)(2,1)} %copy-done.10, bf16[2,4,16,1408]{3,2,1,0:T(8,128)(2,1)} %copy-done.9, ...), custom_call_target="tpu_custom_call" | custom-call | flops 507510784 | bytes 6848512 | tf_op jit(solution)/shard_map/pallas_call | solution.py:105
  55.0 10.2 %collective-permute-done.15.refs_7_ = bf16[352,704]{1,0:T(8,128)(2,1)} collective-permute-done((bf16[352,704]{1,0:T(8,128)(2,1)S(1)}, bf16[352,704]{1,0:T(8,128)(2,1)}, u32[]{:S(2)}, u32[]{:S(2)}) %collective-permute-start.15) | collective-permute-done | bytes 495648 | tf_op jit(solution)/shard_map/ppermute | solution.py:95
  65.2 1.1 collective-permute-start.16
  66.3 2.2 %collective-permute-start.18 = (bf16[4,16,352]{2,1,0:T(8,128)(2,1)S(1)}, bf16[4,16,352]{2,1,0:T(8,128)(2,1)S(1)}, u32[]{:S(2)}, u32[]{:S(2)}) collective-permute-start(bf16[4,16,352]{2,1,0:T(8,128)(2,1)S(1)} %get-tuple-element.55), channel_id=1, source_target_pairs={{0,12},{1,13},{2,14},{3,15},{4,0},{5,1},{6,2},{7,3},{8,4},{9,5},{1... | collective-permute-start | bytes 135176 | tf_op jit(solution)/shard_map/ppermute | solution.py:95
  68.6 1.4 %collective-permute-done.16.refs_1_ = bf16[4,16,352]{2,1,0:T(8,128)(2,1)S(1)} collective-permute-done((bf16[4,16,352]{2,1,0:T(8,128)(2,1)S(1)}, bf16[4,16,352]{2,1,0:T(8,128)(2,1)S(1)}, u32[]{:S(2)}, u32[]{:S(2)}) %collective-permute-start.16) | collective-permute-done | bytes 45088 | tf_op jit(solution)/shard_map/ppermute | solution.py:95
  70.0 1.0 collective-permute-done.17.refs_2_
  71.0 0.8 shard_map.78.refs_0_
  71.9 0.9 collective-permute-start.23
  72.7 2.5 %collective-permute-start.20 = (bf16[4,4,16,352]{3,2,1,0:T(8,128)(2,1)S(1)}, bf16[4,4,16,352]{3,2,1,0:T(8,128)(2,1)S(1)}, u32[]{:S(2)}, u32[]{:S(2)}) collective-permute-start(bf16[4,4,16,352]{3,2,1,0:T(8,128)(2,1)S(1)} %shard_map.78.refs_0_), channel_id=1, source_target_pairs={{0,2},{1,3},{2,0},{3,1},{4,6},{5,7},{6,4},{7,5},{8,10},{9,11},{10,... | collective-permute-start | bytes 540680 | tf_op jit(solution)/shard_map/ppermute | solution.py:95
  75.2 1.2 collective-permute-start.19
  76.4 2.5 %collective-permute-done.21.refs_3_ = bf16[4,4,16,352]{3,2,1,0:T(8,128)(2,1)S(1)} collective-permute-done((bf16[4,4,16,352]{3,2,1,0:T(8,128)(2,1)S(1)}, bf16[4,4,16,352]{3,2,1,0:T(8,128)(2,1)S(1)}, u32[]{:S(2)}, u32[]{:S(2)}) %collective-permute-start.21) | collective-permute-done | bytes 180256 | tf_op jit(solution)/shard_map/ppermute | solution.py:95
  78.9 4.8 %collective-permute-done.20.refs_2_ = bf16[4,4,16,352]{3,2,1,0:T(8,128)(2,1)S(1)} collective-permute-done((bf16[4,4,16,352]{3,2,1,0:T(8,128)(2,1)S(1)}, bf16[4,4,16,352]{3,2,1,0:T(8,128)(2,1)S(1)}, u32[]{:S(2)}, u32[]{:S(2)}) %collective-permute-start.20) | collective-permute-done | bytes 180256 | tf_op jit(solution)/shard_map/ppermute | solution.py:95
  83.7 0.7 collective-permute-done.19.refs_1_
  84.4 2.1 %collective-permute-start.24 = (bf16[352,704]{1,0:T(8,128)(2,1)S(1)}, bf16[352,704]{1,0:T(8,128)(2,1)}, u32[]{:S(2)}, u32[]{:S(2)}) collective-permute-start(bf16[352,704]{1,0:T(8,128)(2,1)S(1)} %shard_map.77.refs_6_), channel_id=1, source_target_pairs={{0,1},{1,0},{2,3},{3,2},{4,5},{5,4},{6,7},{7,6},{8,9},{9,8},{10,11... | collective-permute-start | bytes 1486856 | tf_op jit(solution)/shard_map/ppermute | solution.py:95
  86.6 0.4 collective-permute-start.26
  87.3 0.7 reshape.44.refs_5_
  88.0 0.7 reshape.43.refs_4_
  88.6 1.3 collective-permute-done.25.refs_11_
  89.9 0.8 collective-permute-done.26.refs_12_
  90.8 11.8 %shard_map.79 = (bf16[2,64,704]{2,1,0:T(8,128)(2,1)S(1)}, bf16[2,64,704]{2,1,0:T(8,128)(2,1)S(1)}, bf16[2,64,704]{2,1,0:T(8,128)(2,1)S(1)}, bf16[2,64,704]{2,1,0:T(8,128)(2,1)S(1)}, bf16[4,64,352]{2,1,0:T(8,128)(2,1)S(1)}) custom-call(s32[4]{0:T(128)S(1)} %pad_add_fusion.where, bf16[4,4,16,352]{3,2,1,0:T(8,128)(2,1)} %copy-done.3, ...), custom_call_target="tpu_custom_call" | custom-call | flops 1268776960 | bytes 9394176 | tf_op jit(solution)/shard_map/pallas_call | solution.py:105
  102.7 0.8 collective-permute-start.29
  103.5 1.8 %collective-permute-start.30 = (bf16[2,64,704]{2,1,0:T(8,128)(2,1)S(1)}, bf16[2,64,704]{2,1,0:T(8,128)(2,1)S(1)}, u32[]{:S(2)}, u32[]{:S(2)}) collective-permute-start(bf16[2,64,704]{2,1,0:T(8,128)(2,1)S(1)} %get-tuple-element.64), channel_id=1, source_target_pairs={{0,18},{1,19},{2,16},{3,17},{4,22},{5,23},{6,20},{7,21},{8,26},{9,... | collective-permute-start | bytes 540680 | tf_op jit(solution)/shard_map/ppermute | solution.py:95
  105.3 3.5 %collective-permute-done.28.refs_1_ = bf16[2,64,704]{2,1,0:T(8,128)(2,1)S(1)} collective-permute-done((bf16[2,64,704]{2,1,0:T(8,128)(2,1)S(1)}, bf16[2,64,704]{2,1,0:T(8,128)(2,1)S(1)}, u32[]{:S(2)}, u32[]{:S(2)}) %collective-permute-start.28) | collective-permute-done | bytes 180256 | tf_op jit(solution)/shard_map/ppermute | solution.py:95
  108.8 4.2 %collective-permute-done.30.refs_3_ = bf16[2,64,704]{2,1,0:T(8,128)(2,1)S(1)} collective-permute-done((bf16[2,64,704]{2,1,0:T(8,128)(2,1)S(1)}, bf16[2,64,704]{2,1,0:T(8,128)(2,1)S(1)}, u32[]{:S(2)}, u32[]{:S(2)}) %collective-permute-start.30) | collective-permute-done | bytes 180256 | tf_op jit(solution)/shard_map/ppermute | solution.py:95
  113.0 0.7 shard_map.80
  113.7 4.4 %collective-permute-start.31 = (bf16[16,1408]{1,0:T(8,128)(2,1)S(1)}, bf16[16,1408]{1,0:T(8,128)(2,1)S(1)}, u32[]{:S(2)}, u32[]{:S(2)}) collective-permute-start(bf16[16,1408]{1,0:T(8,128)(2,1)S(1)} %get-tuple-element.65), channel_id=1, source_target_pairs={{0,0},{1,16},{2,2},{3,18},{4,4},{5,20},{6,6},{7,22},{8,8},{9,24},{... | collective-permute-start | bytes 135176 | tf_op jit(solution)/shard_map/ppermute | solution.py:95
  118.2 1.8 %collective-permute-start.32 = (bf16[16,1408]{1,0:T(8,128)(2,1)S(1)}, bf16[16,1408]{1,0:T(8,128)(2,1)S(1)}, u32[]{:S(2)}, u32[]{:S(2)}) collective-permute-start(bf16[16,1408]{1,0:T(8,128)(2,1)S(1)} %get-tuple-element.66), channel_id=1, source_target_pairs={{0,12},{1,28},{2,14},{3,30},{4,0},{5,16},{6,2},{7,18},{8,4},{9,20}... | collective-permute-start | bytes 135176 | tf_op jit(solution)/shard_map/ppermute | solution.py:95
  120.0 1.8 %collective-permute-start.33 = (bf16[16,1408]{1,0:T(8,128)(2,1)S(1)}, bf16[16,1408]{1,0:T(8,128)(2,1)S(1)}, u32[]{:S(2)}, u32[]{:S(2)}) collective-permute-start(bf16[16,1408]{1,0:T(8,128)(2,1)S(1)} %get-tuple-element.67), channel_id=1, source_target_pairs={{0,8},{1,24},{2,10},{3,26},{4,12},{5,28},{6,14},{7,30},{8,0},{9,16... | collective-permute-start | bytes 135176 | tf_op jit(solution)/shard_map/ppermute | solution.py:95
  121.8 1.2 collective-permute-start.34
  123.0 0.3 collective-permute-done.32.refs_1_
  123.3 2.4 %collective-permute-done.33.refs_2_ = bf16[16,1408]{1,0:T(8,128)(2,1)S(1)} collective-permute-done((bf16[16,1408]{1,0:T(8,128)(2,1)S(1)}, bf16[16,1408]{1,0:T(8,128)(2,1)S(1)}, u32[]{:S(2)}, u32[]{:S(2)}) %collective-permute-start.33) | collective-permute-done | bytes 45088 | tf_op jit(solution)/shard_map/ppermute | solution.py:95
  125.6 2.3 %collective-permute-done.34.refs_3_ = bf16[16,1408]{1,0:T(8,128)(2,1)S(1)} collective-permute-done((bf16[16,1408]{1,0:T(8,128)(2,1)S(1)}, bf16[16,1408]{1,0:T(8,128)(2,1)S(1)}, u32[]{:S(2)}, u32[]{:S(2)}) %collective-permute-start.34) | collective-permute-done | bytes 45088 | tf_op jit(solution)/shard_map/ppermute | solution.py:95
  128.0 1.2 shard_map.81
  (66 shorter events, 1.2 us)
Async XLA Ops:
  0.0 48.3 %copy-start = (bf16[256,4224]{1,0:T(8,128)(2,1)S(1)}, bf16[256,4224]{1,0:T(8,128)(2,1)}, u32[]{:S(2)}) copy-start(bf16[256,4224]{1,0:T(8,128)(2,1)} %param.11) | copy-start | bytes 6488068
  0.0 31.7 %copy-start.20 = (s32[4]{0:T(128)S(1)}, s32[4]{0:T(128)}, u32[]{:S(2)}) copy-start(s32[4]{0:T(128)} %param.9) | copy-start | bytes 52
  3.6 25.3 %copy-start.4 = (bf16[88,704]{1,0:T(8,128)(2,1)}, bf16[88,704]{1,0:T(8,128)(2,1)S(1)}, u32[]{:S(2)}) copy-start(bf16[88,704]{1,0:T(8,128)(2,1)S(1)} %get-tuple-element.49.refs_4_) | copy-start | bytes 371716
  3.6 7.9 %collective-permute-start.5 = (bf16[88,1232]{1,0:T(8,128)(2,1)S(1)}, bf16[88,1232]{1,0:T(8,128)(2,1)S(1)}, u32[]{:S(2)}, u32[]{:S(2)}) collective-permute-start(bf16[88,1232]{1,0:T(8,128)(2,1)S(1)} %get-tuple-element.39), channel_id=1, source_target_pairs={{0,2},{1,3},{2,0},{3,1},{4,6},{5,7},{6,4},{7,5},{8,10},{9,11},{10,... | collective-permute-start | bytes 650504 | tf_op jit(solution)/shard_map/ppermute | solution.py:95
  7.4 7.1 %collective-permute-start.2 = (bf16[2,4,16,1408]{3,2,1,0:T(8,128)(2,1)S(1)}, bf16[2,4,16,1408]{3,2,1,0:T(8,128)(2,1)S(1)}, u32[]{:S(2)}, u32[]{:S(2)}) collective-permute-start(bf16[2,4,16,1408]{3,2,1,0:T(8,128)(2,1)S(1)} %shard_map.73), channel_id=1, source_target_pairs={{0,16},{1,0},{2,18},{3,2},{4,20},{5,4},{6,22},{7,6},{8,24},{9,8},{... | collective-permute-start | bytes 1081352 | tf_op jit(solution)/shard_map/ppermute | solution.py:95
  8.3 13.0 %collective-permute-start.1 = (bf16[2,4,16,1408]{3,2,1,0:T(8,128)(2,1)S(1)}, bf16[2,4,16,1408]{3,2,1,0:T(8,128)(2,1)S(1)}, u32[]{:S(2)}, u32[]{:S(2)}) collective-permute-start(bf16[2,4,16,1408]{3,2,1,0:T(8,128)(2,1)S(1)} %shard_map.73), channel_id=1, source_target_pairs={{0,0},{1,16},{2,2},{3,18},{4,4},{5,20},{6,6},{7,22},{8,8},{9,24},{... | collective-permute-start | bytes 1081352 | tf_op jit(solution)/shard_map/ppermute | solution.py:95
  11.3 13.7 %collective-permute-start.4 = (bf16[2,4,16,1408]{3,2,1,0:T(8,128)(2,1)S(1)}, bf16[2,4,16,1408]{3,2,1,0:T(8,128)(2,1)S(1)}, u32[]{:S(2)}, u32[]{:S(2)}) collective-permute-start(bf16[2,4,16,1408]{3,2,1,0:T(8,128)(2,1)S(1)} %shard_map.73), channel_id=1, source_target_pairs={{0,18},{1,2},{2,16},{3,0},{4,22},{5,6},{6,20},{7,4},{8,26},{9,10},... | collective-permute-start | bytes 1081352 | tf_op jit(solution)/shard_map/ppermute | solution.py:95
  11.4 14.6 %collective-permute-start.3 = (bf16[2,4,16,1408]{3,2,1,0:T(8,128)(2,1)S(1)}, bf16[2,4,16,1408]{3,2,1,0:T(8,128)(2,1)S(1)}, u32[]{:S(2)}, u32[]{:S(2)}) collective-permute-start(bf16[2,4,16,1408]{3,2,1,0:T(8,128)(2,1)S(1)} %shard_map.73), channel_id=1, source_target_pairs={{0,2},{1,18},{2,0},{3,16},{4,6},{5,22},{6,4},{7,20},{8,10},{9,26},... | collective-permute-start | bytes 1081352 | tf_op jit(solution)/shard_map/ppermute | solution.py:95
  12.3 37.9 %copy-start.2 = (bf16[352,352]{1,0:T(8,128)(2,1)}, bf16[352,352]{1,0:T(8,128)(2,1)S(1)}, u32[]{:S(2)}) copy-start(bf16[352,352]{1,0:T(8,128)(2,1)S(1)} %shard_map.75.refs_4_) | copy-start | bytes 743428
  12.3 9.0 %collective-permute-start.6 = (bf16[352,352]{1,0:T(8,128)(2,1)S(1)}, bf16[352,352]{1,0:T(8,128)(2,1)S(1)}, u32[]{:S(2)}, u32[]{:S(2)}) collective-permute-start(bf16[352,352]{1,0:T(8,128)(2,1)S(1)} %shard_map.75.refs_4_), channel_id=1, source_target_pairs={{0,4},{1,5},{2,6},{3,7},{4,8},{5,9},{6,10},{7,11},{8,12},{9,13},{1... | collective-permute-start | bytes 743432 | tf_op jit(solution)/shard_map/ppermute | solution.py:95
  14.5 15.4 %copy-start.9 = (bf16[2,4,16,1408]{3,2,1,0:T(8,128)(2,1)}, bf16[2,4,16,1408]{3,2,1,0:T(8,128)(2,1)S(1)}, u32[]{:S(2)}) copy-start(bf16[2,4,16,1408]{3,2,1,0:T(8,128)(2,1)S(1)} %collective-permute-done.2.refs_1_) | copy-start | bytes 1081348
  21.3 9.1 %copy-start.10 = (bf16[2,4,16,1408]{3,2,1,0:T(8,128)(2,1)}, bf16[2,4,16,1408]{3,2,1,0:T(8,128)(2,1)S(1)}, u32[]{:S(2)}) copy-start(bf16[2,4,16,1408]{3,2,1,0:T(8,128)(2,1)S(1)} %collective-permute-done.1.refs_0_) | copy-start | bytes 1081348
  21.3 10.4 %copy-start.13 = (bf16[352,352]{1,0:T(8,128)(2,1)}, bf16[352,352]{1,0:T(8,128)(2,1)S(1)}, u32[]{:S(2)}) copy-start(bf16[352,352]{1,0:T(8,128)(2,1)S(1)} %collective-permute-done.6.refs_5_) | copy-start | bytes 743428
  21.3 9.1 %collective-permute-start.7 = (bf16[352,352]{1,0:T(8,128)(2,1)S(1)}, bf16[352,352]{1,0:T(8,128)(2,1)}, u32[]{:S(2)}, u32[]{:S(2)}) collective-permute-start(bf16[352,352]{1,0:T(8,128)(2,1)S(1)} %collective-permute-done.6.refs_5_), channel_id=1, source_target_pairs={{0,4},{1,5},{2,6},{3,7},{4,8},{5,9},{6,10},{7,11},{8,12},{9,13},{1... | collective-permute-start | bytes 743432 | tf_op jit(solution)/shard_map/ppermute | solution.py:95
  25.0 5.3 %copy-start.11 = (bf16[2,4,16,1408]{3,2,1,0:T(8,128)(2,1)}, bf16[2,4,16,1408]{3,2,1,0:T(8,128)(2,1)S(1)}, u32[]{:S(2)}) copy-start(bf16[2,4,16,1408]{3,2,1,0:T(8,128)(2,1)S(1)} %collective-permute-done.4.refs_3_) | copy-start | bytes 1081348
  26.0 5.7 %copy-start.12 = (bf16[2,4,16,1408]{3,2,1,0:T(8,128)(2,1)}, bf16[2,4,16,1408]{3,2,1,0:T(8,128)(2,1)S(1)}, u32[]{:S(2)}) copy-start(bf16[2,4,16,1408]{3,2,1,0:T(8,128)(2,1)S(1)} %collective-permute-done.3.refs_2_) | copy-start | bytes 1081348
  26.0 15.2 %collective-permute-start.13 = (bf16[88,1232]{1,0:T(8,128)(2,1)}, bf16[88,1232]{1,0:T(8,128)(2,1)S(1)}, u32[]{:S(2)}, u32[]{:S(2)}) collective-permute-start(bf16[88,1232]{1,0:T(8,128)(2,1)} %get-tuple-element.46), channel_id=1, source_target_pairs={{0,1},{1,0},{2,3},{3,2},{4,5},{5,4},{6,7},{7,6},{8,9},{9,8},{10,11... | collective-permute-start | bytes 650504 | tf_op jit(solution)/shard_map/ppermute | solution.py:95
  29.0 11.6 %collective-permute-start.14 = (bf16[88,528]{1,0:T(8,128)(2,1)S(1)}, bf16[88,528]{1,0:T(8,128)(2,1)S(1)}, u32[]{:S(2)}, u32[]{:S(2)}) collective-permute-start(bf16[88,528]{1,0:T(8,128)(2,1)S(1)} %get-tuple-element.48), channel_id=1, source_target_pairs={{0,3},{1,2},{2,1},{3,0},{4,7},{5,6},{6,5},{7,4},{8,11},{9,10},{10,... | collective-permute-start | bytes 278792 | tf_op jit(solution)/shard_map/ppermute | solution.py:95
  29.9 17.8 %collective-permute-start.9 = (bf16[352,352]{1,0:T(8,128)(2,1)S(1)}, bf16[352,352]{1,0:T(8,128)(2,1)}, u32[]{:S(2)}, u32[]{:S(2)}) collective-permute-start(bf16[352,352]{1,0:T(8,128)(2,1)S(1)} %shard_map.75.refs_4_), channel_id=1, source_target_pairs={{0,1},{1,0},{2,3},{3,2},{4,5},{5,4},{6,7},{7,6},{8,9},{9,8},{10,11... | collective-permute-start | bytes 743432 | tf_op jit(solution)/shard_map/ppermute | solution.py:95
  30.4 17.8 %collective-permute-start.8 = (bf16[352,352]{1,0:T(8,128)(2,1)}, bf16[352,352]{1,0:T(8,128)(2,1)}, u32[]{:S(2)}, u32[]{:S(2)}) collective-permute-start(bf16[352,352]{1,0:T(8,128)(2,1)} %collective-permute-done.7.refs_6_), channel_id=1, source_target_pairs={{0,4},{1,5},{2,6},{3,7},{4,8},{5,9},{6,10},{7,11},{8,12},{9,13},{1... | collective-permute-start | bytes 743432 | tf_op jit(solution)/shard_map/ppermute | solution.py:95
  31.7 7.6 %collective-permute-start = (s32[4]{0:T(128)S(1)}, s32[4]{0:T(128)S(1)}, u32[]{:S(2)}, u32[]{:S(2)}) collective-permute-start(s32[4]{0:T(128)S(1)} %copy-done.20), channel_id=1, source_target_pairs={{0,0},{1,16},{2,2},{3,18},{4,4},{5,20},{6,6},{7,22},{8,8},{9,24},{... | collective-permute-start | bytes 56 | tf_op jit(solution)/shard_map/ppermute | solution.py:95
  40.5 0.6 copy-start.6
  41.2 0.9 copy-start.5
  42.1 0.9 copy-start.7
  43.9 40.5 %copy-start.1 = (bf16[352,704]{1,0:T(8,128)(2,1)}, bf16[352,704]{1,0:T(8,128)(2,1)S(1)}, u32[]{:S(2)}) copy-start(bf16[352,704]{1,0:T(8,128)(2,1)S(1)} %shard_map.77.refs_6_) | copy-start | bytes 1486852
  43.9 27.9 %collective-permute-start.22 = (bf16[352,704]{1,0:T(8,128)(2,1)S(1)}, bf16[352,704]{1,0:T(8,128)(2,1)}, u32[]{:S(2)}, u32[]{:S(2)}) collective-permute-start(bf16[352,704]{1,0:T(8,128)(2,1)S(1)} %shard_map.77.refs_6_), channel_id=1, source_target_pairs={{0,8},{1,9},{2,10},{3,11},{4,12},{5,13},{6,14},{7,15},{8,0},{9,1},... | collective-permute-start | bytes 1486856 | tf_op jit(solution)/shard_map/ppermute | solution.py:95
  44.1 21.1 %collective-permute-start.15 = (bf16[352,704]{1,0:T(8,128)(2,1)S(1)}, bf16[352,704]{1,0:T(8,128)(2,1)}, u32[]{:S(2)}, u32[]{:S(2)}) collective-permute-start(bf16[352,704]{1,0:T(8,128)(2,1)S(1)} %shard_map.77.refs_6_), channel_id=1, source_target_pairs={{0,4},{1,5},{2,6},{3,7},{4,0},{5,1},{6,2},{7,3},{8,12},{9,13},{10,... | collective-permute-start | bytes 1486856 | tf_op jit(solution)/shard_map/ppermute | solution.py:95
  47.6 1.8 %collective-permute-start.10 = (bf16[352,352]{1,0:T(8,128)(2,1)}, bf16[352,352]{1,0:T(8,128)(2,1)S(1)}, u32[]{:S(2)}, u32[]{:S(2)}) collective-permute-start(bf16[352,352]{1,0:T(8,128)(2,1)} %copy-done.13), channel_id=1, source_target_pairs={{0,1},{1,0},{2,3},{3,2},{4,5},{5,4},{6,7},{7,6},{8,9},{9,8},{10,11... | collective-permute-start | bytes 743432 | tf_op jit(solution)/shard_map/ppermute | solution.py:95
  47.7 2.1 %collective-permute-start.11 = (bf16[352,352]{1,0:T(8,128)(2,1)}, bf16[352,352]{1,0:T(8,128)(2,1)S(1)}, u32[]{:S(2)}, u32[]{:S(2)}) collective-permute-start(bf16[352,352]{1,0:T(8,128)(2,1)} %collective-permute-done.7.refs_6_), channel_id=1, source_target_pairs={{0,1},{1,0},{2,3},{3,2},{4,5},{5,4},{6,7},{7,6},{8,9},{9,8},{10,11... | collective-permute-start | bytes 743432 | tf_op jit(solution)/shard_map/ppermute | solution.py:95
  48.2 2.0 %collective-permute-start.12 = (bf16[352,352]{1,0:T(8,128)(2,1)}, bf16[352,352]{1,0:T(8,128)(2,1)S(1)}, u32[]{:S(2)}, u32[]{:S(2)}) collective-permute-start(bf16[352,352]{1,0:T(8,128)(2,1)} %collective-permute-done.8.refs_7_), channel_id=1, source_target_pairs={{0,1},{1,0},{2,3},{3,2},{4,5},{5,4},{6,7},{7,6},{8,9},{9,8},{10,11... | collective-permute-start | bytes 743432 | tf_op jit(solution)/shard_map/ppermute | solution.py:95
  49.4 0.8 copy-start.14
  49.8 0.7 copy-start.15
  50.5 0.7 copy-start.16
  65.2 4.8 %collective-permute-start.16 = (bf16[4,16,352]{2,1,0:T(8,128)(2,1)S(1)}, bf16[4,16,352]{2,1,0:T(8,128)(2,1)S(1)}, u32[]{:S(2)}, u32[]{:S(2)}) collective-permute-start(bf16[4,16,352]{2,1,0:T(8,128)(2,1)S(1)} %get-tuple-element.51), channel_id=1, source_target_pairs={{0,4},{1,5},{2,6},{3,7},{4,8},{5,9},{6,10},{7,11},{8,12},{9,13},{1... | collective-permute-start | bytes 135176 | tf_op jit(solution)/shard_map/ppermute | solution.py:95
  66.3 4.7 %collective-permute-start.17 = (bf16[4,16,352]{2,1,0:T(8,128)(2,1)S(1)}, bf16[4,16,352]{2,1,0:T(8,128)(2,1)S(1)}, u32[]{:S(2)}, u32[]{:S(2)}) collective-permute-start(bf16[4,16,352]{2,1,0:T(8,128)(2,1)S(1)} %get-tuple-element.53), channel_id=1, source_target_pairs={{0,8},{1,9},{2,10},{3,11},{4,12},{5,13},{6,14},{7,15},{8,0},{9,1},... | collective-permute-start | bytes 135176 | tf_op jit(solution)/shard_map/ppermute | solution.py:95
  66.3 4.7 %collective-permute-start.18 = (bf16[4,16,352]{2,1,0:T(8,128)(2,1)S(1)}, bf16[4,16,352]{2,1,0:T(8,128)(2,1)S(1)}, u32[]{:S(2)}, u32[]{:S(2)}) collective-permute-start(bf16[4,16,352]{2,1,0:T(8,128)(2,1)S(1)} %get-tuple-element.55), channel_id=1, source_target_pairs={{0,12},{1,13},{2,14},{3,15},{4,0},{5,1},{6,2},{7,3},{8,4},{9,5},{1... | collective-permute-start | bytes 135176 | tf_op jit(solution)/shard_map/ppermute | solution.py:95
  71.8 18.9 %copy-start.3 = (bf16[4,4,16,352]{3,2,1,0:T(8,128)(2,1)}, bf16[4,4,16,352]{3,2,1,0:T(8,128)(2,1)S(1)}, u32[]{:S(2)}) copy-start(bf16[4,4,16,352]{3,2,1,0:T(8,128)(2,1)S(1)} %shard_map.78.refs_0_) | copy-start | bytes 540676
  71.9 15.2 %collective-permute-start.23 = (bf16[352,704]{1,0:T(8,128)(2,1)}, bf16[352,704]{1,0:T(8,128)(2,1)S(1)}, u32[]{:S(2)}, u32[]{:S(2)}) collective-permute-start(bf16[352,704]{1,0:T(8,128)(2,1)} %collective-permute-done.22.refs_8_), channel_id=1, source_target_pairs={{0,4},{1,5},{2,6},{3,7},{4,0},{5,1},{6,2},{7,3},{8,12},{9,13},{10,... | collective-permute-start | bytes 1486856 | tf_op jit(solution)/shard_map/ppermute | solution.py:95
  72.7 6.2 %collective-permute-start.21 = (bf16[4,4,16,352]{3,2,1,0:T(8,128)(2,1)S(1)}, bf16[4,4,16,352]{3,2,1,0:T(8,128)(2,1)S(1)}, u32[]{:S(2)}, u32[]{:S(2)}) collective-permute-start(bf16[4,4,16,352]{3,2,1,0:T(8,128)(2,1)S(1)} %shard_map.78.refs_0_), channel_id=1, source_target_pairs={{0,18},{1,19},{2,16},{3,17},{4,22},{5,23},{6,20},{7,21},{8,26},{9,... | collective-permute-start | bytes 540680 | tf_op jit(solution)/shard_map/ppermute | solution.py:95
  72.7 11.0 %collective-permute-start.20 = (bf16[4,4,16,352]{3,2,1,0:T(8,128)(2,1)S(1)}, bf16[4,4,16,352]{3,2,1,0:T(8,128)(2,1)S(1)}, u32[]{:S(2)}, u32[]{:S(2)}) collective-permute-start(bf16[4,4,16,352]{3,2,1,0:T(8,128)(2,1)S(1)} %shard_map.78.refs_0_), channel_id=1, source_target_pairs={{0,2},{1,3},{2,0},{3,1},{4,6},{5,7},{6,4},{7,5},{8,10},{9,11},{10,... | collective-permute-start | bytes 540680 | tf_op jit(solution)/shard_map/ppermute | solution.py:95
  75.2 9.2 %collective-permute-start.19 = (bf16[4,4,16,352]{3,2,1,0:T(8,128)(2,1)S(1)}, bf16[4,4,16,352]{3,2,1,0:T(8,128)(2,1)S(1)}, u32[]{:S(2)}, u32[]{:S(2)}) collective-permute-start(bf16[4,4,16,352]{3,2,1,0:T(8,128)(2,1)S(1)} %shard_map.78.refs_0_), channel_id=1, source_target_pairs={{0,16},{1,17},{2,18},{3,19},{4,20},{5,21},{6,22},{7,23},{8,24},{9,... | collective-permute-start | bytes 540680 | tf_op jit(solution)/shard_map/ppermute | solution.py:95
  78.9 8.2 %copy-start.17 = (bf16[4,4,16,352]{3,2,1,0:T(8,128)(2,1)}, bf16[4,4,16,352]{3,2,1,0:T(8,128)(2,1)S(1)}, u32[]{:S(2)}) copy-start(bf16[4,4,16,352]{3,2,1,0:T(8,128)(2,1)S(1)} %collective-permute-done.21.refs_3_) | copy-start | bytes 540676
  83.7 3.4 %copy-start.18 = (bf16[4,4,16,352]{3,2,1,0:T(8,128)(2,1)}, bf16[4,4,16,352]{3,2,1,0:T(8,128)(2,1)S(1)}, u32[]{:S(2)}) copy-start(bf16[4,4,16,352]{3,2,1,0:T(8,128)(2,1)S(1)} %collective-permute-done.20.refs_2_) | copy-start | bytes 540676
  84.4 2.6 %copy-start.19 = (bf16[4,4,16,352]{3,2,1,0:T(8,128)(2,1)}, bf16[4,4,16,352]{3,2,1,0:T(8,128)(2,1)S(1)}, u32[]{:S(2)}) copy-start(bf16[4,4,16,352]{3,2,1,0:T(8,128)(2,1)S(1)} %collective-permute-done.19.refs_1_) | copy-start | bytes 540676
  84.4 4.2 %collective-permute-start.24 = (bf16[352,704]{1,0:T(8,128)(2,1)S(1)}, bf16[352,704]{1,0:T(8,128)(2,1)}, u32[]{:S(2)}, u32[]{:S(2)}) collective-permute-start(bf16[352,704]{1,0:T(8,128)(2,1)S(1)} %shard_map.77.refs_6_), channel_id=1, source_target_pairs={{0,1},{1,0},{2,3},{3,2},{4,5},{5,4},{6,7},{7,6},{8,9},{9,8},{10,11... | collective-permute-start | bytes 1486856 | tf_op jit(solution)/shard_map/ppermute | solution.py:95
  86.5 3.4 %collective-permute-start.25 = (bf16[352,704]{1,0:T(8,128)(2,1)}, bf16[352,704]{1,0:T(8,128)(2,1)}, u32[]{:S(2)}, u32[]{:S(2)}) collective-permute-start(bf16[352,704]{1,0:T(8,128)(2,1)} %collective-permute-done.15.refs_7_), channel_id=1, source_target_pairs={{0,1},{1,0},{2,3},{3,2},{4,5},{5,4},{6,7},{7,6},{8,9},{9,8},{10,11... | collective-permute-start | bytes 1486856 | tf_op jit(solution)/shard_map/ppermute | solution.py:95
  86.6 4.2 %collective-permute-start.26 = (bf16[352,704]{1,0:T(8,128)(2,1)}, bf16[352,704]{1,0:T(8,128)(2,1)}, u32[]{:S(2)}, u32[]{:S(2)}) collective-permute-start(bf16[352,704]{1,0:T(8,128)(2,1)} %collective-permute-done.22.refs_8_), channel_id=1, source_target_pairs={{0,1},{1,0},{2,3},{3,2},{4,5},{5,4},{6,7},{7,6},{8,9},{9,8},{10,11... | collective-permute-start | bytes 1486856 | tf_op jit(solution)/shard_map/ppermute | solution.py:95
  87.1 3.7 %copy-start.8 = (bf16[352,704]{1,0:T(8,128)(2,1)}, bf16[352,704]{1,0:T(8,128)(2,1)S(1)}, u32[]{:S(2)}) copy-start(bf16[352,704]{1,0:T(8,128)(2,1)S(1)} %collective-permute-done.23.refs_9_) | copy-start | bytes 1486852
  87.1 3.7 %collective-permute-start.27 = (bf16[352,704]{1,0:T(8,128)(2,1)S(1)}, bf16[352,704]{1,0:T(8,128)(2,1)}, u32[]{:S(2)}, u32[]{:S(2)}) collective-permute-start(bf16[352,704]{1,0:T(8,128)(2,1)S(1)} %collective-permute-done.23.refs_9_), channel_id=1, source_target_pairs={{0,1},{1,0},{2,3},{3,2},{4,5},{5,4},{6,7},{7,6},{8,9},{9,8},{10,11... | collective-permute-start | bytes 1486856 | tf_op jit(solution)/shard_map/ppermute | solution.py:95
  102.6 6.2 %collective-permute-start.28 = (bf16[2,64,704]{2,1,0:T(8,128)(2,1)S(1)}, bf16[2,64,704]{2,1,0:T(8,128)(2,1)S(1)}, u32[]{:S(2)}, u32[]{:S(2)}) collective-permute-start(bf16[2,64,704]{2,1,0:T(8,128)(2,1)S(1)} %get-tuple-element.62), channel_id=1, source_target_pairs={{0,16},{1,17},{2,18},{3,19},{4,20},{5,21},{6,22},{7,23},{8,24},{9,... | collective-permute-start | bytes 540680 | tf_op jit(solution)/shard_map/ppermute | solution.py:95
  102.7 6.1 %collective-permute-start.29 = (bf16[2,64,704]{2,1,0:T(8,128)(2,1)S(1)}, bf16[2,64,704]{2,1,0:T(8,128)(2,1)S(1)}, u32[]{:S(2)}, u32[]{:S(2)}) collective-permute-start(bf16[2,64,704]{2,1,0:T(8,128)(2,1)S(1)} %get-tuple-element.63), channel_id=1, source_target_pairs={{0,2},{1,3},{2,0},{3,1},{4,6},{5,7},{6,4},{7,5},{8,10},{9,11},{10,... | collective-permute-start | bytes 540680 | tf_op jit(solution)/shard_map/ppermute | solution.py:95
  103.5 9.5 %collective-permute-start.30 = (bf16[2,64,704]{2,1,0:T(8,128)(2,1)S(1)}, bf16[2,64,704]{2,1,0:T(8,128)(2,1)S(1)}, u32[]{:S(2)}, u32[]{:S(2)}) collective-permute-start(bf16[2,64,704]{2,1,0:T(8,128)(2,1)S(1)} %get-tuple-element.64), channel_id=1, source_target_pairs={{0,18},{1,19},{2,16},{3,17},{4,22},{5,23},{6,20},{7,21},{8,26},{9,... | collective-permute-start | bytes 540680 | tf_op jit(solution)/shard_map/ppermute | solution.py:95
  113.7 9.2 %collective-permute-start.31 = (bf16[16,1408]{1,0:T(8,128)(2,1)S(1)}, bf16[16,1408]{1,0:T(8,128)(2,1)S(1)}, u32[]{:S(2)}, u32[]{:S(2)}) collective-permute-start(bf16[16,1408]{1,0:T(8,128)(2,1)S(1)} %get-tuple-element.65), channel_id=1, source_target_pairs={{0,0},{1,16},{2,2},{3,18},{4,4},{5,20},{6,6},{7,22},{8,8},{9,24},{... | collective-permute-start | bytes 135176 | tf_op jit(solution)/shard_map/ppermute | solution.py:95
  118.2 5.1 %collective-permute-start.32 = (bf16[16,1408]{1,0:T(8,128)(2,1)S(1)}, bf16[16,1408]{1,0:T(8,128)(2,1)S(1)}, u32[]{:S(2)}, u32[]{:S(2)}) collective-permute-start(bf16[16,1408]{1,0:T(8,128)(2,1)S(1)} %get-tuple-element.66), channel_id=1, source_target_pairs={{0,12},{1,28},{2,14},{3,30},{4,0},{5,16},{6,2},{7,18},{8,4},{9,20}... | collective-permute-start | bytes 135176 | tf_op jit(solution)/shard_map/ppermute | solution.py:95
  120.0 5.7 %collective-permute-start.33 = (bf16[16,1408]{1,0:T(8,128)(2,1)S(1)}, bf16[16,1408]{1,0:T(8,128)(2,1)S(1)}, u32[]{:S(2)}, u32[]{:S(2)}) collective-permute-start(bf16[16,1408]{1,0:T(8,128)(2,1)S(1)} %get-tuple-element.67), channel_id=1, source_target_pairs={{0,8},{1,24},{2,10},{3,26},{4,12},{5,28},{6,14},{7,30},{8,0},{9,16... | collective-permute-start | bytes 135176 | tf_op jit(solution)/shard_map/ppermute | solution.py:95
  121.8 6.2 %collective-permute-start.34 = (bf16[16,1408]{1,0:T(8,128)(2,1)S(1)}, bf16[16,1408]{1,0:T(8,128)(2,1)S(1)}, u32[]{:S(2)}, u32[]{:S(2)}) collective-permute-start(bf16[16,1408]{1,0:T(8,128)(2,1)S(1)} %get-tuple-element.68), channel_id=1, source_target_pairs={{0,4},{1,20},{2,6},{3,22},{4,8},{5,24},{6,10},{7,26},{8,12},{9,28}... | collective-permute-start | bytes 135176 | tf_op jit(solution)/shard_map/ppermute | solution.py:95

commit v7 on v6

--- a/solution.py
+++ b/solution.py
@@ -98,15 +98,18 @@
         return x * self.n + (z * self.Y + y) * self.G + c
 
 
-def call(kernel, outs, where, *arrays, scratch=(), copies=0, flops=0, fast=(), fast_in=False, still=False):
+def call(kernel, outs, where, *arrays, scratch=(), copies=0, flops=0, fast=(), fast_in=(), still=False):
     moved = sum(a.size * a.dtype.itemsize for a in arrays)
-    space = pltpu.VMEM if fast_in else pltpu.HBM
+    fast_in = range(len(arrays)) if fast_in is True else fast_in
     sems = [pltpu.SemaphoreType.DMA((copies,))] if copies else []
     return pl.pallas_call(
         kernel,
         out_shape=[jax.ShapeDtypeStruct(s, BF) for s in outs],
         in_specs=[pl.BlockSpec(memory_space=pltpu.SMEM)]
-        + [pl.BlockSpec(memory_space=space)] * len(arrays),
+        + [
+            pl.BlockSpec(memory_space=pltpu.VMEM if k in fast_in else pl.ANY)
+            for k in range(len(arrays))
+        ],
         out_specs=[
             pl.BlockSpec(memory_space=pltpu.VMEM if k in fast else pl.ANY)
             for k in range(len(outs))
@@ -114,7 +117,13 @@
         scratch_shapes=list(scratch) + sems,
         compiler_params=pltpu.CompilerParams(vmem_limit_bytes=40 * 2**20),
         cost_estimate=pl.CostEstimate(flops=flops, bytes_accessed=2 * moved, transcendentals=0),
-    )(where, *(pltpu.with_memory_space_constraint(a, pltpu.HBM) if still else a for a in arrays))
+    )(
+        where,
+        *(
+            pltpu.with_memory_space_constraint(a, pltpu.HBM) if still and k not in fast_in else a
+            for k, a in enumerate(arrays)
+        ),
+    )
 
 
 def after(value, *others):
@@ -252,27 +261,17 @@
     return d * lax.rsqrt(var + 1e-06)
 
 
-def attend_kernel(G, S, Y, where, *refs):
-    x, z, y, c = where[0], where[1], where[2], where[3]
+def norm_kernel(G, S, Y, where, *refs):
+    x, y = where[0], where[2]
     blocks = Y * G
-    merged_any, (shift, scale) = refs[:blocks], refs[blocks : blocks + 2]
-    refs = refs[blocks + 2 :]
-    w_any, refs = refs[: G * S], refs[G * S :]
-    outs, base, (merged, norm, shifts, scales, ws, att, sems) = (
-        refs[:blocks],
-        refs[blocks],
-        refs[blocks + 1 :],
-    )
+    merged_any, mods_any = refs[:blocks], refs[blocks]
+    norm, base, merged, mods, sems = refs[blocks + 1 :]
     cols = merged_any[0].shape[3]
     toks = S * merged_any[0].shape[2]
     rows = blocks * toks
     width = cols * blocks
 
-    pairs = [(shift, shifts), (scale, scales)]
-    for f in range(G):
-        for s in range(S):
-            at = pl.multiple_of((z ^ s) * cols, 16)
-            pairs.append((w_any[f * S + s], ws.at[(c + G - f) % G, pl.ds(at, cols)]))
+    pairs = [(mods_any, mods)]
     for e in range(Y):
         for d in range(G):
             b = (x + d) % G * Y + (y + e) % Y
@@ -295,41 +294,50 @@
         square = square + jnp.sum((m - mean) ** 2, axis=-1, keepdims=True)
     inv = lax.rsqrt(square * (1.0 / width) + 1e-06)
     for b in range(blocks):
-        norm[b] = ((wide[b] - mean) * inv * (1.0 + scales[b]) + shifts[b]).astype(BF)
+        norm[b] = ((wide[b] - mean) * inv * (1.0 + mods[blocks + b]) + mods[b]).astype(BF)
+
+
+def attend_kernel(G, S, Y, where, norm, *refs):
+    z, c = where[1], where[3]
+    blocks = Y * G
+    ws, refs = refs[: G * S], refs[G * S :]
+    outs, att = refs[:blocks], refs[blocks]
+    rows = norm.shape[1]
+    toks = rows // blocks
     per = S // G
     part = 3 * per * HD
     for f in range(G):
-        qkv = jnp.dot(norm[0], ws[f, :cols, :part], preferred_element_type=F32)
-        for b in range(1, blocks):
-            rows_b = slice(b * cols, (b + 1) * cols)
-            qkv = qkv + jnp.dot(norm[b], ws[f, rows_b, :part], preferred_element_type=F32)
+        qkv = jnp.dot(norm[z], ws[f * S][:, :part], preferred_element_type=F32)
+        for s in range(1, S):
+            qkv = qkv + jnp.dot(
+                norm[z ^ s], ws[f * S + s][:, :part], preferred_element_type=F32
+            )
         for t in range(per):
             q, k, v = (qkv[:, (p * per + t) * HD : (p * per + t + 1) * HD] for p in range(3))
             q = (norm88(q) * HD ** (-0.5)).astype(BF)
             k = norm88(k).astype(BF)
             v = v.astype(BF)
             scores = lax.dot_general(q, k, (((1,), (1,)), ((), ())), preferred_element_type=F32)
-            top = jnp.max(scores, axis=-1, keepdims=True)
-            probs = jnp.exp(scores - top)
-            probs = (probs / jnp.sum(probs, axis=-1, keepdims=True)).astype(BF)
-            att[f * per + t] = jnp.dot(probs, v, preferred_element_type=F32).astype(BF)
-    wide = ws.shape[2] - part
+            probs = jnp.exp(scores)
+            scaled = 1.0 / jnp.sum(probs, axis=-1, keepdims=True)
+            mixed = jnp.dot(probs.astype(BF), v, preferred_element_type=F32)
+            att[(c + G - f) % G * per + t] = (mixed * scaled).astype(BF)
     for f in range(G):
         whole = []
         for s in range(S):
             pieces = [
-                ws[f, s * cols + k * HD : s * cols + (k + 1) * HD, part:] for k in range(blocks)
+                ws[f * S + s][k * HD : (k + 1) * HD, part:] for k in range(blocks)
             ]
             whole.append(jnp.concatenate(pieces, axis=1))
-        acc = jnp.dot(att[0], whole[0], preferred_element_type=F32)
+        acc = jnp.dot(att[z], whole[0], preferred_element_type=F32)
         for s in range(1, S):
-            acc = acc + jnp.dot(att[s], whole[s], preferred_element_type=F32)
+            acc = acc + jnp.dot(att[z ^ s], whole[s], preferred_element_type=F32)
         acc = acc.astype(BF)
         for k in range(blocks):
-            outs[k][f] = acc[k * toks : (k + 1) * toks, :]
-
-
-def result_kernel(G, S, Y, where, gate, base, *refs):
+            outs[k][(c + G - f) % G] = acc[k * toks : (k + 1) * toks, :]
+
+
+def result_kernel(G, S, Y, where, mods, base, *refs):
     blocks = Y * G
     parts, outs = refs[:blocks], refs[blocks:]
     toks = base.shape[1]
@@ -342,7 +350,8 @@
         halves.append(acc)
     projected = jnp.concatenate(halves, axis=1)
     merged = jnp.concatenate([base[b] for b in range(blocks)], axis=1).astype(F32)
-    result = (merged + gate[...] * projected).astype(BF)
+    gate = jnp.concatenate([mods[2 * blocks + b] for b in range(blocks)], axis=1)
+    result = (merged + gate * projected).astype(BF)
     for s in range(S):
         outs[s][...] = result[s * local : (s + 1) * local, :]
 
@@ -431,10 +440,7 @@
 
     times = p.send(timestep, lambda x, z, y, c: (c, z, y, x))
     mod = modulation(lax.dynamic_slice(times, (p.z,), (1,)), w_mod)
-    shift = mod[:, :width].reshape(blocks, 1, cols)
-    scale = mod[:, width : 2 * width].reshape(blocks, 1, cols)
-    gate = mod[:, 2 * width :]
-    parts[0] = after(parts[0], mod)
+    mods = after(mod, p.where).reshape(3 * blocks, 1, cols)
 
     pieces = call(
         partial(merged_kernel, G, S, Y),
@@ -453,7 +459,7 @@
         fast=range(S),
     )
     pieces = [pieces[0]] + [
-        p.send(after(pieces[s], held[1]), lambda x, z, y, c, s=s: (x, z + s, y, c)) for s in range(1, S)
+        p.send(after(pieces[s], held[1], mods), lambda x, z, y, c, s=s: (x, z + s, y, c)) for s in range(1, S)
     ]
     (merged,) = call(stack_kernel, [(S, blocks, local, cols)], p.where, *pieces, copies=S)
     held.append(p.send(after(held[2], merged), lambda x, z, y, c: (x, z ^ 1, y, c)))
@@ -464,26 +470,30 @@
     ]
     early = [after(v, *merged[1:]) for v in held[:3]]
     held += [swap(v, 0, f) for f in range(1, G) for v in (*early, held[3])]
-    *parts, base = call(
-        partial(attend_kernel, G, S, Y),
-        [(G, toks, half)] * blocks + [(blocks, toks, cols)],
+    norm, base = call(
+        partial(norm_kernel, G, S, Y),
+        [(blocks, every, cols), (blocks, toks, cols)],
         p.where,
         *merged,
-        shift,
-        scale,
-        *held,
+        mods,
         scratch=[
             pltpu.VMEM((blocks, blocks, S, local, cols), BF),
-            pltpu.VMEM((blocks, every, cols), BF),
-            pltpu.VMEM((blocks, 1, cols), F32),
-            pltpu.VMEM((blocks, 1, cols), F32),
-            pltpu.VMEM((G, width, part + half // blocks), BF),
-            pltpu.VMEM((S, every, HD), BF),
+            pltpu.VMEM((3 * blocks, 1, cols), F32),
         ],
-        copies=2 + G * S + blocks * blocks,
+        copies=1 + blocks * blocks,
+        fast=range(2),
+        still=True,
+    )
+    parts = call(
+        partial(attend_kernel, G, S, Y),
+        [(G, toks, half)] * blocks,
+        p.where,
+        norm,
+        *held,
+        scratch=[pltpu.VMEM((S, every, HD), BF)],
         flops=10 * every * width * cols,
-        still=True,
-        fast=range(blocks + 1),
+        fast=range(blocks),
+        fast_in=True,
     )
     parts = [
         p.send(parts[e * G + d], lambda x, z, y, c, e=e, d=d: (x + d, z, y + e, c))
@@ -496,7 +506,7 @@
         partial(result_kernel, G, S, Y),
         [(local, width)] * S,
         p.where,
-        gate,
+        mods,
         base,
         *parts,
         fast=range(S),

time: 130 us -> 125 us (0.962)
  starting transfers between devices: 48 us -> 43.4 us
  local copies, waits for them, and re-layouts: 5.54 us -> 3.85 us
  Pallas kernels: 25.1 us -> 23.6 us
  waiting for transfers between devices: 49.2 us -> 50.7 us
    ppermute x35, starting transfers between devices: 48 us -> 43.4 us  [send(): return lax.ppermute(value, ('group', 'seq'), pairs)]
    pallas_call x9 -> x10, Pallas kernels: 25.1 us -> 23.6 us  [call(): pl.pallas_call(kernel, out_shape=[jax.ShapeDtypeStruct(s, BF) for s in ou...]
    ppermute x35, waiting for transfers between devices: 49.2 us -> 50.7 us  [send(): return lax.ppermute(value, ('group', 'seq'), pairs)]
    unnamed x42 -> x32, local copies, waits for them, and re-layouts: 3.55 us -> 2.49 us
  transfers between devices with their start and end apart: 35 -> 35, of which waited for: 21 -> 17; matrix products, arithmetic and copies ran while one was open for 2% -> 3% of each run, Pallas kernels for 6% -> 8%
where the time goes in v7:
time: 125 us
  waiting for transfers between devices  50.7 us (41%)
  starting transfers between devices  43.4 us (35%)
  Pallas kernels  23.6 us (19%)
  local copies, waits for them, and re-layouts  3.85 us (3%)
    ppermute x35, waiting for transfers between devices, send(): return lax.ppermute(value, ('group', 'seq'), pairs)  50.7 us
    ppermute x35, starting transfers between devices, send(): return lax.ppermute(value, ('group', 'seq'), pairs)  43.4 us
    pallas_call x10, Pallas kernels, call(): pl.pallas_call(kernel, out_shape=[jax.ShapeDtypeStruct(s, BF) for s in ou...  23.6 us
  transfers between devices with their start and end apart: 35, of which 17 were waited for; matrix products, arithmetic and copies ran while one was open for 3% of the time, Pallas kernels for 8%

profile of v7, /device:TPU:1, one launch (start us, length us, event | category | flops | bytes accessed | tf_op | source)
XLA Modules:
  0.0 124.6 jit_solution(4752658193889899660)
XLA Ops:
  0.0 0.1 pad_add_fusion.where
  0.1 3.5 %shard_map.74 = (bf16[176,352]{1,0:T(8,128)(2,1)S(1)}, bf16[88,528]{1,0:T(8,128)(2,1)S(1)}, bf16[88,1232]{1,0:T(8,128)(2,1)}, bf16[88,1232]{1,0:T(8,128)(2,1)S(1...) custom-call(s32[4]{0:T(128)S(1)} %pad_add_fusion.where, bf16[176,1408]{1,0:T(8,128)(2,1)} %w_skip_any.1, ...), custom_call_target="tpu_custom_call" | custom-call | bytes 2973696 | tf_op jit(solution)/shard_map/pallas_call | solution.py:105
  3.6 2.2 %collective-permute-start.5 = (bf16[88,1232]{1,0:T(8,128)(2,1)S(1)}, bf16[88,1232]{1,0:T(8,128)(2,1)S(1)}, u32[]{:S(2)}, u32[]{:S(2)}) collective-permute-start(bf16[88,1232]{1,0:T(8,128)(2,1)S(1)} %get-tuple-element.40), channel_id=1, source_target_pairs={{0,2},{1,3},{2,0},{3,1},{4,6},{5,7},{6,4},{7,5},{8,10},{9,11},{10,... | collective-permute-start | bytes 650504 | tf_op jit(solution)/shard_map/ppermute | solution.py:95
  5.9 1.6 %shard_map.73 = bf16[2,4,16,1408]{3,2,1,0:T(8,128)(2,1)S(1)} custom-call(s32[4]{0:T(128)S(1)} %pad_add_fusion.where, bf16[4,16,1408]{2,1,0:T(8,128)(2,1)} %hidden.1, bf16[4,16,1408]{2,1,0:T(8,128)(2,1)} %skip.1), custom_call_target="tpu_custom_call" | custom-call | bytes 720896 | tf_op jit(solution)/shard_map/pallas_call | solution.py:105
  7.4 3.8 %collective-permute-start.1 = (bf16[2,4,16,1408]{3,2,1,0:T(8,128)(2,1)S(1)}, bf16[2,4,16,1408]{3,2,1,0:T(8,128)(2,1)S(1)}, u32[]{:S(2)}, u32[]{:S(2)}) collective-permute-start(bf16[2,4,16,1408]{3,2,1,0:T(8,128)(2,1)S(1)} %shard_map.73), channel_id=1, source_target_pairs={{0,0},{1,16},{2,2},{3,18},{4,4},{5,20},{6,6},{7,22},{8,8},{9,24},{... | collective-permute-start | bytes 1081352 | tf_op jit(solution)/shard_map/ppermute | solution.py:95
  11.4 1.9 %collective-permute-start.4 = (bf16[2,4,16,1408]{3,2,1,0:T(8,128)(2,1)S(1)}, bf16[2,4,16,1408]{3,2,1,0:T(8,128)(2,1)S(1)}, u32[]{:S(2)}, u32[]{:S(2)}) collective-permute-start(bf16[2,4,16,1408]{3,2,1,0:T(8,128)(2,1)S(1)} %shard_map.73), channel_id=1, source_target_pairs={{0,18},{1,2},{2,16},{3,0},{4,22},{5,6},{6,20},{7,4},{8,26},{9,10},... | collective-permute-start | bytes 1081352 | tf_op jit(solution)/shard_map/ppermute | solution.py:95
  13.3 0.7 shard_map.75.refs_4_
  14.1 1.3 %collective-permute-start.6 = (bf16[352,352]{1,0:T(8,128)(2,1)S(1)}, bf16[352,352]{1,0:T(8,128)(2,1)}, u32[]{:S(2)}, u32[]{:S(2)}) collective-permute-start(bf16[352,352]{1,0:T(8,128)(2,1)S(1)} %shard_map.75.refs_4_), channel_id=1, source_target_pairs={{0,4},{1,5},{2,6},{3,7},{4,8},{5,9},{6,10},{7,11},{8,12},{9,13},{1... | collective-permute-start | bytes 743432 | tf_op jit(solution)/shard_map/ppermute | solution.py:95
  15.4 3.9 %collective-permute-done.1.refs_0_ = bf16[2,4,16,1408]{3,2,1,0:T(8,128)(2,1)S(1)} collective-permute-done((bf16[2,4,16,1408]{3,2,1,0:T(8,128)(2,1)S(1)}, bf16[2,4,16,1408]{3,2,1,0:T(8,128)(2,1)S(1)}, u32[]{:S(2)}, u32[]{:S(2)}) %collective-permute-start.1) | collective-permute-done | bytes 360480 | tf_op jit(solution)/shard_map/ppermute | solution.py:95
  19.3 2.6 %collective-permute-done.2.refs_1_ = bf16[2,4,16,1408]{3,2,1,0:T(8,128)(2,1)S(1)} collective-permute-done((bf16[2,4,16,1408]{3,2,1,0:T(8,128)(2,1)S(1)}, bf16[2,4,16,1408]{3,2,1,0:T(8,128)(2,1)S(1)}, u32[]{:S(2)}, u32[]{:S(2)}) %collective-permute-start.2) | collective-permute-done | bytes 360480 | tf_op jit(solution)/shard_map/ppermute | solution.py:95
  21.9 1.2 collective-permute-done.6.refs_5_
  23.0 0.1 collective-permute-start.7
  23.2 3.6 %collective-permute-done.3.refs_2_ = bf16[2,4,16,1408]{3,2,1,0:T(8,128)(2,1)S(1)} collective-permute-done((bf16[2,4,16,1408]{3,2,1,0:T(8,128)(2,1)S(1)}, bf16[2,4,16,1408]{3,2,1,0:T(8,128)(2,1)S(1)}, u32[]{:S(2)}, u32[]{:S(2)}) %collective-permute-start.3) | collective-permute-done | bytes 360480 | tf_op jit(solution)/shard_map/ppermute | solution.py:95
  26.8 1.6 %collective-permute-done.4.refs_3_ = bf16[2,4,16,1408]{3,2,1,0:T(8,128)(2,1)S(1)} collective-permute-done((bf16[2,4,16,1408]{3,2,1,0:T(8,128)(2,1)S(1)}, bf16[2,4,16,1408]{3,2,1,0:T(8,128)(2,1)S(1)}, u32[]{:S(2)}, u32[]{:S(2)}) %collective-permute-start.4) | collective-permute-done | bytes 360480 | tf_op jit(solution)/shard_map/ppermute | solution.py:95
  28.4 2.4 %collective-permute-start.13 = (bf16[88,1232]{1,0:T(8,128)(2,1)}, bf16[88,1232]{1,0:T(8,128)(2,1)S(1)}, u32[]{:S(2)}, u32[]{:S(2)}) collective-permute-start(bf16[88,1232]{1,0:T(8,128)(2,1)} %get-tuple-element.47), channel_id=1, source_target_pairs={{0,1},{1,0},{2,3},{3,2},{4,5},{5,4},{6,7},{7,6},{8,9},{9,8},{10,11... | collective-permute-start | bytes 650504 | tf_op jit(solution)/shard_map/ppermute | solution.py:95
  30.7 0.2 collective-permute-start.14
  30.9 0.4 collective-permute-start.9
  31.4 1.3 %collective-permute-start.8 = (bf16[352,352]{1,0:T(8,128)(2,1)}, bf16[352,352]{1,0:T(8,128)(2,1)}, u32[]{:S(2)}, u32[]{:S(2)}) collective-permute-start(bf16[352,352]{1,0:T(8,128)(2,1)} %collective-permute-done.7.refs_6_), channel_id=1, source_target_pairs={{0,4},{1,5},{2,6},{3,7},{4,8},{5,9},{6,10},{7,11},{8,12},{9,13},{1... | collective-permute-start | bytes 743432 | tf_op jit(solution)/shard_map/ppermute | solution.py:95
  32.7 3.8 %collective-permute-start = (s32[4]{0:T(128)S(1)}, s32[4]{0:T(128)S(1)}, u32[]{:S(2)}, u32[]{:S(2)}) collective-permute-start(s32[4]{0:T(128)S(1)} %copy-done.15), channel_id=1, source_target_pairs={{0,0},{1,16},{2,2},{3,18},{4,4},{5,20},{6,6},{7,22},{8,8},{9,24},{... | collective-permute-start | bytes 56 | tf_op jit(solution)/shard_map/ppermute | solution.py:95
  36.5 1.2 collective-permute-done
  37.8 0.7 dynamic_slice.3
  39.1 0.6 copy-done.6
  39.7 0.9 copy-done.5
  40.7 0.9 copy-done.7
  41.6 0.9 shard_map.77.refs_0_
  42.5 1.6 %collective-permute-start.15 = (bf16[352,704]{1,0:T(8,128)(2,1)S(1)}, bf16[352,704]{1,0:T(8,128)(2,1)S(1)}, u32[]{:S(2)}, u32[]{:S(2)}) collective-permute-start(bf16[352,704]{1,0:T(8,128)(2,1)S(1)} %shard_map.77.refs_0_), channel_id=1, source_target_pairs={{0,4},{1,5},{2,6},{3,7},{4,0},{5,1},{6,2},{7,3},{8,12},{9,13},{10,... | collective-permute-start | bytes 1486856 | tf_op jit(solution)/shard_map/ppermute | solution.py:95
  44.0 2.7 %collective-permute-start.22 = (bf16[352,704]{1,0:T(8,128)(2,1)S(1)}, bf16[352,704]{1,0:T(8,128)(2,1)}, u32[]{:S(2)}, u32[]{:S(2)}) collective-permute-start(bf16[352,704]{1,0:T(8,128)(2,1)S(1)} %shard_map.77.refs_0_), channel_id=1, source_target_pairs={{0,8},{1,9},{2,10},{3,11},{4,12},{5,13},{6,14},{7,15},{8,0},{9,1},... | collective-permute-start | bytes 1486856 | tf_op jit(solution)/shard_map/ppermute | solution.py:95
  46.9 0.5 collective-permute-start.11
  47.4 0.1 collective-permute-start.12
  47.5 1.0 fusion.3
  48.5 0.8 reduce
  49.3 0.7 reshape.35.refs_4_.mods
  50.0 3.8 %shard_map.76 = (bf16[4,16,352]{2,1,0:T(8,128)(2,1)S(1)}, bf16[4,16,352]{2,1,0:T(8,128)(2,1)S(1)}, bf16[4,16,352]{2,1,0:T(8,128)(2,1)S(1)}, bf16[4,16,352]{2,1,0:T(8,128)(2,1)S(1)}) custom-call(s32[4]{0:T(128)S(1)} %pad_add_fusion.where, bf16[2,4,16,1408]{3,2,1,0:T(8,128)(2,1)} %copy-done.8, bf16[2,4,16,1408]{3,2,1,0:T(8,128)(2,1)} %copy-done.9, ...), custom_call_target="tpu_custom_call" | custom-call | flops 507510784 | bytes 6848512 | tf_op jit(solution)/shard_map/pallas_call | solution.py:105
  53.7 11.3 %collective-permute-done.15.refs_1_ = bf16[352,704]{1,0:T(8,128)(2,1)S(1)} collective-permute-done((bf16[352,704]{1,0:T(8,128)(2,1)S(1)}, bf16[352,704]{1,0:T(8,128)(2,1)S(1)}, u32[]{:S(2)}, u32[]{:S(2)}) %collective-permute-start.15) | collective-permute-done | bytes 495648 | tf_op jit(solution)/shard_map/ppermute | solution.py:95
  65.1 2.5 %collective-permute-start.17 = (bf16[4,16,352]{2,1,0:T(8,128)(2,1)S(1)}, bf16[4,16,352]{2,1,0:T(8,128)(2,1)S(1)}, u32[]{:S(2)}, u32[]{:S(2)}) collective-permute-start(bf16[4,16,352]{2,1,0:T(8,128)(2,1)S(1)} %get-tuple-element.54), channel_id=1, source_target_pairs={{0,8},{1,9},{2,10},{3,11},{4,12},{5,13},{6,14},{7,15},{8,0},{9,1},... | collective-permute-start | bytes 135176 | tf_op jit(solution)/shard_map/ppermute | solution.py:95
  67.6 0.8 collective-permute-start.18
  68.3 1.8 %collective-permute-done.16.refs_1_ = bf16[4,16,352]{2,1,0:T(8,128)(2,1)S(1)} collective-permute-done((bf16[4,16,352]{2,1,0:T(8,128)(2,1)S(1)}, bf16[4,16,352]{2,1,0:T(8,128)(2,1)S(1)}, u32[]{:S(2)}, u32[]{:S(2)}) %collective-permute-start.16) | collective-permute-done | bytes 45088 | tf_op jit(solution)/shard_map/ppermute | solution.py:95
  70.2 1.2 %collective-permute-done.17.refs_2_ = bf16[4,16,352]{2,1,0:T(8,128)(2,1)S(1)} collective-permute-done((bf16[4,16,352]{2,1,0:T(8,128)(2,1)S(1)}, bf16[4,16,352]{2,1,0:T(8,128)(2,1)S(1)}, u32[]{:S(2)}, u32[]{:S(2)}) %collective-permute-start.17) | collective-permute-done | bytes 45088 | tf_op jit(solution)/shard_map/ppermute | solution.py:95
  71.4 0.3 collective-permute-done.18.refs_3_
  71.8 0.8 shard_map.78.refs_0_
  72.6 1.1 collective-permute-start.23
  73.7 0.7 collective-permute-start.20
  74.4 1.9 %collective-permute-start.21 = (bf16[4,4,16,352]{3,2,1,0:T(8,128)(2,1)S(1)}, bf16[4,4,16,352]{3,2,1,0:T(8,128)(2,1)S(1)}, u32[]{:S(2)}, u32[]{:S(2)}) collective-permute-start(bf16[4,4,16,352]{3,2,1,0:T(8,128)(2,1)S(1)} %shard_map.78.refs_0_), channel_id=1, source_target_pairs={{0,18},{1,19},{2,16},{3,17},{4,22},{5,23},{6,20},{7,21},{8,26},{9,... | collective-permute-start | bytes 540680 | tf_op jit(solution)/shard_map/ppermute | solution.py:95
  76.4 3.1 %collective-permute-done.19.refs_1_ = bf16[4,4,16,352]{3,2,1,0:T(8,128)(2,1)S(1)} collective-permute-done((bf16[4,4,16,352]{3,2,1,0:T(8,128)(2,1)S(1)}, bf16[4,4,16,352]{3,2,1,0:T(8,128)(2,1)S(1)}, u32[]{:S(2)}, u32[]{:S(2)}) %collective-permute-start.19) | collective-permute-done | bytes 180256 | tf_op jit(solution)/shard_map/ppermute | solution.py:95
  79.5 4.7 %collective-permute-done.21.refs_3_ = bf16[4,4,16,352]{3,2,1,0:T(8,128)(2,1)S(1)} collective-permute-done((bf16[4,4,16,352]{3,2,1,0:T(8,128)(2,1)S(1)}, bf16[4,4,16,352]{3,2,1,0:T(8,128)(2,1)S(1)}, u32[]{:S(2)}, u32[]{:S(2)}) %collective-permute-start.21) | collective-permute-done | bytes 180256 | tf_op jit(solution)/shard_map/ppermute | solution.py:95
  84.2 1.6 %collective-permute-start.24 = (bf16[352,704]{1,0:T(8,128)(2,1)S(1)}, bf16[352,704]{1,0:T(8,128)(2,1)S(1)}, u32[]{:S(2)}, u32[]{:S(2)}) collective-permute-start(bf16[352,704]{1,0:T(8,128)(2,1)S(1)} %shard_map.77.refs_0_), channel_id=1, source_target_pairs={{0,1},{1,0},{2,3},{3,2},{4,5},{5,4},{6,7},{7,6},{8,9},{9,8},{10,11... | collective-permute-start | bytes 1486856 | tf_op jit(solution)/shard_map/ppermute | solution.py:95
  85.8 0.5 collective-permute-start.26
  86.3 1.3 %collective-permute-start.27 = (bf16[352,704]{1,0:T(8,128)(2,1)S(1)}, bf16[352,704]{1,0:T(8,128)(2,1)S(1)}, u32[]{:S(2)}, u32[]{:S(2)}) collective-permute-start(bf16[352,704]{1,0:T(8,128)(2,1)S(1)} %collective-permute-done.23.refs_3_), channel_id=1, source_target_pairs={{0,1},{1,0},{2,3},{3,2},{4,5},{5,4},{6,7},{7,6},{8,9},{9,8},{10,11... | collective-permute-start | bytes 1486856 | tf_op jit(solution)/shard_map/ppermute | solution.py:95
  87.6 2.5 %shard_map.79 = (bf16[4,256,352]{2,1,0:T(8,128)(2,1)S(1)}, bf16[4,64,352]{2,1,0:T(8,128)(2,1)S(1)}) custom-call(s32[4]{0:T(128)S(1)} %pad_add_fusion.where, bf16[4,4,16,352]{3,2,1,0:T(8,128)(2,1)} %copy-done.2, bf16[4,4,16,352]{3,2,1,0:T(8,128)(2,1)} %copy-done.12, bf16[4,4,16,352]{3,2,1,0:T(8,128)(2,1)} %copy-done.13, bf16[4,4,16,352]{3,2,1,0:T(8,128)(2,1)} %copy-done.14, ...), custom_call_target="tpu_custom_call" | custom-call | bytes 1475584 | tf_op jit(solution)/shard_map/pallas_call | solution.py:105
  90.2 7.8 %shard_map.80 = (bf16[2,64,704]{2,1,0:T(8,128)(2,1)S(1)}, bf16[2,64,704]{2,1,0:T(8,128)(2,1)S(1)}, bf16[2,64,704]{2,1,0:T(8,128)(2,1)S(1)}, bf16[2,64,704]{2,1,0:T(8,128)(2,1)S(1)}) custom-call(s32[4]{0:T(128)S(1)} %pad_add_fusion.where, bf16[4,256,352]{2,1,0:T(8,128)(2,1)S(1)} %get-tuple-element.58.norm, bf16[352,704]{1,0:T(8,128)(2,1)S(1)} %shard_map.77.refs_0_, ...), custom_call_target="tpu_custom_call" | custom-call | flops 1268776960 | bytes 9371648 | tf_op jit(solution)/shard_map/pallas_call | solution.py:105
  98.0 0.5 collective-permute-start.28
  98.5 0.7 collective-permute-start.29
  99.2 1.4 %collective-permute-start.30 = (bf16[2,64,704]{2,1,0:T(8,128)(2,1)S(1)}, bf16[2,64,704]{2,1,0:T(8,128)(2,1)S(1)}, u32[]{:S(2)}, u32[]{:S(2)}) collective-permute-start(bf16[2,64,704]{2,1,0:T(8,128)(2,1)S(1)} %get-tuple-element.66), channel_id=1, source_target_pairs={{0,18},{1,19},{2,16},{3,17},{4,22},{5,23},{6,20},{7,21},{8,26},{9,... | collective-permute-start | bytes 540680 | tf_op jit(solution)/shard_map/ppermute | solution.py:95
  100.7 3.9 %collective-permute-done.28.refs_1_ = bf16[2,64,704]{2,1,0:T(8,128)(2,1)S(1)} collective-permute-done((bf16[2,64,704]{2,1,0:T(8,128)(2,1)S(1)}, bf16[2,64,704]{2,1,0:T(8,128)(2,1)S(1)}, u32[]{:S(2)}, u32[]{:S(2)}) %collective-permute-start.28) | collective-permute-done | bytes 180256 | tf_op jit(solution)/shard_map/ppermute | solution.py:95
  104.6 4.7 %collective-permute-done.30.refs_3_ = bf16[2,64,704]{2,1,0:T(8,128)(2,1)S(1)} collective-permute-done((bf16[2,64,704]{2,1,0:T(8,128)(2,1)S(1)}, bf16[2,64,704]{2,1,0:T(8,128)(2,1)S(1)}, u32[]{:S(2)}, u32[]{:S(2)}) %collective-permute-start.30) | collective-permute-done | bytes 180256 | tf_op jit(solution)/shard_map/ppermute | solution.py:95
  109.3 0.7 shard_map.81
  110.0 3.5 %collective-permute-start.31 = (bf16[16,1408]{1,0:T(8,128)(2,1)S(1)}, bf16[16,1408]{1,0:T(8,128)(2,1)S(1)}, u32[]{:S(2)}, u32[]{:S(2)}) collective-permute-start(bf16[16,1408]{1,0:T(8,128)(2,1)S(1)} %get-tuple-element.67), channel_id=1, source_target_pairs={{0,0},{1,16},{2,2},{3,18},{4,4},{5,20},{6,6},{7,22},{8,8},{9,24},{... | collective-permute-start | bytes 135176 | tf_op jit(solution)/shard_map/ppermute | solution.py:95
  113.6 2.3 %collective-permute-start.32 = (bf16[16,1408]{1,0:T(8,128)(2,1)S(1)}, bf16[16,1408]{1,0:T(8,128)(2,1)S(1)}, u32[]{:S(2)}, u32[]{:S(2)}) collective-permute-start(bf16[16,1408]{1,0:T(8,128)(2,1)S(1)} %get-tuple-element.68), channel_id=1, source_target_pairs={{0,12},{1,28},{2,14},{3,30},{4,0},{5,16},{6,2},{7,18},{8,4},{9,20}... | collective-permute-start | bytes 135176 | tf_op jit(solution)/shard_map/ppermute | solution.py:95
  115.9 1.1 collective-permute-start.33
  117.0 0.8 collective-permute-start.34
  117.7 1.0 collective-permute-done.32.refs_1_
  118.7 2.5 %collective-permute-done.33.refs_2_ = bf16[16,1408]{1,0:T(8,128)(2,1)S(1)} collective-permute-done((bf16[16,1408]{1,0:T(8,128)(2,1)S(1)}, bf16[16,1408]{1,0:T(8,128)(2,1)S(1)}, u32[]{:S(2)}, u32[]{:S(2)}) %collective-permute-start.33) | collective-permute-done | bytes 45088 | tf_op jit(solution)/shard_map/ppermute | solution.py:95
  121.2 2.0 %collective-permute-done.34.refs_3_ = bf16[16,1408]{1,0:T(8,128)(2,1)S(1)} collective-permute-done((bf16[16,1408]{1,0:T(8,128)(2,1)S(1)}, bf16[16,1408]{1,0:T(8,128)(2,1)S(1)}, u32[]{:S(2)}, u32[]{:S(2)}) %collective-permute-start.34) | collective-permute-done | bytes 45088 | tf_op jit(solution)/shard_map/ppermute | solution.py:95
  123.1 1.2 %shard_map.82 = bf16[4,16,1408]{2,1,0:T(8,128)(2,1)} custom-call(s32[4]{0:T(128)S(1)} %pad_add_fusion.where, bf16[16,1408]{1,0:T(8,128)(2,1)S(1)} %collective-permute-done.31.refs_0_, bf16[16,1408]{1,0:T(8,128)(2,1)S(1)} %collective-permute-done.32.refs_1_, bf16[16,1408]{1,0:T(8,128)(2,1)S(1)} %collective-permute-done.33.refs_2_, ...), custom_call_target="tpu_custom_call" | custom-call | bytes 360448 | tf_op jit(solution)/shard_map/pallas_call | solution.py:105
  (56 shorter events, 0.3 us)
Async XLA Ops:
  0.0 47.5 %copy-start = (bf16[256,4224]{1,0:T(8,128)(2,1)S(1)}, bf16[256,4224]{1,0:T(8,128)(2,1)}, u32[]{:S(2)}) copy-start(bf16[256,4224]{1,0:T(8,128)(2,1)} %param.11) | copy-start | bytes 6488068
  0.0 32.7 %copy-start.15 = (s32[4]{0:T(128)S(1)}, s32[4]{0:T(128)}, u32[]{:S(2)}) copy-start(s32[4]{0:T(128)} %param.9) | copy-start | bytes 52
  3.6 27.1 %copy-start.4 = (bf16[88,704]{1,0:T(8,128)(2,1)}, bf16[88,704]{1,0:T(8,128)(2,1)S(1)}, u32[]{:S(2)}) copy-start(bf16[88,704]{1,0:T(8,128)(2,1)S(1)} %get-tuple-element.50.refs_4_) | copy-start | bytes 371716
  3.6 9.7 %collective-permute-start.5 = (bf16[88,1232]{1,0:T(8,128)(2,1)S(1)}, bf16[88,1232]{1,0:T(8,128)(2,1)S(1)}, u32[]{:S(2)}, u32[]{:S(2)}) collective-permute-start(bf16[88,1232]{1,0:T(8,128)(2,1)S(1)} %get-tuple-element.40), channel_id=1, source_target_pairs={{0,2},{1,3},{2,0},{3,1},{4,6},{5,7},{6,4},{7,5},{8,10},{9,11},{10,... | collective-permute-start | bytes 650504 | tf_op jit(solution)/shard_map/ppermute | solution.py:95
  7.4 11.9 %collective-permute-start.1 = (bf16[2,4,16,1408]{3,2,1,0:T(8,128)(2,1)S(1)}, bf16[2,4,16,1408]{3,2,1,0:T(8,128)(2,1)S(1)}, u32[]{:S(2)}, u32[]{:S(2)}) collective-permute-start(bf16[2,4,16,1408]{3,2,1,0:T(8,128)(2,1)S(1)} %shard_map.73), channel_id=1, source_target_pairs={{0,0},{1,16},{2,2},{3,18},{4,4},{5,20},{6,6},{7,22},{8,8},{9,24},{... | collective-permute-start | bytes 1081352 | tf_op jit(solution)/shard_map/ppermute | solution.py:95
  11.3 10.6 %collective-permute-start.2 = (bf16[2,4,16,1408]{3,2,1,0:T(8,128)(2,1)S(1)}, bf16[2,4,16,1408]{3,2,1,0:T(8,128)(2,1)S(1)}, u32[]{:S(2)}, u32[]{:S(2)}) collective-permute-start(bf16[2,4,16,1408]{3,2,1,0:T(8,128)(2,1)S(1)} %shard_map.73), channel_id=1, source_target_pairs={{0,16},{1,0},{2,18},{3,2},{4,20},{5,4},{6,22},{7,6},{8,24},{9,8},{... | collective-permute-start | bytes 1081352 | tf_op jit(solution)/shard_map/ppermute | solution.py:95
  11.3 15.5 %collective-permute-start.3 = (bf16[2,4,16,1408]{3,2,1,0:T(8,128)(2,1)S(1)}, bf16[2,4,16,1408]{3,2,1,0:T(8,128)(2,1)S(1)}, u32[]{:S(2)}, u32[]{:S(2)}) collective-permute-start(bf16[2,4,16,1408]{3,2,1,0:T(8,128)(2,1)S(1)} %shard_map.73), channel_id=1, source_target_pairs={{0,2},{1,18},{2,0},{3,16},{4,6},{5,22},{6,4},{7,20},{8,10},{9,26},... | collective-permute-start | bytes 1081352 | tf_op jit(solution)/shard_map/ppermute | solution.py:95
  11.4 17.0 %collective-permute-start.4 = (bf16[2,4,16,1408]{3,2,1,0:T(8,128)(2,1)S(1)}, bf16[2,4,16,1408]{3,2,1,0:T(8,128)(2,1)S(1)}, u32[]{:S(2)}, u32[]{:S(2)}) collective-permute-start(bf16[2,4,16,1408]{3,2,1,0:T(8,128)(2,1)S(1)} %shard_map.73), channel_id=1, source_target_pairs={{0,18},{1,2},{2,16},{3,0},{4,22},{5,6},{6,20},{7,4},{8,26},{9,10},... | collective-permute-start | bytes 1081352 | tf_op jit(solution)/shard_map/ppermute | solution.py:95
  14.1 35.9 %copy-start.1 = (bf16[352,352]{1,0:T(8,128)(2,1)}, bf16[352,352]{1,0:T(8,128)(2,1)S(1)}, u32[]{:S(2)}) copy-start(bf16[352,352]{1,0:T(8,128)(2,1)S(1)} %shard_map.75.refs_4_) | copy-start | bytes 743428
  14.1 9.0 %collective-permute-start.6 = (bf16[352,352]{1,0:T(8,128)(2,1)S(1)}, bf16[352,352]{1,0:T(8,128)(2,1)}, u32[]{:S(2)}, u32[]{:S(2)}) collective-permute-start(bf16[352,352]{1,0:T(8,128)(2,1)S(1)} %shard_map.75.refs_4_), channel_id=1, source_target_pairs={{0,4},{1,5},{2,6},{3,7},{4,8},{5,9},{6,10},{7,11},{8,12},{9,13},{1... | collective-permute-start | bytes 743432 | tf_op jit(solution)/shard_map/ppermute | solution.py:95
  19.3 11.6 %copy-start.8 = (bf16[2,4,16,1408]{3,2,1,0:T(8,128)(2,1)}, bf16[2,4,16,1408]{3,2,1,0:T(8,128)(2,1)S(1)}, u32[]{:S(2)}) copy-start(bf16[2,4,16,1408]{3,2,1,0:T(8,128)(2,1)S(1)} %collective-permute-done.1.refs_0_) | copy-start | bytes 1081348
  21.9 9.5 %copy-start.9 = (bf16[2,4,16,1408]{3,2,1,0:T(8,128)(2,1)}, bf16[2,4,16,1408]{3,2,1,0:T(8,128)(2,1)S(1)}, u32[]{:S(2)}) copy-start(bf16[2,4,16,1408]{3,2,1,0:T(8,128)(2,1)S(1)} %collective-permute-done.2.refs_1_) | copy-start | bytes 1081348
  23.0 8.3 %collective-permute-start.7 = (bf16[352,352]{1,0:T(8,128)(2,1)}, bf16[352,352]{1,0:T(8,128)(2,1)}, u32[]{:S(2)}, u32[]{:S(2)}) collective-permute-start(bf16[352,352]{1,0:T(8,128)(2,1)} %collective-permute-done.6.refs_5_), channel_id=1, source_target_pairs={{0,4},{1,5},{2,6},{3,7},{4,8},{5,9},{6,10},{7,11},{8,12},{9,13},{1... | collective-permute-start | bytes 743432 | tf_op jit(solution)/shard_map/ppermute | solution.py:95
  26.8 4.6 %copy-start.10 = (bf16[2,4,16,1408]{3,2,1,0:T(8,128)(2,1)}, bf16[2,4,16,1408]{3,2,1,0:T(8,128)(2,1)S(1)}, u32[]{:S(2)}) copy-start(bf16[2,4,16,1408]{3,2,1,0:T(8,128)(2,1)S(1)} %collective-permute-done.3.refs_2_) | copy-start | bytes 1081348
  28.3 4.4 %copy-start.11 = (bf16[2,4,16,1408]{3,2,1,0:T(8,128)(2,1)}, bf16[2,4,16,1408]{3,2,1,0:T(8,128)(2,1)S(1)}, u32[]{:S(2)}) copy-start(bf16[2,4,16,1408]{3,2,1,0:T(8,128)(2,1)S(1)} %collective-permute-done.4.refs_3_) | copy-start | bytes 1081348
  28.4 11.4 %collective-permute-start.13 = (bf16[88,1232]{1,0:T(8,128)(2,1)}, bf16[88,1232]{1,0:T(8,128)(2,1)S(1)}, u32[]{:S(2)}, u32[]{:S(2)}) collective-permute-start(bf16[88,1232]{1,0:T(8,128)(2,1)} %get-tuple-element.47), channel_id=1, source_target_pairs={{0,1},{1,0},{2,3},{3,2},{4,5},{5,4},{6,7},{7,6},{8,9},{9,8},{10,11... | collective-permute-start | bytes 650504 | tf_op jit(solution)/shard_map/ppermute | solution.py:95
  30.7 8.4 %collective-permute-start.14 = (bf16[88,528]{1,0:T(8,128)(2,1)S(1)}, bf16[88,528]{1,0:T(8,128)(2,1)S(1)}, u32[]{:S(2)}, u32[]{:S(2)}) collective-permute-start(bf16[88,528]{1,0:T(8,128)(2,1)S(1)} %get-tuple-element.49), channel_id=1, source_target_pairs={{0,3},{1,2},{2,1},{3,0},{4,7},{5,6},{6,5},{7,4},{8,11},{9,10},{10,... | collective-permute-start | bytes 278792 | tf_op jit(solution)/shard_map/ppermute | solution.py:95
  30.9 16.0 %collective-permute-start.9 = (bf16[352,352]{1,0:T(8,128)(2,1)S(1)}, bf16[352,352]{1,0:T(8,128)(2,1)}, u32[]{:S(2)}, u32[]{:S(2)}) collective-permute-start(bf16[352,352]{1,0:T(8,128)(2,1)S(1)} %shard_map.75.refs_4_), channel_id=1, source_target_pairs={{0,1},{1,0},{2,3},{3,2},{4,5},{5,4},{6,7},{7,6},{8,9},{9,8},{10,11... | collective-permute-start | bytes 743432 | tf_op jit(solution)/shard_map/ppermute | solution.py:95
  31.4 16.0 %collective-permute-start.8 = (bf16[352,352]{1,0:T(8,128)(2,1)}, bf16[352,352]{1,0:T(8,128)(2,1)}, u32[]{:S(2)}, u32[]{:S(2)}) collective-permute-start(bf16[352,352]{1,0:T(8,128)(2,1)} %collective-permute-done.7.refs_6_), channel_id=1, source_target_pairs={{0,4},{1,5},{2,6},{3,7},{4,8},{5,9},{6,10},{7,11},{8,12},{9,13},{1... | collective-permute-start | bytes 743432 | tf_op jit(solution)/shard_map/ppermute | solution.py:95
  32.7 5.0 %collective-permute-start = (s32[4]{0:T(128)S(1)}, s32[4]{0:T(128)S(1)}, u32[]{:S(2)}, u32[]{:S(2)}) collective-permute-start(s32[4]{0:T(128)S(1)} %copy-done.15), channel_id=1, source_target_pairs={{0,0},{1,16},{2,2},{3,18},{4,4},{5,20},{6,6},{7,22},{8,8},{9,24},{... | collective-permute-start | bytes 56 | tf_op jit(solution)/shard_map/ppermute | solution.py:95
  39.1 0.6 copy-start.6
  39.7 0.9 copy-start.5
  40.7 0.9 copy-start.7
  42.5 22.6 %collective-permute-start.15 = (bf16[352,704]{1,0:T(8,128)(2,1)S(1)}, bf16[352,704]{1,0:T(8,128)(2,1)S(1)}, u32[]{:S(2)}, u32[]{:S(2)}) collective-permute-start(bf16[352,704]{1,0:T(8,128)(2,1)S(1)} %shard_map.77.refs_0_), channel_id=1, source_target_pairs={{0,4},{1,5},{2,6},{3,7},{4,0},{5,1},{6,2},{7,3},{8,12},{9,13},{10,... | collective-permute-start | bytes 1486856 | tf_op jit(solution)/shard_map/ppermute | solution.py:95
  44.0 28.6 %collective-permute-start.22 = (bf16[352,704]{1,0:T(8,128)(2,1)S(1)}, bf16[352,704]{1,0:T(8,128)(2,1)}, u32[]{:S(2)}, u32[]{:S(2)}) collective-permute-start(bf16[352,704]{1,0:T(8,128)(2,1)S(1)} %shard_map.77.refs_0_), channel_id=1, source_target_pairs={{0,8},{1,9},{2,10},{3,11},{4,12},{5,13},{6,14},{7,15},{8,0},{9,1},... | collective-permute-start | bytes 1486856 | tf_op jit(solution)/shard_map/ppermute | solution.py:95
  46.8 3.1 %collective-permute-start.10 = (bf16[352,352]{1,0:T(8,128)(2,1)}, bf16[352,352]{1,0:T(8,128)(2,1)}, u32[]{:S(2)}, u32[]{:S(2)}) collective-permute-start(bf16[352,352]{1,0:T(8,128)(2,1)} %collective-permute-done.6.refs_5_), channel_id=1, source_target_pairs={{0,1},{1,0},{2,3},{3,2},{4,5},{5,4},{6,7},{7,6},{8,9},{9,8},{10,11... | collective-permute-start | bytes 743432 | tf_op jit(solution)/shard_map/ppermute | solution.py:95
  46.9 3.1 %collective-permute-start.11 = (bf16[352,352]{1,0:T(8,128)(2,1)}, bf16[352,352]{1,0:T(8,128)(2,1)}, u32[]{:S(2)}, u32[]{:S(2)}) collective-permute-start(bf16[352,352]{1,0:T(8,128)(2,1)} %collective-permute-done.7.refs_6_), channel_id=1, source_target_pairs={{0,1},{1,0},{2,3},{3,2},{4,5},{5,4},{6,7},{7,6},{8,9},{9,8},{10,11... | collective-permute-start | bytes 743432 | tf_op jit(solution)/shard_map/ppermute | solution.py:95
  47.4 2.6 %collective-permute-start.12 = (bf16[352,352]{1,0:T(8,128)(2,1)}, bf16[352,352]{1,0:T(8,128)(2,1)}, u32[]{:S(2)}, u32[]{:S(2)}) collective-permute-start(bf16[352,352]{1,0:T(8,128)(2,1)} %collective-permute-done.8.refs_7_), channel_id=1, source_target_pairs={{0,1},{1,0},{2,3},{3,2},{4,5},{5,4},{6,7},{7,6},{8,9},{9,8},{10,11... | collective-permute-start | bytes 743432 | tf_op jit(solution)/shard_map/ppermute | solution.py:95
  65.1 5.1 %collective-permute-start.16 = (bf16[4,16,352]{2,1,0:T(8,128)(2,1)S(1)}, bf16[4,16,352]{2,1,0:T(8,128)(2,1)S(1)}, u32[]{:S(2)}, u32[]{:S(2)}) collective-permute-start(bf16[4,16,352]{2,1,0:T(8,128)(2,1)S(1)} %get-tuple-element.52), channel_id=1, source_target_pairs={{0,4},{1,5},{2,6},{3,7},{4,8},{5,9},{6,10},{7,11},{8,12},{9,13},{1... | collective-permute-start | bytes 135176 | tf_op jit(solution)/shard_map/ppermute | solution.py:95
  65.1 6.4 %collective-permute-start.17 = (bf16[4,16,352]{2,1,0:T(8,128)(2,1)S(1)}, bf16[4,16,352]{2,1,0:T(8,128)(2,1)S(1)}, u32[]{:S(2)}, u32[]{:S(2)}) collective-permute-start(bf16[4,16,352]{2,1,0:T(8,128)(2,1)S(1)} %get-tuple-element.54), channel_id=1, source_target_pairs={{0,8},{1,9},{2,10},{3,11},{4,12},{5,13},{6,14},{7,15},{8,0},{9,1},... | collective-permute-start | bytes 135176 | tf_op jit(solution)/shard_map/ppermute | solution.py:95
  67.6 4.2 %collective-permute-start.18 = (bf16[4,16,352]{2,1,0:T(8,128)(2,1)S(1)}, bf16[4,16,352]{2,1,0:T(8,128)(2,1)S(1)}, u32[]{:S(2)}, u32[]{:S(2)}) collective-permute-start(bf16[4,16,352]{2,1,0:T(8,128)(2,1)S(1)} %get-tuple-element.56), channel_id=1, source_target_pairs={{0,12},{1,13},{2,14},{3,15},{4,0},{5,1},{6,2},{7,3},{8,4},{9,5},{1... | collective-permute-start | bytes 135176 | tf_op jit(solution)/shard_map/ppermute | solution.py:95
  72.6 15.0 %copy-start.2 = (bf16[4,4,16,352]{3,2,1,0:T(8,128)(2,1)}, bf16[4,4,16,352]{3,2,1,0:T(8,128)(2,1)S(1)}, u32[]{:S(2)}) copy-start(bf16[4,4,16,352]{3,2,1,0:T(8,128)(2,1)S(1)} %shard_map.78.refs_0_) | copy-start | bytes 540676
  72.6 13.6 %collective-permute-start.23 = (bf16[352,704]{1,0:T(8,128)(2,1)}, bf16[352,704]{1,0:T(8,128)(2,1)S(1)}, u32[]{:S(2)}, u32[]{:S(2)}) collective-permute-start(bf16[352,704]{1,0:T(8,128)(2,1)} %collective-permute-done.22.refs_2_), channel_id=1, source_target_pairs={{0,4},{1,5},{2,6},{3,7},{4,0},{5,1},{6,2},{7,3},{8,12},{9,13},{10,... | collective-permute-start | bytes 1486856 | tf_op jit(solution)/shard_map/ppermute | solution.py:95
  73.7 5.8 %collective-permute-start.19 = (bf16[4,4,16,352]{3,2,1,0:T(8,128)(2,1)S(1)}, bf16[4,4,16,352]{3,2,1,0:T(8,128)(2,1)S(1)}, u32[]{:S(2)}, u32[]{:S(2)}) collective-permute-start(bf16[4,4,16,352]{3,2,1,0:T(8,128)(2,1)S(1)} %shard_map.78.refs_0_), channel_id=1, source_target_pairs={{0,16},{1,17},{2,18},{3,19},{4,20},{5,21},{6,22},{7,23},{8,24},{9,... | collective-permute-start | bytes 540680 | tf_op jit(solution)/shard_map/ppermute | solution.py:95
  73.7 5.8 %collective-permute-start.20 = (bf16[4,4,16,352]{3,2,1,0:T(8,128)(2,1)S(1)}, bf16[4,4,16,352]{3,2,1,0:T(8,128)(2,1)S(1)}, u32[]{:S(2)}, u32[]{:S(2)}) collective-permute-start(bf16[4,4,16,352]{3,2,1,0:T(8,128)(2,1)S(1)} %shard_map.78.refs_0_), channel_id=1, source_target_pairs={{0,2},{1,3},{2,0},{3,1},{4,6},{5,7},{6,4},{7,5},{8,10},{9,11},{10,... | collective-permute-start | bytes 540680 | tf_op jit(solution)/shard_map/ppermute | solution.py:95
  74.4 9.7 %collective-permute-start.21 = (bf16[4,4,16,352]{3,2,1,0:T(8,128)(2,1)S(1)}, bf16[4,4,16,352]{3,2,1,0:T(8,128)(2,1)S(1)}, u32[]{:S(2)}, u32[]{:S(2)}) collective-permute-start(bf16[4,4,16,352]{3,2,1,0:T(8,128)(2,1)S(1)} %shard_map.78.refs_0_), channel_id=1, source_target_pairs={{0,18},{1,19},{2,16},{3,17},{4,22},{5,23},{6,20},{7,21},{8,26},{9,... | collective-permute-start | bytes 540680 | tf_op jit(solution)/shard_map/ppermute | solution.py:95
  79.5 8.1 %copy-start.12 = (bf16[4,4,16,352]{3,2,1,0:T(8,128)(2,1)}, bf16[4,4,16,352]{3,2,1,0:T(8,128)(2,1)S(1)}, u32[]{:S(2)}) copy-start(bf16[4,4,16,352]{3,2,1,0:T(8,128)(2,1)S(1)} %collective-permute-done.19.refs_1_) | copy-start | bytes 540676
  79.5 8.1 %copy-start.13 = (bf16[4,4,16,352]{3,2,1,0:T(8,128)(2,1)}, bf16[4,4,16,352]{3,2,1,0:T(8,128)(2,1)S(1)}, u32[]{:S(2)}) copy-start(bf16[4,4,16,352]{3,2,1,0:T(8,128)(2,1)S(1)} %collective-permute-done.20.refs_2_) | copy-start | bytes 540676
  84.2 3.4 %copy-start.14 = (bf16[4,4,16,352]{3,2,1,0:T(8,128)(2,1)}, bf16[4,4,16,352]{3,2,1,0:T(8,128)(2,1)S(1)}, u32[]{:S(2)}) copy-start(bf16[4,4,16,352]{3,2,1,0:T(8,128)(2,1)S(1)} %collective-permute-done.21.refs_3_) | copy-start | bytes 540676
  84.2 6.0 %collective-permute-start.24 = (bf16[352,704]{1,0:T(8,128)(2,1)S(1)}, bf16[352,704]{1,0:T(8,128)(2,1)S(1)}, u32[]{:S(2)}, u32[]{:S(2)}) collective-permute-start(bf16[352,704]{1,0:T(8,128)(2,1)S(1)} %shard_map.77.refs_0_), channel_id=1, source_target_pairs={{0,1},{1,0},{2,3},{3,2},{4,5},{5,4},{6,7},{7,6},{8,9},{9,8},{10,11... | collective-permute-start | bytes 1486856 | tf_op jit(solution)/shard_map/ppermute | solution.py:95
  85.8 4.4 %collective-permute-start.25 = (bf16[352,704]{1,0:T(8,128)(2,1)S(1)}, bf16[352,704]{1,0:T(8,128)(2,1)S(1)}, u32[]{:S(2)}, u32[]{:S(2)}) collective-permute-start(bf16[352,704]{1,0:T(8,128)(2,1)S(1)} %collective-permute-done.15.refs_1_), channel_id=1, source_target_pairs={{0,1},{1,0},{2,3},{3,2},{4,5},{5,4},{6,7},{7,6},{8,9},{9,8},{10,11... | collective-permute-start | bytes 1486856 | tf_op jit(solution)/shard_map/ppermute | solution.py:95
  85.8 4.4 %collective-permute-start.26 = (bf16[352,704]{1,0:T(8,128)(2,1)}, bf16[352,704]{1,0:T(8,128)(2,1)S(1)}, u32[]{:S(2)}, u32[]{:S(2)}) collective-permute-start(bf16[352,704]{1,0:T(8,128)(2,1)} %collective-permute-done.22.refs_2_), channel_id=1, source_target_pairs={{0,1},{1,0},{2,3},{3,2},{4,5},{5,4},{6,7},{7,6},{8,9},{9,8},{10,11... | collective-permute-start | bytes 1486856 | tf_op jit(solution)/shard_map/ppermute | solution.py:95
  86.3 3.9 %collective-permute-start.27 = (bf16[352,704]{1,0:T(8,128)(2,1)S(1)}, bf16[352,704]{1,0:T(8,128)(2,1)S(1)}, u32[]{:S(2)}, u32[]{:S(2)}) collective-permute-start(bf16[352,704]{1,0:T(8,128)(2,1)S(1)} %collective-permute-done.23.refs_3_), channel_id=1, source_target_pairs={{0,1},{1,0},{2,3},{3,2},{4,5},{5,4},{6,7},{7,6},{8,9},{9,8},{10,11... | collective-permute-start | bytes 1486856 | tf_op jit(solution)/shard_map/ppermute | solution.py:95
  90.2 19.1 %copy-start.3 = (f32[12,1,352]{2,1,0:T(1,128)S(1)}, f32[12,1,352]{2,1,0:T(1,128)}, u32[]{:S(2)}) copy-start(f32[12,1,352]{2,1,0:T(1,128)} %reshape.35.refs_4_.mods) | copy-start | bytes 50692
  98.0 6.6 %collective-permute-start.28 = (bf16[2,64,704]{2,1,0:T(8,128)(2,1)S(1)}, bf16[2,64,704]{2,1,0:T(8,128)(2,1)S(1)}, u32[]{:S(2)}, u32[]{:S(2)}) collective-permute-start(bf16[2,64,704]{2,1,0:T(8,128)(2,1)S(1)} %get-tuple-element.64), channel_id=1, source_target_pairs={{0,16},{1,17},{2,18},{3,19},{4,20},{5,21},{6,22},{7,23},{8,24},{9,... | collective-permute-start | bytes 540680 | tf_op jit(solution)/shard_map/ppermute | solution.py:95
  98.5 6.1 %collective-permute-start.29 = (bf16[2,64,704]{2,1,0:T(8,128)(2,1)S(1)}, bf16[2,64,704]{2,1,0:T(8,128)(2,1)S(1)}, u32[]{:S(2)}, u32[]{:S(2)}) collective-permute-start(bf16[2,64,704]{2,1,0:T(8,128)(2,1)S(1)} %get-tuple-element.65), channel_id=1, source_target_pairs={{0,2},{1,3},{2,0},{3,1},{4,6},{5,7},{6,4},{7,5},{8,10},{9,11},{10,... | collective-permute-start | bytes 540680 | tf_op jit(solution)/shard_map/ppermute | solution.py:95
  99.2 10.1 %collective-permute-start.30 = (bf16[2,64,704]{2,1,0:T(8,128)(2,1)S(1)}, bf16[2,64,704]{2,1,0:T(8,128)(2,1)S(1)}, u32[]{:S(2)}, u32[]{:S(2)}) collective-permute-start(bf16[2,64,704]{2,1,0:T(8,128)(2,1)S(1)} %get-tuple-element.66), channel_id=1, source_target_pairs={{0,18},{1,19},{2,16},{3,17},{4,22},{5,23},{6,20},{7,21},{8,26},{9,... | collective-permute-start | bytes 540680 | tf_op jit(solution)/shard_map/ppermute | solution.py:95
  110.0 7.7 %collective-permute-start.31 = (bf16[16,1408]{1,0:T(8,128)(2,1)S(1)}, bf16[16,1408]{1,0:T(8,128)(2,1)S(1)}, u32[]{:S(2)}, u32[]{:S(2)}) collective-permute-start(bf16[16,1408]{1,0:T(8,128)(2,1)S(1)} %get-tuple-element.67), channel_id=1, source_target_pairs={{0,0},{1,16},{2,2},{3,18},{4,4},{5,20},{6,6},{7,22},{8,8},{9,24},{... | collective-permute-start | bytes 135176 | tf_op jit(solution)/shard_map/ppermute | solution.py:95
  113.6 5.1 %collective-permute-start.32 = (bf16[16,1408]{1,0:T(8,128)(2,1)S(1)}, bf16[16,1408]{1,0:T(8,128)(2,1)S(1)}, u32[]{:S(2)}, u32[]{:S(2)}) collective-permute-start(bf16[16,1408]{1,0:T(8,128)(2,1)S(1)} %get-tuple-element.68), channel_id=1, source_target_pairs={{0,12},{1,28},{2,14},{3,30},{4,0},{5,16},{6,2},{7,18},{8,4},{9,20}... | collective-permute-start | bytes 135176 | tf_op jit(solution)/shard_map/ppermute | solution.py:95
  115.9 5.3 %collective-permute-start.33 = (bf16[16,1408]{1,0:T(8,128)(2,1)S(1)}, bf16[16,1408]{1,0:T(8,128)(2,1)S(1)}, u32[]{:S(2)}, u32[]{:S(2)}) collective-permute-start(bf16[16,1408]{1,0:T(8,128)(2,1)S(1)} %get-tuple-element.69), channel_id=1, source_target_pairs={{0,8},{1,24},{2,10},{3,26},{4,12},{5,28},{6,14},{7,30},{8,0},{9,16... | collective-permute-start | bytes 135176 | tf_op jit(solution)/shard_map/ppermute | solution.py:95
  117.0 6.2 %collective-permute-start.34 = (bf16[16,1408]{1,0:T(8,128)(2,1)S(1)}, bf16[16,1408]{1,0:T(8,128)(2,1)S(1)}, u32[]{:S(2)}, u32[]{:S(2)}) collective-permute-start(bf16[16,1408]{1,0:T(8,128)(2,1)S(1)} %get-tuple-element.70), channel_id=1, source_target_pairs={{0,4},{1,20},{2,6},{3,22},{4,8},{5,24},{6,10},{7,26},{8,12},{9,28}... | collective-permute-start | bytes 135176 | tf_op jit(solution)/shard_map/ppermute | solution.py:95

commit v8 on v7

--- a/solution.py
+++ b/solution.py
@@ -264,37 +264,34 @@
 def norm_kernel(G, S, Y, where, *refs):
     x, y = where[0], where[2]
     blocks = Y * G
-    merged_any, mods_any = refs[:blocks], refs[blocks]
-    norm, base, merged, mods, sems = refs[blocks + 1 :]
-    cols = merged_any[0].shape[3]
-    toks = S * merged_any[0].shape[2]
+    merged, mods, norm, base = refs[:blocks], refs[blocks], refs[blocks + 1], refs[blocks + 2]
+    cols = merged[0].shape[3]
+    toks = S * merged[0].shape[2]
     rows = blocks * toks
     width = cols * blocks
 
-    pairs = [(mods_any, mods)]
+    total = jnp.zeros((rows, 1), F32)
+    wide = []
     for e in range(Y):
         for d in range(G):
-            b = (x + d) % G * Y + (y + e) % Y
-            for em in range(Y):
-                for dm in range(G):
-                    at = (em - e) % Y * G + (dm - d) % G
-                    pairs.append(
-                        (merged_any[e * G + d].at[:, at], merged.at[b, em * G + dm])
-                    )
-    copy_all(pairs, sems)
-    total = jnp.zeros((rows, 1), F32)
-    wide = []
-    for b in range(blocks):
-        base[b] = merged[b, 0].reshape(toks, cols)
-        wide.append(merged[b].reshape(rows, cols).astype(F32))
-        total = total + jnp.sum(wide[-1], axis=-1, keepdims=True)
+            own = [
+                merged[e * G + d][:, (em - e) % Y * G + (dm - d) % G].reshape(toks, cols)
+                for em in range(Y)
+                for dm in range(G)
+            ]
+            base[(x + d) % G * Y + (y + e) % Y] = own[0]
+            wide.append(jnp.concatenate(own, axis=0).astype(F32))
+            total = total + jnp.sum(wide[-1], axis=-1, keepdims=True)
     mean = total * (1.0 / width)
     square = jnp.zeros((rows, 1), F32)
     for m in wide:
         square = square + jnp.sum((m - mean) ** 2, axis=-1, keepdims=True)
     inv = lax.rsqrt(square * (1.0 / width) + 1e-06)
-    for b in range(blocks):
-        norm[b] = ((wide[b] - mean) * inv * (1.0 + mods[blocks + b]) + mods[b]).astype(BF)
+    for e in range(Y):
+        for d in range(G):
+            b = (x + d) % G * Y + (y + e) % Y
+            m = wide[e * G + d]
+            norm[b] = ((m - mean) * inv * (1.0 + mods[blocks + b]) + mods[b]).astype(BF)
 
 
 def attend_kernel(G, S, Y, where, norm, *refs):
@@ -404,7 +401,7 @@
     ]
     for e in range(Y):
         for f in range(1, G):
-            qkvs[e * G + f] = swap(after(qkvs[e * G + f], *parts[G:]), e, f)
+            qkvs[e * G + f] = swap(after(qkvs[e * G + f], parts[G]), e, f)
 
     def step(value):
         return p.send(value, lambda x, z, y, c: (x, z + 1, y, c))
@@ -476,13 +473,8 @@
         p.where,
         *merged,
         mods,
-        scratch=[
-            pltpu.VMEM((blocks, blocks, S, local, cols), BF),
-            pltpu.VMEM((3 * blocks, 1, cols), F32),
-        ],
-        copies=1 + blocks * blocks,
         fast=range(2),
-        still=True,
+        fast_in=True,
     )
     parts = call(
         partial(attend_kernel, G, S, Y),

time: 125 us -> 123 us (0.984)
  transfers between devices with their start and end apart: 35 -> 35, of which waited for: 17 -> 21; matrix products, arithmetic and copies ran while one was open for 3% -> 2% of each run, Pallas kernels for 8% -> 7%
where the time goes in v8:
time: 123 us; the launch traced here: 122 us
  waiting for transfers between devices  49.7 us (40%)
  starting transfers between devices  44.2 us (36%)
  Pallas kernels  22.4 us (18%)
  local copies, waits for them, and re-layouts  3.9 us (3%)
    ppermute x35, waiting for transfers between devices, send(): return lax.ppermute(value, ('group', 'seq'), pairs)  49.7 us
    ppermute x35, starting transfers between devices, send(): return lax.ppermute(value, ('group', 'seq'), pairs)  44.2 us
    pallas_call x10, Pallas kernels, call(): pl.pallas_call(kernel, out_shape=[jax.ShapeDtypeStruct(s, BF) for s in ou...  22.4 us
    unnamed x22, local copies, waits for them, and re-layouts  2.48 us
  transfers between devices with their start and end apart: 35, of which 21 were waited for; matrix products, arithmetic and copies ran while one was open for 2% of the time, Pallas kernels for 7%

profile of v8, /device:TPU:1, one launch (start us, length us, event | category | flops | bytes accessed | tf_op | source)
XLA Modules:
  0.0 122.4 jit_solution(3745222529313075727)
XLA Ops:
  0.1 3.6 %shard_map.74 = (bf16[176,352]{1,0:T(8,128)(2,1)S(1)}, bf16[88,528]{1,0:T(8,128)(2,1)S(1)}, bf16[88,1232]{1,0:T(8,128)(2,1)}, bf16[88,1232]{1,0:T(8,128)(2,1)S(1...) custom-call(s32[4]{0:T(128)S(1)} %pad_add_fusion.where, bf16[176,1408]{1,0:T(8,128)(2,1)} %w_skip_any.1, ...), custom_call_target="tpu_custom_call" | custom-call | bytes 2973696 | tf_op jit(solution)/shard_map/pallas_call | solution.py:105
  3.7 2.2 %collective-permute-start.5 = (bf16[88,1232]{1,0:T(8,128)(2,1)S(1)}, bf16[88,1232]{1,0:T(8,128)(2,1)S(1)}, u32[]{:S(2)}, u32[]{:S(2)}) collective-permute-start(bf16[88,1232]{1,0:T(8,128)(2,1)S(1)} %get-tuple-element.40), channel_id=1, source_target_pairs={{0,2},{1,3},{2,0},{3,1},{4,6},{5,7},{6,4},{7,5},{8,10},{9,11},{10,... | collective-permute-start | bytes 650504 | tf_op jit(solution)/shard_map/ppermute | solution.py:95
  5.9 1.6 %shard_map.73 = bf16[2,4,16,1408]{3,2,1,0:T(8,128)(2,1)S(1)} custom-call(s32[4]{0:T(128)S(1)} %pad_add_fusion.where, bf16[4,16,1408]{2,1,0:T(8,128)(2,1)} %hidden.1, bf16[4,16,1408]{2,1,0:T(8,128)(2,1)} %skip.1), custom_call_target="tpu_custom_call" | custom-call | bytes 720896 | tf_op jit(solution)/shard_map/pallas_call | solution.py:105
  7.5 3.8 %collective-permute-start.1 = (bf16[2,4,16,1408]{3,2,1,0:T(8,128)(2,1)S(1)}, bf16[2,4,16,1408]{3,2,1,0:T(8,128)(2,1)S(1)}, u32[]{:S(2)}, u32[]{:S(2)}) collective-permute-start(bf16[2,4,16,1408]{3,2,1,0:T(8,128)(2,1)S(1)} %shard_map.73), channel_id=1, source_target_pairs={{0,0},{1,16},{2,2},{3,18},{4,4},{5,20},{6,6},{7,22},{8,8},{9,24},{... | collective-permute-start | bytes 1081352 | tf_op jit(solution)/shard_map/ppermute | solution.py:95
  11.4 0.7 shard_map.75.refs_4_
  12.2 1.3 %collective-permute-start.6 = (bf16[352,352]{1,0:T(8,128)(2,1)S(1)}, bf16[352,352]{1,0:T(8,128)(2,1)}, u32[]{:S(2)}, u32[]{:S(2)}) collective-permute-start(bf16[352,352]{1,0:T(8,128)(2,1)S(1)} %shard_map.75.refs_4_), channel_id=1, source_target_pairs={{0,4},{1,5},{2,6},{3,7},{4,8},{5,9},{6,10},{7,11},{8,12},{9,13},{1... | collective-permute-start | bytes 743432 | tf_op jit(solution)/shard_map/ppermute | solution.py:95
  13.5 2.6 %collective-permute-start.4 = (bf16[2,4,16,1408]{3,2,1,0:T(8,128)(2,1)S(1)}, bf16[2,4,16,1408]{3,2,1,0:T(8,128)(2,1)S(1)}, u32[]{:S(2)}, u32[]{:S(2)}) collective-permute-start(bf16[2,4,16,1408]{3,2,1,0:T(8,128)(2,1)S(1)} %shard_map.73), channel_id=1, source_target_pairs={{0,18},{1,2},{2,16},{3,0},{4,22},{5,6},{6,20},{7,4},{8,26},{9,10},... | collective-permute-start | bytes 1081352 | tf_op jit(solution)/shard_map/ppermute | solution.py:95
  16.1 3.4 %collective-permute-done.1.refs_0_ = bf16[2,4,16,1408]{3,2,1,0:T(8,128)(2,1)S(1)} collective-permute-done((bf16[2,4,16,1408]{3,2,1,0:T(8,128)(2,1)S(1)}, bf16[2,4,16,1408]{3,2,1,0:T(8,128)(2,1)S(1)}, u32[]{:S(2)}, u32[]{:S(2)}) %collective-permute-start.1) | collective-permute-done | bytes 360480 | tf_op jit(solution)/shard_map/ppermute | solution.py:95
  19.5 2.4 %collective-permute-done.2.refs_1_ = bf16[2,4,16,1408]{3,2,1,0:T(8,128)(2,1)S(1)} collective-permute-done((bf16[2,4,16,1408]{3,2,1,0:T(8,128)(2,1)S(1)}, bf16[2,4,16,1408]{3,2,1,0:T(8,128)(2,1)S(1)}, u32[]{:S(2)}, u32[]{:S(2)}) %collective-permute-start.2) | collective-permute-done | bytes 360480 | tf_op jit(solution)/shard_map/ppermute | solution.py:95
  21.9 1.2 collective-permute-start.7
  23.1 3.7 %collective-permute-done.3.refs_2_ = bf16[2,4,16,1408]{3,2,1,0:T(8,128)(2,1)S(1)} collective-permute-done((bf16[2,4,16,1408]{3,2,1,0:T(8,128)(2,1)S(1)}, bf16[2,4,16,1408]{3,2,1,0:T(8,128)(2,1)S(1)}, u32[]{:S(2)}, u32[]{:S(2)}) %collective-permute-start.3) | collective-permute-done | bytes 360480 | tf_op jit(solution)/shard_map/ppermute | solution.py:95
  26.8 1.6 %collective-permute-start.14 = (bf16[88,528]{1,0:T(8,128)(2,1)}, bf16[88,528]{1,0:T(8,128)(2,1)S(1)}, u32[]{:S(2)}, u32[]{:S(2)}) collective-permute-start(bf16[88,528]{1,0:T(8,128)(2,1)} %get-tuple-element.49), channel_id=1, source_target_pairs={{0,3},{1,2},{2,1},{3,0},{4,7},{5,6},{6,5},{7,4},{8,11},{9,10},{10,... | collective-permute-start | bytes 278792 | tf_op jit(solution)/shard_map/ppermute | solution.py:95
  28.5 2.3 %collective-permute-done.7.refs_6_ = bf16[352,352]{1,0:T(8,128)(2,1)} collective-permute-done((bf16[352,352]{1,0:T(8,128)(2,1)}, bf16[352,352]{1,0:T(8,128)(2,1)}, u32[]{:S(2)}, u32[]{:S(2)}) %collective-permute-start.7) | collective-permute-done | bytes 247840 | tf_op jit(solution)/shard_map/ppermute | solution.py:95
  30.8 0.9 collective-permute-start.8
  31.8 4.2 %collective-permute-start = (s32[4]{0:T(128)S(1)}, s32[4]{0:T(128)S(1)}, u32[]{:S(2)}, u32[]{:S(2)}) collective-permute-start(s32[4]{0:T(128)S(1)} %copy-done.10), channel_id=1, source_target_pairs={{0,0},{1,16},{2,2},{3,18},{4,4},{5,20},{6,6},{7,22},{8,8},{9,24},{... | collective-permute-start | bytes 56 | tf_op jit(solution)/shard_map/ppermute | solution.py:95
  36.0 1.2 collective-permute-done
  37.2 0.6 dynamic_slice.3
  38.4 0.6 copy-done.4
  39.1 0.9 copy-done.3
  40.0 0.9 copy-done.5
  40.9 0.9 shard_map.77.refs_0_
  41.8 1.2 collective-permute-start.15
  43.0 3.1 %collective-permute-start.22 = (bf16[352,704]{1,0:T(8,128)(2,1)S(1)}, bf16[352,704]{1,0:T(8,128)(2,1)}, u32[]{:S(2)}, u32[]{:S(2)}) collective-permute-start(bf16[352,704]{1,0:T(8,128)(2,1)S(1)} %shard_map.77.refs_0_), channel_id=1, source_target_pairs={{0,8},{1,9},{2,10},{3,11},{4,12},{5,13},{6,14},{7,15},{8,0},{9,1},... | collective-permute-start | bytes 1486856 | tf_op jit(solution)/shard_map/ppermute | solution.py:95
  46.2 0.5 collective-permute-start.11
  46.8 0.4 fusion.3
  47.2 0.7 reduce
  47.9 0.8 reshape.35.refs_4_.mods
  48.7 0.2 collective-permute-done.12.refs_11_
  48.9 3.7 %shard_map.76 = (bf16[4,16,352]{2,1,0:T(8,128)(2,1)S(1)}, bf16[4,16,352]{2,1,0:T(8,128)(2,1)S(1)}, bf16[4,16,352]{2,1,0:T(8,128)(2,1)S(1)}, bf16[4,16,352]{2,1,0:T(8,128)(2,1)S(1)}) custom-call(s32[4]{0:T(128)S(1)} %pad_add_fusion.where, bf16[2,4,16,1408]{3,2,1,0:T(8,128)(2,1)} %copy-done.6, bf16[2,4,16,1408]{3,2,1,0:T(8,128)(2,1)} %copy-done.7, ...), custom_call_target="tpu_custom_call" | custom-call | flops 507510784 | bytes 6848512 | tf_op jit(solution)/shard_map/pallas_call | solution.py:105
  52.6 11.3 %collective-permute-done.15.refs_1_ = bf16[352,704]{1,0:T(8,128)(2,1)S(1)} collective-permute-done((bf16[352,704]{1,0:T(8,128)(2,1)S(1)}, bf16[352,704]{1,0:T(8,128)(2,1)S(1)}, u32[]{:S(2)}, u32[]{:S(2)}) %collective-permute-start.15) | collective-permute-done | bytes 495648 | tf_op jit(solution)/shard_map/ppermute | solution.py:95
  63.9 2.4 %collective-permute-start.17 = (bf16[4,16,352]{2,1,0:T(8,128)(2,1)S(1)}, bf16[4,16,352]{2,1,0:T(8,128)(2,1)S(1)}, u32[]{:S(2)}, u32[]{:S(2)}) collective-permute-start(bf16[4,16,352]{2,1,0:T(8,128)(2,1)S(1)} %get-tuple-element.54), channel_id=1, source_target_pairs={{0,8},{1,9},{2,10},{3,11},{4,12},{5,13},{6,14},{7,15},{8,0},{9,1},... | collective-permute-start | bytes 135176 | tf_op jit(solution)/shard_map/ppermute | solution.py:95
  66.3 0.9 collective-permute-start.18
  67.2 1.7 %collective-permute-done.16.refs_1_ = bf16[4,16,352]{2,1,0:T(8,128)(2,1)S(1)} collective-permute-done((bf16[4,16,352]{2,1,0:T(8,128)(2,1)S(1)}, bf16[4,16,352]{2,1,0:T(8,128)(2,1)S(1)}, u32[]{:S(2)}, u32[]{:S(2)}) %collective-permute-start.16) | collective-permute-done | bytes 45088 | tf_op jit(solution)/shard_map/ppermute | solution.py:95
  68.8 1.4 %collective-permute-done.17.refs_2_ = bf16[4,16,352]{2,1,0:T(8,128)(2,1)S(1)} collective-permute-done((bf16[4,16,352]{2,1,0:T(8,128)(2,1)S(1)}, bf16[4,16,352]{2,1,0:T(8,128)(2,1)S(1)}, u32[]{:S(2)}, u32[]{:S(2)}) %collective-permute-start.17) | collective-permute-done | bytes 45088 | tf_op jit(solution)/shard_map/ppermute | solution.py:95
  70.2 0.3 collective-permute-done.18.refs_3_
  70.5 0.8 shard_map.78.refs_0_
  71.4 1.1 collective-permute-start.23
  72.5 0.4 collective-permute-start.19
  72.9 1.3 %collective-permute-start.20 = (bf16[4,4,16,352]{3,2,1,0:T(8,128)(2,1)S(1)}, bf16[4,4,16,352]{3,2,1,0:T(8,128)(2,1)S(1)}, u32[]{:S(2)}, u32[]{:S(2)}) collective-permute-start(bf16[4,4,16,352]{3,2,1,0:T(8,128)(2,1)S(1)} %shard_map.78.refs_0_), channel_id=1, source_target_pairs={{0,2},{1,3},{2,0},{3,1},{4,6},{5,7},{6,4},{7,5},{8,10},{9,11},{10,... | collective-permute-start | bytes 540680 | tf_op jit(solution)/shard_map/ppermute | solution.py:95
  74.2 1.0 collective-permute-start.21
  75.1 3.1 %collective-permute-done.19.refs_1_ = bf16[4,4,16,352]{3,2,1,0:T(8,128)(2,1)S(1)} collective-permute-done((bf16[4,4,16,352]{3,2,1,0:T(8,128)(2,1)S(1)}, bf16[4,4,16,352]{3,2,1,0:T(8,128)(2,1)S(1)}, u32[]{:S(2)}, u32[]{:S(2)}) %collective-permute-start.19) | collective-permute-done | bytes 180256 | tf_op jit(solution)/shard_map/ppermute | solution.py:95
  78.2 4.2 %collective-permute-done.21.refs_3_ = bf16[4,4,16,352]{3,2,1,0:T(8,128)(2,1)S(1)} collective-permute-done((bf16[4,4,16,352]{3,2,1,0:T(8,128)(2,1)S(1)}, bf16[4,4,16,352]{3,2,1,0:T(8,128)(2,1)S(1)}, u32[]{:S(2)}, u32[]{:S(2)}) %collective-permute-start.21) | collective-permute-done | bytes 180256 | tf_op jit(solution)/shard_map/ppermute | solution.py:95
  82.5 2.5 %collective-permute-start.24 = (bf16[352,704]{1,0:T(8,128)(2,1)S(1)}, bf16[352,704]{1,0:T(8,128)(2,1)S(1)}, u32[]{:S(2)}, u32[]{:S(2)}) collective-permute-start(bf16[352,704]{1,0:T(8,128)(2,1)S(1)} %shard_map.77.refs_0_), channel_id=1, source_target_pairs={{0,1},{1,0},{2,3},{3,2},{4,5},{5,4},{6,7},{7,6},{8,9},{9,8},{10,11... | collective-permute-start | bytes 1486856 | tf_op jit(solution)/shard_map/ppermute | solution.py:95
  85.0 0.5 collective-permute-start.26
  85.6 0.8 collective-permute-start.27
  86.4 1.3 %shard_map.79 = (bf16[4,256,352]{2,1,0:T(8,128)(2,1)S(1)}, bf16[4,64,352]{2,1,0:T(8,128)(2,1)S(1)}) custom-call(s32[4]{0:T(128)S(1)} %pad_add_fusion.where, bf16[4,4,16,352]{3,2,1,0:T(8,128)(2,1)S(1)} %shard_map.78.refs_0_, bf16[4,4,16,352]{3,2,1,0:T(8,128)(2,1)S(1)} %collective-permute-done.19.refs_1_, ...), custom_call_target="tpu_custom_call" | custom-call | bytes 1475584 | tf_op jit(solution)/shard_map/pallas_call | solution.py:105
  87.6 0.5 collective-permute-done.25.refs_5_
  88.1 0.2 collective-permute-done.26.refs_6_
  88.4 0.6 collective-permute-done.27.refs_7_
  88.9 7.8 %shard_map.80 = (bf16[2,64,704]{2,1,0:T(8,128)(2,1)S(1)}, bf16[2,64,704]{2,1,0:T(8,128)(2,1)S(1)}, bf16[2,64,704]{2,1,0:T(8,128)(2,1)S(1)}, bf16[2,64,704]{2,1,0:T(8,128)(2,1)S(1)}) custom-call(s32[4]{0:T(128)S(1)} %pad_add_fusion.where, bf16[4,256,352]{2,1,0:T(8,128)(2,1)S(1)} %get-tuple-element.58.norm, bf16[352,704]{1,0:T(8,128)(2,1)S(1)} %shard_map.77.refs_0_, ...), custom_call_target="tpu_custom_call" | custom-call | flops 1268776960 | bytes 9371648 | tf_op jit(solution)/shard_map/pallas_call | solution.py:105
  96.7 0.5 collective-permute-start.28
  97.2 0.8 collective-permute-start.29
  98.0 1.4 %collective-permute-start.30 = (bf16[2,64,704]{2,1,0:T(8,128)(2,1)S(1)}, bf16[2,64,704]{2,1,0:T(8,128)(2,1)S(1)}, u32[]{:S(2)}, u32[]{:S(2)}) collective-permute-start(bf16[2,64,704]{2,1,0:T(8,128)(2,1)S(1)} %get-tuple-element.66), channel_id=1, source_target_pairs={{0,18},{1,19},{2,16},{3,17},{4,22},{5,23},{6,20},{7,21},{8,26},{9,... | collective-permute-start | bytes 540680 | tf_op jit(solution)/shard_map/ppermute | solution.py:95
  99.4 3.5 %collective-permute-done.28.refs_1_ = bf16[2,64,704]{2,1,0:T(8,128)(2,1)S(1)} collective-permute-done((bf16[2,64,704]{2,1,0:T(8,128)(2,1)S(1)}, bf16[2,64,704]{2,1,0:T(8,128)(2,1)S(1)}, u32[]{:S(2)}, u32[]{:S(2)}) %collective-permute-start.28) | collective-permute-done | bytes 180256 | tf_op jit(solution)/shard_map/ppermute | solution.py:95
  103.0 5.0 %collective-permute-done.30.refs_3_ = bf16[2,64,704]{2,1,0:T(8,128)(2,1)S(1)} collective-permute-done((bf16[2,64,704]{2,1,0:T(8,128)(2,1)S(1)}, bf16[2,64,704]{2,1,0:T(8,128)(2,1)S(1)}, u32[]{:S(2)}, u32[]{:S(2)}) %collective-permute-start.30) | collective-permute-done | bytes 180256 | tf_op jit(solution)/shard_map/ppermute | solution.py:95
  108.0 0.7 shard_map.81
  108.7 3.5 %collective-permute-start.31 = (bf16[16,1408]{1,0:T(8,128)(2,1)S(1)}, bf16[16,1408]{1,0:T(8,128)(2,1)S(1)}, u32[]{:S(2)}, u32[]{:S(2)}) collective-permute-start(bf16[16,1408]{1,0:T(8,128)(2,1)S(1)} %get-tuple-element.67), channel_id=1, source_target_pairs={{0,0},{1,16},{2,2},{3,18},{4,4},{5,20},{6,6},{7,22},{8,8},{9,24},{... | collective-permute-start | bytes 135176 | tf_op jit(solution)/shard_map/ppermute | solution.py:95
  112.3 1.4 %collective-permute-start.32 = (bf16[16,1408]{1,0:T(8,128)(2,1)S(1)}, bf16[16,1408]{1,0:T(8,128)(2,1)S(1)}, u32[]{:S(2)}, u32[]{:S(2)}) collective-permute-start(bf16[16,1408]{1,0:T(8,128)(2,1)S(1)} %get-tuple-element.68), channel_id=1, source_target_pairs={{0,12},{1,28},{2,14},{3,30},{4,0},{5,16},{6,2},{7,18},{8,4},{9,20}... | collective-permute-start | bytes 135176 | tf_op jit(solution)/shard_map/ppermute | solution.py:95
  113.7 1.1 collective-permute-start.33
  114.8 1.6 %collective-permute-start.34 = (bf16[16,1408]{1,0:T(8,128)(2,1)S(1)}, bf16[16,1408]{1,0:T(8,128)(2,1)S(1)}, u32[]{:S(2)}, u32[]{:S(2)}) collective-permute-start(bf16[16,1408]{1,0:T(8,128)(2,1)S(1)} %get-tuple-element.70), channel_id=1, source_target_pairs={{0,4},{1,20},{2,6},{3,22},{4,8},{5,24},{6,10},{7,26},{8,12},{9,28}... | collective-permute-start | bytes 135176 | tf_op jit(solution)/shard_map/ppermute | solution.py:95
  116.4 0.6 collective-permute-done.32.refs_1_
  117.0 2.1 %collective-permute-done.33.refs_2_ = bf16[16,1408]{1,0:T(8,128)(2,1)S(1)} collective-permute-done((bf16[16,1408]{1,0:T(8,128)(2,1)S(1)}, bf16[16,1408]{1,0:T(8,128)(2,1)S(1)}, u32[]{:S(2)}, u32[]{:S(2)}) %collective-permute-start.33) | collective-permute-done | bytes 45088 | tf_op jit(solution)/shard_map/ppermute | solution.py:95
  119.1 1.9 %collective-permute-done.34.refs_3_ = bf16[16,1408]{1,0:T(8,128)(2,1)S(1)} collective-permute-done((bf16[16,1408]{1,0:T(8,128)(2,1)S(1)}, bf16[16,1408]{1,0:T(8,128)(2,1)S(1)}, u32[]{:S(2)}, u32[]{:S(2)}) %collective-permute-start.34) | collective-permute-done | bytes 45088 | tf_op jit(solution)/shard_map/ppermute | solution.py:95
  121.0 1.2 %shard_map.82 = bf16[4,16,1408]{2,1,0:T(8,128)(2,1)} custom-call(s32[4]{0:T(128)S(1)} %pad_add_fusion.where, bf16[16,1408]{1,0:T(8,128)(2,1)S(1)} %collective-permute-done.31.refs_0_, bf16[16,1408]{1,0:T(8,128)(2,1)S(1)} %collective-permute-done.32.refs_1_, bf16[16,1408]{1,0:T(8,128)(2,1)S(1)} %collective-permute-done.33.refs_2_, ...), custom_call_target="tpu_custom_call" | custom-call | bytes 360448 | tf_op jit(solution)/shard_map/pallas_call | solution.py:105
  (46 shorter events, 0.6 us)
Async XLA Ops:
  0.0 46.8 %copy-start = (bf16[256,4224]{1,0:T(8,128)(2,1)S(1)}, bf16[256,4224]{1,0:T(8,128)(2,1)}, u32[]{:S(2)}) copy-start(bf16[256,4224]{1,0:T(8,128)(2,1)} %param.11) | copy-start | bytes 6488068
  0.0 31.8 %copy-start.10 = (s32[4]{0:T(128)S(1)}, s32[4]{0:T(128)}, u32[]{:S(2)}) copy-start(s32[4]{0:T(128)} %param.9) | copy-start | bytes 52
  3.7 24.8 %copy-start.2 = (bf16[88,704]{1,0:T(8,128)(2,1)}, bf16[88,704]{1,0:T(8,128)(2,1)S(1)}, u32[]{:S(2)}) copy-start(bf16[88,704]{1,0:T(8,128)(2,1)S(1)} %get-tuple-element.50.refs_4_) | copy-start | bytes 371716
  3.7 7.8 %collective-permute-start.5 = (bf16[88,1232]{1,0:T(8,128)(2,1)S(1)}, bf16[88,1232]{1,0:T(8,128)(2,1)S(1)}, u32[]{:S(2)}, u32[]{:S(2)}) collective-permute-start(bf16[88,1232]{1,0:T(8,128)(2,1)S(1)} %get-tuple-element.40), channel_id=1, source_target_pairs={{0,2},{1,3},{2,0},{3,1},{4,6},{5,7},{6,4},{7,5},{8,10},{9,11},{10,... | collective-permute-start | bytes 650504 | tf_op jit(solution)/shard_map/ppermute | solution.py:95
  7.5 12.0 %collective-permute-start.1 = (bf16[2,4,16,1408]{3,2,1,0:T(8,128)(2,1)S(1)}, bf16[2,4,16,1408]{3,2,1,0:T(8,128)(2,1)S(1)}, u32[]{:S(2)}, u32[]{:S(2)}) collective-permute-start(bf16[2,4,16,1408]{3,2,1,0:T(8,128)(2,1)S(1)} %shard_map.73), channel_id=1, source_target_pairs={{0,0},{1,16},{2,2},{3,18},{4,4},{5,20},{6,6},{7,22},{8,8},{9,24},{... | collective-permute-start | bytes 1081352 | tf_op jit(solution)/shard_map/ppermute | solution.py:95
  11.3 10.6 %collective-permute-start.2 = (bf16[2,4,16,1408]{3,2,1,0:T(8,128)(2,1)S(1)}, bf16[2,4,16,1408]{3,2,1,0:T(8,128)(2,1)S(1)}, u32[]{:S(2)}, u32[]{:S(2)}) collective-permute-start(bf16[2,4,16,1408]{3,2,1,0:T(8,128)(2,1)S(1)} %shard_map.73), channel_id=1, source_target_pairs={{0,16},{1,0},{2,18},{3,2},{4,20},{5,4},{6,22},{7,6},{8,24},{9,8},{... | collective-permute-start | bytes 1081352 | tf_op jit(solution)/shard_map/ppermute | solution.py:95
  11.4 15.5 %collective-permute-start.3 = (bf16[2,4,16,1408]{3,2,1,0:T(8,128)(2,1)S(1)}, bf16[2,4,16,1408]{3,2,1,0:T(8,128)(2,1)S(1)}, u32[]{:S(2)}, u32[]{:S(2)}) collective-permute-start(bf16[2,4,16,1408]{3,2,1,0:T(8,128)(2,1)S(1)} %shard_map.73), channel_id=1, source_target_pairs={{0,2},{1,18},{2,0},{3,16},{4,6},{5,22},{6,4},{7,20},{8,10},{9,26},... | collective-permute-start | bytes 1081352 | tf_op jit(solution)/shard_map/ppermute | solution.py:95
  12.2 36.7 %copy-start.1 = (bf16[352,352]{1,0:T(8,128)(2,1)}, bf16[352,352]{1,0:T(8,128)(2,1)S(1)}, u32[]{:S(2)}) copy-start(bf16[352,352]{1,0:T(8,128)(2,1)S(1)} %shard_map.75.refs_4_) | copy-start | bytes 743428
  12.2 9.7 %collective-permute-start.6 = (bf16[352,352]{1,0:T(8,128)(2,1)S(1)}, bf16[352,352]{1,0:T(8,128)(2,1)}, u32[]{:S(2)}, u32[]{:S(2)}) collective-permute-start(bf16[352,352]{1,0:T(8,128)(2,1)S(1)} %shard_map.75.refs_4_), channel_id=1, source_target_pairs={{0,4},{1,5},{2,6},{3,7},{4,8},{5,9},{6,10},{7,11},{8,12},{9,13},{1... | collective-permute-start | bytes 743432 | tf_op jit(solution)/shard_map/ppermute | solution.py:95
  13.5 15.0 %collective-permute-start.4 = (bf16[2,4,16,1408]{3,2,1,0:T(8,128)(2,1)S(1)}, bf16[2,4,16,1408]{3,2,1,0:T(8,128)(2,1)S(1)}, u32[]{:S(2)}, u32[]{:S(2)}) collective-permute-start(bf16[2,4,16,1408]{3,2,1,0:T(8,128)(2,1)S(1)} %shard_map.73), channel_id=1, source_target_pairs={{0,18},{1,2},{2,16},{3,0},{4,22},{5,6},{6,20},{7,4},{8,26},{9,10},... | collective-permute-start | bytes 1081352 | tf_op jit(solution)/shard_map/ppermute | solution.py:95
  19.5 11.4 %copy-start.6 = (bf16[2,4,16,1408]{3,2,1,0:T(8,128)(2,1)}, bf16[2,4,16,1408]{3,2,1,0:T(8,128)(2,1)S(1)}, u32[]{:S(2)}) copy-start(bf16[2,4,16,1408]{3,2,1,0:T(8,128)(2,1)S(1)} %collective-permute-done.1.refs_0_) | copy-start | bytes 1081348
  21.9 9.9 %copy-start.7 = (bf16[2,4,16,1408]{3,2,1,0:T(8,128)(2,1)}, bf16[2,4,16,1408]{3,2,1,0:T(8,128)(2,1)S(1)}, u32[]{:S(2)}) copy-start(bf16[2,4,16,1408]{3,2,1,0:T(8,128)(2,1)S(1)} %collective-permute-done.2.refs_1_) | copy-start | bytes 1081348
  21.9 8.9 %collective-permute-start.7 = (bf16[352,352]{1,0:T(8,128)(2,1)}, bf16[352,352]{1,0:T(8,128)(2,1)}, u32[]{:S(2)}, u32[]{:S(2)}) collective-permute-start(bf16[352,352]{1,0:T(8,128)(2,1)} %collective-permute-done.6.refs_5_), channel_id=1, source_target_pairs={{0,4},{1,5},{2,6},{3,7},{4,8},{5,9},{6,10},{7,11},{8,12},{9,13},{1... | collective-permute-start | bytes 743432 | tf_op jit(solution)/shard_map/ppermute | solution.py:95
  26.8 4.9 %copy-start.8 = (bf16[2,4,16,1408]{3,2,1,0:T(8,128)(2,1)}, bf16[2,4,16,1408]{3,2,1,0:T(8,128)(2,1)S(1)}, u32[]{:S(2)}) copy-start(bf16[2,4,16,1408]{3,2,1,0:T(8,128)(2,1)S(1)} %collective-permute-done.3.refs_2_) | copy-start | bytes 1081348
  26.8 12.2 %collective-permute-start.13 = (bf16[88,1232]{1,0:T(8,128)(2,1)}, bf16[88,1232]{1,0:T(8,128)(2,1)S(1)}, u32[]{:S(2)}, u32[]{:S(2)}) collective-permute-start(bf16[88,1232]{1,0:T(8,128)(2,1)} %get-tuple-element.47), channel_id=1, source_target_pairs={{0,1},{1,0},{2,3},{3,2},{4,5},{5,4},{6,7},{7,6},{8,9},{9,8},{10,11... | collective-permute-start | bytes 650504 | tf_op jit(solution)/shard_map/ppermute | solution.py:95
  26.8 11.6 %collective-permute-start.14 = (bf16[88,528]{1,0:T(8,128)(2,1)}, bf16[88,528]{1,0:T(8,128)(2,1)S(1)}, u32[]{:S(2)}, u32[]{:S(2)}) collective-permute-start(bf16[88,528]{1,0:T(8,128)(2,1)} %get-tuple-element.49), channel_id=1, source_target_pairs={{0,3},{1,2},{2,1},{3,0},{4,7},{5,6},{6,5},{7,4},{8,11},{9,10},{10,... | collective-permute-start | bytes 278792 | tf_op jit(solution)/shard_map/ppermute | solution.py:95
  28.5 17.7 %collective-permute-start.9 = (bf16[352,352]{1,0:T(8,128)(2,1)S(1)}, bf16[352,352]{1,0:T(8,128)(2,1)}, u32[]{:S(2)}, u32[]{:S(2)}) collective-permute-start(bf16[352,352]{1,0:T(8,128)(2,1)S(1)} %shard_map.75.refs_4_), channel_id=1, source_target_pairs={{0,1},{1,0},{2,3},{3,2},{4,5},{5,4},{6,7},{7,6},{8,9},{9,8},{10,11... | collective-permute-start | bytes 743432 | tf_op jit(solution)/shard_map/ppermute | solution.py:95
  28.5 3.3 %copy-start.9 = (bf16[2,4,16,1408]{3,2,1,0:T(8,128)(2,1)}, bf16[2,4,16,1408]{3,2,1,0:T(8,128)(2,1)S(1)}, u32[]{:S(2)}) copy-start(bf16[2,4,16,1408]{3,2,1,0:T(8,128)(2,1)S(1)} %collective-permute-done.4.refs_3_) | copy-start | bytes 1081348
  30.8 15.9 %collective-permute-start.8 = (bf16[352,352]{1,0:T(8,128)(2,1)}, bf16[352,352]{1,0:T(8,128)(2,1)}, u32[]{:S(2)}, u32[]{:S(2)}) collective-permute-start(bf16[352,352]{1,0:T(8,128)(2,1)} %collective-permute-done.7.refs_6_), channel_id=1, source_target_pairs={{0,4},{1,5},{2,6},{3,7},{4,8},{5,9},{6,10},{7,11},{8,12},{9,13},{1... | collective-permute-start | bytes 743432 | tf_op jit(solution)/shard_map/ppermute | solution.py:95
  31.8 5.4 %collective-permute-start = (s32[4]{0:T(128)S(1)}, s32[4]{0:T(128)S(1)}, u32[]{:S(2)}, u32[]{:S(2)}) collective-permute-start(s32[4]{0:T(128)S(1)} %copy-done.10), channel_id=1, source_target_pairs={{0,0},{1,16},{2,2},{3,18},{4,4},{5,20},{6,6},{7,22},{8,8},{9,24},{... | collective-permute-start | bytes 56 | tf_op jit(solution)/shard_map/ppermute | solution.py:95
  38.4 0.6 copy-start.4
  39.1 0.9 copy-start.3
  40.0 0.9 copy-start.5
  41.8 22.1 %collective-permute-start.15 = (bf16[352,704]{1,0:T(8,128)(2,1)S(1)}, bf16[352,704]{1,0:T(8,128)(2,1)S(1)}, u32[]{:S(2)}, u32[]{:S(2)}) collective-permute-start(bf16[352,704]{1,0:T(8,128)(2,1)S(1)} %shard_map.77.refs_0_), channel_id=1, source_target_pairs={{0,4},{1,5},{2,6},{3,7},{4,0},{5,1},{6,2},{7,3},{8,12},{9,13},{10,... | collective-permute-start | bytes 1486856 | tf_op jit(solution)/shard_map/ppermute | solution.py:95
  43.0 28.4 %collective-permute-start.22 = (bf16[352,704]{1,0:T(8,128)(2,1)S(1)}, bf16[352,704]{1,0:T(8,128)(2,1)}, u32[]{:S(2)}, u32[]{:S(2)}) collective-permute-start(bf16[352,704]{1,0:T(8,128)(2,1)S(1)} %shard_map.77.refs_0_), channel_id=1, source_target_pairs={{0,8},{1,9},{2,10},{3,11},{4,12},{5,13},{6,14},{7,15},{8,0},{9,1},... | collective-permute-start | bytes 1486856 | tf_op jit(solution)/shard_map/ppermute | solution.py:95
  46.1 2.5 %collective-permute-start.10 = (bf16[352,352]{1,0:T(8,128)(2,1)}, bf16[352,352]{1,0:T(8,128)(2,1)}, u32[]{:S(2)}, u32[]{:S(2)}) collective-permute-start(bf16[352,352]{1,0:T(8,128)(2,1)} %collective-permute-done.6.refs_5_), channel_id=1, source_target_pairs={{0,1},{1,0},{2,3},{3,2},{4,5},{5,4},{6,7},{7,6},{8,9},{9,8},{10,11... | collective-permute-start | bytes 743432 | tf_op jit(solution)/shard_map/ppermute | solution.py:95
  46.2 2.5 %collective-permute-start.11 = (bf16[352,352]{1,0:T(8,128)(2,1)}, bf16[352,352]{1,0:T(8,128)(2,1)}, u32[]{:S(2)}, u32[]{:S(2)}) collective-permute-start(bf16[352,352]{1,0:T(8,128)(2,1)} %collective-permute-done.7.refs_6_), channel_id=1, source_target_pairs={{0,1},{1,0},{2,3},{3,2},{4,5},{5,4},{6,7},{7,6},{8,9},{9,8},{10,11... | collective-permute-start | bytes 743432 | tf_op jit(solution)/shard_map/ppermute | solution.py:95
  46.7 2.1 %collective-permute-start.12 = (bf16[352,352]{1,0:T(8,128)(2,1)}, bf16[352,352]{1,0:T(8,128)(2,1)}, u32[]{:S(2)}, u32[]{:S(2)}) collective-permute-start(bf16[352,352]{1,0:T(8,128)(2,1)} %collective-permute-done.8.refs_7_), channel_id=1, source_target_pairs={{0,1},{1,0},{2,3},{3,2},{4,5},{5,4},{6,7},{7,6},{8,9},{9,8},{10,11... | collective-permute-start | bytes 743432 | tf_op jit(solution)/shard_map/ppermute | solution.py:95
  63.9 5.0 %collective-permute-start.16 = (bf16[4,16,352]{2,1,0:T(8,128)(2,1)S(1)}, bf16[4,16,352]{2,1,0:T(8,128)(2,1)S(1)}, u32[]{:S(2)}, u32[]{:S(2)}) collective-permute-start(bf16[4,16,352]{2,1,0:T(8,128)(2,1)S(1)} %get-tuple-element.52), channel_id=1, source_target_pairs={{0,4},{1,5},{2,6},{3,7},{4,8},{5,9},{6,10},{7,11},{8,12},{9,13},{1... | collective-permute-start | bytes 135176 | tf_op jit(solution)/shard_map/ppermute | solution.py:95
  63.9 6.3 %collective-permute-start.17 = (bf16[4,16,352]{2,1,0:T(8,128)(2,1)S(1)}, bf16[4,16,352]{2,1,0:T(8,128)(2,1)S(1)}, u32[]{:S(2)}, u32[]{:S(2)}) collective-permute-start(bf16[4,16,352]{2,1,0:T(8,128)(2,1)S(1)} %get-tuple-element.54), channel_id=1, source_target_pairs={{0,8},{1,9},{2,10},{3,11},{4,12},{5,13},{6,14},{7,15},{8,0},{9,1},... | collective-permute-start | bytes 135176 | tf_op jit(solution)/shard_map/ppermute | solution.py:95
  66.3 4.2 %collective-permute-start.18 = (bf16[4,16,352]{2,1,0:T(8,128)(2,1)S(1)}, bf16[4,16,352]{2,1,0:T(8,128)(2,1)S(1)}, u32[]{:S(2)}, u32[]{:S(2)}) collective-permute-start(bf16[4,16,352]{2,1,0:T(8,128)(2,1)S(1)} %get-tuple-element.56), channel_id=1, source_target_pairs={{0,12},{1,13},{2,14},{3,15},{4,0},{5,1},{6,2},{7,3},{8,4},{9,5},{1... | collective-permute-start | bytes 135176 | tf_op jit(solution)/shard_map/ppermute | solution.py:95
  71.4 14.2 %collective-permute-start.23 = (bf16[352,704]{1,0:T(8,128)(2,1)}, bf16[352,704]{1,0:T(8,128)(2,1)S(1)}, u32[]{:S(2)}, u32[]{:S(2)}) collective-permute-start(bf16[352,704]{1,0:T(8,128)(2,1)} %collective-permute-done.22.refs_2_), channel_id=1, source_target_pairs={{0,4},{1,5},{2,6},{3,7},{4,0},{5,1},{6,2},{7,3},{8,12},{9,13},{10,... | collective-permute-start | bytes 1486856 | tf_op jit(solution)/shard_map/ppermute | solution.py:95
  72.5 5.8 %collective-permute-start.19 = (bf16[4,4,16,352]{3,2,1,0:T(8,128)(2,1)S(1)}, bf16[4,4,16,352]{3,2,1,0:T(8,128)(2,1)S(1)}, u32[]{:S(2)}, u32[]{:S(2)}) collective-permute-start(bf16[4,4,16,352]{3,2,1,0:T(8,128)(2,1)S(1)} %shard_map.78.refs_0_), channel_id=1, source_target_pairs={{0,16},{1,17},{2,18},{3,19},{4,20},{5,21},{6,22},{7,23},{8,24},{9,... | collective-permute-start | bytes 540680 | tf_op jit(solution)/shard_map/ppermute | solution.py:95
  72.9 5.4 %collective-permute-start.20 = (bf16[4,4,16,352]{3,2,1,0:T(8,128)(2,1)S(1)}, bf16[4,4,16,352]{3,2,1,0:T(8,128)(2,1)S(1)}, u32[]{:S(2)}, u32[]{:S(2)}) collective-permute-start(bf16[4,4,16,352]{3,2,1,0:T(8,128)(2,1)S(1)} %shard_map.78.refs_0_), channel_id=1, source_target_pairs={{0,2},{1,3},{2,0},{3,1},{4,6},{5,7},{6,4},{7,5},{8,10},{9,11},{10,... | collective-permute-start | bytes 540680 | tf_op jit(solution)/shard_map/ppermute | solution.py:95
  74.2 8.3 %collective-permute-start.21 = (bf16[4,4,16,352]{3,2,1,0:T(8,128)(2,1)S(1)}, bf16[4,4,16,352]{3,2,1,0:T(8,128)(2,1)S(1)}, u32[]{:S(2)}, u32[]{:S(2)}) collective-permute-start(bf16[4,4,16,352]{3,2,1,0:T(8,128)(2,1)S(1)} %shard_map.78.refs_0_), channel_id=1, source_target_pairs={{0,18},{1,19},{2,16},{3,17},{4,22},{5,23},{6,20},{7,21},{8,26},{9,... | collective-permute-start | bytes 540680 | tf_op jit(solution)/shard_map/ppermute | solution.py:95
  82.5 5.1 %collective-permute-start.24 = (bf16[352,704]{1,0:T(8,128)(2,1)S(1)}, bf16[352,704]{1,0:T(8,128)(2,1)S(1)}, u32[]{:S(2)}, u32[]{:S(2)}) collective-permute-start(bf16[352,704]{1,0:T(8,128)(2,1)S(1)} %shard_map.77.refs_0_), channel_id=1, source_target_pairs={{0,1},{1,0},{2,3},{3,2},{4,5},{5,4},{6,7},{7,6},{8,9},{9,8},{10,11... | collective-permute-start | bytes 1486856 | tf_op jit(solution)/shard_map/ppermute | solution.py:95
  85.0 3.1 %collective-permute-start.25 = (bf16[352,704]{1,0:T(8,128)(2,1)S(1)}, bf16[352,704]{1,0:T(8,128)(2,1)S(1)}, u32[]{:S(2)}, u32[]{:S(2)}) collective-permute-start(bf16[352,704]{1,0:T(8,128)(2,1)S(1)} %collective-permute-done.15.refs_1_), channel_id=1, source_target_pairs={{0,1},{1,0},{2,3},{3,2},{4,5},{5,4},{6,7},{7,6},{8,9},{9,8},{10,11... | collective-permute-start | bytes 1486856 | tf_op jit(solution)/shard_map/ppermute | solution.py:95
  85.0 3.3 %collective-permute-start.26 = (bf16[352,704]{1,0:T(8,128)(2,1)}, bf16[352,704]{1,0:T(8,128)(2,1)S(1)}, u32[]{:S(2)}, u32[]{:S(2)}) collective-permute-start(bf16[352,704]{1,0:T(8,128)(2,1)} %collective-permute-done.22.refs_2_), channel_id=1, source_target_pairs={{0,1},{1,0},{2,3},{3,2},{4,5},{5,4},{6,7},{7,6},{8,9},{9,8},{10,11... | collective-permute-start | bytes 1486856 | tf_op jit(solution)/shard_map/ppermute | solution.py:95
  85.6 3.4 %collective-permute-start.27 = (bf16[352,704]{1,0:T(8,128)(2,1)S(1)}, bf16[352,704]{1,0:T(8,128)(2,1)S(1)}, u32[]{:S(2)}, u32[]{:S(2)}) collective-permute-start(bf16[352,704]{1,0:T(8,128)(2,1)S(1)} %collective-permute-done.23.refs_3_), channel_id=1, source_target_pairs={{0,1},{1,0},{2,3},{3,2},{4,5},{5,4},{6,7},{7,6},{8,9},{9,8},{10,11... | collective-permute-start | bytes 1486856 | tf_op jit(solution)/shard_map/ppermute | solution.py:95
  96.7 6.2 %collective-permute-start.28 = (bf16[2,64,704]{2,1,0:T(8,128)(2,1)S(1)}, bf16[2,64,704]{2,1,0:T(8,128)(2,1)S(1)}, u32[]{:S(2)}, u32[]{:S(2)}) collective-permute-start(bf16[2,64,704]{2,1,0:T(8,128)(2,1)S(1)} %get-tuple-element.64), channel_id=1, source_target_pairs={{0,16},{1,17},{2,18},{3,19},{4,20},{5,21},{6,22},{7,23},{8,24},{9,... | collective-permute-start | bytes 540680 | tf_op jit(solution)/shard_map/ppermute | solution.py:95
  97.2 5.8 %collective-permute-start.29 = (bf16[2,64,704]{2,1,0:T(8,128)(2,1)S(1)}, bf16[2,64,704]{2,1,0:T(8,128)(2,1)S(1)}, u32[]{:S(2)}, u32[]{:S(2)}) collective-permute-start(bf16[2,64,704]{2,1,0:T(8,128)(2,1)S(1)} %get-tuple-element.65), channel_id=1, source_target_pairs={{0,2},{1,3},{2,0},{3,1},{4,6},{5,7},{6,4},{7,5},{8,10},{9,11},{10,... | collective-permute-start | bytes 540680 | tf_op jit(solution)/shard_map/ppermute | solution.py:95
  98.0 10.0 %collective-permute-start.30 = (bf16[2,64,704]{2,1,0:T(8,128)(2,1)S(1)}, bf16[2,64,704]{2,1,0:T(8,128)(2,1)S(1)}, u32[]{:S(2)}, u32[]{:S(2)}) collective-permute-start(bf16[2,64,704]{2,1,0:T(8,128)(2,1)S(1)} %get-tuple-element.66), channel_id=1, source_target_pairs={{0,18},{1,19},{2,16},{3,17},{4,22},{5,23},{6,20},{7,21},{8,26},{9,... | collective-permute-start | bytes 540680 | tf_op jit(solution)/shard_map/ppermute | solution.py:95
  108.7 7.7 %collective-permute-start.31 = (bf16[16,1408]{1,0:T(8,128)(2,1)S(1)}, bf16[16,1408]{1,0:T(8,128)(2,1)S(1)}, u32[]{:S(2)}, u32[]{:S(2)}) collective-permute-start(bf16[16,1408]{1,0:T(8,128)(2,1)S(1)} %get-tuple-element.67), channel_id=1, source_target_pairs={{0,0},{1,16},{2,2},{3,18},{4,4},{5,20},{6,6},{7,22},{8,8},{9,24},{... | collective-permute-start | bytes 135176 | tf_op jit(solution)/shard_map/ppermute | solution.py:95
  112.3 4.7 %collective-permute-start.32 = (bf16[16,1408]{1,0:T(8,128)(2,1)S(1)}, bf16[16,1408]{1,0:T(8,128)(2,1)S(1)}, u32[]{:S(2)}, u32[]{:S(2)}) collective-permute-start(bf16[16,1408]{1,0:T(8,128)(2,1)S(1)} %get-tuple-element.68), channel_id=1, source_target_pairs={{0,12},{1,28},{2,14},{3,30},{4,0},{5,16},{6,2},{7,18},{8,4},{9,20}... | collective-permute-start | bytes 135176 | tf_op jit(solution)/shard_map/ppermute | solution.py:95
  113.7 5.4 %collective-permute-start.33 = (bf16[16,1408]{1,0:T(8,128)(2,1)S(1)}, bf16[16,1408]{1,0:T(8,128)(2,1)S(1)}, u32[]{:S(2)}, u32[]{:S(2)}) collective-permute-start(bf16[16,1408]{1,0:T(8,128)(2,1)S(1)} %get-tuple-element.69), channel_id=1, source_target_pairs={{0,8},{1,24},{2,10},{3,26},{4,12},{5,28},{6,14},{7,30},{8,0},{9,16... | collective-permute-start | bytes 135176 | tf_op jit(solution)/shard_map/ppermute | solution.py:95
  114.8 6.2 %collective-permute-start.34 = (bf16[16,1408]{1,0:T(8,128)(2,1)S(1)}, bf16[16,1408]{1,0:T(8,128)(2,1)S(1)}, u32[]{:S(2)}, u32[]{:S(2)}) collective-permute-start(bf16[16,1408]{1,0:T(8,128)(2,1)S(1)} %get-tuple-element.70), channel_id=1, source_target_pairs={{0,4},{1,20},{2,6},{3,22},{4,8},{5,24},{6,10},{7,26},{8,12},{9,28}... | collective-permute-start | bytes 135176 | tf_op jit(solution)/shard_map/ppermute | solution.py:95

commit v9 on v8

--- a/solution.py
+++ b/solution.py
@@ -392,7 +392,6 @@
     (joined,) = call(
         join_kernel, [(2, S, local, width)], p.where, hidden, skip, copies=2, fast=[0], still=True
     )
-    own = qkvs[0]
     qkvs[1 * G] = swap(qkvs[1 * G], 1, 0)
     parts = [
         p.send(joined, lambda x, z, y, c, e=e, d=d: (c - d, z, y - e, x))
@@ -456,7 +455,8 @@
         fast=range(S),
     )
     pieces = [pieces[0]] + [
-        p.send(after(pieces[s], held[1], mods), lambda x, z, y, c, s=s: (x, z + s, y, c)) for s in range(1, S)
+        p.send(after(pieces[s], held[1], mods), lambda x, z, y, c, s=s: (x, z + s, y, c))
+        for s in range(1, S)
     ]
     (merged,) = call(stack_kernel, [(S, blocks, local, cols)], p.where, *pieces, copies=S)
     held.append(p.send(after(held[2], merged), lambda x, z, y, c: (x, z ^ 1, y, c)))
@@ -519,10 +519,10 @@
         seqs, _, width = hidden.shape
         blocks = n // seqs
         fits = (
-            n % seqs == 0
-            and blocks % groups == 0
+            groups == 2
+            and blocks == groups * groups
+            and n == seqs * blocks
             and blocks == seqs
-            and seqs % groups == 0
             and w_out.shape[0] == HD
             and width % blocks == 0
             and (width // blocks) % 16 == 0

time: 123 us -> 123 us (level)
  no operation moved by 1% of the time
where the time goes in v9:
time: 123 us; the launch traced here: 122 us
  waiting for transfers between devices  49.7 us (40%)
  starting transfers between devices  44.2 us (36%)
  Pallas kernels  22.4 us (18%)
  local copies, waits for them, and re-layouts  3.9 us (3%)
    ppermute x35, waiting for transfers between devices, send(): return lax.ppermute(value, ('group', 'seq'), pairs)  49.7 us
    ppermute x35, starting transfers between devices, send(): return lax.ppermute(value, ('group', 'seq'), pairs)  44.2 us
    pallas_call x10, Pallas kernels, call(): pl.pallas_call(kernel, out_shape=[jax.ShapeDtypeStruct(s, BF) for s in ou...  22.4 us
    unnamed x22, local copies, waits for them, and re-layouts  2.48 us
  transfers between devices with their start and end apart: 35, of which 21 were waited for; matrix products, arithmetic and copies ran while one was open for 2% of the time, Pallas kernels for 7%

profile of v9, /device:TPU:1, one launch (start us, length us, event | category | flops | bytes accessed | tf_op | source)
XLA Modules:
  0.0 122.4 jit_solution(3745222529313075727)
XLA Ops:
  0.1 3.6 %shard_map.74 = (bf16[176,352]{1,0:T(8,128)(2,1)S(1)}, bf16[88,528]{1,0:T(8,128)(2,1)S(1)}, bf16[88,1232]{1,0:T(8,128)(2,1)}, bf16[88,1232]{1,0:T(8,128)(2,1)S(1...) custom-call(s32[4]{0:T(128)S(1)} %pad_add_fusion.where, bf16[176,1408]{1,0:T(8,128)(2,1)} %w_skip_any.1, ...), custom_call_target="tpu_custom_call" | custom-call | bytes 2973696 | tf_op jit(solution)/shard_map/pallas_call | solution.py:105
  3.7 2.2 %collective-permute-start.5 = (bf16[88,1232]{1,0:T(8,128)(2,1)S(1)}, bf16[88,1232]{1,0:T(8,128)(2,1)S(1)}, u32[]{:S(2)}, u32[]{:S(2)}) collective-permute-start(bf16[88,1232]{1,0:T(8,128)(2,1)S(1)} %get-tuple-element.40), channel_id=1, source_target_pairs={{0,2},{1,3},{2,0},{3,1},{4,6},{5,7},{6,4},{7,5},{8,10},{9,11},{10,... | collective-permute-start | bytes 650504 | tf_op jit(solution)/shard_map/ppermute | solution.py:95
  5.9 1.6 %shard_map.73 = bf16[2,4,16,1408]{3,2,1,0:T(8,128)(2,1)S(1)} custom-call(s32[4]{0:T(128)S(1)} %pad_add_fusion.where, bf16[4,16,1408]{2,1,0:T(8,128)(2,1)} %hidden.1, bf16[4,16,1408]{2,1,0:T(8,128)(2,1)} %skip.1), custom_call_target="tpu_custom_call" | custom-call | bytes 720896 | tf_op jit(solution)/shard_map/pallas_call | solution.py:105
  7.5 3.8 %collective-permute-start.1 = (bf16[2,4,16,1408]{3,2,1,0:T(8,128)(2,1)S(1)}, bf16[2,4,16,1408]{3,2,1,0:T(8,128)(2,1)S(1)}, u32[]{:S(2)}, u32[]{:S(2)}) collective-permute-start(bf16[2,4,16,1408]{3,2,1,0:T(8,128)(2,1)S(1)} %shard_map.73), channel_id=1, source_target_pairs={{0,0},{1,16},{2,2},{3,18},{4,4},{5,20},{6,6},{7,22},{8,8},{9,24},{... | collective-permute-start | bytes 1081352 | tf_op jit(solution)/shard_map/ppermute | solution.py:95
  11.4 0.7 shard_map.75.refs_4_
  12.2 1.3 %collective-permute-start.6 = (bf16[352,352]{1,0:T(8,128)(2,1)S(1)}, bf16[352,352]{1,0:T(8,128)(2,1)}, u32[]{:S(2)}, u32[]{:S(2)}) collective-permute-start(bf16[352,352]{1,0:T(8,128)(2,1)S(1)} %shard_map.75.refs_4_), channel_id=1, source_target_pairs={{0,4},{1,5},{2,6},{3,7},{4,8},{5,9},{6,10},{7,11},{8,12},{9,13},{1... | collective-permute-start | bytes 743432 | tf_op jit(solution)/shard_map/ppermute | solution.py:95
  13.5 2.6 %collective-permute-start.4 = (bf16[2,4,16,1408]{3,2,1,0:T(8,128)(2,1)S(1)}, bf16[2,4,16,1408]{3,2,1,0:T(8,128)(2,1)S(1)}, u32[]{:S(2)}, u32[]{:S(2)}) collective-permute-start(bf16[2,4,16,1408]{3,2,1,0:T(8,128)(2,1)S(1)} %shard_map.73), channel_id=1, source_target_pairs={{0,18},{1,2},{2,16},{3,0},{4,22},{5,6},{6,20},{7,4},{8,26},{9,10},... | collective-permute-start | bytes 1081352 | tf_op jit(solution)/shard_map/ppermute | solution.py:95
  16.1 3.4 %collective-permute-done.1.refs_0_ = bf16[2,4,16,1408]{3,2,1,0:T(8,128)(2,1)S(1)} collective-permute-done((bf16[2,4,16,1408]{3,2,1,0:T(8,128)(2,1)S(1)}, bf16[2,4,16,1408]{3,2,1,0:T(8,128)(2,1)S(1)}, u32[]{:S(2)}, u32[]{:S(2)}) %collective-permute-start.1) | collective-permute-done | bytes 360480 | tf_op jit(solution)/shard_map/ppermute | solution.py:95
  19.5 2.4 %collective-permute-done.2.refs_1_ = bf16[2,4,16,1408]{3,2,1,0:T(8,128)(2,1)S(1)} collective-permute-done((bf16[2,4,16,1408]{3,2,1,0:T(8,128)(2,1)S(1)}, bf16[2,4,16,1408]{3,2,1,0:T(8,128)(2,1)S(1)}, u32[]{:S(2)}, u32[]{:S(2)}) %collective-permute-start.2) | collective-permute-done | bytes 360480 | tf_op jit(solution)/shard_map/ppermute | solution.py:95
  21.9 1.2 collective-permute-start.7
  23.1 3.7 %collective-permute-done.3.refs_2_ = bf16[2,4,16,1408]{3,2,1,0:T(8,128)(2,1)S(1)} collective-permute-done((bf16[2,4,16,1408]{3,2,1,0:T(8,128)(2,1)S(1)}, bf16[2,4,16,1408]{3,2,1,0:T(8,128)(2,1)S(1)}, u32[]{:S(2)}, u32[]{:S(2)}) %collective-permute-start.3) | collective-permute-done | bytes 360480 | tf_op jit(solution)/shard_map/ppermute | solution.py:95
  26.8 1.6 %collective-permute-start.14 = (bf16[88,528]{1,0:T(8,128)(2,1)}, bf16[88,528]{1,0:T(8,128)(2,1)S(1)}, u32[]{:S(2)}, u32[]{:S(2)}) collective-permute-start(bf16[88,528]{1,0:T(8,128)(2,1)} %get-tuple-element.49), channel_id=1, source_target_pairs={{0,3},{1,2},{2,1},{3,0},{4,7},{5,6},{6,5},{7,4},{8,11},{9,10},{10,... | collective-permute-start | bytes 278792 | tf_op jit(solution)/shard_map/ppermute | solution.py:95
  28.5 2.3 %collective-permute-done.7.refs_6_ = bf16[352,352]{1,0:T(8,128)(2,1)} collective-permute-done((bf16[352,352]{1,0:T(8,128)(2,1)}, bf16[352,352]{1,0:T(8,128)(2,1)}, u32[]{:S(2)}, u32[]{:S(2)}) %collective-permute-start.7) | collective-permute-done | bytes 247840 | tf_op jit(solution)/shard_map/ppermute | solution.py:95
  30.8 0.9 collective-permute-start.8
  31.8 4.2 %collective-permute-start = (s32[4]{0:T(128)S(1)}, s32[4]{0:T(128)S(1)}, u32[]{:S(2)}, u32[]{:S(2)}) collective-permute-start(s32[4]{0:T(128)S(1)} %copy-done.10), channel_id=1, source_target_pairs={{0,0},{1,16},{2,2},{3,18},{4,4},{5,20},{6,6},{7,22},{8,8},{9,24},{... | collective-permute-start | bytes 56 | tf_op jit(solution)/shard_map/ppermute | solution.py:95
  36.0 1.2 collective-permute-done
  37.2 0.6 dynamic_slice.3
  38.4 0.6 copy-done.4
  39.1 0.9 copy-done.3
  40.0 0.9 copy-done.5
  40.9 0.9 shard_map.77.refs_0_
  41.8 1.2 collective-permute-start.15
  43.0 3.1 %collective-permute-start.22 = (bf16[352,704]{1,0:T(8,128)(2,1)S(1)}, bf16[352,704]{1,0:T(8,128)(2,1)}, u32[]{:S(2)}, u32[]{:S(2)}) collective-permute-start(bf16[352,704]{1,0:T(8,128)(2,1)S(1)} %shard_map.77.refs_0_), channel_id=1, source_target_pairs={{0,8},{1,9},{2,10},{3,11},{4,12},{5,13},{6,14},{7,15},{8,0},{9,1},... | collective-permute-start | bytes 1486856 | tf_op jit(solution)/shard_map/ppermute | solution.py:95
  46.2 0.5 collective-permute-start.11
  46.8 0.4 fusion.3
  47.2 0.7 reduce
  47.9 0.8 reshape.35.refs_4_.mods
  48.7 0.2 collective-permute-done.12.refs_11_
  48.9 3.7 %shard_map.76 = (bf16[4,16,352]{2,1,0:T(8,128)(2,1)S(1)}, bf16[4,16,352]{2,1,0:T(8,128)(2,1)S(1)}, bf16[4,16,352]{2,1,0:T(8,128)(2,1)S(1)}, bf16[4,16,352]{2,1,0:T(8,128)(2,1)S(1)}) custom-call(s32[4]{0:T(128)S(1)} %pad_add_fusion.where, bf16[2,4,16,1408]{3,2,1,0:T(8,128)(2,1)} %copy-done.6, bf16[2,4,16,1408]{3,2,1,0:T(8,128)(2,1)} %copy-done.7, ...), custom_call_target="tpu_custom_call" | custom-call | flops 507510784 | bytes 6848512 | tf_op jit(solution)/shard_map/pallas_call | solution.py:105
  52.6 11.3 %collective-permute-done.15.refs_1_ = bf16[352,704]{1,0:T(8,128)(2,1)S(1)} collective-permute-done((bf16[352,704]{1,0:T(8,128)(2,1)S(1)}, bf16[352,704]{1,0:T(8,128)(2,1)S(1)}, u32[]{:S(2)}, u32[]{:S(2)}) %collective-permute-start.15) | collective-permute-done | bytes 495648 | tf_op jit(solution)/shard_map/ppermute | solution.py:95
  63.9 2.4 %collective-permute-start.17 = (bf16[4,16,352]{2,1,0:T(8,128)(2,1)S(1)}, bf16[4,16,352]{2,1,0:T(8,128)(2,1)S(1)}, u32[]{:S(2)}, u32[]{:S(2)}) collective-permute-start(bf16[4,16,352]{2,1,0:T(8,128)(2,1)S(1)} %get-tuple-element.54), channel_id=1, source_target_pairs={{0,8},{1,9},{2,10},{3,11},{4,12},{5,13},{6,14},{7,15},{8,0},{9,1},... | collective-permute-start | bytes 135176 | tf_op jit(solution)/shard_map/ppermute | solution.py:95
  66.3 0.9 collective-permute-start.18
  67.2 1.7 %collective-permute-done.16.refs_1_ = bf16[4,16,352]{2,1,0:T(8,128)(2,1)S(1)} collective-permute-done((bf16[4,16,352]{2,1,0:T(8,128)(2,1)S(1)}, bf16[4,16,352]{2,1,0:T(8,128)(2,1)S(1)}, u32[]{:S(2)}, u32[]{:S(2)}) %collective-permute-start.16) | collective-permute-done | bytes 45088 | tf_op jit(solution)/shard_map/ppermute | solution.py:95
  68.8 1.4 %collective-permute-done.17.refs_2_ = bf16[4,16,352]{2,1,0:T(8,128)(2,1)S(1)} collective-permute-done((bf16[4,16,352]{2,1,0:T(8,128)(2,1)S(1)}, bf16[4,16,352]{2,1,0:T(8,128)(2,1)S(1)}, u32[]{:S(2)}, u32[]{:S(2)}) %collective-permute-start.17) | collective-permute-done | bytes 45088 | tf_op jit(solution)/shard_map/ppermute | solution.py:95
  70.2 0.3 collective-permute-done.18.refs_3_
  70.5 0.8 shard_map.78.refs_0_
  71.4 1.1 collective-permute-start.23
  72.5 0.4 collective-permute-start.19
  72.9 1.3 %collective-permute-start.20 = (bf16[4,4,16,352]{3,2,1,0:T(8,128)(2,1)S(1)}, bf16[4,4,16,352]{3,2,1,0:T(8,128)(2,1)S(1)}, u32[]{:S(2)}, u32[]{:S(2)}) collective-permute-start(bf16[4,4,16,352]{3,2,1,0:T(8,128)(2,1)S(1)} %shard_map.78.refs_0_), channel_id=1, source_target_pairs={{0,2},{1,3},{2,0},{3,1},{4,6},{5,7},{6,4},{7,5},{8,10},{9,11},{10,... | collective-permute-start | bytes 540680 | tf_op jit(solution)/shard_map/ppermute | solution.py:95
  74.2 1.0 collective-permute-start.21
  75.1 3.1 %collective-permute-done.19.refs_1_ = bf16[4,4,16,352]{3,2,1,0:T(8,128)(2,1)S(1)} collective-permute-done((bf16[4,4,16,352]{3,2,1,0:T(8,128)(2,1)S(1)}, bf16[4,4,16,352]{3,2,1,0:T(8,128)(2,1)S(1)}, u32[]{:S(2)}, u32[]{:S(2)}) %collective-permute-start.19) | collective-permute-done | bytes 180256 | tf_op jit(solution)/shard_map/ppermute | solution.py:95
  78.2 4.2 %collective-permute-done.21.refs_3_ = bf16[4,4,16,352]{3,2,1,0:T(8,128)(2,1)S(1)} collective-permute-done((bf16[4,4,16,352]{3,2,1,0:T(8,128)(2,1)S(1)}, bf16[4,4,16,352]{3,2,1,0:T(8,128)(2,1)S(1)}, u32[]{:S(2)}, u32[]{:S(2)}) %collective-permute-start.21) | collective-permute-done | bytes 180256 | tf_op jit(solution)/shard_map/ppermute | solution.py:95
  82.5 2.5 %collective-permute-start.24 = (bf16[352,704]{1,0:T(8,128)(2,1)S(1)}, bf16[352,704]{1,0:T(8,128)(2,1)S(1)}, u32[]{:S(2)}, u32[]{:S(2)}) collective-permute-start(bf16[352,704]{1,0:T(8,128)(2,1)S(1)} %shard_map.77.refs_0_), channel_id=1, source_target_pairs={{0,1},{1,0},{2,3},{3,2},{4,5},{5,4},{6,7},{7,6},{8,9},{9,8},{10,11... | collective-permute-start | bytes 1486856 | tf_op jit(solution)/shard_map/ppermute | solution.py:95
  85.0 0.5 collective-permute-start.26
  85.6 0.8 collective-permute-start.27
  86.4 1.3 %shard_map.79 = (bf16[4,256,352]{2,1,0:T(8,128)(2,1)S(1)}, bf16[4,64,352]{2,1,0:T(8,128)(2,1)S(1)}) custom-call(s32[4]{0:T(128)S(1)} %pad_add_fusion.where, bf16[4,4,16,352]{3,2,1,0:T(8,128)(2,1)S(1)} %shard_map.78.refs_0_, bf16[4,4,16,352]{3,2,1,0:T(8,128)(2,1)S(1)} %collective-permute-done.19.refs_1_, ...), custom_call_target="tpu_custom_call" | custom-call | bytes 1475584 | tf_op jit(solution)/shard_map/pallas_call | solution.py:105
  87.6 0.5 collective-permute-done.25.refs_5_
  88.1 0.2 collective-permute-done.26.refs_6_
  88.4 0.6 collective-permute-done.27.refs_7_
  88.9 7.8 %shard_map.80 = (bf16[2,64,704]{2,1,0:T(8,128)(2,1)S(1)}, bf16[2,64,704]{2,1,0:T(8,128)(2,1)S(1)}, bf16[2,64,704]{2,1,0:T(8,128)(2,1)S(1)}, bf16[2,64,704]{2,1,0:T(8,128)(2,1)S(1)}) custom-call(s32[4]{0:T(128)S(1)} %pad_add_fusion.where, bf16[4,256,352]{2,1,0:T(8,128)(2,1)S(1)} %get-tuple-element.58.norm, bf16[352,704]{1,0:T(8,128)(2,1)S(1)} %shard_map.77.refs_0_, ...), custom_call_target="tpu_custom_call" | custom-call | flops 1268776960 | bytes 9371648 | tf_op jit(solution)/shard_map/pallas_call | solution.py:105
  96.7 0.5 collective-permute-start.28
  97.2 0.8 collective-permute-start.29
  98.0 1.4 %collective-permute-start.30 = (bf16[2,64,704]{2,1,0:T(8,128)(2,1)S(1)}, bf16[2,64,704]{2,1,0:T(8,128)(2,1)S(1)}, u32[]{:S(2)}, u32[]{:S(2)}) collective-permute-start(bf16[2,64,704]{2,1,0:T(8,128)(2,1)S(1)} %get-tuple-element.66), channel_id=1, source_target_pairs={{0,18},{1,19},{2,16},{3,17},{4,22},{5,23},{6,20},{7,21},{8,26},{9,... | collective-permute-start | bytes 540680 | tf_op jit(solution)/shard_map/ppermute | solution.py:95
  99.4 3.5 %collective-permute-done.28.refs_1_ = bf16[2,64,704]{2,1,0:T(8,128)(2,1)S(1)} collective-permute-done((bf16[2,64,704]{2,1,0:T(8,128)(2,1)S(1)}, bf16[2,64,704]{2,1,0:T(8,128)(2,1)S(1)}, u32[]{:S(2)}, u32[]{:S(2)}) %collective-permute-start.28) | collective-permute-done | bytes 180256 | tf_op jit(solution)/shard_map/ppermute | solution.py:95
  103.0 5.0 %collective-permute-done.30.refs_3_ = bf16[2,64,704]{2,1,0:T(8,128)(2,1)S(1)} collective-permute-done((bf16[2,64,704]{2,1,0:T(8,128)(2,1)S(1)}, bf16[2,64,704]{2,1,0:T(8,128)(2,1)S(1)}, u32[]{:S(2)}, u32[]{:S(2)}) %collective-permute-start.30) | collective-permute-done | bytes 180256 | tf_op jit(solution)/shard_map/ppermute | solution.py:95
  108.0 0.7 shard_map.81
  108.7 3.5 %collective-permute-start.31 = (bf16[16,1408]{1,0:T(8,128)(2,1)S(1)}, bf16[16,1408]{1,0:T(8,128)(2,1)S(1)}, u32[]{:S(2)}, u32[]{:S(2)}) collective-permute-start(bf16[16,1408]{1,0:T(8,128)(2,1)S(1)} %get-tuple-element.67), channel_id=1, source_target_pairs={{0,0},{1,16},{2,2},{3,18},{4,4},{5,20},{6,6},{7,22},{8,8},{9,24},{... | collective-permute-start | bytes 135176 | tf_op jit(solution)/shard_map/ppermute | solution.py:95
  112.3 1.4 %collective-permute-start.32 = (bf16[16,1408]{1,0:T(8,128)(2,1)S(1)}, bf16[16,1408]{1,0:T(8,128)(2,1)S(1)}, u32[]{:S(2)}, u32[]{:S(2)}) collective-permute-start(bf16[16,1408]{1,0:T(8,128)(2,1)S(1)} %get-tuple-element.68), channel_id=1, source_target_pairs={{0,12},{1,28},{2,14},{3,30},{4,0},{5,16},{6,2},{7,18},{8,4},{9,20}... | collective-permute-start | bytes 135176 | tf_op jit(solution)/shard_map/ppermute | solution.py:95
  113.7 1.1 collective-permute-start.33
  114.8 1.6 %collective-permute-start.34 = (bf16[16,1408]{1,0:T(8,128)(2,1)S(1)}, bf16[16,1408]{1,0:T(8,128)(2,1)S(1)}, u32[]{:S(2)}, u32[]{:S(2)}) collective-permute-start(bf16[16,1408]{1,0:T(8,128)(2,1)S(1)} %get-tuple-element.70), channel_id=1, source_target_pairs={{0,4},{1,20},{2,6},{3,22},{4,8},{5,24},{6,10},{7,26},{8,12},{9,28}... | collective-permute-start | bytes 135176 | tf_op jit(solution)/shard_map/ppermute | solution.py:95
  116.4 0.6 collective-permute-done.32.refs_1_
  117.0 2.1 %collective-permute-done.33.refs_2_ = bf16[16,1408]{1,0:T(8,128)(2,1)S(1)} collective-permute-done((bf16[16,1408]{1,0:T(8,128)(2,1)S(1)}, bf16[16,1408]{1,0:T(8,128)(2,1)S(1)}, u32[]{:S(2)}, u32[]{:S(2)}) %collective-permute-start.33) | collective-permute-done | bytes 45088 | tf_op jit(solution)/shard_map/ppermute | solution.py:95
  119.1 1.9 %collective-permute-done.34.refs_3_ = bf16[16,1408]{1,0:T(8,128)(2,1)S(1)} collective-permute-done((bf16[16,1408]{1,0:T(8,128)(2,1)S(1)}, bf16[16,1408]{1,0:T(8,128)(2,1)S(1)}, u32[]{:S(2)}, u32[]{:S(2)}) %collective-permute-start.34) | collective-permute-done | bytes 45088 | tf_op jit(solution)/shard_map/ppermute | solution.py:95
  121.0 1.2 %shard_map.82 = bf16[4,16,1408]{2,1,0:T(8,128)(2,1)} custom-call(s32[4]{0:T(128)S(1)} %pad_add_fusion.where, bf16[16,1408]{1,0:T(8,128)(2,1)S(1)} %collective-permute-done.31.refs_0_, bf16[16,1408]{1,0:T(8,128)(2,1)S(1)} %collective-permute-done.32.refs_1_, bf16[16,1408]{1,0:T(8,128)(2,1)S(1)} %collective-permute-done.33.refs_2_, ...), custom_call_target="tpu_custom_call" | custom-call | bytes 360448 | tf_op jit(solution)/shard_map/pallas_call | solution.py:105
  (46 shorter events, 0.6 us)
Async XLA Ops:
  0.0 46.8 %copy-start = (bf16[256,4224]{1,0:T(8,128)(2,1)S(1)}, bf16[256,4224]{1,0:T(8,128)(2,1)}, u32[]{:S(2)}) copy-start(bf16[256,4224]{1,0:T(8,128)(2,1)} %param.11) | copy-start | bytes 6488068
  0.0 31.8 %copy-start.10 = (s32[4]{0:T(128)S(1)}, s32[4]{0:T(128)}, u32[]{:S(2)}) copy-start(s32[4]{0:T(128)} %param.9) | copy-start | bytes 52
  3.7 24.8 %copy-start.2 = (bf16[88,704]{1,0:T(8,128)(2,1)}, bf16[88,704]{1,0:T(8,128)(2,1)S(1)}, u32[]{:S(2)}) copy-start(bf16[88,704]{1,0:T(8,128)(2,1)S(1)} %get-tuple-element.50.refs_4_) | copy-start | bytes 371716
  3.7 7.8 %collective-permute-start.5 = (bf16[88,1232]{1,0:T(8,128)(2,1)S(1)}, bf16[88,1232]{1,0:T(8,128)(2,1)S(1)}, u32[]{:S(2)}, u32[]{:S(2)}) collective-permute-start(bf16[88,1232]{1,0:T(8,128)(2,1)S(1)} %get-tuple-element.40), channel_id=1, source_target_pairs={{0,2},{1,3},{2,0},{3,1},{4,6},{5,7},{6,4},{7,5},{8,10},{9,11},{10,... | collective-permute-start | bytes 650504 | tf_op jit(solution)/shard_map/ppermute | solution.py:95
  7.5 12.0 %collective-permute-start.1 = (bf16[2,4,16,1408]{3,2,1,0:T(8,128)(2,1)S(1)}, bf16[2,4,16,1408]{3,2,1,0:T(8,128)(2,1)S(1)}, u32[]{:S(2)}, u32[]{:S(2)}) collective-permute-start(bf16[2,4,16,1408]{3,2,1,0:T(8,128)(2,1)S(1)} %shard_map.73), channel_id=1, source_target_pairs={{0,0},{1,16},{2,2},{3,18},{4,4},{5,20},{6,6},{7,22},{8,8},{9,24},{... | collective-permute-start | bytes 1081352 | tf_op jit(solution)/shard_map/ppermute | solution.py:95
  11.3 10.6 %collective-permute-start.2 = (bf16[2,4,16,1408]{3,2,1,0:T(8,128)(2,1)S(1)}, bf16[2,4,16,1408]{3,2,1,0:T(8,128)(2,1)S(1)}, u32[]{:S(2)}, u32[]{:S(2)}) collective-permute-start(bf16[2,4,16,1408]{3,2,1,0:T(8,128)(2,1)S(1)} %shard_map.73), channel_id=1, source_target_pairs={{0,16},{1,0},{2,18},{3,2},{4,20},{5,4},{6,22},{7,6},{8,24},{9,8},{... | collective-permute-start | bytes 1081352 | tf_op jit(solution)/shard_map/ppermute | solution.py:95
  11.4 15.5 %collective-permute-start.3 = (bf16[2,4,16,1408]{3,2,1,0:T(8,128)(2,1)S(1)}, bf16[2,4,16,1408]{3,2,1,0:T(8,128)(2,1)S(1)}, u32[]{:S(2)}, u32[]{:S(2)}) collective-permute-start(bf16[2,4,16,1408]{3,2,1,0:T(8,128)(2,1)S(1)} %shard_map.73), channel_id=1, source_target_pairs={{0,2},{1,18},{2,0},{3,16},{4,6},{5,22},{6,4},{7,20},{8,10},{9,26},... | collective-permute-start | bytes 1081352 | tf_op jit(solution)/shard_map/ppermute | solution.py:95
  12.2 36.7 %copy-start.1 = (bf16[352,352]{1,0:T(8,128)(2,1)}, bf16[352,352]{1,0:T(8,128)(2,1)S(1)}, u32[]{:S(2)}) copy-start(bf16[352,352]{1,0:T(8,128)(2,1)S(1)} %shard_map.75.refs_4_) | copy-start | bytes 743428
  12.2 9.7 %collective-permute-start.6 = (bf16[352,352]{1,0:T(8,128)(2,1)S(1)}, bf16[352,352]{1,0:T(8,128)(2,1)}, u32[]{:S(2)}, u32[]{:S(2)}) collective-permute-start(bf16[352,352]{1,0:T(8,128)(2,1)S(1)} %shard_map.75.refs_4_), channel_id=1, source_target_pairs={{0,4},{1,5},{2,6},{3,7},{4,8},{5,9},{6,10},{7,11},{8,12},{9,13},{1... | collective-permute-start | bytes 743432 | tf_op jit(solution)/shard_map/ppermute | solution.py:95
  13.5 15.0 %collective-permute-start.4 = (bf16[2,4,16,1408]{3,2,1,0:T(8,128)(2,1)S(1)}, bf16[2,4,16,1408]{3,2,1,0:T(8,128)(2,1)S(1)}, u32[]{:S(2)}, u32[]{:S(2)}) collective-permute-start(bf16[2,4,16,1408]{3,2,1,0:T(8,128)(2,1)S(1)} %shard_map.73), channel_id=1, source_target_pairs={{0,18},{1,2},{2,16},{3,0},{4,22},{5,6},{6,20},{7,4},{8,26},{9,10},... | collective-permute-start | bytes 1081352 | tf_op jit(solution)/shard_map/ppermute | solution.py:95
  19.5 11.4 %copy-start.6 = (bf16[2,4,16,1408]{3,2,1,0:T(8,128)(2,1)}, bf16[2,4,16,1408]{3,2,1,0:T(8,128)(2,1)S(1)}, u32[]{:S(2)}) copy-start(bf16[2,4,16,1408]{3,2,1,0:T(8,128)(2,1)S(1)} %collective-permute-done.1.refs_0_) | copy-start | bytes 1081348
  21.9 9.9 %copy-start.7 = (bf16[2,4,16,1408]{3,2,1,0:T(8,128)(2,1)}, bf16[2,4,16,1408]{3,2,1,0:T(8,128)(2,1)S(1)}, u32[]{:S(2)}) copy-start(bf16[2,4,16,1408]{3,2,1,0:T(8,128)(2,1)S(1)} %collective-permute-done.2.refs_1_) | copy-start | bytes 1081348
  21.9 8.9 %collective-permute-start.7 = (bf16[352,352]{1,0:T(8,128)(2,1)}, bf16[352,352]{1,0:T(8,128)(2,1)}, u32[]{:S(2)}, u32[]{:S(2)}) collective-permute-start(bf16[352,352]{1,0:T(8,128)(2,1)} %collective-permute-done.6.refs_5_), channel_id=1, source_target_pairs={{0,4},{1,5},{2,6},{3,7},{4,8},{5,9},{6,10},{7,11},{8,12},{9,13},{1... | collective-permute-start | bytes 743432 | tf_op jit(solution)/shard_map/ppermute | solution.py:95
  26.8 4.9 %copy-start.8 = (bf16[2,4,16,1408]{3,2,1,0:T(8,128)(2,1)}, bf16[2,4,16,1408]{3,2,1,0:T(8,128)(2,1)S(1)}, u32[]{:S(2)}) copy-start(bf16[2,4,16,1408]{3,2,1,0:T(8,128)(2,1)S(1)} %collective-permute-done.3.refs_2_) | copy-start | bytes 1081348
  26.8 12.2 %collective-permute-start.13 = (bf16[88,1232]{1,0:T(8,128)(2,1)}, bf16[88,1232]{1,0:T(8,128)(2,1)S(1)}, u32[]{:S(2)}, u32[]{:S(2)}) collective-permute-start(bf16[88,1232]{1,0:T(8,128)(2,1)} %get-tuple-element.47), channel_id=1, source_target_pairs={{0,1},{1,0},{2,3},{3,2},{4,5},{5,4},{6,7},{7,6},{8,9},{9,8},{10,11... | collective-permute-start | bytes 650504 | tf_op jit(solution)/shard_map/ppermute | solution.py:95
  26.8 11.6 %collective-permute-start.14 = (bf16[88,528]{1,0:T(8,128)(2,1)}, bf16[88,528]{1,0:T(8,128)(2,1)S(1)}, u32[]{:S(2)}, u32[]{:S(2)}) collective-permute-start(bf16[88,528]{1,0:T(8,128)(2,1)} %get-tuple-element.49), channel_id=1, source_target_pairs={{0,3},{1,2},{2,1},{3,0},{4,7},{5,6},{6,5},{7,4},{8,11},{9,10},{10,... | collective-permute-start | bytes 278792 | tf_op jit(solution)/shard_map/ppermute | solution.py:95
  28.5 17.7 %collective-permute-start.9 = (bf16[352,352]{1,0:T(8,128)(2,1)S(1)}, bf16[352,352]{1,0:T(8,128)(2,1)}, u32[]{:S(2)}, u32[]{:S(2)}) collective-permute-start(bf16[352,352]{1,0:T(8,128)(2,1)S(1)} %shard_map.75.refs_4_), channel_id=1, source_target_pairs={{0,1},{1,0},{2,3},{3,2},{4,5},{5,4},{6,7},{7,6},{8,9},{9,8},{10,11... | collective-permute-start | bytes 743432 | tf_op jit(solution)/shard_map/ppermute | solution.py:95
  28.5 3.3 %copy-start.9 = (bf16[2,4,16,1408]{3,2,1,0:T(8,128)(2,1)}, bf16[2,4,16,1408]{3,2,1,0:T(8,128)(2,1)S(1)}, u32[]{:S(2)}) copy-start(bf16[2,4,16,1408]{3,2,1,0:T(8,128)(2,1)S(1)} %collective-permute-done.4.refs_3_) | copy-start | bytes 1081348
  30.8 15.9 %collective-permute-start.8 = (bf16[352,352]{1,0:T(8,128)(2,1)}, bf16[352,352]{1,0:T(8,128)(2,1)}, u32[]{:S(2)}, u32[]{:S(2)}) collective-permute-start(bf16[352,352]{1,0:T(8,128)(2,1)} %collective-permute-done.7.refs_6_), channel_id=1, source_target_pairs={{0,4},{1,5},{2,6},{3,7},{4,8},{5,9},{6,10},{7,11},{8,12},{9,13},{1... | collective-permute-start | bytes 743432 | tf_op jit(solution)/shard_map/ppermute | solution.py:95
  31.8 5.4 %collective-permute-start = (s32[4]{0:T(128)S(1)}, s32[4]{0:T(128)S(1)}, u32[]{:S(2)}, u32[]{:S(2)}) collective-permute-start(s32[4]{0:T(128)S(1)} %copy-done.10), channel_id=1, source_target_pairs={{0,0},{1,16},{2,2},{3,18},{4,4},{5,20},{6,6},{7,22},{8,8},{9,24},{... | collective-permute-start | bytes 56 | tf_op jit(solution)/shard_map/ppermute | solution.py:95
  38.4 0.6 copy-start.4
  39.1 0.9 copy-start.3
  40.0 0.9 copy-start.5
  41.8 22.1 %collective-permute-start.15 = (bf16[352,704]{1,0:T(8,128)(2,1)S(1)}, bf16[352,704]{1,0:T(8,128)(2,1)S(1)}, u32[]{:S(2)}, u32[]{:S(2)}) collective-permute-start(bf16[352,704]{1,0:T(8,128)(2,1)S(1)} %shard_map.77.refs_0_), channel_id=1, source_target_pairs={{0,4},{1,5},{2,6},{3,7},{4,0},{5,1},{6,2},{7,3},{8,12},{9,13},{10,... | collective-permute-start | bytes 1486856 | tf_op jit(solution)/shard_map/ppermute | solution.py:95
  43.0 28.4 %collective-permute-start.22 = (bf16[352,704]{1,0:T(8,128)(2,1)S(1)}, bf16[352,704]{1,0:T(8,128)(2,1)}, u32[]{:S(2)}, u32[]{:S(2)}) collective-permute-start(bf16[352,704]{1,0:T(8,128)(2,1)S(1)} %shard_map.77.refs_0_), channel_id=1, source_target_pairs={{0,8},{1,9},{2,10},{3,11},{4,12},{5,13},{6,14},{7,15},{8,0},{9,1},... | collective-permute-start | bytes 1486856 | tf_op jit(solution)/shard_map/ppermute | solution.py:95
  46.1 2.5 %collective-permute-start.10 = (bf16[352,352]{1,0:T(8,128)(2,1)}, bf16[352,352]{1,0:T(8,128)(2,1)}, u32[]{:S(2)}, u32[]{:S(2)}) collective-permute-start(bf16[352,352]{1,0:T(8,128)(2,1)} %collective-permute-done.6.refs_5_), channel_id=1, source_target_pairs={{0,1},{1,0},{2,3},{3,2},{4,5},{5,4},{6,7},{7,6},{8,9},{9,8},{10,11... | collective-permute-start | bytes 743432 | tf_op jit(solution)/shard_map/ppermute | solution.py:95
  46.2 2.5 %collective-permute-start.11 = (bf16[352,352]{1,0:T(8,128)(2,1)}, bf16[352,352]{1,0:T(8,128)(2,1)}, u32[]{:S(2)}, u32[]{:S(2)}) collective-permute-start(bf16[352,352]{1,0:T(8,128)(2,1)} %collective-permute-done.7.refs_6_), channel_id=1, source_target_pairs={{0,1},{1,0},{2,3},{3,2},{4,5},{5,4},{6,7},{7,6},{8,9},{9,8},{10,11... | collective-permute-start | bytes 743432 | tf_op jit(solution)/shard_map/ppermute | solution.py:95
  46.7 2.1 %collective-permute-start.12 = (bf16[352,352]{1,0:T(8,128)(2,1)}, bf16[352,352]{1,0:T(8,128)(2,1)}, u32[]{:S(2)}, u32[]{:S(2)}) collective-permute-start(bf16[352,352]{1,0:T(8,128)(2,1)} %collective-permute-done.8.refs_7_), channel_id=1, source_target_pairs={{0,1},{1,0},{2,3},{3,2},{4,5},{5,4},{6,7},{7,6},{8,9},{9,8},{10,11... | collective-permute-start | bytes 743432 | tf_op jit(solution)/shard_map/ppermute | solution.py:95
  63.9 5.0 %collective-permute-start.16 = (bf16[4,16,352]{2,1,0:T(8,128)(2,1)S(1)}, bf16[4,16,352]{2,1,0:T(8,128)(2,1)S(1)}, u32[]{:S(2)}, u32[]{:S(2)}) collective-permute-start(bf16[4,16,352]{2,1,0:T(8,128)(2,1)S(1)} %get-tuple-element.52), channel_id=1, source_target_pairs={{0,4},{1,5},{2,6},{3,7},{4,8},{5,9},{6,10},{7,11},{8,12},{9,13},{1... | collective-permute-start | bytes 135176 | tf_op jit(solution)/shard_map/ppermute | solution.py:95
  63.9 6.3 %collective-permute-start.17 = (bf16[4,16,352]{2,1,0:T(8,128)(2,1)S(1)}, bf16[4,16,352]{2,1,0:T(8,128)(2,1)S(1)}, u32[]{:S(2)}, u32[]{:S(2)}) collective-permute-start(bf16[4,16,352]{2,1,0:T(8,128)(2,1)S(1)} %get-tuple-element.54), channel_id=1, source_target_pairs={{0,8},{1,9},{2,10},{3,11},{4,12},{5,13},{6,14},{7,15},{8,0},{9,1},... | collective-permute-start | bytes 135176 | tf_op jit(solution)/shard_map/ppermute | solution.py:95
  66.3 4.2 %collective-permute-start.18 = (bf16[4,16,352]{2,1,0:T(8,128)(2,1)S(1)}, bf16[4,16,352]{2,1,0:T(8,128)(2,1)S(1)}, u32[]{:S(2)}, u32[]{:S(2)}) collective-permute-start(bf16[4,16,352]{2,1,0:T(8,128)(2,1)S(1)} %get-tuple-element.56), channel_id=1, source_target_pairs={{0,12},{1,13},{2,14},{3,15},{4,0},{5,1},{6,2},{7,3},{8,4},{9,5},{1... | collective-permute-start | bytes 135176 | tf_op jit(solution)/shard_map/ppermute | solution.py:95
  71.4 14.2 %collective-permute-start.23 = (bf16[352,704]{1,0:T(8,128)(2,1)}, bf16[352,704]{1,0:T(8,128)(2,1)S(1)}, u32[]{:S(2)}, u32[]{:S(2)}) collective-permute-start(bf16[352,704]{1,0:T(8,128)(2,1)} %collective-permute-done.22.refs_2_), channel_id=1, source_target_pairs={{0,4},{1,5},{2,6},{3,7},{4,0},{5,1},{6,2},{7,3},{8,12},{9,13},{10,... | collective-permute-start | bytes 1486856 | tf_op jit(solution)/shard_map/ppermute | solution.py:95
  72.5 5.8 %collective-permute-start.19 = (bf16[4,4,16,352]{3,2,1,0:T(8,128)(2,1)S(1)}, bf16[4,4,16,352]{3,2,1,0:T(8,128)(2,1)S(1)}, u32[]{:S(2)}, u32[]{:S(2)}) collective-permute-start(bf16[4,4,16,352]{3,2,1,0:T(8,128)(2,1)S(1)} %shard_map.78.refs_0_), channel_id=1, source_target_pairs={{0,16},{1,17},{2,18},{3,19},{4,20},{5,21},{6,22},{7,23},{8,24},{9,... | collective-permute-start | bytes 540680 | tf_op jit(solution)/shard_map/ppermute | solution.py:95
  72.9 5.4 %collective-permute-start.20 = (bf16[4,4,16,352]{3,2,1,0:T(8,128)(2,1)S(1)}, bf16[4,4,16,352]{3,2,1,0:T(8,128)(2,1)S(1)}, u32[]{:S(2)}, u32[]{:S(2)}) collective-permute-start(bf16[4,4,16,352]{3,2,1,0:T(8,128)(2,1)S(1)} %shard_map.78.refs_0_), channel_id=1, source_target_pairs={{0,2},{1,3},{2,0},{3,1},{4,6},{5,7},{6,4},{7,5},{8,10},{9,11},{10,... | collective-permute-start | bytes 540680 | tf_op jit(solution)/shard_map/ppermute | solution.py:95
  74.2 8.3 %collective-permute-start.21 = (bf16[4,4,16,352]{3,2,1,0:T(8,128)(2,1)S(1)}, bf16[4,4,16,352]{3,2,1,0:T(8,128)(2,1)S(1)}, u32[]{:S(2)}, u32[]{:S(2)}) collective-permute-start(bf16[4,4,16,352]{3,2,1,0:T(8,128)(2,1)S(1)} %shard_map.78.refs_0_), channel_id=1, source_target_pairs={{0,18},{1,19},{2,16},{3,17},{4,22},{5,23},{6,20},{7,21},{8,26},{9,... | collective-permute-start | bytes 540680 | tf_op jit(solution)/shard_map/ppermute | solution.py:95
  82.5 5.1 %collective-permute-start.24 = (bf16[352,704]{1,0:T(8,128)(2,1)S(1)}, bf16[352,704]{1,0:T(8,128)(2,1)S(1)}, u32[]{:S(2)}, u32[]{:S(2)}) collective-permute-start(bf16[352,704]{1,0:T(8,128)(2,1)S(1)} %shard_map.77.refs_0_), channel_id=1, source_target_pairs={{0,1},{1,0},{2,3},{3,2},{4,5},{5,4},{6,7},{7,6},{8,9},{9,8},{10,11... | collective-permute-start | bytes 1486856 | tf_op jit(solution)/shard_map/ppermute | solution.py:95
  85.0 3.1 %collective-permute-start.25 = (bf16[352,704]{1,0:T(8,128)(2,1)S(1)}, bf16[352,704]{1,0:T(8,128)(2,1)S(1)}, u32[]{:S(2)}, u32[]{:S(2)}) collective-permute-start(bf16[352,704]{1,0:T(8,128)(2,1)S(1)} %collective-permute-done.15.refs_1_), channel_id=1, source_target_pairs={{0,1},{1,0},{2,3},{3,2},{4,5},{5,4},{6,7},{7,6},{8,9},{9,8},{10,11... | collective-permute-start | bytes 1486856 | tf_op jit(solution)/shard_map/ppermute | solution.py:95
  85.0 3.3 %collective-permute-start.26 = (bf16[352,704]{1,0:T(8,128)(2,1)}, bf16[352,704]{1,0:T(8,128)(2,1)S(1)}, u32[]{:S(2)}, u32[]{:S(2)}) collective-permute-start(bf16[352,704]{1,0:T(8,128)(2,1)} %collective-permute-done.22.refs_2_), channel_id=1, source_target_pairs={{0,1},{1,0},{2,3},{3,2},{4,5},{5,4},{6,7},{7,6},{8,9},{9,8},{10,11... | collective-permute-start | bytes 1486856 | tf_op jit(solution)/shard_map/ppermute | solution.py:95
  85.6 3.4 %collective-permute-start.27 = (bf16[352,704]{1,0:T(8,128)(2,1)S(1)}, bf16[352,704]{1,0:T(8,128)(2,1)S(1)}, u32[]{:S(2)}, u32[]{:S(2)}) collective-permute-start(bf16[352,704]{1,0:T(8,128)(2,1)S(1)} %collective-permute-done.23.refs_3_), channel_id=1, source_target_pairs={{0,1},{1,0},{2,3},{3,2},{4,5},{5,4},{6,7},{7,6},{8,9},{9,8},{10,11... | collective-permute-start | bytes 1486856 | tf_op jit(solution)/shard_map/ppermute | solution.py:95
  96.7 6.2 %collective-permute-start.28 = (bf16[2,64,704]{2,1,0:T(8,128)(2,1)S(1)}, bf16[2,64,704]{2,1,0:T(8,128)(2,1)S(1)}, u32[]{:S(2)}, u32[]{:S(2)}) collective-permute-start(bf16[2,64,704]{2,1,0:T(8,128)(2,1)S(1)} %get-tuple-element.64), channel_id=1, source_target_pairs={{0,16},{1,17},{2,18},{3,19},{4,20},{5,21},{6,22},{7,23},{8,24},{9,... | collective-permute-start | bytes 540680 | tf_op jit(solution)/shard_map/ppermute | solution.py:95
  97.2 5.8 %collective-permute-start.29 = (bf16[2,64,704]{2,1,0:T(8,128)(2,1)S(1)}, bf16[2,64,704]{2,1,0:T(8,128)(2,1)S(1)}, u32[]{:S(2)}, u32[]{:S(2)}) collective-permute-start(bf16[2,64,704]{2,1,0:T(8,128)(2,1)S(1)} %get-tuple-element.65), channel_id=1, source_target_pairs={{0,2},{1,3},{2,0},{3,1},{4,6},{5,7},{6,4},{7,5},{8,10},{9,11},{10,... | collective-permute-start | bytes 540680 | tf_op jit(solution)/shard_map/ppermute | solution.py:95
  98.0 10.0 %collective-permute-start.30 = (bf16[2,64,704]{2,1,0:T(8,128)(2,1)S(1)}, bf16[2,64,704]{2,1,0:T(8,128)(2,1)S(1)}, u32[]{:S(2)}, u32[]{:S(2)}) collective-permute-start(bf16[2,64,704]{2,1,0:T(8,128)(2,1)S(1)} %get-tuple-element.66), channel_id=1, source_target_pairs={{0,18},{1,19},{2,16},{3,17},{4,22},{5,23},{6,20},{7,21},{8,26},{9,... | collective-permute-start | bytes 540680 | tf_op jit(solution)/shard_map/ppermute | solution.py:95
  108.7 7.7 %collective-permute-start.31 = (bf16[16,1408]{1,0:T(8,128)(2,1)S(1)}, bf16[16,1408]{1,0:T(8,128)(2,1)S(1)}, u32[]{:S(2)}, u32[]{:S(2)}) collective-permute-start(bf16[16,1408]{1,0:T(8,128)(2,1)S(1)} %get-tuple-element.67), channel_id=1, source_target_pairs={{0,0},{1,16},{2,2},{3,18},{4,4},{5,20},{6,6},{7,22},{8,8},{9,24},{... | collective-permute-start | bytes 135176 | tf_op jit(solution)/shard_map/ppermute | solution.py:95
  112.3 4.7 %collective-permute-start.32 = (bf16[16,1408]{1,0:T(8,128)(2,1)S(1)}, bf16[16,1408]{1,0:T(8,128)(2,1)S(1)}, u32[]{:S(2)}, u32[]{:S(2)}) collective-permute-start(bf16[16,1408]{1,0:T(8,128)(2,1)S(1)} %get-tuple-element.68), channel_id=1, source_target_pairs={{0,12},{1,28},{2,14},{3,30},{4,0},{5,16},{6,2},{7,18},{8,4},{9,20}... | collective-permute-start | bytes 135176 | tf_op jit(solution)/shard_map/ppermute | solution.py:95
  113.7 5.4 %collective-permute-start.33 = (bf16[16,1408]{1,0:T(8,128)(2,1)S(1)}, bf16[16,1408]{1,0:T(8,128)(2,1)S(1)}, u32[]{:S(2)}, u32[]{:S(2)}) collective-permute-start(bf16[16,1408]{1,0:T(8,128)(2,1)S(1)} %get-tuple-element.69), channel_id=1, source_target_pairs={{0,8},{1,24},{2,10},{3,26},{4,12},{5,28},{6,14},{7,30},{8,0},{9,16... | collective-permute-start | bytes 135176 | tf_op jit(solution)/shard_map/ppermute | solution.py:95
  114.8 6.2 %collective-permute-start.34 = (bf16[16,1408]{1,0:T(8,128)(2,1)S(1)}, bf16[16,1408]{1,0:T(8,128)(2,1)S(1)}, u32[]{:S(2)}, u32[]{:S(2)}) collective-permute-start(bf16[16,1408]{1,0:T(8,128)(2,1)S(1)} %get-tuple-element.70), channel_id=1, source_target_pairs={{0,4},{1,20},{2,6},{3,22},{4,8},{5,24},{6,10},{7,26},{8,12},{9,28}... | collective-permute-start | bytes 135176 | tf_op jit(solution)/shard_map/ppermute | solution.py:95

commit v10 on v9

--- a/solution.py
+++ b/solution.py
@@ -186,8 +186,9 @@
                 to[:, at : at + half] = w_out[:, gc * half : (gc + 1) * half]
 
 def stack_kernel(where, *refs):
-    *pieces, out, sems = refs
-    copy_all([(v, out.at[s]) for s, v in enumerate(pieces)], sems)
+    *pieces, out = refs
+    for s, v in enumerate(pieces):
+        out[s] = v[...]
 
 
 def ring_kernel(Y, part, where, own, *refs):
@@ -458,7 +459,7 @@
         p.send(after(pieces[s], held[1], mods), lambda x, z, y, c, s=s: (x, z + s, y, c))
         for s in range(1, S)
     ]
-    (merged,) = call(stack_kernel, [(S, blocks, local, cols)], p.where, *pieces, copies=S)
+    (merged,) = call(stack_kernel, [(S, blocks, local, cols)], p.where, *pieces, fast=[0], fast_in=True)
     held.append(p.send(after(held[2], merged), lambda x, z, y, c: (x, z ^ 1, y, c)))
     merged = [
         p.send(merged, lambda x, z, y, c, e=e, d=d: (x - d, z, y - e, c)) if e or d else merged

time: 123 us -> 122 us (level)
  no operation moved by 1% of the time
where the time goes in v10:
time: 122 us
  waiting for transfers between devices  49.7 us (41%)
  starting transfers between devices  44.2 us (36%)
  Pallas kernels  22.1 us (18%)
  local copies, waits for them, and re-layouts  3.9 us (3%)
    ppermute x35, waiting for transfers between devices, send(): return lax.ppermute(value, ('group', 'seq'), pairs)  49.7 us
    ppermute x35, starting transfers between devices, send(): return lax.ppermute(value, ('group', 'seq'), pairs)  44.2 us
    pallas_call x10, Pallas kernels, call(): pl.pallas_call(kernel, out_shape=[jax.ShapeDtypeStruct(s, BF) for s in ou...  22.1 us
    unnamed x22, local copies, waits for them, and re-layouts  2.48 us
  transfers between devices with their start and end apart: 35, of which 21 were waited for; matrix products, arithmetic and copies ran while one was open for 2% of the time, Pallas kernels for 7%

profile of v10, /device:TPU:1, one launch (start us, length us, event | category | flops | bytes accessed | tf_op | source)
XLA Modules:
  0.0 122.1 jit_solution(7866735083656337063)
XLA Ops:
  0.1 3.6 %shard_map.74 = (bf16[176,352]{1,0:T(8,128)(2,1)S(1)}, bf16[88,528]{1,0:T(8,128)(2,1)S(1)}, bf16[88,1232]{1,0:T(8,128)(2,1)}, bf16[88,1232]{1,0:T(8,128)(2,1)S(1...) custom-call(s32[4]{0:T(128)S(1)} %pad_add_fusion.where, bf16[176,1408]{1,0:T(8,128)(2,1)} %w_skip_any.1, ...), custom_call_target="tpu_custom_call" | custom-call | bytes 2973696 | tf_op jit(solution)/shard_map/pallas_call | solution.py:105
  3.7 2.2 %collective-permute-start.5 = (bf16[88,1232]{1,0:T(8,128)(2,1)S(1)}, bf16[88,1232]{1,0:T(8,128)(2,1)S(1)}, u32[]{:S(2)}, u32[]{:S(2)}) collective-permute-start(bf16[88,1232]{1,0:T(8,128)(2,1)S(1)} %get-tuple-element.40), channel_id=1, source_target_pairs={{0,2},{1,3},{2,0},{3,1},{4,6},{5,7},{6,4},{7,5},{8,10},{9,11},{10,... | collective-permute-start | bytes 650504 | tf_op jit(solution)/shard_map/ppermute | solution.py:95
  5.9 1.6 %shard_map.73 = bf16[2,4,16,1408]{3,2,1,0:T(8,128)(2,1)S(1)} custom-call(s32[4]{0:T(128)S(1)} %pad_add_fusion.where, bf16[4,16,1408]{2,1,0:T(8,128)(2,1)} %hidden.1, bf16[4,16,1408]{2,1,0:T(8,128)(2,1)} %skip.1), custom_call_target="tpu_custom_call" | custom-call | bytes 720896 | tf_op jit(solution)/shard_map/pallas_call | solution.py:105
  7.5 3.8 %collective-permute-start.1 = (bf16[2,4,16,1408]{3,2,1,0:T(8,128)(2,1)S(1)}, bf16[2,4,16,1408]{3,2,1,0:T(8,128)(2,1)S(1)}, u32[]{:S(2)}, u32[]{:S(2)}) collective-permute-start(bf16[2,4,16,1408]{3,2,1,0:T(8,128)(2,1)S(1)} %shard_map.73), channel_id=1, source_target_pairs={{0,0},{1,16},{2,2},{3,18},{4,4},{5,20},{6,6},{7,22},{8,8},{9,24},{... | collective-permute-start | bytes 1081352 | tf_op jit(solution)/shard_map/ppermute | solution.py:95
  11.4 0.7 shard_map.75.refs_4_
  12.2 1.3 %collective-permute-start.6 = (bf16[352,352]{1,0:T(8,128)(2,1)S(1)}, bf16[352,352]{1,0:T(8,128)(2,1)}, u32[]{:S(2)}, u32[]{:S(2)}) collective-permute-start(bf16[352,352]{1,0:T(8,128)(2,1)S(1)} %shard_map.75.refs_4_), channel_id=1, source_target_pairs={{0,4},{1,5},{2,6},{3,7},{4,8},{5,9},{6,10},{7,11},{8,12},{9,13},{1... | collective-permute-start | bytes 743432 | tf_op jit(solution)/shard_map/ppermute | solution.py:95
  13.5 2.6 %collective-permute-start.4 = (bf16[2,4,16,1408]{3,2,1,0:T(8,128)(2,1)S(1)}, bf16[2,4,16,1408]{3,2,1,0:T(8,128)(2,1)S(1)}, u32[]{:S(2)}, u32[]{:S(2)}) collective-permute-start(bf16[2,4,16,1408]{3,2,1,0:T(8,128)(2,1)S(1)} %shard_map.73), channel_id=1, source_target_pairs={{0,18},{1,2},{2,16},{3,0},{4,22},{5,6},{6,20},{7,4},{8,26},{9,10},... | collective-permute-start | bytes 1081352 | tf_op jit(solution)/shard_map/ppermute | solution.py:95
  16.1 3.4 %collective-permute-done.1.refs_0_ = bf16[2,4,16,1408]{3,2,1,0:T(8,128)(2,1)S(1)} collective-permute-done((bf16[2,4,16,1408]{3,2,1,0:T(8,128)(2,1)S(1)}, bf16[2,4,16,1408]{3,2,1,0:T(8,128)(2,1)S(1)}, u32[]{:S(2)}, u32[]{:S(2)}) %collective-permute-start.1) | collective-permute-done | bytes 360480 | tf_op jit(solution)/shard_map/ppermute | solution.py:95
  19.5 2.4 %collective-permute-done.2.refs_1_ = bf16[2,4,16,1408]{3,2,1,0:T(8,128)(2,1)S(1)} collective-permute-done((bf16[2,4,16,1408]{3,2,1,0:T(8,128)(2,1)S(1)}, bf16[2,4,16,1408]{3,2,1,0:T(8,128)(2,1)S(1)}, u32[]{:S(2)}, u32[]{:S(2)}) %collective-permute-start.2) | collective-permute-done | bytes 360480 | tf_op jit(solution)/shard_map/ppermute | solution.py:95
  21.9 1.2 collective-permute-start.7
  23.1 3.7 %collective-permute-done.3.refs_2_ = bf16[2,4,16,1408]{3,2,1,0:T(8,128)(2,1)S(1)} collective-permute-done((bf16[2,4,16,1408]{3,2,1,0:T(8,128)(2,1)S(1)}, bf16[2,4,16,1408]{3,2,1,0:T(8,128)(2,1)S(1)}, u32[]{:S(2)}, u32[]{:S(2)}) %collective-permute-start.3) | collective-permute-done | bytes 360480 | tf_op jit(solution)/shard_map/ppermute | solution.py:95
  26.8 1.6 %collective-permute-start.14 = (bf16[88,528]{1,0:T(8,128)(2,1)}, bf16[88,528]{1,0:T(8,128)(2,1)S(1)}, u32[]{:S(2)}, u32[]{:S(2)}) collective-permute-start(bf16[88,528]{1,0:T(8,128)(2,1)} %get-tuple-element.49), channel_id=1, source_target_pairs={{0,3},{1,2},{2,1},{3,0},{4,7},{5,6},{6,5},{7,4},{8,11},{9,10},{10,... | collective-permute-start | bytes 278792 | tf_op jit(solution)/shard_map/ppermute | solution.py:95
  28.5 2.3 %collective-permute-done.7.refs_6_ = bf16[352,352]{1,0:T(8,128)(2,1)} collective-permute-done((bf16[352,352]{1,0:T(8,128)(2,1)}, bf16[352,352]{1,0:T(8,128)(2,1)}, u32[]{:S(2)}, u32[]{:S(2)}) %collective-permute-start.7) | collective-permute-done | bytes 247840 | tf_op jit(solution)/shard_map/ppermute | solution.py:95
  30.8 0.9 collective-permute-start.8
  31.8 4.2 %collective-permute-start = (s32[4]{0:T(128)S(1)}, s32[4]{0:T(128)S(1)}, u32[]{:S(2)}, u32[]{:S(2)}) collective-permute-start(s32[4]{0:T(128)S(1)} %copy-done.10), channel_id=1, source_target_pairs={{0,0},{1,16},{2,2},{3,18},{4,4},{5,20},{6,6},{7,22},{8,8},{9,24},{... | collective-permute-start | bytes 56 | tf_op jit(solution)/shard_map/ppermute | solution.py:95
  36.0 1.2 collective-permute-done
  37.2 0.6 dynamic_slice.3
  38.4 0.6 copy-done.4
  39.1 0.9 copy-done.3
  40.0 0.9 copy-done.5
  40.9 0.9 shard_map.77.refs_0_
  41.8 1.2 collective-permute-start.15
  43.0 3.1 %collective-permute-start.22 = (bf16[352,704]{1,0:T(8,128)(2,1)S(1)}, bf16[352,704]{1,0:T(8,128)(2,1)}, u32[]{:S(2)}, u32[]{:S(2)}) collective-permute-start(bf16[352,704]{1,0:T(8,128)(2,1)S(1)} %shard_map.77.refs_0_), channel_id=1, source_target_pairs={{0,8},{1,9},{2,10},{3,11},{4,12},{5,13},{6,14},{7,15},{8,0},{9,1},... | collective-permute-start | bytes 1486856 | tf_op jit(solution)/shard_map/ppermute | solution.py:95
  46.2 0.5 collective-permute-start.11
  46.8 0.4 fusion.3
  47.2 0.7 reduce
  47.9 0.8 reshape.35.refs_4_.mods
  48.7 0.2 collective-permute-done.12.refs_11_
  48.9 3.7 %shard_map.76 = (bf16[4,16,352]{2,1,0:T(8,128)(2,1)S(1)}, bf16[4,16,352]{2,1,0:T(8,128)(2,1)S(1)}, bf16[4,16,352]{2,1,0:T(8,128)(2,1)S(1)}, bf16[4,16,352]{2,1,0:T(8,128)(2,1)S(1)}) custom-call(s32[4]{0:T(128)S(1)} %pad_add_fusion.where, bf16[2,4,16,1408]{3,2,1,0:T(8,128)(2,1)} %copy-done.6, bf16[2,4,16,1408]{3,2,1,0:T(8,128)(2,1)} %copy-done.7, ...), custom_call_target="tpu_custom_call" | custom-call | flops 507510784 | bytes 6848512 | tf_op jit(solution)/shard_map/pallas_call | solution.py:105
  52.6 11.3 %collective-permute-done.15.refs_1_ = bf16[352,704]{1,0:T(8,128)(2,1)S(1)} collective-permute-done((bf16[352,704]{1,0:T(8,128)(2,1)S(1)}, bf16[352,704]{1,0:T(8,128)(2,1)S(1)}, u32[]{:S(2)}, u32[]{:S(2)}) %collective-permute-start.15) | collective-permute-done | bytes 495648 | tf_op jit(solution)/shard_map/ppermute | solution.py:95
  63.9 2.4 %collective-permute-start.17 = (bf16[4,16,352]{2,1,0:T(8,128)(2,1)S(1)}, bf16[4,16,352]{2,1,0:T(8,128)(2,1)S(1)}, u32[]{:S(2)}, u32[]{:S(2)}) collective-permute-start(bf16[4,16,352]{2,1,0:T(8,128)(2,1)S(1)} %get-tuple-element.54), channel_id=1, source_target_pairs={{0,8},{1,9},{2,10},{3,11},{4,12},{5,13},{6,14},{7,15},{8,0},{9,1},... | collective-permute-start | bytes 135176 | tf_op jit(solution)/shard_map/ppermute | solution.py:95
  66.3 0.9 collective-permute-start.18
  67.2 1.7 %collective-permute-done.16.refs_1_ = bf16[4,16,352]{2,1,0:T(8,128)(2,1)S(1)} collective-permute-done((bf16[4,16,352]{2,1,0:T(8,128)(2,1)S(1)}, bf16[4,16,352]{2,1,0:T(8,128)(2,1)S(1)}, u32[]{:S(2)}, u32[]{:S(2)}) %collective-permute-start.16) | collective-permute-done | bytes 45088 | tf_op jit(solution)/shard_map/ppermute | solution.py:95
  68.8 1.4 %collective-permute-done.17.refs_2_ = bf16[4,16,352]{2,1,0:T(8,128)(2,1)S(1)} collective-permute-done((bf16[4,16,352]{2,1,0:T(8,128)(2,1)S(1)}, bf16[4,16,352]{2,1,0:T(8,128)(2,1)S(1)}, u32[]{:S(2)}, u32[]{:S(2)}) %collective-permute-start.17) | collective-permute-done | bytes 45088 | tf_op jit(solution)/shard_map/ppermute | solution.py:95
  70.2 0.3 collective-permute-done.18.refs_3_
  70.5 0.6 shard_map.78.refs_0_
  71.1 1.1 collective-permute-start.23
  72.2 0.4 collective-permute-start.19
  72.6 1.3 %collective-permute-start.20 = (bf16[4,4,16,352]{3,2,1,0:T(8,128)(2,1)S(1)}, bf16[4,4,16,352]{3,2,1,0:T(8,128)(2,1)S(1)}, u32[]{:S(2)}, u32[]{:S(2)}) collective-permute-start(bf16[4,4,16,352]{3,2,1,0:T(8,128)(2,1)S(1)} %shard_map.78.refs_0_), channel_id=1, source_target_pairs={{0,2},{1,3},{2,0},{3,1},{4,6},{5,7},{6,4},{7,5},{8,10},{9,11},{10,... | collective-permute-start | bytes 540680 | tf_op jit(solution)/shard_map/ppermute | solution.py:95
  73.9 1.0 collective-permute-start.21
  74.9 3.1 %collective-permute-done.19.refs_1_ = bf16[4,4,16,352]{3,2,1,0:T(8,128)(2,1)S(1)} collective-permute-done((bf16[4,4,16,352]{3,2,1,0:T(8,128)(2,1)S(1)}, bf16[4,4,16,352]{3,2,1,0:T(8,128)(2,1)S(1)}, u32[]{:S(2)}, u32[]{:S(2)}) %collective-permute-start.19) | collective-permute-done | bytes 180256 | tf_op jit(solution)/shard_map/ppermute | solution.py:95
  78.0 4.2 %collective-permute-done.21.refs_3_ = bf16[4,4,16,352]{3,2,1,0:T(8,128)(2,1)S(1)} collective-permute-done((bf16[4,4,16,352]{3,2,1,0:T(8,128)(2,1)S(1)}, bf16[4,4,16,352]{3,2,1,0:T(8,128)(2,1)S(1)}, u32[]{:S(2)}, u32[]{:S(2)}) %collective-permute-start.21) | collective-permute-done | bytes 180256 | tf_op jit(solution)/shard_map/ppermute | solution.py:95
  82.2 2.5 %collective-permute-start.24 = (bf16[352,704]{1,0:T(8,128)(2,1)S(1)}, bf16[352,704]{1,0:T(8,128)(2,1)S(1)}, u32[]{:S(2)}, u32[]{:S(2)}) collective-permute-start(bf16[352,704]{1,0:T(8,128)(2,1)S(1)} %shard_map.77.refs_0_), channel_id=1, source_target_pairs={{0,1},{1,0},{2,3},{3,2},{4,5},{5,4},{6,7},{7,6},{8,9},{9,8},{10,11... | collective-permute-start | bytes 1486856 | tf_op jit(solution)/shard_map/ppermute | solution.py:95
  84.8 0.5 collective-permute-start.26
  85.3 0.8 collective-permute-start.27
  86.1 1.3 %shard_map.79 = (bf16[4,256,352]{2,1,0:T(8,128)(2,1)S(1)}, bf16[4,64,352]{2,1,0:T(8,128)(2,1)S(1)}) custom-call(s32[4]{0:T(128)S(1)} %pad_add_fusion.where, bf16[4,4,16,352]{3,2,1,0:T(8,128)(2,1)S(1)} %shard_map.78.refs_0_, bf16[4,4,16,352]{3,2,1,0:T(8,128)(2,1)S(1)} %collective-permute-done.19.refs_1_, ...), custom_call_target="tpu_custom_call" | custom-call | bytes 1475584 | tf_op jit(solution)/shard_map/pallas_call | solution.py:105
  87.4 0.5 collective-permute-done.25.refs_5_
  87.9 0.2 collective-permute-done.26.refs_6_
  88.1 0.6 collective-permute-done.27.refs_7_
  88.6 7.8 %shard_map.80 = (bf16[2,64,704]{2,1,0:T(8,128)(2,1)S(1)}, bf16[2,64,704]{2,1,0:T(8,128)(2,1)S(1)}, bf16[2,64,704]{2,1,0:T(8,128)(2,1)S(1)}, bf16[2,64,704]{2,1,0:T(8,128)(2,1)S(1)}) custom-call(s32[4]{0:T(128)S(1)} %pad_add_fusion.where, bf16[4,256,352]{2,1,0:T(8,128)(2,1)S(1)} %get-tuple-element.58.norm, bf16[352,704]{1,0:T(8,128)(2,1)S(1)} %shard_map.77.refs_0_, ...), custom_call_target="tpu_custom_call" | custom-call | flops 1268776960 | bytes 9371648 | tf_op jit(solution)/shard_map/pallas_call | solution.py:105
  96.4 0.5 collective-permute-start.28
  96.9 0.8 collective-permute-start.29
  97.8 1.4 %collective-permute-start.30 = (bf16[2,64,704]{2,1,0:T(8,128)(2,1)S(1)}, bf16[2,64,704]{2,1,0:T(8,128)(2,1)S(1)}, u32[]{:S(2)}, u32[]{:S(2)}) collective-permute-start(bf16[2,64,704]{2,1,0:T(8,128)(2,1)S(1)} %get-tuple-element.66), channel_id=1, source_target_pairs={{0,18},{1,19},{2,16},{3,17},{4,22},{5,23},{6,20},{7,21},{8,26},{9,... | collective-permute-start | bytes 540680 | tf_op jit(solution)/shard_map/ppermute | solution.py:95
  99.1 3.5 %collective-permute-done.28.refs_1_ = bf16[2,64,704]{2,1,0:T(8,128)(2,1)S(1)} collective-permute-done((bf16[2,64,704]{2,1,0:T(8,128)(2,1)S(1)}, bf16[2,64,704]{2,1,0:T(8,128)(2,1)S(1)}, u32[]{:S(2)}, u32[]{:S(2)}) %collective-permute-start.28) | collective-permute-done | bytes 180256 | tf_op jit(solution)/shard_map/ppermute | solution.py:95
  102.7 5.0 %collective-permute-done.30.refs_3_ = bf16[2,64,704]{2,1,0:T(8,128)(2,1)S(1)} collective-permute-done((bf16[2,64,704]{2,1,0:T(8,128)(2,1)S(1)}, bf16[2,64,704]{2,1,0:T(8,128)(2,1)S(1)}, u32[]{:S(2)}, u32[]{:S(2)}) %collective-permute-start.30) | collective-permute-done | bytes 180256 | tf_op jit(solution)/shard_map/ppermute | solution.py:95
  107.7 0.7 shard_map.81
  108.5 3.5 %collective-permute-start.31 = (bf16[16,1408]{1,0:T(8,128)(2,1)S(1)}, bf16[16,1408]{1,0:T(8,128)(2,1)S(1)}, u32[]{:S(2)}, u32[]{:S(2)}) collective-permute-start(bf16[16,1408]{1,0:T(8,128)(2,1)S(1)} %get-tuple-element.67), channel_id=1, source_target_pairs={{0,0},{1,16},{2,2},{3,18},{4,4},{5,20},{6,6},{7,22},{8,8},{9,24},{... | collective-permute-start | bytes 135176 | tf_op jit(solution)/shard_map/ppermute | solution.py:95
  112.0 1.4 %collective-permute-start.32 = (bf16[16,1408]{1,0:T(8,128)(2,1)S(1)}, bf16[16,1408]{1,0:T(8,128)(2,1)S(1)}, u32[]{:S(2)}, u32[]{:S(2)}) collective-permute-start(bf16[16,1408]{1,0:T(8,128)(2,1)S(1)} %get-tuple-element.68), channel_id=1, source_target_pairs={{0,12},{1,28},{2,14},{3,30},{4,0},{5,16},{6,2},{7,18},{8,4},{9,20}... | collective-permute-start | bytes 135176 | tf_op jit(solution)/shard_map/ppermute | solution.py:95
  113.4 1.1 collective-permute-start.33
  114.5 1.6 %collective-permute-start.34 = (bf16[16,1408]{1,0:T(8,128)(2,1)S(1)}, bf16[16,1408]{1,0:T(8,128)(2,1)S(1)}, u32[]{:S(2)}, u32[]{:S(2)}) collective-permute-start(bf16[16,1408]{1,0:T(8,128)(2,1)S(1)} %get-tuple-element.70), channel_id=1, source_target_pairs={{0,4},{1,20},{2,6},{3,22},{4,8},{5,24},{6,10},{7,26},{8,12},{9,28}... | collective-permute-start | bytes 135176 | tf_op jit(solution)/shard_map/ppermute | solution.py:95
  116.2 0.6 collective-permute-done.32.refs_1_
  116.7 2.1 %collective-permute-done.33.refs_2_ = bf16[16,1408]{1,0:T(8,128)(2,1)S(1)} collective-permute-done((bf16[16,1408]{1,0:T(8,128)(2,1)S(1)}, bf16[16,1408]{1,0:T(8,128)(2,1)S(1)}, u32[]{:S(2)}, u32[]{:S(2)}) %collective-permute-start.33) | collective-permute-done | bytes 45088 | tf_op jit(solution)/shard_map/ppermute | solution.py:95
  118.8 1.9 %collective-permute-done.34.refs_3_ = bf16[16,1408]{1,0:T(8,128)(2,1)S(1)} collective-permute-done((bf16[16,1408]{1,0:T(8,128)(2,1)S(1)}, bf16[16,1408]{1,0:T(8,128)(2,1)S(1)}, u32[]{:S(2)}, u32[]{:S(2)}) %collective-permute-start.34) | collective-permute-done | bytes 45088 | tf_op jit(solution)/shard_map/ppermute | solution.py:95
  120.7 1.2 %shard_map.82 = bf16[4,16,1408]{2,1,0:T(8,128)(2,1)} custom-call(s32[4]{0:T(128)S(1)} %pad_add_fusion.where, bf16[16,1408]{1,0:T(8,128)(2,1)S(1)} %collective-permute-done.31.refs_0_, bf16[16,1408]{1,0:T(8,128)(2,1)S(1)} %collective-permute-done.32.refs_1_, bf16[16,1408]{1,0:T(8,128)(2,1)S(1)} %collective-permute-done.33.refs_2_, ...), custom_call_target="tpu_custom_call" | custom-call | bytes 360448 | tf_op jit(solution)/shard_map/pallas_call | solution.py:105
  (46 shorter events, 0.6 us)
Async XLA Ops:
  0.0 46.8 %copy-start = (bf16[256,4224]{1,0:T(8,128)(2,1)S(1)}, bf16[256,4224]{1,0:T(8,128)(2,1)}, u32[]{:S(2)}) copy-start(bf16[256,4224]{1,0:T(8,128)(2,1)} %param.11) | copy-start | bytes 6488068
  0.0 31.8 %copy-start.10 = (s32[4]{0:T(128)S(1)}, s32[4]{0:T(128)}, u32[]{:S(2)}) copy-start(s32[4]{0:T(128)} %param.9) | copy-start | bytes 52
  3.7 24.8 %copy-start.2 = (bf16[88,704]{1,0:T(8,128)(2,1)}, bf16[88,704]{1,0:T(8,128)(2,1)S(1)}, u32[]{:S(2)}) copy-start(bf16[88,704]{1,0:T(8,128)(2,1)S(1)} %get-tuple-element.50.refs_4_) | copy-start | bytes 371716
  3.7 7.8 %collective-permute-start.5 = (bf16[88,1232]{1,0:T(8,128)(2,1)S(1)}, bf16[88,1232]{1,0:T(8,128)(2,1)S(1)}, u32[]{:S(2)}, u32[]{:S(2)}) collective-permute-start(bf16[88,1232]{1,0:T(8,128)(2,1)S(1)} %get-tuple-element.40), channel_id=1, source_target_pairs={{0,2},{1,3},{2,0},{3,1},{4,6},{5,7},{6,4},{7,5},{8,10},{9,11},{10,... | collective-permute-start | bytes 650504 | tf_op jit(solution)/shard_map/ppermute | solution.py:95
  7.5 12.0 %collective-permute-start.1 = (bf16[2,4,16,1408]{3,2,1,0:T(8,128)(2,1)S(1)}, bf16[2,4,16,1408]{3,2,1,0:T(8,128)(2,1)S(1)}, u32[]{:S(2)}, u32[]{:S(2)}) collective-permute-start(bf16[2,4,16,1408]{3,2,1,0:T(8,128)(2,1)S(1)} %shard_map.73), channel_id=1, source_target_pairs={{0,0},{1,16},{2,2},{3,18},{4,4},{5,20},{6,6},{7,22},{8,8},{9,24},{... | collective-permute-start | bytes 1081352 | tf_op jit(solution)/shard_map/ppermute | solution.py:95
  11.3 10.6 %collective-permute-start.2 = (bf16[2,4,16,1408]{3,2,1,0:T(8,128)(2,1)S(1)}, bf16[2,4,16,1408]{3,2,1,0:T(8,128)(2,1)S(1)}, u32[]{:S(2)}, u32[]{:S(2)}) collective-permute-start(bf16[2,4,16,1408]{3,2,1,0:T(8,128)(2,1)S(1)} %shard_map.73), channel_id=1, source_target_pairs={{0,16},{1,0},{2,18},{3,2},{4,20},{5,4},{6,22},{7,6},{8,24},{9,8},{... | collective-permute-start | bytes 1081352 | tf_op jit(solution)/shard_map/ppermute | solution.py:95
  11.4 15.5 %collective-permute-start.3 = (bf16[2,4,16,1408]{3,2,1,0:T(8,128)(2,1)S(1)}, bf16[2,4,16,1408]{3,2,1,0:T(8,128)(2,1)S(1)}, u32[]{:S(2)}, u32[]{:S(2)}) collective-permute-start(bf16[2,4,16,1408]{3,2,1,0:T(8,128)(2,1)S(1)} %shard_map.73), channel_id=1, source_target_pairs={{0,2},{1,18},{2,0},{3,16},{4,6},{5,22},{6,4},{7,20},{8,10},{9,26},... | collective-permute-start | bytes 1081352 | tf_op jit(solution)/shard_map/ppermute | solution.py:95
  12.2 36.7 %copy-start.1 = (bf16[352,352]{1,0:T(8,128)(2,1)}, bf16[352,352]{1,0:T(8,128)(2,1)S(1)}, u32[]{:S(2)}) copy-start(bf16[352,352]{1,0:T(8,128)(2,1)S(1)} %shard_map.75.refs_4_) | copy-start | bytes 743428
  12.2 9.7 %collective-permute-start.6 = (bf16[352,352]{1,0:T(8,128)(2,1)S(1)}, bf16[352,352]{1,0:T(8,128)(2,1)}, u32[]{:S(2)}, u32[]{:S(2)}) collective-permute-start(bf16[352,352]{1,0:T(8,128)(2,1)S(1)} %shard_map.75.refs_4_), channel_id=1, source_target_pairs={{0,4},{1,5},{2,6},{3,7},{4,8},{5,9},{6,10},{7,11},{8,12},{9,13},{1... | collective-permute-start | bytes 743432 | tf_op jit(solution)/shard_map/ppermute | solution.py:95
  13.5 15.0 %collective-permute-start.4 = (bf16[2,4,16,1408]{3,2,1,0:T(8,128)(2,1)S(1)}, bf16[2,4,16,1408]{3,2,1,0:T(8,128)(2,1)S(1)}, u32[]{:S(2)}, u32[]{:S(2)}) collective-permute-start(bf16[2,4,16,1408]{3,2,1,0:T(8,128)(2,1)S(1)} %shard_map.73), channel_id=1, source_target_pairs={{0,18},{1,2},{2,16},{3,0},{4,22},{5,6},{6,20},{7,4},{8,26},{9,10},... | collective-permute-start | bytes 1081352 | tf_op jit(solution)/shard_map/ppermute | solution.py:95
  19.5 11.4 %copy-start.6 = (bf16[2,4,16,1408]{3,2,1,0:T(8,128)(2,1)}, bf16[2,4,16,1408]{3,2,1,0:T(8,128)(2,1)S(1)}, u32[]{:S(2)}) copy-start(bf16[2,4,16,1408]{3,2,1,0:T(8,128)(2,1)S(1)} %collective-permute-done.1.refs_0_) | copy-start | bytes 1081348
  21.9 9.9 %copy-start.7 = (bf16[2,4,16,1408]{3,2,1,0:T(8,128)(2,1)}, bf16[2,4,16,1408]{3,2,1,0:T(8,128)(2,1)S(1)}, u32[]{:S(2)}) copy-start(bf16[2,4,16,1408]{3,2,1,0:T(8,128)(2,1)S(1)} %collective-permute-done.2.refs_1_) | copy-start | bytes 1081348
  21.9 8.9 %collective-permute-start.7 = (bf16[352,352]{1,0:T(8,128)(2,1)}, bf16[352,352]{1,0:T(8,128)(2,1)}, u32[]{:S(2)}, u32[]{:S(2)}) collective-permute-start(bf16[352,352]{1,0:T(8,128)(2,1)} %collective-permute-done.6.refs_5_), channel_id=1, source_target_pairs={{0,4},{1,5},{2,6},{3,7},{4,8},{5,9},{6,10},{7,11},{8,12},{9,13},{1... | collective-permute-start | bytes 743432 | tf_op jit(solution)/shard_map/ppermute | solution.py:95
  26.8 4.9 %copy-start.8 = (bf16[2,4,16,1408]{3,2,1,0:T(8,128)(2,1)}, bf16[2,4,16,1408]{3,2,1,0:T(8,128)(2,1)S(1)}, u32[]{:S(2)}) copy-start(bf16[2,4,16,1408]{3,2,1,0:T(8,128)(2,1)S(1)} %collective-permute-done.3.refs_2_) | copy-start | bytes 1081348
  26.8 12.2 %collective-permute-start.13 = (bf16[88,1232]{1,0:T(8,128)(2,1)}, bf16[88,1232]{1,0:T(8,128)(2,1)S(1)}, u32[]{:S(2)}, u32[]{:S(2)}) collective-permute-start(bf16[88,1232]{1,0:T(8,128)(2,1)} %get-tuple-element.47), channel_id=1, source_target_pairs={{0,1},{1,0},{2,3},{3,2},{4,5},{5,4},{6,7},{7,6},{8,9},{9,8},{10,11... | collective-permute-start | bytes 650504 | tf_op jit(solution)/shard_map/ppermute | solution.py:95
  26.8 11.6 %collective-permute-start.14 = (bf16[88,528]{1,0:T(8,128)(2,1)}, bf16[88,528]{1,0:T(8,128)(2,1)S(1)}, u32[]{:S(2)}, u32[]{:S(2)}) collective-permute-start(bf16[88,528]{1,0:T(8,128)(2,1)} %get-tuple-element.49), channel_id=1, source_target_pairs={{0,3},{1,2},{2,1},{3,0},{4,7},{5,6},{6,5},{7,4},{8,11},{9,10},{10,... | collective-permute-start | bytes 278792 | tf_op jit(solution)/shard_map/ppermute | solution.py:95
  28.5 17.7 %collective-permute-start.9 = (bf16[352,352]{1,0:T(8,128)(2,1)S(1)}, bf16[352,352]{1,0:T(8,128)(2,1)}, u32[]{:S(2)}, u32[]{:S(2)}) collective-permute-start(bf16[352,352]{1,0:T(8,128)(2,1)S(1)} %shard_map.75.refs_4_), channel_id=1, source_target_pairs={{0,1},{1,0},{2,3},{3,2},{4,5},{5,4},{6,7},{7,6},{8,9},{9,8},{10,11... | collective-permute-start | bytes 743432 | tf_op jit(solution)/shard_map/ppermute | solution.py:95
  28.5 3.3 %copy-start.9 = (bf16[2,4,16,1408]{3,2,1,0:T(8,128)(2,1)}, bf16[2,4,16,1408]{3,2,1,0:T(8,128)(2,1)S(1)}, u32[]{:S(2)}) copy-start(bf16[2,4,16,1408]{3,2,1,0:T(8,128)(2,1)S(1)} %collective-permute-done.4.refs_3_) | copy-start | bytes 1081348
  30.8 15.9 %collective-permute-start.8 = (bf16[352,352]{1,0:T(8,128)(2,1)}, bf16[352,352]{1,0:T(8,128)(2,1)}, u32[]{:S(2)}, u32[]{:S(2)}) collective-permute-start(bf16[352,352]{1,0:T(8,128)(2,1)} %collective-permute-done.7.refs_6_), channel_id=1, source_target_pairs={{0,4},{1,5},{2,6},{3,7},{4,8},{5,9},{6,10},{7,11},{8,12},{9,13},{1... | collective-permute-start | bytes 743432 | tf_op jit(solution)/shard_map/ppermute | solution.py:95
  31.8 5.4 %collective-permute-start = (s32[4]{0:T(128)S(1)}, s32[4]{0:T(128)S(1)}, u32[]{:S(2)}, u32[]{:S(2)}) collective-permute-start(s32[4]{0:T(128)S(1)} %copy-done.10), channel_id=1, source_target_pairs={{0,0},{1,16},{2,2},{3,18},{4,4},{5,20},{6,6},{7,22},{8,8},{9,24},{... | collective-permute-start | bytes 56 | tf_op jit(solution)/shard_map/ppermute | solution.py:95
  38.4 0.6 copy-start.4
  39.1 0.9 copy-start.3
  40.0 0.9 copy-start.5
  41.8 22.1 %collective-permute-start.15 = (bf16[352,704]{1,0:T(8,128)(2,1)S(1)}, bf16[352,704]{1,0:T(8,128)(2,1)S(1)}, u32[]{:S(2)}, u32[]{:S(2)}) collective-permute-start(bf16[352,704]{1,0:T(8,128)(2,1)S(1)} %shard_map.77.refs_0_), channel_id=1, source_target_pairs={{0,4},{1,5},{2,6},{3,7},{4,0},{5,1},{6,2},{7,3},{8,12},{9,13},{10,... | collective-permute-start | bytes 1486856 | tf_op jit(solution)/shard_map/ppermute | solution.py:95
  43.0 28.1 %collective-permute-start.22 = (bf16[352,704]{1,0:T(8,128)(2,1)S(1)}, bf16[352,704]{1,0:T(8,128)(2,1)}, u32[]{:S(2)}, u32[]{:S(2)}) collective-permute-start(bf16[352,704]{1,0:T(8,128)(2,1)S(1)} %shard_map.77.refs_0_), channel_id=1, source_target_pairs={{0,8},{1,9},{2,10},{3,11},{4,12},{5,13},{6,14},{7,15},{8,0},{9,1},... | collective-permute-start | bytes 1486856 | tf_op jit(solution)/shard_map/ppermute | solution.py:95
  46.1 2.5 %collective-permute-start.10 = (bf16[352,352]{1,0:T(8,128)(2,1)}, bf16[352,352]{1,0:T(8,128)(2,1)}, u32[]{:S(2)}, u32[]{:S(2)}) collective-permute-start(bf16[352,352]{1,0:T(8,128)(2,1)} %collective-permute-done.6.refs_5_), channel_id=1, source_target_pairs={{0,1},{1,0},{2,3},{3,2},{4,5},{5,4},{6,7},{7,6},{8,9},{9,8},{10,11... | collective-permute-start | bytes 743432 | tf_op jit(solution)/shard_map/ppermute | solution.py:95
  46.2 2.5 %collective-permute-start.11 = (bf16[352,352]{1,0:T(8,128)(2,1)}, bf16[352,352]{1,0:T(8,128)(2,1)}, u32[]{:S(2)}, u32[]{:S(2)}) collective-permute-start(bf16[352,352]{1,0:T(8,128)(2,1)} %collective-permute-done.7.refs_6_), channel_id=1, source_target_pairs={{0,1},{1,0},{2,3},{3,2},{4,5},{5,4},{6,7},{7,6},{8,9},{9,8},{10,11... | collective-permute-start | bytes 743432 | tf_op jit(solution)/shard_map/ppermute | solution.py:95
  46.7 2.1 %collective-permute-start.12 = (bf16[352,352]{1,0:T(8,128)(2,1)}, bf16[352,352]{1,0:T(8,128)(2,1)}, u32[]{:S(2)}, u32[]{:S(2)}) collective-permute-start(bf16[352,352]{1,0:T(8,128)(2,1)} %collective-permute-done.8.refs_7_), channel_id=1, source_target_pairs={{0,1},{1,0},{2,3},{3,2},{4,5},{5,4},{6,7},{7,6},{8,9},{9,8},{10,11... | collective-permute-start | bytes 743432 | tf_op jit(solution)/shard_map/ppermute | solution.py:95
  63.9 5.0 %collective-permute-start.16 = (bf16[4,16,352]{2,1,0:T(8,128)(2,1)S(1)}, bf16[4,16,352]{2,1,0:T(8,128)(2,1)S(1)}, u32[]{:S(2)}, u32[]{:S(2)}) collective-permute-start(bf16[4,16,352]{2,1,0:T(8,128)(2,1)S(1)} %get-tuple-element.52), channel_id=1, source_target_pairs={{0,4},{1,5},{2,6},{3,7},{4,8},{5,9},{6,10},{7,11},{8,12},{9,13},{1... | collective-permute-start | bytes 135176 | tf_op jit(solution)/shard_map/ppermute | solution.py:95
  63.9 6.3 %collective-permute-start.17 = (bf16[4,16,352]{2,1,0:T(8,128)(2,1)S(1)}, bf16[4,16,352]{2,1,0:T(8,128)(2,1)S(1)}, u32[]{:S(2)}, u32[]{:S(2)}) collective-permute-start(bf16[4,16,352]{2,1,0:T(8,128)(2,1)S(1)} %get-tuple-element.54), channel_id=1, source_target_pairs={{0,8},{1,9},{2,10},{3,11},{4,12},{5,13},{6,14},{7,15},{8,0},{9,1},... | collective-permute-start | bytes 135176 | tf_op jit(solution)/shard_map/ppermute | solution.py:95
  66.3 4.2 %collective-permute-start.18 = (bf16[4,16,352]{2,1,0:T(8,128)(2,1)S(1)}, bf16[4,16,352]{2,1,0:T(8,128)(2,1)S(1)}, u32[]{:S(2)}, u32[]{:S(2)}) collective-permute-start(bf16[4,16,352]{2,1,0:T(8,128)(2,1)S(1)} %get-tuple-element.56), channel_id=1, source_target_pairs={{0,12},{1,13},{2,14},{3,15},{4,0},{5,1},{6,2},{7,3},{8,4},{9,5},{1... | collective-permute-start | bytes 135176 | tf_op jit(solution)/shard_map/ppermute | solution.py:95
  71.1 14.2 %collective-permute-start.23 = (bf16[352,704]{1,0:T(8,128)(2,1)}, bf16[352,704]{1,0:T(8,128)(2,1)S(1)}, u32[]{:S(2)}, u32[]{:S(2)}) collective-permute-start(bf16[352,704]{1,0:T(8,128)(2,1)} %collective-permute-done.22.refs_2_), channel_id=1, source_target_pairs={{0,4},{1,5},{2,6},{3,7},{4,0},{5,1},{6,2},{7,3},{8,12},{9,13},{10,... | collective-permute-start | bytes 1486856 | tf_op jit(solution)/shard_map/ppermute | solution.py:95
  72.2 5.8 %collective-permute-start.19 = (bf16[4,4,16,352]{3,2,1,0:T(8,128)(2,1)S(1)}, bf16[4,4,16,352]{3,2,1,0:T(8,128)(2,1)S(1)}, u32[]{:S(2)}, u32[]{:S(2)}) collective-permute-start(bf16[4,4,16,352]{3,2,1,0:T(8,128)(2,1)S(1)} %shard_map.78.refs_0_), channel_id=1, source_target_pairs={{0,16},{1,17},{2,18},{3,19},{4,20},{5,21},{6,22},{7,23},{8,24},{9,... | collective-permute-start | bytes 540680 | tf_op jit(solution)/shard_map/ppermute | solution.py:95
  72.6 5.4 %collective-permute-start.20 = (bf16[4,4,16,352]{3,2,1,0:T(8,128)(2,1)S(1)}, bf16[4,4,16,352]{3,2,1,0:T(8,128)(2,1)S(1)}, u32[]{:S(2)}, u32[]{:S(2)}) collective-permute-start(bf16[4,4,16,352]{3,2,1,0:T(8,128)(2,1)S(1)} %shard_map.78.refs_0_), channel_id=1, source_target_pairs={{0,2},{1,3},{2,0},{3,1},{4,6},{5,7},{6,4},{7,5},{8,10},{9,11},{10,... | collective-permute-start | bytes 540680 | tf_op jit(solution)/shard_map/ppermute | solution.py:95
  73.9 8.3 %collective-permute-start.21 = (bf16[4,4,16,352]{3,2,1,0:T(8,128)(2,1)S(1)}, bf16[4,4,16,352]{3,2,1,0:T(8,128)(2,1)S(1)}, u32[]{:S(2)}, u32[]{:S(2)}) collective-permute-start(bf16[4,4,16,352]{3,2,1,0:T(8,128)(2,1)S(1)} %shard_map.78.refs_0_), channel_id=1, source_target_pairs={{0,18},{1,19},{2,16},{3,17},{4,22},{5,23},{6,20},{7,21},{8,26},{9,... | collective-permute-start | bytes 540680 | tf_op jit(solution)/shard_map/ppermute | solution.py:95
  82.2 5.1 %collective-permute-start.24 = (bf16[352,704]{1,0:T(8,128)(2,1)S(1)}, bf16[352,704]{1,0:T(8,128)(2,1)S(1)}, u32[]{:S(2)}, u32[]{:S(2)}) collective-permute-start(bf16[352,704]{1,0:T(8,128)(2,1)S(1)} %shard_map.77.refs_0_), channel_id=1, source_target_pairs={{0,1},{1,0},{2,3},{3,2},{4,5},{5,4},{6,7},{7,6},{8,9},{9,8},{10,11... | collective-permute-start | bytes 1486856 | tf_op jit(solution)/shard_map/ppermute | solution.py:95
  84.8 3.1 %collective-permute-start.25 = (bf16[352,704]{1,0:T(8,128)(2,1)S(1)}, bf16[352,704]{1,0:T(8,128)(2,1)S(1)}, u32[]{:S(2)}, u32[]{:S(2)}) collective-permute-start(bf16[352,704]{1,0:T(8,128)(2,1)S(1)} %collective-permute-done.15.refs_1_), channel_id=1, source_target_pairs={{0,1},{1,0},{2,3},{3,2},{4,5},{5,4},{6,7},{7,6},{8,9},{9,8},{10,11... | collective-permute-start | bytes 1486856 | tf_op jit(solution)/shard_map/ppermute | solution.py:95
  84.8 3.3 %collective-permute-start.26 = (bf16[352,704]{1,0:T(8,128)(2,1)}, bf16[352,704]{1,0:T(8,128)(2,1)S(1)}, u32[]{:S(2)}, u32[]{:S(2)}) collective-permute-start(bf16[352,704]{1,0:T(8,128)(2,1)} %collective-permute-done.22.refs_2_), channel_id=1, source_target_pairs={{0,1},{1,0},{2,3},{3,2},{4,5},{5,4},{6,7},{7,6},{8,9},{9,8},{10,11... | collective-permute-start | bytes 1486856 | tf_op jit(solution)/shard_map/ppermute | solution.py:95
  85.3 3.4 %collective-permute-start.27 = (bf16[352,704]{1,0:T(8,128)(2,1)S(1)}, bf16[352,704]{1,0:T(8,128)(2,1)S(1)}, u32[]{:S(2)}, u32[]{:S(2)}) collective-permute-start(bf16[352,704]{1,0:T(8,128)(2,1)S(1)} %collective-permute-done.23.refs_3_), channel_id=1, source_target_pairs={{0,1},{1,0},{2,3},{3,2},{4,5},{5,4},{6,7},{7,6},{8,9},{9,8},{10,11... | collective-permute-start | bytes 1486856 | tf_op jit(solution)/shard_map/ppermute | solution.py:95
  96.4 6.2 %collective-permute-start.28 = (bf16[2,64,704]{2,1,0:T(8,128)(2,1)S(1)}, bf16[2,64,704]{2,1,0:T(8,128)(2,1)S(1)}, u32[]{:S(2)}, u32[]{:S(2)}) collective-permute-start(bf16[2,64,704]{2,1,0:T(8,128)(2,1)S(1)} %get-tuple-element.64), channel_id=1, source_target_pairs={{0,16},{1,17},{2,18},{3,19},{4,20},{5,21},{6,22},{7,23},{8,24},{9,... | collective-permute-start | bytes 540680 | tf_op jit(solution)/shard_map/ppermute | solution.py:95
  96.9 5.8 %collective-permute-start.29 = (bf16[2,64,704]{2,1,0:T(8,128)(2,1)S(1)}, bf16[2,64,704]{2,1,0:T(8,128)(2,1)S(1)}, u32[]{:S(2)}, u32[]{:S(2)}) collective-permute-start(bf16[2,64,704]{2,1,0:T(8,128)(2,1)S(1)} %get-tuple-element.65), channel_id=1, source_target_pairs={{0,2},{1,3},{2,0},{3,1},{4,6},{5,7},{6,4},{7,5},{8,10},{9,11},{10,... | collective-permute-start | bytes 540680 | tf_op jit(solution)/shard_map/ppermute | solution.py:95
  97.8 10.0 %collective-permute-start.30 = (bf16[2,64,704]{2,1,0:T(8,128)(2,1)S(1)}, bf16[2,64,704]{2,1,0:T(8,128)(2,1)S(1)}, u32[]{:S(2)}, u32[]{:S(2)}) collective-permute-start(bf16[2,64,704]{2,1,0:T(8,128)(2,1)S(1)} %get-tuple-element.66), channel_id=1, source_target_pairs={{0,18},{1,19},{2,16},{3,17},{4,22},{5,23},{6,20},{7,21},{8,26},{9,... | collective-permute-start | bytes 540680 | tf_op jit(solution)/shard_map/ppermute | solution.py:95
  108.5 7.7 %collective-permute-start.31 = (bf16[16,1408]{1,0:T(8,128)(2,1)S(1)}, bf16[16,1408]{1,0:T(8,128)(2,1)S(1)}, u32[]{:S(2)}, u32[]{:S(2)}) collective-permute-start(bf16[16,1408]{1,0:T(8,128)(2,1)S(1)} %get-tuple-element.67), channel_id=1, source_target_pairs={{0,0},{1,16},{2,2},{3,18},{4,4},{5,20},{6,6},{7,22},{8,8},{9,24},{... | collective-permute-start | bytes 135176 | tf_op jit(solution)/shard_map/ppermute | solution.py:95
  112.0 4.7 %collective-permute-start.32 = (bf16[16,1408]{1,0:T(8,128)(2,1)S(1)}, bf16[16,1408]{1,0:T(8,128)(2,1)S(1)}, u32[]{:S(2)}, u32[]{:S(2)}) collective-permute-start(bf16[16,1408]{1,0:T(8,128)(2,1)S(1)} %get-tuple-element.68), channel_id=1, source_target_pairs={{0,12},{1,28},{2,14},{3,30},{4,0},{5,16},{6,2},{7,18},{8,4},{9,20}... | collective-permute-start | bytes 135176 | tf_op jit(solution)/shard_map/ppermute | solution.py:95
  113.4 5.4 %collective-permute-start.33 = (bf16[16,1408]{1,0:T(8,128)(2,1)S(1)}, bf16[16,1408]{1,0:T(8,128)(2,1)S(1)}, u32[]{:S(2)}, u32[]{:S(2)}) collective-permute-start(bf16[16,1408]{1,0:T(8,128)(2,1)S(1)} %get-tuple-element.69), channel_id=1, source_target_pairs={{0,8},{1,24},{2,10},{3,26},{4,12},{5,28},{6,14},{7,30},{8,0},{9,16... | collective-permute-start | bytes 135176 | tf_op jit(solution)/shard_map/ppermute | solution.py:95
  114.5 6.2 %collective-permute-start.34 = (bf16[16,1408]{1,0:T(8,128)(2,1)S(1)}, bf16[16,1408]{1,0:T(8,128)(2,1)S(1)}, u32[]{:S(2)}, u32[]{:S(2)}) collective-permute-start(bf16[16,1408]{1,0:T(8,128)(2,1)S(1)} %get-tuple-element.70), channel_id=1, source_target_pairs={{0,4},{1,20},{2,6},{3,22},{4,8},{5,24},{6,10},{7,26},{8,12},{9,28}... | collective-permute-start | bytes 135176 | tf_op jit(solution)/shard_map/ppermute | solution.py:95

commit v11 on v10

--- a/solution.py
+++ b/solution.py
@@ -437,7 +437,7 @@
 
     times = p.send(timestep, lambda x, z, y, c: (c, z, y, x))
     mod = modulation(lax.dynamic_slice(times, (p.z,), (1,)), w_mod)
-    mods = after(mod, p.where).reshape(3 * blocks, 1, cols)
+    mods = mod.reshape(3 * blocks, 1, cols)
 
     pieces = call(
         partial(merged_kernel, G, S, Y),

time: 122 us -> 123 us (level)
  local copies, waits for them, and re-layouts: 3.9 us -> 6.26 us
  waiting for transfers between devices: 49.7 us -> 47.5 us
  matrix products: 0.39 us -> 2.29 us
  Pallas kernels: 22.1 us -> 20.8 us
    unnamed x22 -> x23, local copies, waits for them, and re-layouts: 2.48 us -> 5.63 us
    ppermute x35, waiting for transfers between devices: 49.7 us -> 47.5 us  [send(): return lax.ppermute(value, ('group', 'seq'), pairs)]
    dot_general x1, matrix products: 0.39 us -> 2.29 us  [modulation(): return jnp.dot(act, w_mod, preferred_element_type=F32)]
    pallas_call x10, Pallas kernels: 22.1 us -> 20.8 us  [call(): pl.pallas_call(kernel, out_shape=[jax.ShapeDtypeStruct(s, BF) for s in ou...]
  transfers between devices with their start and end apart: 35 -> 35, of which waited for: 21 -> 19; matrix products, arithmetic and copies ran while one was open for 2% -> 6% of each run, Pallas kernels for 7% -> 7%
where the time goes in v11:
time: 123 us; the launch traced here: 122 us
  waiting for transfers between devices  47.5 us (39%)
  starting transfers between devices  44.4 us (36%)
  Pallas kernels  20.8 us (17%)
  local copies, waits for them, and re-layouts  6.26 us (5%)
  matrix products  2.29 us (2%)
    ppermute x35, waiting for transfers between devices, send(): return lax.ppermute(value, ('group', 'seq'), pairs)  47.5 us
    ppermute x35, starting transfers between devices, send(): return lax.ppermute(value, ('group', 'seq'), pairs)  44.4 us
    pallas_call x10, Pallas kernels, call(): pl.pallas_call(kernel, out_shape=[jax.ShapeDtypeStruct(s, BF) for s in ou...  20.8 us
    unnamed x23, local copies, waits for them, and re-layouts  5.63 us
  transfers between devices with their start and end apart: 35, of which 19 were waited for; matrix products, arithmetic and copies ran while one was open for 6% of the time, Pallas kernels for 7%

profile of v11, /device:TPU:1, one launch (start us, length us, event | category | flops | bytes accessed | tf_op | source)
XLA Modules:
  0.0 122.5 jit_solution(5732966694028685246)
XLA Ops:
  0.0 0.1 pad_add_fusion.where
  0.1 2.8 %shard_map.74 = (bf16[176,352]{1,0:T(8,128)(2,1)S(1)}, bf16[88,528]{1,0:T(8,128)(2,1)S(1)}, bf16[88,1232]{1,0:T(8,128)(2,1)S(1)}, bf16[88,1232]{1,0:T(8,128)(2,1...) custom-call(s32[4]{0:T(128)S(1)} %pad_add_fusion.where, bf16[176,1408]{1,0:T(8,128)(2,1)} %w_skip_any.1, ...), custom_call_target="tpu_custom_call" | custom-call | bytes 2973696 | tf_op jit(solution)/shard_map/pallas_call | solution.py:105
  2.9 2.2 %collective-permute-start.5 = (bf16[88,1232]{1,0:T(8,128)(2,1)S(1)}, bf16[88,1232]{1,0:T(8,128)(2,1)S(1)}, u32[]{:S(2)}, u32[]{:S(2)}) collective-permute-start(bf16[88,1232]{1,0:T(8,128)(2,1)S(1)} %get-tuple-element.38), channel_id=1, source_target_pairs={{0,2},{1,3},{2,0},{3,1},{4,6},{5,7},{6,4},{7,5},{8,10},{9,11},{10,... | collective-permute-start | bytes 650504 | tf_op jit(solution)/shard_map/ppermute | solution.py:95
  5.1 1.6 %shard_map.73 = bf16[2,4,16,1408]{3,2,1,0:T(8,128)(2,1)S(1)} custom-call(s32[4]{0:T(128)S(1)} %pad_add_fusion.where, bf16[4,16,1408]{2,1,0:T(8,128)(2,1)} %hidden.1, bf16[4,16,1408]{2,1,0:T(8,128)(2,1)} %skip.1), custom_call_target="tpu_custom_call" | custom-call | bytes 720896 | tf_op jit(solution)/shard_map/pallas_call | solution.py:105
  6.7 3.8 %collective-permute-start.1 = (bf16[2,4,16,1408]{3,2,1,0:T(8,128)(2,1)S(1)}, bf16[2,4,16,1408]{3,2,1,0:T(8,128)(2,1)S(1)}, u32[]{:S(2)}, u32[]{:S(2)}) collective-permute-start(bf16[2,4,16,1408]{3,2,1,0:T(8,128)(2,1)S(1)} %shard_map.73), channel_id=1, source_target_pairs={{0,0},{1,16},{2,2},{3,18},{4,4},{5,20},{6,6},{7,22},{8,8},{9,24},{... | collective-permute-start | bytes 1081352 | tf_op jit(solution)/shard_map/ppermute | solution.py:95
  10.5 0.0 collective-permute-start.2
  10.6 0.1 collective-permute-start.3
  10.7 0.7 shard_map.75.refs_4_
  11.4 1.3 %collective-permute-start.6 = (bf16[352,352]{1,0:T(8,128)(2,1)S(1)}, bf16[352,352]{1,0:T(8,128)(2,1)S(1)}, u32[]{:S(2)}, u32[]{:S(2)}) collective-permute-start(bf16[352,352]{1,0:T(8,128)(2,1)S(1)} %shard_map.75.refs_4_), channel_id=1, source_target_pairs={{0,4},{1,5},{2,6},{3,7},{4,8},{5,9},{6,10},{7,11},{8,12},{9,13},{1... | collective-permute-start | bytes 743432 | tf_op jit(solution)/shard_map/ppermute | solution.py:95
  12.7 2.6 %collective-permute-start.4 = (bf16[2,4,16,1408]{3,2,1,0:T(8,128)(2,1)S(1)}, bf16[2,4,16,1408]{3,2,1,0:T(8,128)(2,1)S(1)}, u32[]{:S(2)}, u32[]{:S(2)}) collective-permute-start(bf16[2,4,16,1408]{3,2,1,0:T(8,128)(2,1)S(1)} %shard_map.73), channel_id=1, source_target_pairs={{0,18},{1,2},{2,16},{3,0},{4,22},{5,6},{6,20},{7,4},{8,26},{9,10},... | collective-permute-start | bytes 1081352 | tf_op jit(solution)/shard_map/ppermute | solution.py:95
  15.3 3.3 %collective-permute-done.1.refs_0_ = bf16[2,4,16,1408]{3,2,1,0:T(8,128)(2,1)S(1)} collective-permute-done((bf16[2,4,16,1408]{3,2,1,0:T(8,128)(2,1)S(1)}, bf16[2,4,16,1408]{3,2,1,0:T(8,128)(2,1)S(1)}, u32[]{:S(2)}, u32[]{:S(2)}) %collective-permute-start.1) | collective-permute-done | bytes 360480 | tf_op jit(solution)/shard_map/ppermute | solution.py:95
  18.6 2.4 %collective-permute-done.2.refs_1_ = bf16[2,4,16,1408]{3,2,1,0:T(8,128)(2,1)S(1)} collective-permute-done((bf16[2,4,16,1408]{3,2,1,0:T(8,128)(2,1)S(1)}, bf16[2,4,16,1408]{3,2,1,0:T(8,128)(2,1)S(1)}, u32[]{:S(2)}, u32[]{:S(2)}) %collective-permute-start.2) | collective-permute-done | bytes 360480 | tf_op jit(solution)/shard_map/ppermute | solution.py:95
  21.0 1.3 %collective-permute-start.7 = (bf16[352,352]{1,0:T(8,128)(2,1)S(1)}, bf16[352,352]{1,0:T(8,128)(2,1)S(1)}, u32[]{:S(2)}, u32[]{:S(2)}) collective-permute-start(bf16[352,352]{1,0:T(8,128)(2,1)S(1)} %collective-permute-done.6.refs_5_), channel_id=1, source_target_pairs={{0,4},{1,5},{2,6},{3,7},{4,8},{5,9},{6,10},{7,11},{8,12},{9,13},{1... | collective-permute-start | bytes 743432 | tf_op jit(solution)/shard_map/ppermute | solution.py:95
  22.4 3.7 %collective-permute-done.3.refs_2_ = bf16[2,4,16,1408]{3,2,1,0:T(8,128)(2,1)S(1)} collective-permute-done((bf16[2,4,16,1408]{3,2,1,0:T(8,128)(2,1)S(1)}, bf16[2,4,16,1408]{3,2,1,0:T(8,128)(2,1)S(1)}, u32[]{:S(2)}, u32[]{:S(2)}) %collective-permute-start.3) | collective-permute-done | bytes 360480 | tf_op jit(solution)/shard_map/ppermute | solution.py:95
  26.0 1.6 %collective-permute-start.14 = (bf16[88,528]{1,0:T(8,128)(2,1)S(1)}, bf16[88,528]{1,0:T(8,128)(2,1)S(1)}, u32[]{:S(2)}, u32[]{:S(2)}) collective-permute-start(bf16[88,528]{1,0:T(8,128)(2,1)S(1)} %get-tuple-element.47), channel_id=1, source_target_pairs={{0,3},{1,2},{2,1},{3,0},{4,7},{5,6},{6,5},{7,4},{8,11},{9,10},{10,... | collective-permute-start | bytes 278792 | tf_op jit(solution)/shard_map/ppermute | solution.py:95
  27.7 2.2 %collective-permute-done.7.refs_6_ = bf16[352,352]{1,0:T(8,128)(2,1)S(1)} collective-permute-done((bf16[352,352]{1,0:T(8,128)(2,1)S(1)}, bf16[352,352]{1,0:T(8,128)(2,1)S(1)}, u32[]{:S(2)}, u32[]{:S(2)}) %collective-permute-start.7) | collective-permute-done | bytes 247840 | tf_op jit(solution)/shard_map/ppermute | solution.py:95
  29.8 1.0 collective-permute-start.8
  30.9 3.8 %collective-permute-start = (s32[4]{0:T(128)S(1)}, s32[4]{0:T(128)S(1)}, u32[]{:S(2)}, u32[]{:S(2)}) collective-permute-start(s32[4]{0:T(128)S(1)} %copy-done.10), channel_id=1, source_target_pairs={{0,0},{1,16},{2,2},{3,18},{4,4},{5,20},{6,6},{7,22},{8,8},{9,24},{... | collective-permute-start | bytes 56 | tf_op jit(solution)/shard_map/ppermute | solution.py:95
  34.7 4.1 %copy.8 = bf16[256,4224]{0,1:T(8,128)(2,1)} copy(bf16[256,4224]{1,0:T(8,128)(2,1)} %param.11) | data formatting | bytes 4325376 | tf_op args[4]
  38.9 0.6 dynamic_slice.3
  40.2 0.9 shard_map.77.refs_0_
  41.1 0.3 collective-permute-start.15
  41.4 3.6 %collective-permute-start.22 = (bf16[352,704]{1,0:T(8,128)(2,1)S(1)}, bf16[352,704]{1,0:T(8,128)(2,1)S(1)}, u32[]{:S(2)}, u32[]{:S(2)}) collective-permute-start(bf16[352,704]{1,0:T(8,128)(2,1)S(1)} %shard_map.77.refs_0_), channel_id=1, source_target_pairs={{0,8},{1,9},{2,10},{3,11},{4,12},{5,13},{6,14},{7,15},{8,0},{9,1},... | collective-permute-start | bytes 1486856 | tf_op jit(solution)/shard_map/ppermute | solution.py:95
  45.0 0.1 collective-permute-start.10
  45.1 0.5 collective-permute-start.11
  45.6 0.1 collective-permute-start.12
  45.7 2.3 %fusion.3 = f32[1,12,352]{2,0,1:T(1,128)S(1)} fusion(bf16[256,1,1]{0,1,2:T(2,128)(2,1)S(1)} %reshape.41, bf16[12,352,256]{2,1,0:T(8,128)(2,1)} %bitcast.13), kind=kOutput, calls=%fused_computation.8 | convolution fusion | flops 2162688 | bytes 2180096 | tf_op jit(solution)/shard_map/dot_general | solution.py:30
  48.1 0.7 copy-done.7
  48.8 0.1 copy-done.8
  48.9 0.7 copy-done.9
  49.6 3.7 %shard_map.76 = (bf16[4,16,352]{2,1,0:T(8,128)(2,1)S(1)}, bf16[4,16,352]{2,1,0:T(8,128)(2,1)S(1)}, bf16[4,16,352]{2,1,0:T(8,128)(2,1)S(1)}, bf16[4,16,352]{2,1,0:T(8,128)(2,1)S(1)}) custom-call(s32[4]{0:T(128)S(1)} %pad_add_fusion.where, bf16[2,4,16,1408]{3,2,1,0:T(8,128)(2,1)} %copy-done.1, bf16[2,4,16,1408]{3,2,1,0:T(8,128)(2,1)} %copy-done.2, ...), custom_call_target="tpu_custom_call" | custom-call | flops 507510784 | bytes 6848512 | tf_op jit(solution)/shard_map/pallas_call | solution.py:105
  53.3 11.1 %collective-permute-done.15.refs_1_ = bf16[352,704]{1,0:T(8,128)(2,1)S(1)} collective-permute-done((bf16[352,704]{1,0:T(8,128)(2,1)S(1)}, bf16[352,704]{1,0:T(8,128)(2,1)S(1)}, u32[]{:S(2)}, u32[]{:S(2)}) %collective-permute-start.15) | collective-permute-done | bytes 495648 | tf_op jit(solution)/shard_map/ppermute | solution.py:95
  64.4 3.0 %collective-permute-start.17 = (bf16[4,16,352]{2,1,0:T(8,128)(2,1)S(1)}, bf16[4,16,352]{2,1,0:T(8,128)(2,1)S(1)}, u32[]{:S(2)}, u32[]{:S(2)}) collective-permute-start(bf16[4,16,352]{2,1,0:T(8,128)(2,1)S(1)} %get-tuple-element.52), channel_id=1, source_target_pairs={{0,8},{1,9},{2,10},{3,11},{4,12},{5,13},{6,14},{7,15},{8,0},{9,1},... | collective-permute-start | bytes 135176 | tf_op jit(solution)/shard_map/ppermute | solution.py:95
  67.4 0.5 collective-permute-start.18
  67.8 1.6 %collective-permute-done.16.refs_1_ = bf16[4,16,352]{2,1,0:T(8,128)(2,1)S(1)} collective-permute-done((bf16[4,16,352]{2,1,0:T(8,128)(2,1)S(1)}, bf16[4,16,352]{2,1,0:T(8,128)(2,1)S(1)}, u32[]{:S(2)}, u32[]{:S(2)}) %collective-permute-start.16) | collective-permute-done | bytes 45088 | tf_op jit(solution)/shard_map/ppermute | solution.py:95
  69.5 1.9 %collective-permute-done.17.refs_2_ = bf16[4,16,352]{2,1,0:T(8,128)(2,1)S(1)} collective-permute-done((bf16[4,16,352]{2,1,0:T(8,128)(2,1)S(1)}, bf16[4,16,352]{2,1,0:T(8,128)(2,1)S(1)}, u32[]{:S(2)}, u32[]{:S(2)}) %collective-permute-start.17) | collective-permute-done | bytes 45088 | tf_op jit(solution)/shard_map/ppermute | solution.py:95
  71.4 0.4 collective-permute-done.18.refs_3_
  71.8 0.6 shard_map.78.refs_0_
  72.4 1.0 collective-permute-start.23
  73.4 2.6 %collective-permute-start.21 = (bf16[4,4,16,352]{3,2,1,0:T(8,128)(2,1)S(1)}, bf16[4,4,16,352]{3,2,1,0:T(8,128)(2,1)S(1)}, u32[]{:S(2)}, u32[]{:S(2)}) collective-permute-start(bf16[4,4,16,352]{3,2,1,0:T(8,128)(2,1)S(1)} %shard_map.78.refs_0_), channel_id=1, source_target_pairs={{0,18},{1,19},{2,16},{3,17},{4,22},{5,23},{6,20},{7,21},{8,26},{9,... | collective-permute-start | bytes 540680 | tf_op jit(solution)/shard_map/ppermute | solution.py:95
  76.0 3.1 %collective-permute-done.19.refs_1_ = bf16[4,4,16,352]{3,2,1,0:T(8,128)(2,1)S(1)} collective-permute-done((bf16[4,4,16,352]{3,2,1,0:T(8,128)(2,1)S(1)}, bf16[4,4,16,352]{3,2,1,0:T(8,128)(2,1)S(1)}, u32[]{:S(2)}, u32[]{:S(2)}) %collective-permute-start.19) | collective-permute-done | bytes 180256 | tf_op jit(solution)/shard_map/ppermute | solution.py:95
  79.1 0.4 collective-permute-done.20.refs_2_
  79.5 3.2 %collective-permute-done.21.refs_3_ = bf16[4,4,16,352]{3,2,1,0:T(8,128)(2,1)S(1)} collective-permute-done((bf16[4,4,16,352]{3,2,1,0:T(8,128)(2,1)S(1)}, bf16[4,4,16,352]{3,2,1,0:T(8,128)(2,1)S(1)}, u32[]{:S(2)}, u32[]{:S(2)}) %collective-permute-start.21) | collective-permute-done | bytes 180256 | tf_op jit(solution)/shard_map/ppermute | solution.py:95
  82.7 2.2 %collective-permute-start.24 = (bf16[352,704]{1,0:T(8,128)(2,1)S(1)}, bf16[352,704]{1,0:T(8,128)(2,1)S(1)}, u32[]{:S(2)}, u32[]{:S(2)}) collective-permute-start(bf16[352,704]{1,0:T(8,128)(2,1)S(1)} %shard_map.77.refs_0_), channel_id=1, source_target_pairs={{0,1},{1,0},{2,3},{3,2},{4,5},{5,4},{6,7},{7,6},{8,9},{9,8},{10,11... | collective-permute-start | bytes 1486856 | tf_op jit(solution)/shard_map/ppermute | solution.py:95
  84.9 0.5 collective-permute-start.26
  85.4 0.2 collective-permute-done.23.refs_3_
  85.6 1.5 %collective-permute-start.27 = (bf16[352,704]{1,0:T(8,128)(2,1)S(1)}, bf16[352,704]{1,0:T(8,128)(2,1)S(1)}, u32[]{:S(2)}, u32[]{:S(2)}) collective-permute-start(bf16[352,704]{1,0:T(8,128)(2,1)S(1)} %collective-permute-done.23.refs_3_), channel_id=1, source_target_pairs={{0,1},{1,0},{2,3},{3,2},{4,5},{5,4},{6,7},{7,6},{8,9},{9,8},{10,11... | collective-permute-start | bytes 1486856 | tf_op jit(solution)/shard_map/ppermute | solution.py:95
  87.1 1.3 %shard_map.79 = (bf16[4,256,352]{2,1,0:T(8,128)(2,1)S(1)}, bf16[4,64,352]{2,1,0:T(8,128)(2,1)S(1)}) custom-call(s32[4]{0:T(128)S(1)} %pad_add_fusion.where, bf16[4,4,16,352]{3,2,1,0:T(8,128)(2,1)S(1)} %shard_map.78.refs_0_, bf16[4,4,16,352]{3,2,1,0:T(8,128)(2,1)S(1)} %collective-permute-done.19.refs_1_, ...), custom_call_target="tpu_custom_call" | custom-call | bytes 1475584 | tf_op jit(solution)/shard_map/pallas_call | solution.py:105
  88.5 0.3 collective-permute-done.27.refs_7_
  88.8 7.3 %shard_map.80 = (bf16[2,64,704]{2,1,0:T(8,128)(2,1)S(1)}, bf16[2,64,704]{2,1,0:T(8,128)(2,1)S(1)}, bf16[2,64,704]{2,1,0:T(8,128)(2,1)S(1)}, bf16[2,64,704]{2,1,0:T(8,128)(2,1)S(1)}) custom-call(s32[4]{0:T(128)S(1)} %pad_add_fusion.where, bf16[4,256,352]{2,1,0:T(8,128)(2,1)S(1)} %get-tuple-element.56.norm, bf16[352,704]{1,0:T(8,128)(2,1)S(1)} %shard_map.77.refs_0_, ...), custom_call_target="tpu_custom_call" | custom-call | flops 1268776960 | bytes 9371648 | tf_op jit(solution)/shard_map/pallas_call | solution.py:105
  96.1 1.5 %collective-permute-start.28 = (bf16[2,64,704]{2,1,0:T(8,128)(2,1)S(1)}, bf16[2,64,704]{2,1,0:T(8,128)(2,1)S(1)}, u32[]{:S(2)}, u32[]{:S(2)}) collective-permute-start(bf16[2,64,704]{2,1,0:T(8,128)(2,1)S(1)} %get-tuple-element.62), channel_id=1, source_target_pairs={{0,16},{1,17},{2,18},{3,19},{4,20},{5,21},{6,22},{7,23},{8,24},{9,... | collective-permute-start | bytes 540680 | tf_op jit(solution)/shard_map/ppermute | solution.py:95
  97.6 1.3 %collective-permute-start.30 = (bf16[2,64,704]{2,1,0:T(8,128)(2,1)S(1)}, bf16[2,64,704]{2,1,0:T(8,128)(2,1)S(1)}, u32[]{:S(2)}, u32[]{:S(2)}) collective-permute-start(bf16[2,64,704]{2,1,0:T(8,128)(2,1)S(1)} %get-tuple-element.64), channel_id=1, source_target_pairs={{0,18},{1,19},{2,16},{3,17},{4,22},{5,23},{6,20},{7,21},{8,26},{9,... | collective-permute-start | bytes 540680 | tf_op jit(solution)/shard_map/ppermute | solution.py:95
  98.8 3.4 %collective-permute-done.28.refs_1_ = bf16[2,64,704]{2,1,0:T(8,128)(2,1)S(1)} collective-permute-done((bf16[2,64,704]{2,1,0:T(8,128)(2,1)S(1)}, bf16[2,64,704]{2,1,0:T(8,128)(2,1)S(1)}, u32[]{:S(2)}, u32[]{:S(2)}) %collective-permute-start.28) | collective-permute-done | bytes 180256 | tf_op jit(solution)/shard_map/ppermute | solution.py:95
  102.2 1.4 %collective-permute-done.29.refs_2_ = bf16[2,64,704]{2,1,0:T(8,128)(2,1)S(1)} collective-permute-done((bf16[2,64,704]{2,1,0:T(8,128)(2,1)S(1)}, bf16[2,64,704]{2,1,0:T(8,128)(2,1)S(1)}, u32[]{:S(2)}, u32[]{:S(2)}) %collective-permute-start.29) | collective-permute-done | bytes 180256 | tf_op jit(solution)/shard_map/ppermute | solution.py:95
  103.6 3.8 %collective-permute-done.30.refs_3_ = bf16[2,64,704]{2,1,0:T(8,128)(2,1)S(1)} collective-permute-done((bf16[2,64,704]{2,1,0:T(8,128)(2,1)S(1)}, bf16[2,64,704]{2,1,0:T(8,128)(2,1)S(1)}, u32[]{:S(2)}, u32[]{:S(2)}) %collective-permute-start.30) | collective-permute-done | bytes 180256 | tf_op jit(solution)/shard_map/ppermute | solution.py:95
  107.4 0.7 shard_map.81
  108.1 3.6 %collective-permute-start.31 = (bf16[16,1408]{1,0:T(8,128)(2,1)S(1)}, bf16[16,1408]{1,0:T(8,128)(2,1)S(1)}, u32[]{:S(2)}, u32[]{:S(2)}) collective-permute-start(bf16[16,1408]{1,0:T(8,128)(2,1)S(1)} %get-tuple-element.65), channel_id=1, source_target_pairs={{0,0},{1,16},{2,2},{3,18},{4,4},{5,20},{6,6},{7,22},{8,8},{9,24},{... | collective-permute-start | bytes 135176 | tf_op jit(solution)/shard_map/ppermute | solution.py:95
  111.7 1.5 %collective-permute-start.32 = (bf16[16,1408]{1,0:T(8,128)(2,1)S(1)}, bf16[16,1408]{1,0:T(8,128)(2,1)S(1)}, u32[]{:S(2)}, u32[]{:S(2)}) collective-permute-start(bf16[16,1408]{1,0:T(8,128)(2,1)S(1)} %get-tuple-element.66), channel_id=1, source_target_pairs={{0,12},{1,28},{2,14},{3,30},{4,0},{5,16},{6,2},{7,18},{8,4},{9,20}... | collective-permute-start | bytes 135176 | tf_op jit(solution)/shard_map/ppermute | solution.py:95
  113.3 1.6 %collective-permute-start.33 = (bf16[16,1408]{1,0:T(8,128)(2,1)S(1)}, bf16[16,1408]{1,0:T(8,128)(2,1)S(1)}, u32[]{:S(2)}, u32[]{:S(2)}) collective-permute-start(bf16[16,1408]{1,0:T(8,128)(2,1)S(1)} %get-tuple-element.67), channel_id=1, source_target_pairs={{0,8},{1,24},{2,10},{3,26},{4,12},{5,28},{6,14},{7,30},{8,0},{9,16... | collective-permute-start | bytes 135176 | tf_op jit(solution)/shard_map/ppermute | solution.py:95
  114.9 1.0 collective-permute-start.34
  115.9 0.6 collective-permute-done.32.refs_1_
  116.5 2.2 %collective-permute-done.33.refs_2_ = bf16[16,1408]{1,0:T(8,128)(2,1)S(1)} collective-permute-done((bf16[16,1408]{1,0:T(8,128)(2,1)S(1)}, bf16[16,1408]{1,0:T(8,128)(2,1)S(1)}, u32[]{:S(2)}, u32[]{:S(2)}) %collective-permute-start.33) | collective-permute-done | bytes 45088 | tf_op jit(solution)/shard_map/ppermute | solution.py:95
  118.7 2.4 %collective-permute-done.34.refs_3_ = bf16[16,1408]{1,0:T(8,128)(2,1)S(1)} collective-permute-done((bf16[16,1408]{1,0:T(8,128)(2,1)S(1)}, bf16[16,1408]{1,0:T(8,128)(2,1)S(1)}, u32[]{:S(2)}, u32[]{:S(2)}) %collective-permute-start.34) | collective-permute-done | bytes 45088 | tf_op jit(solution)/shard_map/ppermute | solution.py:95
  121.1 1.2 %shard_map.82 = bf16[4,16,1408]{2,1,0:T(8,128)(2,1)} custom-call(s32[4]{0:T(128)S(1)} %pad_add_fusion.where, bf16[16,1408]{1,0:T(8,128)(2,1)S(1)} %collective-permute-done.31.refs_0_, bf16[16,1408]{1,0:T(8,128)(2,1)S(1)} %collective-permute-done.32.refs_1_, bf16[16,1408]{1,0:T(8,128)(2,1)S(1)} %collective-permute-done.33.refs_2_, ...), custom_call_target="tpu_custom_call" | custom-call | bytes 360448 | tf_op jit(solution)/shard_map/pallas_call | solution.py:105
  (47 shorter events, 0.2 us)
Async XLA Ops:
  0.0 30.9 %copy-start.10 = (s32[4]{0:T(128)S(1)}, s32[4]{0:T(128)}, u32[]{:S(2)}) copy-start(s32[4]{0:T(128)} %param.9) | copy-start | bytes 52
  2.9 7.8 %collective-permute-start.5 = (bf16[88,1232]{1,0:T(8,128)(2,1)S(1)}, bf16[88,1232]{1,0:T(8,128)(2,1)S(1)}, u32[]{:S(2)}, u32[]{:S(2)}) collective-permute-start(bf16[88,1232]{1,0:T(8,128)(2,1)S(1)} %get-tuple-element.38), channel_id=1, source_target_pairs={{0,2},{1,3},{2,0},{3,1},{4,6},{5,7},{6,4},{7,5},{8,10},{9,11},{10,... | collective-permute-start | bytes 650504 | tf_op jit(solution)/shard_map/ppermute | solution.py:95
  6.7 11.9 %collective-permute-start.1 = (bf16[2,4,16,1408]{3,2,1,0:T(8,128)(2,1)S(1)}, bf16[2,4,16,1408]{3,2,1,0:T(8,128)(2,1)S(1)}, u32[]{:S(2)}, u32[]{:S(2)}) collective-permute-start(bf16[2,4,16,1408]{3,2,1,0:T(8,128)(2,1)S(1)} %shard_map.73), channel_id=1, source_target_pairs={{0,0},{1,16},{2,2},{3,18},{4,4},{5,20},{6,6},{7,22},{8,8},{9,24},{... | collective-permute-start | bytes 1081352 | tf_op jit(solution)/shard_map/ppermute | solution.py:95
  10.5 10.5 %collective-permute-start.2 = (bf16[2,4,16,1408]{3,2,1,0:T(8,128)(2,1)S(1)}, bf16[2,4,16,1408]{3,2,1,0:T(8,128)(2,1)S(1)}, u32[]{:S(2)}, u32[]{:S(2)}) collective-permute-start(bf16[2,4,16,1408]{3,2,1,0:T(8,128)(2,1)S(1)} %shard_map.73), channel_id=1, source_target_pairs={{0,16},{1,0},{2,18},{3,2},{4,20},{5,4},{6,22},{7,6},{8,24},{9,8},{... | collective-permute-start | bytes 1081352 | tf_op jit(solution)/shard_map/ppermute | solution.py:95
  10.6 15.5 %collective-permute-start.3 = (bf16[2,4,16,1408]{3,2,1,0:T(8,128)(2,1)S(1)}, bf16[2,4,16,1408]{3,2,1,0:T(8,128)(2,1)S(1)}, u32[]{:S(2)}, u32[]{:S(2)}) collective-permute-start(bf16[2,4,16,1408]{3,2,1,0:T(8,128)(2,1)S(1)} %shard_map.73), channel_id=1, source_target_pairs={{0,2},{1,18},{2,0},{3,16},{4,6},{5,22},{6,4},{7,20},{8,10},{9,26},... | collective-permute-start | bytes 1081352 | tf_op jit(solution)/shard_map/ppermute | solution.py:95
  11.4 27.5 %copy-start = (bf16[352,352]{1,0:T(8,128)(2,1)}, bf16[352,352]{1,0:T(8,128)(2,1)S(1)}, u32[]{:S(2)}) copy-start(bf16[352,352]{1,0:T(8,128)(2,1)S(1)} %shard_map.75.refs_4_) | copy-start | bytes 743428
  11.4 9.6 %collective-permute-start.6 = (bf16[352,352]{1,0:T(8,128)(2,1)S(1)}, bf16[352,352]{1,0:T(8,128)(2,1)S(1)}, u32[]{:S(2)}, u32[]{:S(2)}) collective-permute-start(bf16[352,352]{1,0:T(8,128)(2,1)S(1)} %shard_map.75.refs_4_), channel_id=1, source_target_pairs={{0,4},{1,5},{2,6},{3,7},{4,8},{5,9},{6,10},{7,11},{8,12},{9,13},{1... | collective-permute-start | bytes 743432 | tf_op jit(solution)/shard_map/ppermute | solution.py:95
  12.7 15.0 %collective-permute-start.4 = (bf16[2,4,16,1408]{3,2,1,0:T(8,128)(2,1)S(1)}, bf16[2,4,16,1408]{3,2,1,0:T(8,128)(2,1)S(1)}, u32[]{:S(2)}, u32[]{:S(2)}) collective-permute-start(bf16[2,4,16,1408]{3,2,1,0:T(8,128)(2,1)S(1)} %shard_map.73), channel_id=1, source_target_pairs={{0,18},{1,2},{2,16},{3,0},{4,22},{5,6},{6,20},{7,4},{8,26},{9,10},... | collective-permute-start | bytes 1081352 | tf_op jit(solution)/shard_map/ppermute | solution.py:95
  18.6 20.3 %copy-start.1 = (bf16[2,4,16,1408]{3,2,1,0:T(8,128)(2,1)}, bf16[2,4,16,1408]{3,2,1,0:T(8,128)(2,1)S(1)}, u32[]{:S(2)}) copy-start(bf16[2,4,16,1408]{3,2,1,0:T(8,128)(2,1)S(1)} %collective-permute-done.1.refs_0_) | copy-start | bytes 1081348
  21.0 17.9 %copy-start.2 = (bf16[2,4,16,1408]{3,2,1,0:T(8,128)(2,1)}, bf16[2,4,16,1408]{3,2,1,0:T(8,128)(2,1)S(1)}, u32[]{:S(2)}) copy-start(bf16[2,4,16,1408]{3,2,1,0:T(8,128)(2,1)S(1)} %collective-permute-done.2.refs_1_) | copy-start | bytes 1081348
  21.0 24.0 %copy-start.5 = (bf16[352,352]{1,0:T(8,128)(2,1)}, bf16[352,352]{1,0:T(8,128)(2,1)S(1)}, u32[]{:S(2)}) copy-start(bf16[352,352]{1,0:T(8,128)(2,1)S(1)} %collective-permute-done.6.refs_5_) | copy-start | bytes 743428
  21.0 8.8 %collective-permute-start.7 = (bf16[352,352]{1,0:T(8,128)(2,1)S(1)}, bf16[352,352]{1,0:T(8,128)(2,1)S(1)}, u32[]{:S(2)}, u32[]{:S(2)}) collective-permute-start(bf16[352,352]{1,0:T(8,128)(2,1)S(1)} %collective-permute-done.6.refs_5_), channel_id=1, source_target_pairs={{0,4},{1,5},{2,6},{3,7},{4,8},{5,9},{6,10},{7,11},{8,12},{9,13},{1... | collective-permute-start | bytes 743432 | tf_op jit(solution)/shard_map/ppermute | solution.py:95
  26.0 12.8 %copy-start.3 = (bf16[2,4,16,1408]{3,2,1,0:T(8,128)(2,1)}, bf16[2,4,16,1408]{3,2,1,0:T(8,128)(2,1)S(1)}, u32[]{:S(2)}) copy-start(bf16[2,4,16,1408]{3,2,1,0:T(8,128)(2,1)S(1)} %collective-permute-done.3.refs_2_) | copy-start | bytes 1081348
  26.0 14.1 %collective-permute-start.13 = (bf16[88,1232]{1,0:T(8,128)(2,1)S(1)}, bf16[88,1232]{1,0:T(8,128)(2,1)S(1)}, u32[]{:S(2)}, u32[]{:S(2)}) collective-permute-start(bf16[88,1232]{1,0:T(8,128)(2,1)S(1)} %get-tuple-element.45), channel_id=1, source_target_pairs={{0,1},{1,0},{2,3},{3,2},{4,5},{5,4},{6,7},{7,6},{8,9},{9,8},{10,11... | collective-permute-start | bytes 650504 | tf_op jit(solution)/shard_map/ppermute | solution.py:95
  26.0 14.1 %collective-permute-start.14 = (bf16[88,528]{1,0:T(8,128)(2,1)S(1)}, bf16[88,528]{1,0:T(8,128)(2,1)S(1)}, u32[]{:S(2)}, u32[]{:S(2)}) collective-permute-start(bf16[88,528]{1,0:T(8,128)(2,1)S(1)} %get-tuple-element.47), channel_id=1, source_target_pairs={{0,3},{1,2},{2,1},{3,0},{4,7},{5,6},{6,5},{7,4},{8,11},{9,10},{10,... | collective-permute-start | bytes 278792 | tf_op jit(solution)/shard_map/ppermute | solution.py:95
  27.7 17.5 %collective-permute-start.9 = (bf16[352,352]{1,0:T(8,128)(2,1)S(1)}, bf16[352,352]{1,0:T(8,128)(2,1)}, u32[]{:S(2)}, u32[]{:S(2)}) collective-permute-start(bf16[352,352]{1,0:T(8,128)(2,1)S(1)} %shard_map.75.refs_4_), channel_id=1, source_target_pairs={{0,1},{1,0},{2,3},{3,2},{4,5},{5,4},{6,7},{7,6},{8,9},{9,8},{10,11... | collective-permute-start | bytes 743432 | tf_op jit(solution)/shard_map/ppermute | solution.py:95
  27.7 11.2 %copy-start.4 = (bf16[2,4,16,1408]{3,2,1,0:T(8,128)(2,1)}, bf16[2,4,16,1408]{3,2,1,0:T(8,128)(2,1)S(1)}, u32[]{:S(2)}) copy-start(bf16[2,4,16,1408]{3,2,1,0:T(8,128)(2,1)S(1)} %collective-permute-done.4.refs_3_) | copy-start | bytes 1081348
  29.8 15.3 %copy-start.6 = (bf16[352,352]{1,0:T(8,128)(2,1)}, bf16[352,352]{1,0:T(8,128)(2,1)S(1)}, u32[]{:S(2)}) copy-start(bf16[352,352]{1,0:T(8,128)(2,1)S(1)} %collective-permute-done.7.refs_6_) | copy-start | bytes 743428
  29.8 15.8 %collective-permute-start.8 = (bf16[352,352]{1,0:T(8,128)(2,1)S(1)}, bf16[352,352]{1,0:T(8,128)(2,1)}, u32[]{:S(2)}, u32[]{:S(2)}) collective-permute-start(bf16[352,352]{1,0:T(8,128)(2,1)S(1)} %collective-permute-done.7.refs_6_), channel_id=1, source_target_pairs={{0,4},{1,5},{2,6},{3,7},{4,8},{5,9},{6,10},{7,11},{8,12},{9,13},{1... | collective-permute-start | bytes 743432 | tf_op jit(solution)/shard_map/ppermute | solution.py:95
  30.9 8.0 %collective-permute-start = (s32[4]{0:T(128)S(1)}, s32[4]{0:T(128)S(1)}, u32[]{:S(2)}, u32[]{:S(2)}) collective-permute-start(s32[4]{0:T(128)S(1)} %copy-done.10), channel_id=1, source_target_pairs={{0,0},{1,16},{2,2},{3,18},{4,4},{5,20},{6,6},{7,22},{8,8},{9,24},{... | collective-permute-start | bytes 56 | tf_op jit(solution)/shard_map/ppermute | solution.py:95
  41.1 23.3 %collective-permute-start.15 = (bf16[352,704]{1,0:T(8,128)(2,1)S(1)}, bf16[352,704]{1,0:T(8,128)(2,1)S(1)}, u32[]{:S(2)}, u32[]{:S(2)}) collective-permute-start(bf16[352,704]{1,0:T(8,128)(2,1)S(1)} %shard_map.77.refs_0_), channel_id=1, source_target_pairs={{0,4},{1,5},{2,6},{3,7},{4,0},{5,1},{6,2},{7,3},{8,12},{9,13},{10,... | collective-permute-start | bytes 1486856 | tf_op jit(solution)/shard_map/ppermute | solution.py:95
  41.4 31.0 %collective-permute-start.22 = (bf16[352,704]{1,0:T(8,128)(2,1)S(1)}, bf16[352,704]{1,0:T(8,128)(2,1)S(1)}, u32[]{:S(2)}, u32[]{:S(2)}) collective-permute-start(bf16[352,704]{1,0:T(8,128)(2,1)S(1)} %shard_map.77.refs_0_), channel_id=1, source_target_pairs={{0,8},{1,9},{2,10},{3,11},{4,12},{5,13},{6,14},{7,15},{8,0},{9,1},... | collective-permute-start | bytes 1486856 | tf_op jit(solution)/shard_map/ppermute | solution.py:95
  45.0 3.0 %collective-permute-start.10 = (bf16[352,352]{1,0:T(8,128)(2,1)S(1)}, bf16[352,352]{1,0:T(8,128)(2,1)S(1)}, u32[]{:S(2)}, u32[]{:S(2)}) collective-permute-start(bf16[352,352]{1,0:T(8,128)(2,1)S(1)} %collective-permute-done.6.refs_5_), channel_id=1, source_target_pairs={{0,1},{1,0},{2,3},{3,2},{4,5},{5,4},{6,7},{7,6},{8,9},{9,8},{10,11... | collective-permute-start | bytes 743432 | tf_op jit(solution)/shard_map/ppermute | solution.py:95
  45.1 2.9 %collective-permute-start.11 = (bf16[352,352]{1,0:T(8,128)(2,1)S(1)}, bf16[352,352]{1,0:T(8,128)(2,1)S(1)}, u32[]{:S(2)}, u32[]{:S(2)}) collective-permute-start(bf16[352,352]{1,0:T(8,128)(2,1)S(1)} %collective-permute-done.7.refs_6_), channel_id=1, source_target_pairs={{0,1},{1,0},{2,3},{3,2},{4,5},{5,4},{6,7},{7,6},{8,9},{9,8},{10,11... | collective-permute-start | bytes 743432 | tf_op jit(solution)/shard_map/ppermute | solution.py:95
  45.6 2.5 %collective-permute-start.12 = (bf16[352,352]{1,0:T(8,128)(2,1)}, bf16[352,352]{1,0:T(8,128)(2,1)S(1)}, u32[]{:S(2)}, u32[]{:S(2)}) collective-permute-start(bf16[352,352]{1,0:T(8,128)(2,1)} %collective-permute-done.8.refs_7_), channel_id=1, source_target_pairs={{0,1},{1,0},{2,3},{3,2},{4,5},{5,4},{6,7},{7,6},{8,9},{9,8},{10,11... | collective-permute-start | bytes 743432 | tf_op jit(solution)/shard_map/ppermute | solution.py:95
  48.1 0.7 copy-start.7
  48.1 0.8 copy-start.8
  48.9 0.7 copy-start.9
  64.4 5.1 %collective-permute-start.16 = (bf16[4,16,352]{2,1,0:T(8,128)(2,1)S(1)}, bf16[4,16,352]{2,1,0:T(8,128)(2,1)S(1)}, u32[]{:S(2)}, u32[]{:S(2)}) collective-permute-start(bf16[4,16,352]{2,1,0:T(8,128)(2,1)S(1)} %get-tuple-element.50), channel_id=1, source_target_pairs={{0,4},{1,5},{2,6},{3,7},{4,8},{5,9},{6,10},{7,11},{8,12},{9,13},{1... | collective-permute-start | bytes 135176 | tf_op jit(solution)/shard_map/ppermute | solution.py:95
  64.4 7.0 %collective-permute-start.17 = (bf16[4,16,352]{2,1,0:T(8,128)(2,1)S(1)}, bf16[4,16,352]{2,1,0:T(8,128)(2,1)S(1)}, u32[]{:S(2)}, u32[]{:S(2)}) collective-permute-start(bf16[4,16,352]{2,1,0:T(8,128)(2,1)S(1)} %get-tuple-element.52), channel_id=1, source_target_pairs={{0,8},{1,9},{2,10},{3,11},{4,12},{5,13},{6,14},{7,15},{8,0},{9,1},... | collective-permute-start | bytes 135176 | tf_op jit(solution)/shard_map/ppermute | solution.py:95
  67.4 4.4 %collective-permute-start.18 = (bf16[4,16,352]{2,1,0:T(8,128)(2,1)S(1)}, bf16[4,16,352]{2,1,0:T(8,128)(2,1)S(1)}, u32[]{:S(2)}, u32[]{:S(2)}) collective-permute-start(bf16[4,16,352]{2,1,0:T(8,128)(2,1)S(1)} %get-tuple-element.54), channel_id=1, source_target_pairs={{0,12},{1,13},{2,14},{3,15},{4,0},{5,1},{6,2},{7,3},{8,4},{9,5},{1... | collective-permute-start | bytes 135176 | tf_op jit(solution)/shard_map/ppermute | solution.py:95
  72.4 13.2 %collective-permute-start.23 = (bf16[352,704]{1,0:T(8,128)(2,1)S(1)}, bf16[352,704]{1,0:T(8,128)(2,1)S(1)}, u32[]{:S(2)}, u32[]{:S(2)}) collective-permute-start(bf16[352,704]{1,0:T(8,128)(2,1)S(1)} %collective-permute-done.22.refs_2_), channel_id=1, source_target_pairs={{0,4},{1,5},{2,6},{3,7},{4,0},{5,1},{6,2},{7,3},{8,12},{9,13},{10,... | collective-permute-start | bytes 1486856 | tf_op jit(solution)/shard_map/ppermute | solution.py:95
  73.4 5.8 %collective-permute-start.19 = (bf16[4,4,16,352]{3,2,1,0:T(8,128)(2,1)S(1)}, bf16[4,4,16,352]{3,2,1,0:T(8,128)(2,1)S(1)}, u32[]{:S(2)}, u32[]{:S(2)}) collective-permute-start(bf16[4,4,16,352]{3,2,1,0:T(8,128)(2,1)S(1)} %shard_map.78.refs_0_), channel_id=1, source_target_pairs={{0,16},{1,17},{2,18},{3,19},{4,20},{5,21},{6,22},{7,23},{8,24},{9,... | collective-permute-start | bytes 540680 | tf_op jit(solution)/shard_map/ppermute | solution.py:95
  73.4 6.1 %collective-permute-start.20 = (bf16[4,4,16,352]{3,2,1,0:T(8,128)(2,1)S(1)}, bf16[4,4,16,352]{3,2,1,0:T(8,128)(2,1)S(1)}, u32[]{:S(2)}, u32[]{:S(2)}) collective-permute-start(bf16[4,4,16,352]{3,2,1,0:T(8,128)(2,1)S(1)} %shard_map.78.refs_0_), channel_id=1, source_target_pairs={{0,2},{1,3},{2,0},{3,1},{4,6},{5,7},{6,4},{7,5},{8,10},{9,11},{10,... | collective-permute-start | bytes 540680 | tf_op jit(solution)/shard_map/ppermute | solution.py:95
  73.4 9.3 %collective-permute-start.21 = (bf16[4,4,16,352]{3,2,1,0:T(8,128)(2,1)S(1)}, bf16[4,4,16,352]{3,2,1,0:T(8,128)(2,1)S(1)}, u32[]{:S(2)}, u32[]{:S(2)}) collective-permute-start(bf16[4,4,16,352]{3,2,1,0:T(8,128)(2,1)S(1)} %shard_map.78.refs_0_), channel_id=1, source_target_pairs={{0,18},{1,19},{2,16},{3,17},{4,22},{5,23},{6,20},{7,21},{8,26},{9,... | collective-permute-start | bytes 540680 | tf_op jit(solution)/shard_map/ppermute | solution.py:95
  82.7 5.8 %collective-permute-start.24 = (bf16[352,704]{1,0:T(8,128)(2,1)S(1)}, bf16[352,704]{1,0:T(8,128)(2,1)S(1)}, u32[]{:S(2)}, u32[]{:S(2)}) collective-permute-start(bf16[352,704]{1,0:T(8,128)(2,1)S(1)} %shard_map.77.refs_0_), channel_id=1, source_target_pairs={{0,1},{1,0},{2,3},{3,2},{4,5},{5,4},{6,7},{7,6},{8,9},{9,8},{10,11... | collective-permute-start | bytes 1486856 | tf_op jit(solution)/shard_map/ppermute | solution.py:95
  84.9 3.5 %collective-permute-start.25 = (bf16[352,704]{1,0:T(8,128)(2,1)S(1)}, bf16[352,704]{1,0:T(8,128)(2,1)S(1)}, u32[]{:S(2)}, u32[]{:S(2)}) collective-permute-start(bf16[352,704]{1,0:T(8,128)(2,1)S(1)} %collective-permute-done.15.refs_1_), channel_id=1, source_target_pairs={{0,1},{1,0},{2,3},{3,2},{4,5},{5,4},{6,7},{7,6},{8,9},{9,8},{10,11... | collective-permute-start | bytes 1486856 | tf_op jit(solution)/shard_map/ppermute | solution.py:95
  84.9 3.5 %collective-permute-start.26 = (bf16[352,704]{1,0:T(8,128)(2,1)S(1)}, bf16[352,704]{1,0:T(8,128)(2,1)S(1)}, u32[]{:S(2)}, u32[]{:S(2)}) collective-permute-start(bf16[352,704]{1,0:T(8,128)(2,1)S(1)} %collective-permute-done.22.refs_2_), channel_id=1, source_target_pairs={{0,1},{1,0},{2,3},{3,2},{4,5},{5,4},{6,7},{7,6},{8,9},{9,8},{10,11... | collective-permute-start | bytes 1486856 | tf_op jit(solution)/shard_map/ppermute | solution.py:95
  85.6 3.2 %collective-permute-start.27 = (bf16[352,704]{1,0:T(8,128)(2,1)S(1)}, bf16[352,704]{1,0:T(8,128)(2,1)S(1)}, u32[]{:S(2)}, u32[]{:S(2)}) collective-permute-start(bf16[352,704]{1,0:T(8,128)(2,1)S(1)} %collective-permute-done.23.refs_3_), channel_id=1, source_target_pairs={{0,1},{1,0},{2,3},{3,2},{4,5},{5,4},{6,7},{7,6},{8,9},{9,8},{10,11... | collective-permute-start | bytes 1486856 | tf_op jit(solution)/shard_map/ppermute | solution.py:95
  96.1 6.2 %collective-permute-start.28 = (bf16[2,64,704]{2,1,0:T(8,128)(2,1)S(1)}, bf16[2,64,704]{2,1,0:T(8,128)(2,1)S(1)}, u32[]{:S(2)}, u32[]{:S(2)}) collective-permute-start(bf16[2,64,704]{2,1,0:T(8,128)(2,1)S(1)} %get-tuple-element.62), channel_id=1, source_target_pairs={{0,16},{1,17},{2,18},{3,19},{4,20},{5,21},{6,22},{7,23},{8,24},{9,... | collective-permute-start | bytes 540680 | tf_op jit(solution)/shard_map/ppermute | solution.py:95
  97.6 6.0 %collective-permute-start.29 = (bf16[2,64,704]{2,1,0:T(8,128)(2,1)S(1)}, bf16[2,64,704]{2,1,0:T(8,128)(2,1)S(1)}, u32[]{:S(2)}, u32[]{:S(2)}) collective-permute-start(bf16[2,64,704]{2,1,0:T(8,128)(2,1)S(1)} %get-tuple-element.63), channel_id=1, source_target_pairs={{0,2},{1,3},{2,0},{3,1},{4,6},{5,7},{6,4},{7,5},{8,10},{9,11},{10,... | collective-permute-start | bytes 540680 | tf_op jit(solution)/shard_map/ppermute | solution.py:95
  97.6 9.8 %collective-permute-start.30 = (bf16[2,64,704]{2,1,0:T(8,128)(2,1)S(1)}, bf16[2,64,704]{2,1,0:T(8,128)(2,1)S(1)}, u32[]{:S(2)}, u32[]{:S(2)}) collective-permute-start(bf16[2,64,704]{2,1,0:T(8,128)(2,1)S(1)} %get-tuple-element.64), channel_id=1, source_target_pairs={{0,18},{1,19},{2,16},{3,17},{4,22},{5,23},{6,20},{7,21},{8,26},{9,... | collective-permute-start | bytes 540680 | tf_op jit(solution)/shard_map/ppermute | solution.py:95
  108.1 7.8 %collective-permute-start.31 = (bf16[16,1408]{1,0:T(8,128)(2,1)S(1)}, bf16[16,1408]{1,0:T(8,128)(2,1)S(1)}, u32[]{:S(2)}, u32[]{:S(2)}) collective-permute-start(bf16[16,1408]{1,0:T(8,128)(2,1)S(1)} %get-tuple-element.65), channel_id=1, source_target_pairs={{0,0},{1,16},{2,2},{3,18},{4,4},{5,20},{6,6},{7,22},{8,8},{9,24},{... | collective-permute-start | bytes 135176 | tf_op jit(solution)/shard_map/ppermute | solution.py:95
  111.7 4.8 %collective-permute-start.32 = (bf16[16,1408]{1,0:T(8,128)(2,1)S(1)}, bf16[16,1408]{1,0:T(8,128)(2,1)S(1)}, u32[]{:S(2)}, u32[]{:S(2)}) collective-permute-start(bf16[16,1408]{1,0:T(8,128)(2,1)S(1)} %get-tuple-element.66), channel_id=1, source_target_pairs={{0,12},{1,28},{2,14},{3,30},{4,0},{5,16},{6,2},{7,18},{8,4},{9,20}... | collective-permute-start | bytes 135176 | tf_op jit(solution)/shard_map/ppermute | solution.py:95
  113.3 5.5 %collective-permute-start.33 = (bf16[16,1408]{1,0:T(8,128)(2,1)S(1)}, bf16[16,1408]{1,0:T(8,128)(2,1)S(1)}, u32[]{:S(2)}, u32[]{:S(2)}) collective-permute-start(bf16[16,1408]{1,0:T(8,128)(2,1)S(1)} %get-tuple-element.67), channel_id=1, source_target_pairs={{0,8},{1,24},{2,10},{3,26},{4,12},{5,28},{6,14},{7,30},{8,0},{9,16... | collective-permute-start | bytes 135176 | tf_op jit(solution)/shard_map/ppermute | solution.py:95
  114.9 6.2 %collective-permute-start.34 = (bf16[16,1408]{1,0:T(8,128)(2,1)S(1)}, bf16[16,1408]{1,0:T(8,128)(2,1)S(1)}, u32[]{:S(2)}, u32[]{:S(2)}) collective-permute-start(bf16[16,1408]{1,0:T(8,128)(2,1)S(1)} %get-tuple-element.68), channel_id=1, source_target_pairs={{0,4},{1,20},{2,6},{3,22},{4,8},{5,24},{6,10},{7,26},{8,12},{9,28}... | collective-permute-start | bytes 135176 | tf_op jit(solution)/shard_map/ppermute | solution.py:95
